TPU v7x, 512 devices: a whole 4x4x16 slice. The times are simulated.
512 devices in a mesh: fsdp: 32 (over x, y, core), tensor: 16 (over z).
Axes of the slice: x: 4, y: 4, z: 16, core: 2. Of those that a mesh axis runs over, the one named last changes fastest.
Arguments:
- momentum: bfloat16 [10, 2, 4096, 1536], P(None, None, 'fsdp', 'tensor'), may hold values from -6 to 6
- gradient: bfloat16 [10, 2, 4096, 1536], P(None, None, 'fsdp', 'tensor'), may hold values from -4.2 to 4.2
- right_in: bfloat16 [10, 2, 1536, 128], P(None, None, 'tensor'), may hold values from -6 to 6
- owners: int32 [10], replicated, may hold values from 0 to 15, as said below
Outputs:
- state_out: bfloat16 [32, 2, 4096, 1536], P('tensor', None, 'fsdp')
- left_out: float32 [32, 2, 4096, 128], P('tensor', None, 'fsdp')
- right_out: float32 [10, 2, 1536, 128], P(None, None, 'tensor')
Inputs may be any that keep to these rules, and one draw needn't show every extreme that they name: `owners`: each entry is a tensor index. No tensor index takes more than 2 experts, and some index takes exactly 2.
All inputs are finite; a program needn't handle non-finite values.
Results may differ from a plain program's by a relative error of at most 0.0072.
Values may be sent and summed in bfloat16 or wider, within the bound.
No kernel may reach another device: no remote copies, remote signals or barrier semaphores. Data moves between devices by JAX's collectives and lax.ppermute only.
A program may use at most 64 MiB of HBM per device.

v0:
```python
import math

import jax
import jax.numpy as jnp
from jax import lax
from jax.sharding import PartitionSpec as P

D = 4096
CAP = 2


ridge_term = 0.001
feedback = 0.1
epsilon = 1e-06


def orthonormal(panel, gram_total):
    eye_matrix = jnp.eye(gram_total.shape[-1], dtype=jnp.float32)
    lower_factor = jnp.linalg.cholesky(gram_total + ridge_term * eye_matrix)
    solved = jax.scipy.linalg.solve_triangular(
        lower_factor, jnp.swapaxes(panel, -1, -2), lower=True
    )
    return jnp.swapaxes(solved, -1, -2)


def slot_table(owners, groups, capacity):
    count = owners.shape[0]
    index_line = jnp.arange(count, dtype=jnp.int32)
    same_owner = owners[:, None] == owners[None, :]
    earlier = index_line[None, :] < index_line[:, None]
    position = jnp.sum((same_owner & earlier).astype(jnp.int32), axis=1)
    owner_hit = owners[:, None, None] == jnp.arange(groups, dtype=jnp.int32)[None, :, None]
    slot_hit = position[:, None, None] == jnp.arange(capacity, dtype=jnp.int32)[None, None, :]
    return (owner_hit & slot_hit).astype(jnp.float32)


def shards(momentum, gradient, right_in, owners):
    highest = lax.Precision.HIGHEST
    groups = lax.axis_size("tensor")
    rows = momentum.shape[2]
    columns = momentum.shape[3]
    owner_table = slot_table(owners, groups, CAP)
    table_low = owner_table.astype(jnp.bfloat16)
    summed = (momentum.astype(jnp.float32) + gradient.astype(jnp.float32)).astype(jnp.bfloat16)
    scale = math.sqrt(D)
    send_state = jnp.einsum(
        "edc,emrk->cmrdk", table_low, summed, preferred_element_type=jnp.float32
    ).astype(jnp.bfloat16)
    send_right = jnp.einsum(
        "edc,emkq->cmkdq", table_low, right_in, preferred_element_type=jnp.float32
    ).astype(jnp.bfloat16)
    got_state, got_right = (
        lax.all_to_all(send_state, "tensor", split_axis=3, concat_axis=3, tiled=True),
        lax.all_to_all(send_right, "tensor", split_axis=3, concat_axis=3, tiled=True),
    )
    panel = jnp.einsum(
        "cmrtk,cmktq->cmrq", got_state, got_right, preferred_element_type=jnp.float32
    )
    gram_part = jnp.einsum("cmrq,cmrs->cmqs", panel, panel, precision=highest)
    gram_total = lax.psum(gram_part, "fsdp")
    ortho = orthonormal(panel, gram_total)
    ortho_low = ortho.astype(jnp.bfloat16)
    factor_part = jnp.einsum(
        "cmrtk,cmrq->cmktq", got_state, ortho_low, preferred_element_type=jnp.float32
    )
    factor = lax.psum(factor_part, "fsdp")
    mean_square = jnp.mean(factor * factor, axis=(2, 3))
    right_new = factor * lax.rsqrt(mean_square + epsilon)[:, :, None, None, :]
    update = jnp.einsum("cmrq,cmktq->cmrtk", ortho, factor, precision=highest)
    fresh = (got_state.astype(jnp.float32) - feedback * update).astype(jnp.bfloat16)
    state_out = fresh.reshape(CAP, fresh.shape[1], rows, groups * columns)
    left_out = ortho * scale
    returned = lax.all_to_all(right_new, "tensor", split_axis=3, concat_axis=3, tiled=True)
    right_out = jnp.einsum("edc,cmkdq->emkq", owner_table, returned, precision=highest)
    return (state_out, left_out, right_out)


def solution(mesh):
    return jax.shard_map(
        shards,
        mesh=mesh,
        in_specs=(
            P(None, None, "fsdp", "tensor"),
            P(None, None, "fsdp", "tensor"),
            P(None, None, "tensor", None),
            P(),
        ),
        out_specs=(
            P("tensor", None, "fsdp", None),
            P("tensor", None, "fsdp", None),
            P(None, None, "tensor", None),
        ),
        check_vma=False,
    )
```

profile of v0, /device:TPU:1, one launch (start us, length us, event | category | flops | bytes accessed | tf_op | source)
XLA Modules:
  0.0 713.5 jit_solution(16473253318640347688)
XLA Ops:
  7.2 0.9 convert_reduce_fusion
  8.1 0.7 iota_compare_fusion.3
  8.8 1.3 fusion.20
  10.1 0.7 fusion.12
  10.8 2.8 copy.61
  13.6 15.9 %all-to-all-start = ((bf16[2,2,128,16,96]{2,0,4,1,3:T(2,128)(2,1)}), bf16[2,2,128,16,96]{2,0,4,1,3:T(2,128)(2,1)S(1)}, u32[]{:S(2)}, u32[]{:S(2)}) async-start(bf16[2,2,128,16,96]{2,0,4,1,3:T(2,128)(2,1)} %copy.61), calls=%async_computation | async-start | bytes 3145728 | tf_op jit(solution)/shard_map/all_to_all | solution.py:53
  29.5 0.0 copy-done.4
  29.5 0.7 fusion.13
  30.2 1.6 copy.65
  31.8 66.6 %all-to-all-done = bf16[2,2,128,16,96]{2,0,4,1,3:T(2,128)(2,1)S(1)} async-done(((bf16[2,2,128,16,96]{2,0,4,1,3:T(2,128)(2,1)}), bf16[2,2,128,16,96]{2,0,4,1,3:T(2,128)(2,1)S(1)}, u32[]{:S(2)}, u32[]{:S(2)}) %all-to-all-start) | async-done | bytes 1572896 | tf_op jit(solution)/shard_map/all_to_all | solution.py:53
  98.4 11.6 %all-to-all-start.1 = ((bf16[2,2,96,16,128]{4,2,1,0,3:T(8,128)(2,1)}), bf16[2,2,96,16,128]{4,2,1,0,3:T(8,128)(2,1)S(1)}, u32[]{:S(2)}, u32[]{:S(2)}) async-start(bf16[2,2,96,16,128]{4,2,1,0,3:T(8,128)(2,1)} %copy.65), calls=%async_computation.1 | async-start | bytes 3145728 | tf_op jit(solution)/shard_map/all_to_all | solution.py:54
  110.0 0.0 all-reduce.3.cloned.1.call-start
  110.1 68.9 %all-to-all-done.1 = bf16[2,2,96,16,128]{4,2,1,0,3:T(8,128)(2,1)S(1)} async-done(((bf16[2,2,96,16,128]{4,2,1,0,3:T(8,128)(2,1)}), bf16[2,2,96,16,128]{4,2,1,0,3:T(8,128)(2,1)S(1)}, u32[]{:S(2)}, u32[]{:S(2)}) %all-to-all-start.1) | async-done | bytes 1572896 | tf_op jit(solution)/shard_map/all_to_all | solution.py:54
  179.0 0.6 fusion.14
  179.6 0.0 copy-start.2
  179.6 0.7 copy-done.2
  180.3 1.3 fusion.40
  181.6 0.0 all-reduce.3.cloned.1.call-update
  181.6 0.2 all-reduce.5.cloned.1.call-start
  181.9 0.1 copy.70
  182.0 0.0 copy-done.1
  182.0 0.2 copy.66
  182.2 0.0 copy-start.3
  182.3 132.5 %all-reduce.3.cloned.1.call-done = f32[2,2,128,128]{2,3,1,0:T(8,128)} async-done(((f32[2,2,128,128]{2,3,1,0:T(8,128)}), f32[2,2,128,128]{2,3,1,0:T(8,128)}) %all-reduce.3.cloned.1.call-update) | async-done | bytes 262160 | tf_op jit(solution)/shard_map/psum | solution.py:60
  314.7 1.0 broadcast_add_fusion
  315.7 0.1 copy.71
  315.8 1.0 fusion.24
  316.8 46.9 %custom-call.8 = f32[2,2,128,128]{3,2,1,0:T(8,128)S(1)} custom-call(f32[2,2,128,128]{3,2,1,0:T(8,128)S(1)} %fusion.24), custom_call_target="Cholesky" | custom-call | tf_op jit(solution)/shard_map/jit(cholesky)/cholesky | solution.py:19
  363.8 0.1 compare_reduce_fusion
  363.9 0.1 select_bitcast_fusion
  364.0 39.3 %custom-call.9 = f32[2,2,1,128,128]{3,4,2,1,0:T(8,128)S(1)} custom-call(f32[2,2,1,128,128]{4,3,2,1,0:T(8,128)S(1)} %select_bitcast_fusion), custom_call_target="InvertDiagBlocksLowerTriangular" | custom-call | tf_op jit(solution)/shard_map/jit(_solve_triangular)/vmap(vmap())/triangular_solve | solution.py:20
  403.4 0.6 fusion.22
  404.0 2.3 fusion.25
  406.2 0.0 all-reduce.5.cloned.1.call-update
  406.3 140.5 %all-reduce.5.cloned.1.call-done = f32[2,2,96,16,128]{4,2,3,1,0:T(8,128)} async-done(((f32[2,2,96,16,128]{4,2,3,1,0:T(8,128)}), f32[2,2,96,16,128]{4,2,3,1,0:T(8,128)}) %all-reduce.5.cloned.1.call-update) | async-done | bytes 3145744 | tf_op jit(solution)/shard_map/psum | solution.py:66
  546.7 2.3 multiply_reduce_fusion
  549.1 0.5 copy-done
  549.6 0.3 broadcast_multiply_fusion
  549.8 1.9 copy.76
  551.7 12.1 %all-to-all-start.2 = ((f32[2,2,96,16,128]{4,2,1,0,3:T(8,128)}), f32[2,2,96,16,128]{4,2,1,0,3:T(8,128)}, u32[]{:S(2)}, u32[]{:S(2)}) async-start(f32[2,2,96,16,128]{4,2,1,0,3:T(8,128)} %copy.76), calls=%async_computation.2 | async-start | bytes 6291456 | tf_op jit(solution)/shard_map/all_to_all | solution.py:73
  563.8 0.7 multiply_bitcast_fusion
  564.5 1.8 copy.79
  566.3 6.6 fusion
  572.9 0.4 copy.75
  573.3 1.6 copy.78
  574.9 125.7 %all-to-all-done.2 = f32[2,2,96,16,128]{4,2,1,0,3:T(8,128)} async-done(((f32[2,2,96,16,128]{4,2,1,0,3:T(8,128)}), f32[2,2,96,16,128]{4,2,1,0,3:T(8,128)}, u32[]{:S(2)}, u32[]{:S(2)}) %all-to-all-start.2) | async-done | bytes 3145760 | tf_op jit(solution)/shard_map/all_to_all | solution.py:73
  700.6 4.8 fusion.9
  705.5 1.2 copy.80
  (10 shorter events, 0.1 us)
Async XLA Ops:
  13.6 15.9 %copy-start.4 = (bf16[10,2,96,128]{3,2,1,0:T(8,128)(2,1)S(1)}, bf16[10,2,96,128]{3,2,1,0:T(8,128)(2,1)}, u32[]{:S(2)}) copy-start(bf16[10,2,96,128]{3,2,1,0:T(8,128)(2,1)} %param.6) | copy-start | bytes 1474564
  13.6 84.8 %all-to-all-start = ((bf16[2,2,128,16,96]{2,0,4,1,3:T(2,128)(2,1)}), bf16[2,2,128,16,96]{2,0,4,1,3:T(2,128)(2,1)S(1)}, u32[]{:S(2)}, u32[]{:S(2)}) async-start(bf16[2,2,128,16,96]{2,0,4,1,3:T(2,128)(2,1)} %copy.61), calls=%async_computation | async-start | bytes 3145728 | tf_op jit(solution)/shard_map/all_to_all | solution.py:53
  98.4 83.6 %copy-start.1 = (bf16[2,2,128,16,96]{2,0,4,1,3:T(2,128)(2,1)}, bf16[2,2,128,16,96]{2,0,4,1,3:T(2,128)(2,1)S(1)}, u32[]{:S(2)}) copy-start(bf16[2,2,128,16,96]{2,0,4,1,3:T(2,128)(2,1)S(1)} %all-to-all-done) | copy-start | bytes 4718596
  98.4 80.6 %all-to-all-start.1 = ((bf16[2,2,96,16,128]{4,2,1,0,3:T(8,128)(2,1)}), bf16[2,2,96,16,128]{4,2,1,0,3:T(8,128)(2,1)S(1)}, u32[]{:S(2)}, u32[]{:S(2)}) async-start(bf16[2,2,96,16,128]{4,2,1,0,3:T(8,128)(2,1)} %copy.65), calls=%async_computation.1 | async-start | bytes 3145728 | tf_op jit(solution)/shard_map/all_to_all | solution.py:54
  110.0 204.7 %all-reduce.3.cloned.1.call-start = ((), (), s32[]{:S(2)}) async-start(), calls=%async_computation.3 | async-start | bytes 524288 | tf_op jit(solution)/shard_map/psum | solution.py:60
  179.6 0.7 copy-start.2
  181.6 365.1 %all-reduce.5.cloned.1.call-start = ((), (), s32[]{:S(2)}) async-start(), calls=%async_computation.4 | async-start | bytes 6291456 | tf_op jit(solution)/shard_map/psum | solution.py:66
  182.2 221.1 %copy-start.3 = (f32[2,2,128,128]{3,2,1,0:T(8,128)S(1)}, f32[2,2,128,128]{3,2,1,0:T(8,128)}, u32[]{:S(2)}) copy-start(f32[2,2,128,128]{3,2,1,0:T(8,128)} %copy-done.2) | copy-start | bytes 786436
  546.7 2.8 copy-start
  551.7 148.9 %all-to-all-start.2 = ((f32[2,2,96,16,128]{4,2,1,0,3:T(8,128)}), f32[2,2,96,16,128]{4,2,1,0,3:T(8,128)}, u32[]{:S(2)}, u32[]{:S(2)}) async-start(f32[2,2,96,16,128]{4,2,1,0,3:T(8,128)} %copy.76), calls=%async_computation.2 | async-start | bytes 6291456 | tf_op jit(solution)/shard_map/all_to_all | solution.py:73
Sparse Core Ops, SparseCore 0:
  181.8 132.9 all-reduce.2
  406.4 140.2 all-reduce.4
where the time goes:
time: 716 us; the launch traced here: 714 us
  waiting for transfers between devices  534 us (75%)
  other arithmetic  94.8 us (13%)
  starting transfers between devices  39.8 us (6%)
  matrix products  17.6 us (2%)
  between operations  14.2 us (2%)
  local copies, waits for them, and re-layouts  12.9 us (2%)
    psum x1, waiting for transfers between devices, shards(): factor = lax.psum(factor_part, 'fsdp')  140 us
    psum x1, waiting for transfers between devices, shards(): gram_total = lax.psum(gram_part, 'fsdp')  132 us
    all_to_all x1, waiting for transfers between devices, shards(): lax.all_to_all(right_new, 'tensor', split_axis=3, concat_axis=3, tiled=True)  126 us
    all_to_all x1, waiting for transfers between devices, shards(): lax.all_to_all(send_right, 'tensor', split_axis=3, concat_axis=3, tiled=T...  68.9 us
    all_to_all x1, waiting for transfers between devices, shards(): lax.all_to_all(send_state, 'tensor', split_axis=3, concat_axis=3, tiled=T...  66.6 us
    another operation x4, other arithmetic, orthonormal(): lower_factor = jnp.linalg.cholesky(gram_total + ridge_term * eye_matrix)  47.1 us
    another operation x3, other arithmetic, orthonormal(): jax.scipy.linalg.solve_triangular(lower_factor, jnp.swapaxes(panel, -1, -...  39.5 us
    all_to_all x1, starting transfers between devices, shards(): lax.all_to_all(send_state, 'tensor', split_axis=3, concat_axis=3, tiled=T...  15.9 us
  transfers between devices with their start and end apart: 5, of which 5 were waited for; matrix products, arithmetic and copies ran while one was open for 2% of the time, Pallas kernels for 0%

commit v1 on v0

v1 whole, which is shorter than its diff:
```python
import functools
import math

import jax
import jax.numpy as jnp
from jax import lax
from jax.experimental import pallas as pl
from jax.experimental.pallas import tpu as pltpu
from jax.sharding import Mesh
from jax.sharding import PartitionSpec as P

D = 4096
HID = 1536
CAP = 2
EXPERTS = 10
GROUPS = 16
BLOCK = 96
RANK = 128

ridge_term = 0.001
feedback = 0.1
epsilon = 1e-06

F32 = jnp.float32
BF16 = jnp.bfloat16
HIGHEST = lax.Precision.HIGHEST
XY = ("x", "y")
FSDP = ("x", "y", "c")
SWAP = [(0, 1), (1, 0)]
VMEM = pl.BlockSpec(memory_space=pltpu.VMEM)
SMEM = pl.BlockSpec(memory_space=pltpu.SMEM)


def call(body, outs, scratch=(), flops=0, specs=None, n_in=0):
    return pl.pallas_call(
        body,
        out_shape=outs,
        in_specs=specs if specs is not None else [VMEM] * n_in,
        out_specs=jax.tree.map(lambda _: VMEM, outs),
        scratch_shapes=list(scratch),
        compiler_params=pltpu.CompilerParams(vmem_limit_bytes=48 * 1024 * 1024),
        cost_estimate=pl.CostEstimate(flops=flops, bytes_accessed=4_000_000, transcendentals=0),
    )


def dot(a, b, contract=((1,), (0,)), precision=None):
    return lax.dot_general(
        a, b, (contract, ((), ())), precision=precision, preferred_element_type=F32
    )


def iota(shape, dim):
    return lax.broadcasted_iota(jnp.int32, shape, dim)


def fill_table(own, table, count):
    for g in range(GROUPS):
        count[g] = 0
    for s in range(GROUPS * CAP):
        table[s] = EXPERTS
    for e in range(EXPERTS):
        g = own[e]
        p = count[g]
        count[g] = p + 1
        table[g * CAP + p] = e


def tile_row(position):
    t = position & 7
    return jnp.where(t >= 3, t - 3 + BLOCK, t)


def slice_right(own, place, right, out, table, count, held):
    fill_table(own, table, count)
    f = place[0] * 8 + place[1] * 2 + place[2]
    t = iota((8, 192), 0)
    pick = ((iota((8, 192), 1) == tile_row(t) + 3 * f) & (t < 6)).astype(BF16)
    for e in range(EXPERTS):
        held[e] = dot(pick, right[e].reshape(192, RANK))
    held[EXPERTS] = jnp.zeros((8, RANK), F32)

    def group(g, _):
        pair = jnp.concatenate([held[table[g * CAP]], held[table[g * CAP + 1]]], axis=0)
        out[g] = pair.astype(BF16)
        return 0

    lax.fori_loop(0, GROUPS, group, 0)


def place_state(own, momentum, gradient, out, table, count):
    fill_table(own, table, count)

    def slot(s, _):
        e = table[s]

        @pl.when(e < EXPERTS)
        def _():
            total = momentum[e].astype(F32) + gradient[e].astype(F32)
            out[s] = total.astype(BF16).reshape(192, 128)

        @pl.when(e >= EXPERTS)
        def _():
            out[s] = jnp.zeros((192, 128), BF16)

        return 0

    lax.fori_loop(0, GROUPS * CAP, slot, 0)


def offset(i):
    return jnp.where(i == 1, 3, jnp.where(i == 2, 1, jnp.where(i == 3, 2, 0)))


def unpermute_matrix(place, core):
    col = iota((384, 256), 1)
    chip = col >> 4
    x = (place[0] + offset(chip & 3)) & 3
    y = (place[1] + offset(chip >> 2)) & 3
    f = x * 8 + y * 2 + core
    target = ((col >> 3) & 1) * 192 + tile_row(col) + 3 * f
    return ((iota((384, 256), 0) == target) & ((col & 7) < 6)).astype(BF16)


def join_right(place, near, far, out, matrix):
    c = place[2]
    matrix[:, :256] = unpermute_matrix(place, c)
    matrix[:, 256:] = unpermute_matrix(place, 1 - c)

    def block(z, _):
        a = near[:, z].reshape(256, RANK)
        b = far[:, z].reshape(256, RANK)
        both = jnp.concatenate([a, b], axis=0)
        out[z] = dot(matrix[...], both).astype(BF16)
        return 0

    lax.fori_loop(0, GROUPS, block, 0)


def split3(value):
    high = value.astype(BF16)
    rest = value - high.astype(F32)
    middle = rest.astype(BF16)
    low = (rest - middle.astype(F32)).astype(BF16)
    return high, middle, low


def permute_matrix(place, kind):
    row = iota((256, BLOCK), 0)
    f = ((row >> 3) & 15) * 2 + ((row >> 7) ^ place[2])
    t = row & 7
    j = t - 3 * kind
    return ((iota((256, BLOCK), 1) == 3 * f + j) & (j >= 0) & (j < 3)).astype(BF16)


def panels(state, right, panel, gram):
    for i in range(2 * CAP):
        rows = pl.ds(i * BLOCK, BLOCK)

        def block(z, total):
            return total + dot(state[z, rows, :], right[z, rows, :], ((0,), (0,)))

        value = lax.fori_loop(0, GROUPS, block, jnp.zeros((128, RANK), F32), unroll=4)
        panel[i] = value
        gram[i] = dot(value, value, ((0,), (0,)), HIGHEST)


def weigh(place, state, panel, keep, send):
    order = [permute_matrix(place, k) for k in range(2)]
    for s in range(CAP):
        parts = [split3(panel[2 * s + k]) for k in range(2)]
        stacked = [jnp.concatenate([parts[0][i], parts[1][i]], axis=0) for i in range(3)]

        def block(z, _):
            moved = [
                dot(order[k], state[z, pl.ds((2 * s + k) * BLOCK, BLOCK), :]).astype(BF16)
                for k in range(2)
            ]
            wide = jnp.concatenate(moved, axis=1)
            value = dot(wide, stacked[0]) + (dot(wide, stacked[1]) + dot(wide, stacked[2]))
            rows = pl.ds(s * 8, 8)
            keep[:, z, rows, :] = value[:128].reshape(16, 8, RANK)
            send[:, z, rows, :] = value[128:].reshape(16, 8, RANK)
            return 0

        lax.fori_loop(0, GROUPS, block, 0)


def invert(gram, out, work, *, count, size):
    n = RANK
    eye = (iota((n, n), 0) == iota((n, n), 1)).astype(F32)
    for m in range(count):
        work[m, :, :n] = gram[m] + ridge_term * eye
        work[m, :, n:] = eye
    row = iota((size, 2 * n), 0)
    lane = iota((size, n), 1)
    for k in range(0, n, size):
        blocks = [work[m, k : k + size, :] for m in range(count)]
        for i in range(size):
            for m in range(count):
                b = blocks[m]
                scale = lax.rsqrt(b[i : i + 1, k + i : k + i + 1])
                line = b[i : i + 1, :] * scale
                column = jnp.where(row > i, b[:, k + i : k + i + 1] * scale, 0.0)
                blocks[m] = jnp.where(row == i, line, b - column * line)
        for m in range(count):
            b = blocks[m]
            out[m, k : k + size, :] = b[:, n:]
            if k + size < n:
                left = jnp.where(lane >= k + size, b[:, :n], 0.0)
                change = dot(left, b, ((0,), (0,)), HIGHEST)
                work[m, k + size :, :] -= change[k + size :, :]


def scale_factor(parts, inverse, out):
    total = parts[0]
    for i in range(1, 16):
        total = total + parts[i]
    rows = GROUPS * 8
    t = iota((rows, RANK), 0) & 7
    tiles = []
    for s in range(CAP):
        w = total[:, s * 8 : (s + 1) * 8, :].reshape(rows, RANK)
        both = [dot(w, inverse[2 * s + k], ((1,), (1,)), HIGHEST) for k in range(2)]
        value = jnp.where(t < 3, both[0], both[1])
        square = value * value
        sums = [
            jnp.sum(jnp.where((t >= 3 * k) & (t < 3 * k + 3), square, 0.0), axis=0, keepdims=True)
            for k in range(2)
        ]
        value = jnp.where(t == 6, sums[0], jnp.where(t == 7, sums[1], value))
        tiles.append(value.reshape(GROUPS, 8, RANK))
    out[...] = jnp.concatenate(tiles, axis=1).astype(BF16)


def orthonormal(panel, inverse, left, low):
    for i in range(2 * CAP):
        ortho = dot(panel[i], inverse[i], ((1,), (1,)), HIGHEST)
        left[i] = ortho * math.sqrt(D)
        low[i] = (ortho * (-feedback)).astype(BF16)


def select(own, tiles, out, table, count, held, packed):
    fill_table(own, table, count)
    for g in range(GROUPS):
        value = tiles[g].astype(F32)
        for s in range(CAP):
            held[table[g * CAP + s]] = value[s * 8 : (s + 1) * 8]
    for e in range(0, EXPERTS, 2):
        packed[e * 8 : e * 8 + 16, :] = jnp.concatenate([held[e], held[e + 1]], axis=0).astype(BF16)
    value = packed[...]
    for i in range(16):
        out[i] = value


def finish_right(place, near, far, out):
    col = iota((392, 256), 1)
    row = iota((392, 256), 0)
    t = col & 7
    s = (col >> 3) & 1
    matrices = []
    for core in (place[2], 1 - place[2]):
        f = (col >> 4) * 2 + core
        target = jnp.where(t < 6, s * 192 + tile_row(col) + 3 * f, 384 + s * 2 + (t - 6))
        matrices.append((row == target).astype(BF16))
    both = jnp.concatenate(matrices, axis=1)
    for g in range(EXPERTS // 2):
        rows = slice(g * 16, (g + 1) * 16)
        data = jnp.concatenate(
            [near[:, rows, :].reshape(256, RANK), far[:, rows, :].reshape(256, RANK)], axis=0
        )
        value = dot(both, data)
        for s in range(2):
            for k in range(2):
                i = 2 * s + k
                scale = lax.rsqrt(value[384 + i : 385 + i, :] * (1.0 / HID) + epsilon)
                out[2 * g + s, k] = value[i * BLOCK : (i + 1) * BLOCK, :] * scale


def finish_state(place, state, near, far, low, out, matrix, wide):
    c = place[2]
    matrix[:, :256] = unpermute_matrix(place, c)
    matrix[:, 256:] = unpermute_matrix(place, 1 - c)

    def block(z, _):
        both = jnp.concatenate(
            [near[:, z].reshape(256, RANK), far[:, z].reshape(256, RANK)], axis=0
        )
        value = dot(matrix[...], both).astype(BF16)
        rows = pl.ds(pl.multiple_of(z * BLOCK, BLOCK), BLOCK)
        for i in range(2 * CAP):
            wide[i, rows, :128] = state[z, i * BLOCK : (i + 1) * BLOCK, :]
            wide[i, rows, 128:] = value[i * BLOCK : (i + 1) * BLOCK, :]
        return 0

    lax.fori_loop(0, GROUPS, block, 0)
    eye = (iota((128, 128), 0) == iota((128, 128), 1)).astype(BF16)
    for i in range(2 * CAP):
        lhs = jnp.concatenate([eye, low[i]], axis=1)
        out[i] = dot(lhs, wide[i], ((1,), (1,))).astype(BF16)


def gather_slices(x):
    ring = lambda shift: [(i, (i + shift) % 4) for i in range(4)]
    for axis in ("x", "y"):
        x = jnp.stack([x] + [lax.ppermute(x, axis, ring(d)) for d in (1, 3, 2)])
    x = x.reshape((16,) + x.shape[2:])
    return x, lax.ppermute(x, "c", SWAP)


def exchange(x, axis):
    return lax.all_to_all(x, axis, split_axis=0, concat_axis=0, tiled=True)


def shards(momentum, gradient, right_in, owners):
    sds = jax.ShapeDtypeStruct
    place = jnp.stack([lax.axis_index("x"), lax.axis_index("y"), lax.axis_index("c")]).astype(
        jnp.int32
    )
    tables = [pltpu.SMEM((GROUPS * CAP,), jnp.int32), pltpu.SMEM((GROUPS,), jnp.int32)]
    n = 2 * CAP
    slices = call(
        slice_right,
        sds((16, 16, RANK), BF16),
        tables + [pltpu.VMEM((EXPERTS + 1, 8, RANK), F32)],
        specs=[SMEM, SMEM, VMEM],
    )(owners, place, right_in)
    slices = exchange(slices, "z")
    sent = call(
        place_state, sds((32, 192, 128), BF16), tables, specs=[SMEM, VMEM, VMEM]
    )(owners, jnp.swapaxes(momentum, 2, 3), jnp.swapaxes(gradient, 2, 3))
    sent, slices = lax.optimization_barrier((sent, slices))
    state = exchange(sent.reshape(16, 384, 128), "z")
    near, far = gather_slices(slices)
    matrix = pltpu.VMEM((384, 512), BF16)
    right = call(
        join_right, sds((16, 384, RANK), BF16), [matrix], flops=800_000_000, specs=[SMEM, VMEM, VMEM]
    )(place, near, far)
    panel, gram = call(
        panels, (sds((n, 128, RANK), F32), sds((n, RANK, RANK), F32)), n_in=2, flops=500_000_000
    )(state, right)
    gram = exchange(gram.reshape(32, 4 * n, RANK), FSDP)
    gram = jnp.broadcast_to(jnp.sum(gram, axis=0)[None], gram.shape)
    gram = exchange(gram, FSDP).reshape(n, RANK, RANK)
    half = sds((16, 16, 16, RANK), F32)
    keep, send = call(weigh, (half, half), specs=[SMEM, VMEM, VMEM], flops=2_000_000_000)(
        place, state, panel
    )
    parts = keep + lax.ppermute(send, "c", SWAP)
    parts = exchange(parts.reshape(16, 256, RANK), XY).reshape(16, 16, 16, RANK)
    inverse = call(
        functools.partial(invert, count=n, size=8),
        sds((n, RANK, RANK), F32),
        [pltpu.VMEM((n, RANK, 2 * RANK), F32)],
        n_in=1,
        flops=8_000_000_000,
    )(gram)
    tiles = call(scale_factor, sds((16, 16, RANK), BF16), n_in=2, flops=100_000_000)(parts, inverse)
    left, low = call(
        orthonormal,
        (sds((n, 128, RANK), F32), sds((n, 128, RANK), BF16)),
        n_in=2,
        flops=100_000_000,
    )(panel, inverse)
    back = exchange(tiles, "z")
    near, far = gather_slices(tiles)
    chosen = call(
        select,
        sds((16, 80, RANK), BF16),
        tables + [pltpu.VMEM((EXPERTS + 1, 8, RANK), F32), pltpu.VMEM((80, RANK), BF16)],
        specs=[SMEM, VMEM],
    )(owners, back)
    chosen = exchange(chosen, XY)
    other = lax.ppermute(chosen, "c", SWAP)
    right_out = call(
        finish_right, sds((EXPERTS, 2, BLOCK, RANK), F32), specs=[SMEM, VMEM, VMEM], flops=300_000_000
    )(place, chosen, other)
    state_out = call(
        finish_state,
        sds((n, 128, HID), BF16),
        [matrix, pltpu.VMEM((n, HID, 256), BF16)],
        specs=[SMEM, VMEM, VMEM, VMEM, VMEM],
        flops=1_200_000_000,
    )(place, state, near, far, low)
    return (
        state_out.reshape(CAP, 2, 128, HID),
        left.reshape(CAP, 2, 128, RANK),
        right_out,
    )


def solution(mesh):
    fine = Mesh(mesh.devices.reshape(4, 4, 2, 16), ("x", "y", "c", "z"))
    return jax.shard_map(
        shards,
        mesh=fine,
        in_specs=(
            P(None, None, FSDP, "z"),
            P(None, None, FSDP, "z"),
            P(None, None, "z", None),
            P(),
        ),
        out_specs=(
            P("z", None, FSDP, None),
            P("z", None, FSDP, None),
            P(None, None, "z", None),
        ),
        check_vma=False,
    )
```

time: 716 us -> 280 us (0.39)
  waiting for transfers between devices: 534 us -> 69.7 us
  other arithmetic: 94.8 us -> 4.38 us
  Pallas kernels: 0 us -> 60.4 us
  starting transfers between devices: 39.8 us -> 92.9 us
  blocking collectives: 0 us -> 43.6 us
  matrix products: 17.6 us -> 0 us
  between operations: 14.2 us -> 0.93 us
    psum x2 -> x0, waiting for transfers between devices: 273 us -> none  [the longest x1 140 us: shards(): factor = lax.psum(factor_part, 'fsdp')]
    all_to_all x3 -> x4, waiting for transfers between devices: 261 us -> 47.3 us  [exchange(): return lax.all_to_all(x, axis, split_axis=0, concat_axis=0, tiled=True)]
    another operation x7 -> x5, other arithmetic: 86.6 us -> 0.43 us  [the longest x4 0.35 us: gather_slices(): x = jnp.stack([x] + [lax.ppermute(x, axis, ring(d)) for d in (1, 3, 2)])]
    ppermute x0 -> x16, starting transfers between devices: none -> 63.7 us  [the longest x12 38.1 us: gather_slices(): x = jnp.stack([x] + [lax.ppermute(x, axis, ring(d)) for d in (1, 3, 2)])]
    pallas_call x0 -> x11, Pallas kernels: none -> 60.4 us  [the longest x1 18.7 us: shards(): call(functools.partial(invert, count=n, size=8), sds((n, RANK, RANK), F32...]
    all_to_all x0 -> x3, blocking collectives: none -> 43.6 us  [exchange(): return lax.all_to_all(x, axis, split_axis=0, concat_axis=0, tiled=True)]
    ppermute x0 -> x16, waiting for transfers between devices: none -> 22.4 us  [the longest x12 20.2 us: gather_slices(): x = jnp.stack([x] + [lax.ppermute(x, axis, ring(d)) for d in (1, 3, 2)])]
    dot_general x6 -> x0, matrix products: 14.7 us -> none  [the longest x1 6.59 us: shards(): update = jnp.einsum('cmrq,cmktq->cmrtk', ortho, factor, precision=highest)]
  transfers between devices with their start and end apart: 5 -> 20, of which waited for: 5 -> 11; matrix products, arithmetic and copies ran while one was open for 2% -> 2% of each run, Pallas kernels for 0% -> 11%
where the time goes in v1:
time: 280 us; the launch traced here: 278 us
  starting transfers between devices  92.9 us (33%)
  waiting for transfers between devices  69.7 us (25%)
  Pallas kernels  60.4 us (22%)
  blocking collectives  43.6 us (16%)
  local copies, waits for them, and re-layouts  6.48 us (2%)
  other arithmetic  4.38 us (2%)
    all_to_all x4, waiting for transfers between devices, exchange(): return lax.all_to_all(x, axis, split_axis=0, concat_axis=0, tiled=True)  47.3 us
    all_to_all x3, blocking collectives, exchange(): return lax.all_to_all(x, axis, split_axis=0, concat_axis=0, tiled=True)  43.6 us
    ppermute x12, starting transfers between devices, gather_slices(): x = jnp.stack([x] + [lax.ppermute(x, axis, ring(d)) for d in (1, 3, 2)])  38.1 us
    all_to_all x4, starting transfers between devices, exchange(): return lax.all_to_all(x, axis, split_axis=0, concat_axis=0, tiled=True)  29.2 us
    ppermute x12, waiting for transfers between devices, gather_slices(): x = jnp.stack([x] + [lax.ppermute(x, axis, ring(d)) for d in (1, 3, 2)])  20.2 us
    pallas_call x1, Pallas kernels, shards(): call(functools.partial(invert, count=n, size=8), sds((n, RANK, RANK), F32...  18.7 us
    pallas_call x1, Pallas kernels, shards(): call(weigh, (half, half), specs=[SMEM, VMEM, VMEM], flops=2000000000)  14.6 us
    ppermute x2, starting transfers between devices, gather_slices(): return (x, lax.ppermute(x, 'c', SWAP))  12.5 us
  transfers between devices with their start and end apart: 20, of which 11 were waited for; matrix products, arithmetic and copies ran while one was open for 2% of the time, Pallas kernels for 11%

profile of v1, /device:TPU:1, one launch (start us, length us, event | category | flops | bytes accessed | tf_op | source)
XLA Modules:
  0.0 278.5 jit_solution(4343839873841482919)
XLA Ops:
  0.7 1.0 copy-done.1
  2.4 1.5 shard_map.68
  3.9 15.7 %all-to-all-start = ((bf16[16,16,128]{2,1,0:T(8,128)(2,1)}), bf16[16,16,128]{2,1,0:T(8,128)(2,1)S(1)}, u32[]{:S(2)}, u32[]{:S(2)}) async-start(bf16[16,16,128]{2,1,0:T(8,128)(2,1)} %shard_map.68), calls=%async_computation | async-start | bytes 131072 | tf_op jit(solution)/shard_map/all_to_all | solution.py:311
  20.7 1.0 copy-done.3
  22.4 2.6 shard_map.67
  24.9 6.3 %all-to-all-done = bf16[16,16,128]{2,1,0:T(8,128)(2,1)S(1)} async-done(((bf16[16,16,128]{2,1,0:T(8,128)(2,1)}), bf16[16,16,128]{2,1,0:T(8,128)(2,1)S(1)}, u32[]{:S(2)}, u32[]{:S(2)}) %all-to-all-start) | async-done | bytes 65568 | tf_op jit(solution)/shard_map/all_to_all | solution.py:311
  31.2 5.2 %all-to-all-start.1 = ((bf16[16,384,128]{2,1,0:T(8,128)(2,1)}), bf16[16,384,128]{2,1,0:T(8,128)(2,1)S(1)}, u32[]{:S(2)}, u32[]{:S(2)}) async-start(bf16[16,384,128]{2,1,0:T(8,128)(2,1)} %bitcast.5), calls=%async_computation.1 | async-start | bytes 3145728 | tf_op jit(solution)/shard_map/all_to_all | solution.py:311
  36.4 4.7 %collective-permute-start.2 = (bf16[16,16,128]{2,1,0:T(8,128)(2,1)S(1)}, bf16[16,16,128]{2,1,0:T(8,128)(2,1)S(1)}, u32[]{:S(2)}, u32[]{:S(2)}) collective-permute-start(bf16[16,16,128]{2,1,0:T(8,128)(2,1)S(1)} %all-to-all-done), channel_id=1, source_target_pairs={{0,256},{128,384},{256,0},{384,128},{1,257},{129,385},{257,1},{385... | collective-permute-start | bytes 196616 | tf_op jit(solution)/shard_map/ppermute | solution.py:305
  41.1 2.8 collective-permute-start.1
  43.9 2.5 collective-permute-start
  46.4 4.0 %collective-permute-done = bf16[16,16,128]{2,1,0:T(8,128)(2,1)S(1)} collective-permute-done((bf16[16,16,128]{2,1,0:T(8,128)(2,1)S(1)}, bf16[16,16,128]{2,1,0:T(8,128)(2,1)S(1)}, u32[]{:S(2)}, u32[]{:S(2)}) %collective-permute-start) | collective-permute-done | bytes 65568 | tf_op jit(solution)/shard_map/ppermute | solution.py:305
  50.4 4.8 %collective-permute-start.5 = (bf16[4,16,16,128]{3,2,1,0:T(8,128)(2,1)S(1)}, bf16[4,16,16,128]{3,2,1,0:T(8,128)(2,1)S(1)}, u32[]{:S(2)}, u32[]{:S(2)}) collective-permute-start(bf16[4,16,16,128]{3,2,1,0:T(8,128)(2,1)S(1)} %get-tuple-element.22), channel_id=1, source_target_pairs={{0,64},{32,96},{64,0},{96,32},{1,65},{33,97},{65,1},{97,33},{2,66}... | collective-permute-start | bytes 786440 | tf_op jit(solution)/shard_map/ppermute | solution.py:305
  55.3 2.7 collective-permute-start.4
  57.9 2.6 collective-permute-start.3
  60.6 4.6 %collective-permute-done.4 = bf16[4,16,16,128]{3,2,1,0:T(8,128)(2,1)S(1)} collective-permute-done((bf16[4,16,16,128]{3,2,1,0:T(8,128)(2,1)S(1)}, bf16[4,16,16,128]{3,2,1,0:T(8,128)(2,1)S(1)}, u32[]{:S(2)}, u32[]{:S(2)}) %collective-permute-start.4) | collective-permute-done | bytes 262176 | tf_op jit(solution)/shard_map/ppermute | solution.py:305
  65.2 1.4 collective-permute-done.3
  66.7 6.3 %collective-permute-start.6 = (bf16[16,16,16,128]{3,2,1,0:T(8,128)(2,1)S(1)}, bf16[16,16,16,128]{3,2,1,0:T(8,128)(2,1)S(1)}, u32[]{:S(2)}, u32[]{:S(2)}) collective-permute-start(bf16[16,16,16,128]{3,2,1,0:T(8,128)(2,1)S(1)} %bitcast.34), channel_id=1, source_target_pairs={{0,16},{16,0},{1,17},{17,1},{2,18},{18,2},{3,19},{19,3},{4,20},{20... | collective-permute-start | bytes 3145736 | tf_op jit(solution)/shard_map/ppermute | solution.py:307
  73.0 2.3 collective-permute-done.6.far
  75.2 4.9 %shard_map.69.right = bf16[16,384,128]{2,1,0:T(8,128)(2,1)S(1)} custom-call(s32[3]{0:T(128)S(1)} %pad_add_fusion.place, bf16[16,16,16,128]{3,2,1,0:T(8,128)(2,1)S(1)} %bitcast.35, bf16[16,16,16,128]{3,2,1,0:T(8,128)(2,1)S(1)} %collective-permute-done.6.far), custom_call_target="tpu_custom_call" | custom-call | flops 800000000 | bytes 4000000 | tf_op jit(solution)/shard_map/pallas_call | solution.py:335
  80.1 25.4 %all-to-all-done.1.state = bf16[16,384,128]{2,1,0:T(8,128)(2,1)S(1)} async-done(((bf16[16,384,128]{2,1,0:T(8,128)(2,1)}), bf16[16,384,128]{2,1,0:T(8,128)(2,1)S(1)}, u32[]{:S(2)}, u32[]{:S(2)}) %all-to-all-start.1) | async-done | bytes 1572896 | tf_op jit(solution)/shard_map/all_to_all | solution.py:311
  105.5 4.4 %shard_map.70 = (f32[4,128,128]{2,1,0:T(8,128)S(1)}, f32[4,128,128]{2,1,0:T(8,128)S(1)}) custom-call(bf16[16,384,128]{2,1,0:T(8,128)(2,1)S(1)} %all-to-all-done.1.state, bf16[16,384,128]{2,1,0:T(8,128)(2,1)S(1)} %shard_map.69.right), custom_call_target="tpu_custom_call" | custom-call | flops 500000000 | bytes 4000000 | tf_op jit(solution)/shard_map/pallas_call | solution.py:338
  109.9 14.6 %shard_map.71 = (f32[16,16,16,128]{3,2,1,0:T(8,128)S(1)}, f32[16,16,16,128]{3,2,1,0:T(8,128)}) custom-call(s32[3]{0:T(128)S(1)} %pad_add_fusion.place, bf16[16,384,128]{2,1,0:T(8,128)(2,1)S(1)} %all-to-all-done.1.state, f32[4,128,128]{2,1,0:T(8,128)S(1)} %get-tuple-element.13.panel), custom_call_target="tpu_custom_call" | custom-call | flops 2000000000 | bytes 4000000 | tf_op jit(solution)/shard_map/pallas_call | solution.py:345
  124.5 1.4 copy-done
  125.8 8.0 %collective-permute-start.7 = (f32[16,16,16,128]{3,2,1,0:T(8,128)}, f32[16,16,16,128]{3,2,1,0:T(8,128)}, u32[]{:S(2)}, u32[]{:S(2)}) collective-permute-start(f32[16,16,16,128]{3,2,1,0:T(8,128)} %get-tuple-element.15), channel_id=1, source_target_pairs={{0,16},{16,0},{1,17},{17,1},{2,18},{18,2},{3,19},{19,3},{4,20},{20... | collective-permute-start | bytes 6291464 | tf_op jit(solution)/shard_map/ppermute | solution.py:348
  133.8 16.0 %all_to_all.35 = f32[32,16,128]{2,1,0:T(8,128)S(1)} all-to-all(f32[32,16,128]{2,1,0:T(8,128)S(1)} %bitcast.40), channel_id=1, replica_groups=mesh['x'=4,'y'=4,'c'=2,'z'=16] {'x','y','c'}, dimensions={0} | all-to-all | bytes 524288 | tf_op jit(solution)/shard_map/all_to_all | solution.py:311
  150.6 3.7 %all-to-all-start.4 = ((f32[32,16,128]{2,1,0:T(8,128)}), f32[32,16,128]{2,1,0:T(8,128)S(1)}, u32[]{:S(2)}, u32[]{:S(2)}) async-start(f32[32,16,128]{2,1,0:T(8,128)} %broadcast_in_dim.2), calls=%async_computation.4 | async-start | bytes 524288 | tf_op jit(solution)/shard_map/all_to_all | solution.py:311
  154.3 3.9 %add.3 = f32[16,16,16,128]{3,2,1,0:T(8,128)} add(f32[16,16,16,128]{3,2,1,0:T(8,128)} %copy-done, f32[16,16,16,128]{3,2,1,0:T(8,128)} %collective-permute-done.7) | non-fusion elementwise | flops 524288 | bytes 6291456 | tf_op jit(solution)/shard_map/add | solution.py:348
  158.2 5.2 %all-to-all-done.4 = f32[32,16,128]{2,1,0:T(8,128)S(1)} async-done(((f32[32,16,128]{2,1,0:T(8,128)}), f32[32,16,128]{2,1,0:T(8,128)S(1)}, u32[]{:S(2)}, u32[]{:S(2)}) %all-to-all-start.4) | async-done | bytes 262176 | tf_op jit(solution)/shard_map/all_to_all | solution.py:311
  163.4 4.6 %all-to-all-start.2 = ((f32[16,256,128]{2,1,0:T(8,128)}), f32[16,256,128]{2,1,0:T(8,128)}, u32[]{:S(2)}, u32[]{:S(2)}) async-start(f32[16,256,128]{2,1,0:T(8,128)} %bitcast.41), calls=%async_computation.2 | async-start | bytes 4194304 | tf_op jit(solution)/shard_map/all_to_all | solution.py:311
  168.0 18.7 %shard_map.72.inverse = f32[4,128,128]{2,1,0:T(8,128)S(1)} custom-call(f32[4,128,128]{2,1,0:T(8,128)S(1)} %bitcast.39), custom_call_target="tpu_custom_call" | custom-call | flops 8000000000 | bytes 4000000 | tf_op jit(solution)/shard_map/pallas_call | solution.py:350
  186.7 10.4 %all-to-all-done.2 = f32[16,256,128]{2,1,0:T(8,128)} async-done(((f32[16,256,128]{2,1,0:T(8,128)}), f32[16,256,128]{2,1,0:T(8,128)}, u32[]{:S(2)}, u32[]{:S(2)}) %all-to-all-start.2) | async-done | bytes 2097184 | tf_op jit(solution)/shard_map/all_to_all | solution.py:311
  197.2 2.3 shard_map.73
  199.5 3.6 %collective-permute-start.10 = (bf16[16,16,128]{2,1,0:T(8,128)(2,1)S(1)}, bf16[16,16,128]{2,1,0:T(8,128)(2,1)S(1)}, u32[]{:S(2)}, u32[]{:S(2)}) collective-permute-start(bf16[16,16,128]{2,1,0:T(8,128)(2,1)S(1)} %shard_map.73), channel_id=1, source_target_pairs={{0,256},{128,384},{256,0},{384,128},{1,257},{129,385},{257,1},{385... | collective-permute-start | bytes 196616 | tf_op jit(solution)/shard_map/ppermute | solution.py:305
  203.1 2.8 %collective-permute-start.9 = (bf16[16,16,128]{2,1,0:T(8,128)(2,1)S(1)}, bf16[16,16,128]{2,1,0:T(8,128)(2,1)S(1)}, u32[]{:S(2)}, u32[]{:S(2)}) collective-permute-start(bf16[16,16,128]{2,1,0:T(8,128)(2,1)S(1)} %shard_map.73), channel_id=1, source_target_pairs={{0,384},{128,0},{256,128},{384,256},{1,385},{129,1},{257,129},{385... | collective-permute-start | bytes 196616 | tf_op jit(solution)/shard_map/ppermute | solution.py:305
  205.9 2.5 collective-permute-start.8
  208.4 3.7 %collective-permute-done.8 = bf16[16,16,128]{2,1,0:T(8,128)(2,1)S(1)} collective-permute-done((bf16[16,16,128]{2,1,0:T(8,128)(2,1)S(1)}, bf16[16,16,128]{2,1,0:T(8,128)(2,1)S(1)}, u32[]{:S(2)}, u32[]{:S(2)}) %collective-permute-start.8) | collective-permute-done | bytes 65568 | tf_op jit(solution)/shard_map/ppermute | solution.py:305
  212.2 3.9 %collective-permute-start.13 = (bf16[4,16,16,128]{3,2,1,0:T(8,128)(2,1)S(1)}, bf16[4,16,16,128]{3,2,1,0:T(8,128)(2,1)S(1)}, u32[]{:S(2)}, u32[]{:S(2)}) collective-permute-start(bf16[4,16,16,128]{3,2,1,0:T(8,128)(2,1)S(1)} %get-tuple-element.20), channel_id=1, source_target_pairs={{0,64},{32,96},{64,0},{96,32},{1,65},{33,97},{65,1},{97,33},{2,66}... | collective-permute-start | bytes 786440 | tf_op jit(solution)/shard_map/ppermute | solution.py:305
  216.1 2.4 collective-permute-start.12
  218.6 2.8 %collective-permute-start.11 = (bf16[4,16,16,128]{3,2,1,0:T(8,128)(2,1)S(1)}, bf16[4,16,16,128]{3,2,1,0:T(8,128)(2,1)S(1)}, u32[]{:S(2)}, u32[]{:S(2)}) collective-permute-start(bf16[4,16,16,128]{3,2,1,0:T(8,128)(2,1)S(1)} %get-tuple-element.20), channel_id=1, source_target_pairs={{0,32},{32,64},{64,96},{96,0},{1,33},{33,65},{65,97},{97,1},{2,34}... | collective-permute-start | bytes 786440 | tf_op jit(solution)/shard_map/ppermute | solution.py:305
  221.4 5.2 %collective-permute-done.12 = bf16[4,16,16,128]{3,2,1,0:T(8,128)(2,1)S(1)} collective-permute-done((bf16[4,16,16,128]{3,2,1,0:T(8,128)(2,1)S(1)}, bf16[4,16,16,128]{3,2,1,0:T(8,128)(2,1)S(1)}, u32[]{:S(2)}, u32[]{:S(2)}) %collective-permute-start.12) | collective-permute-done | bytes 262176 | tf_op jit(solution)/shard_map/ppermute | solution.py:305
  226.6 1.3 collective-permute-done.11
  228.0 6.3 %collective-permute-start.14 = (bf16[16,16,16,128]{3,2,1,0:T(8,128)(2,1)S(1)}, bf16[16,16,16,128]{3,2,1,0:T(8,128)(2,1)S(1)}, u32[]{:S(2)}, u32[]{:S(2)}) collective-permute-start(bf16[16,16,16,128]{3,2,1,0:T(8,128)(2,1)S(1)} %bitcast.32), channel_id=1, source_target_pairs={{0,16},{16,0},{1,17},{17,1},{2,18},{18,2},{3,19},{19,3},{4,20},{20... | collective-permute-start | bytes 3145736 | tf_op jit(solution)/shard_map/ppermute | solution.py:307
  234.3 17.3 %all_to_all.36.tiles = bf16[16,16,128]{2,1,0:T(8,128)(2,1)S(1)} all-to-all(bf16[16,16,128]{2,1,0:T(8,128)(2,1)S(1)} %shard_map.73), channel_id=1, replica_groups=mesh['x'=4,'y'=4,'c'=2,'z'=16] {'z'}, dimensions={0} | all-to-all | bytes 131072 | tf_op jit(solution)/shard_map/all_to_all | solution.py:311
  252.3 10.3 %all_to_all.37.near = bf16[16,80,128]{2,1,0:T(8,128)(2,1)S(1)} all-to-all(bf16[16,80,128]{2,1,0:T(8,128)(2,1)S(1)} %shard_map.76), channel_id=1, replica_groups=mesh['x'=4,'y'=4,'c'=2,'z'=16] {'x','y'}, dimensions={0} | all-to-all | bytes 655360 | tf_op jit(solution)/shard_map/all_to_all | solution.py:311
  262.6 5.1 %collective-permute-start.15 = (bf16[16,80,128]{2,1,0:T(8,128)(2,1)S(1)}, bf16[16,80,128]{2,1,0:T(8,128)(2,1)S(1)}, u32[]{:S(2)}, u32[]{:S(2)}) collective-permute-start(bf16[16,80,128]{2,1,0:T(8,128)(2,1)S(1)} %all_to_all.37.near), channel_id=1, source_target_pairs={{0,16},{16,0},{1,17},{17,1},{2,18},{18,2},{3,19},{19,3},{4,20},{20... | collective-permute-start | bytes 983048 | tf_op jit(solution)/shard_map/ppermute | solution.py:373
  267.7 1.4 shard_map.74
  269.1 2.2 shard_map.77
  271.3 7.2 %shard_map.75 = bf16[4,128,1536]{2,1,0:T(8,128)(2,1)} custom-call(s32[3]{0:T(128)S(1)} %pad_add_fusion.place, bf16[16,384,128]{2,1,0:T(8,128)(2,1)S(1)} %all-to-all-done.1.state, bf16[16,16,16,128]{3,2,1,0:T(8,128)(2,1)S(1)} %bitcast.33, bf16[16,16,16,128]{3,2,1,0:T(8,128)(2,1)S(1)} %collective-permute-done.14.far, ...), custom_call_target="tpu_custom_call" | custom-call | flops 1200000000 | bytes 4000000 | tf_op jit(solution)/shard_map/pallas_call | solution.py:377
  (28 shorter events, 4.2 us)
Async XLA Ops:
  0.7 1.0 copy-start.1
  1.7 0.7 copy-start.4
  3.9 27.3 %all-to-all-start = ((bf16[16,16,128]{2,1,0:T(8,128)(2,1)}), bf16[16,16,128]{2,1,0:T(8,128)(2,1)S(1)}, u32[]{:S(2)}, u32[]{:S(2)}) async-start(bf16[16,16,128]{2,1,0:T(8,128)(2,1)} %shard_map.68), calls=%async_computation | async-start | bytes 131072 | tf_op jit(solution)/shard_map/all_to_all | solution.py:311
  19.7 1.0 copy-start.2
  20.7 1.0 copy-start.3
  21.7 0.7 copy-start.5
  31.2 74.2 %all-to-all-start.1 = ((bf16[16,384,128]{2,1,0:T(8,128)(2,1)}), bf16[16,384,128]{2,1,0:T(8,128)(2,1)S(1)}, u32[]{:S(2)}, u32[]{:S(2)}) async-start(bf16[16,384,128]{2,1,0:T(8,128)(2,1)} %bitcast.5), calls=%async_computation.1 | async-start | bytes 3145728 | tf_op jit(solution)/shard_map/all_to_all | solution.py:311
  36.4 10.0 %collective-permute-start.2 = (bf16[16,16,128]{2,1,0:T(8,128)(2,1)S(1)}, bf16[16,16,128]{2,1,0:T(8,128)(2,1)S(1)}, u32[]{:S(2)}, u32[]{:S(2)}) collective-permute-start(bf16[16,16,128]{2,1,0:T(8,128)(2,1)S(1)} %all-to-all-done), channel_id=1, source_target_pairs={{0,256},{128,384},{256,0},{384,128},{1,257},{129,385},{257,1},{385... | collective-permute-start | bytes 196616 | tf_op jit(solution)/shard_map/ppermute | solution.py:305
  41.1 5.3 %collective-permute-start.1 = (bf16[16,16,128]{2,1,0:T(8,128)(2,1)S(1)}, bf16[16,16,128]{2,1,0:T(8,128)(2,1)S(1)}, u32[]{:S(2)}, u32[]{:S(2)}) collective-permute-start(bf16[16,16,128]{2,1,0:T(8,128)(2,1)S(1)} %all-to-all-done), channel_id=1, source_target_pairs={{0,384},{128,0},{256,128},{384,256},{1,385},{129,1},{257,129},{385... | collective-permute-start | bytes 196616 | tf_op jit(solution)/shard_map/ppermute | solution.py:305
  43.9 6.5 %collective-permute-start = (bf16[16,16,128]{2,1,0:T(8,128)(2,1)S(1)}, bf16[16,16,128]{2,1,0:T(8,128)(2,1)S(1)}, u32[]{:S(2)}, u32[]{:S(2)}) collective-permute-start(bf16[16,16,128]{2,1,0:T(8,128)(2,1)S(1)} %all-to-all-done), channel_id=1, source_target_pairs={{0,128},{128,256},{256,384},{384,0},{1,129},{129,257},{257,385},{3... | collective-permute-start | bytes 196616 | tf_op jit(solution)/shard_map/ppermute | solution.py:305
  50.4 10.1 %collective-permute-start.5 = (bf16[4,16,16,128]{3,2,1,0:T(8,128)(2,1)S(1)}, bf16[4,16,16,128]{3,2,1,0:T(8,128)(2,1)S(1)}, u32[]{:S(2)}, u32[]{:S(2)}) collective-permute-start(bf16[4,16,16,128]{3,2,1,0:T(8,128)(2,1)S(1)} %get-tuple-element.22), channel_id=1, source_target_pairs={{0,64},{32,96},{64,0},{96,32},{1,65},{33,97},{65,1},{97,33},{2,66}... | collective-permute-start | bytes 786440 | tf_op jit(solution)/shard_map/ppermute | solution.py:305
  55.3 9.9 %collective-permute-start.4 = (bf16[4,16,16,128]{3,2,1,0:T(8,128)(2,1)S(1)}, bf16[4,16,16,128]{3,2,1,0:T(8,128)(2,1)S(1)}, u32[]{:S(2)}, u32[]{:S(2)}) collective-permute-start(bf16[4,16,16,128]{3,2,1,0:T(8,128)(2,1)S(1)} %get-tuple-element.22), channel_id=1, source_target_pairs={{0,96},{32,0},{64,32},{96,64},{1,97},{33,1},{65,33},{97,65},{2,98}... | collective-permute-start | bytes 786440 | tf_op jit(solution)/shard_map/ppermute | solution.py:305
  57.9 8.6 %collective-permute-start.3 = (bf16[4,16,16,128]{3,2,1,0:T(8,128)(2,1)S(1)}, bf16[4,16,16,128]{3,2,1,0:T(8,128)(2,1)S(1)}, u32[]{:S(2)}, u32[]{:S(2)}) collective-permute-start(bf16[4,16,16,128]{3,2,1,0:T(8,128)(2,1)S(1)} %get-tuple-element.22), channel_id=1, source_target_pairs={{0,32},{32,64},{64,96},{96,0},{1,33},{33,65},{65,97},{97,1},{2,34}... | collective-permute-start | bytes 786440 | tf_op jit(solution)/shard_map/ppermute | solution.py:305
  66.7 8.5 %collective-permute-start.6 = (bf16[16,16,16,128]{3,2,1,0:T(8,128)(2,1)S(1)}, bf16[16,16,16,128]{3,2,1,0:T(8,128)(2,1)S(1)}, u32[]{:S(2)}, u32[]{:S(2)}) collective-permute-start(bf16[16,16,16,128]{3,2,1,0:T(8,128)(2,1)S(1)} %bitcast.34), channel_id=1, source_target_pairs={{0,16},{16,0},{1,17},{17,1},{2,18},{18,2},{3,19},{19,3},{4,20},{20... | collective-permute-start | bytes 3145736 | tf_op jit(solution)/shard_map/ppermute | solution.py:307
  124.5 1.4 copy-start
  125.8 28.5 %collective-permute-start.7 = (f32[16,16,16,128]{3,2,1,0:T(8,128)}, f32[16,16,16,128]{3,2,1,0:T(8,128)}, u32[]{:S(2)}, u32[]{:S(2)}) collective-permute-start(f32[16,16,16,128]{3,2,1,0:T(8,128)} %get-tuple-element.15), channel_id=1, source_target_pairs={{0,16},{16,0},{1,17},{17,1},{2,18},{18,2},{3,19},{19,3},{4,20},{20... | collective-permute-start | bytes 6291464 | tf_op jit(solution)/shard_map/ppermute | solution.py:348
  150.6 12.8 %all-to-all-start.4 = ((f32[32,16,128]{2,1,0:T(8,128)}), f32[32,16,128]{2,1,0:T(8,128)S(1)}, u32[]{:S(2)}, u32[]{:S(2)}) async-start(f32[32,16,128]{2,1,0:T(8,128)} %broadcast_in_dim.2), calls=%async_computation.4 | async-start | bytes 524288 | tf_op jit(solution)/shard_map/all_to_all | solution.py:311
  163.4 33.8 %all-to-all-start.2 = ((f32[16,256,128]{2,1,0:T(8,128)}), f32[16,256,128]{2,1,0:T(8,128)}, u32[]{:S(2)}, u32[]{:S(2)}) async-start(f32[16,256,128]{2,1,0:T(8,128)} %bitcast.41), calls=%async_computation.2 | async-start | bytes 4194304 | tf_op jit(solution)/shard_map/all_to_all | solution.py:311
  199.5 52.2 %copy-start.6 = (s32[10]{0:T(128)S(1)}, s32[10]{0:T(128)}, u32[]{:S(2)}) copy-start(s32[10]{0:T(128)} %own.5) | copy-start | bytes 124
  199.5 8.9 %collective-permute-start.10 = (bf16[16,16,128]{2,1,0:T(8,128)(2,1)S(1)}, bf16[16,16,128]{2,1,0:T(8,128)(2,1)S(1)}, u32[]{:S(2)}, u32[]{:S(2)}) collective-permute-start(bf16[16,16,128]{2,1,0:T(8,128)(2,1)S(1)} %shard_map.73), channel_id=1, source_target_pairs={{0,256},{128,384},{256,0},{384,128},{1,257},{129,385},{257,1},{385... | collective-permute-start | bytes 196616 | tf_op jit(solution)/shard_map/ppermute | solution.py:305
  203.1 5.3 %collective-permute-start.9 = (bf16[16,16,128]{2,1,0:T(8,128)(2,1)S(1)}, bf16[16,16,128]{2,1,0:T(8,128)(2,1)S(1)}, u32[]{:S(2)}, u32[]{:S(2)}) collective-permute-start(bf16[16,16,128]{2,1,0:T(8,128)(2,1)S(1)} %shard_map.73), channel_id=1, source_target_pairs={{0,384},{128,0},{256,128},{384,256},{1,385},{129,1},{257,129},{385... | collective-permute-start | bytes 196616 | tf_op jit(solution)/shard_map/ppermute | solution.py:305
  205.9 6.2 %collective-permute-start.8 = (bf16[16,16,128]{2,1,0:T(8,128)(2,1)S(1)}, bf16[16,16,128]{2,1,0:T(8,128)(2,1)S(1)}, u32[]{:S(2)}, u32[]{:S(2)}) collective-permute-start(bf16[16,16,128]{2,1,0:T(8,128)(2,1)S(1)} %shard_map.73), channel_id=1, source_target_pairs={{0,128},{128,256},{256,384},{384,0},{1,129},{129,257},{257,385},{3... | collective-permute-start | bytes 196616 | tf_op jit(solution)/shard_map/ppermute | solution.py:305
  212.2 9.2 %collective-permute-start.13 = (bf16[4,16,16,128]{3,2,1,0:T(8,128)(2,1)S(1)}, bf16[4,16,16,128]{3,2,1,0:T(8,128)(2,1)S(1)}, u32[]{:S(2)}, u32[]{:S(2)}) collective-permute-start(bf16[4,16,16,128]{3,2,1,0:T(8,128)(2,1)S(1)} %get-tuple-element.20), channel_id=1, source_target_pairs={{0,64},{32,96},{64,0},{96,32},{1,65},{33,97},{65,1},{97,33},{2,66}... | collective-permute-start | bytes 786440 | tf_op jit(solution)/shard_map/ppermute | solution.py:305
  216.1 10.5 %collective-permute-start.12 = (bf16[4,16,16,128]{3,2,1,0:T(8,128)(2,1)S(1)}, bf16[4,16,16,128]{3,2,1,0:T(8,128)(2,1)S(1)}, u32[]{:S(2)}, u32[]{:S(2)}) collective-permute-start(bf16[4,16,16,128]{3,2,1,0:T(8,128)(2,1)S(1)} %get-tuple-element.20), channel_id=1, source_target_pairs={{0,96},{32,0},{64,32},{96,64},{1,97},{33,1},{65,33},{97,65},{2,98}... | collective-permute-start | bytes 786440 | tf_op jit(solution)/shard_map/ppermute | solution.py:305
  218.6 9.3 %collective-permute-start.11 = (bf16[4,16,16,128]{3,2,1,0:T(8,128)(2,1)S(1)}, bf16[4,16,16,128]{3,2,1,0:T(8,128)(2,1)S(1)}, u32[]{:S(2)}, u32[]{:S(2)}) collective-permute-start(bf16[4,16,16,128]{3,2,1,0:T(8,128)(2,1)S(1)} %get-tuple-element.20), channel_id=1, source_target_pairs={{0,32},{32,64},{64,96},{96,0},{1,33},{33,65},{65,97},{97,1},{2,34}... | collective-permute-start | bytes 786440 | tf_op jit(solution)/shard_map/ppermute | solution.py:305
  228.0 43.3 %collective-permute-start.14 = (bf16[16,16,16,128]{3,2,1,0:T(8,128)(2,1)S(1)}, bf16[16,16,16,128]{3,2,1,0:T(8,128)(2,1)S(1)}, u32[]{:S(2)}, u32[]{:S(2)}) collective-permute-start(bf16[16,16,16,128]{3,2,1,0:T(8,128)(2,1)S(1)} %bitcast.32), channel_id=1, source_target_pairs={{0,16},{16,0},{1,17},{17,1},{2,18},{18,2},{3,19},{19,3},{4,20},{20... | collective-permute-start | bytes 3145736 | tf_op jit(solution)/shard_map/ppermute | solution.py:307
  262.6 6.5 %collective-permute-start.15 = (bf16[16,80,128]{2,1,0:T(8,128)(2,1)S(1)}, bf16[16,80,128]{2,1,0:T(8,128)(2,1)S(1)}, u32[]{:S(2)}, u32[]{:S(2)}) collective-permute-start(bf16[16,80,128]{2,1,0:T(8,128)(2,1)S(1)} %all_to_all.37.near), channel_id=1, source_target_pairs={{0,16},{16,0},{1,17},{17,1},{2,18},{18,2},{3,19},{19,3},{4,20},{20... | collective-permute-start | bytes 983048 | tf_op jit(solution)/shard_map/ppermute | solution.py:373

commit v2 on v1

--- a/solution.py
+++ b/solution.py
@@ -111,20 +111,22 @@
     return jnp.where(i == 1, 3, jnp.where(i == 2, 1, jnp.where(i == 3, 2, 0)))
 
 
-def unpermute_matrix(place, core):
+def unpermute_matrix(place, core, relative):
     col = iota((384, 256), 1)
     chip = col >> 4
-    x = (place[0] + offset(chip & 3)) & 3
-    y = (place[1] + offset(chip >> 2)) & 3
-    f = x * 8 + y * 2 + core
+    if relative:
+        x = (place[0] + offset(chip & 3)) & 3
+        y = (place[1] + offset(chip >> 2)) & 3
+        chip = x * 4 + y
+    f = chip * 2 + core
     target = ((col >> 3) & 1) * 192 + tile_row(col) + 3 * f
     return ((iota((384, 256), 0) == target) & ((col & 7) < 6)).astype(BF16)
 
 
 def join_right(place, near, far, out, matrix):
     c = place[2]
-    matrix[:, :256] = unpermute_matrix(place, c)
-    matrix[:, 256:] = unpermute_matrix(place, 1 - c)
+    matrix[:, :256] = unpermute_matrix(place, c, True)
+    matrix[:, 256:] = unpermute_matrix(place, 1 - c, True)
 
     def block(z, _):
         a = near[:, z].reshape(256, RANK)
@@ -182,7 +184,7 @@
             send[:, z, rows, :] = value[128:].reshape(16, 8, RANK)
             return 0
 
-        lax.fori_loop(0, GROUPS, block, 0)
+        lax.fori_loop(0, GROUPS, block, 0, unroll=4)
 
 
 def invert(gram, out, work, *, count, size):
@@ -239,14 +241,15 @@
         low[i] = (ortho * (-feedback)).astype(BF16)
 
 
-def select(own, tiles, out, table, count, held, packed):
+def select(own, mine, tiles, out, table, count, held, packed):
     fill_table(own, table, count)
     for g in range(GROUPS):
         value = tiles[g].astype(F32)
         for s in range(CAP):
             held[table[g * CAP + s]] = value[s * 8 : (s + 1) * 8]
     for e in range(0, EXPERTS, 2):
-        packed[e * 8 : e * 8 + 16, :] = jnp.concatenate([held[e], held[e + 1]], axis=0).astype(BF16)
+        packed[256 + e * 8 : 272 + e * 8, :] = jnp.concatenate([held[e], held[e + 1]], axis=0).astype(BF16)
+    packed[:256, :] = mine[...].reshape(256, RANK)
     value = packed[...]
     for i in range(16):
         out[i] = value
@@ -264,7 +267,7 @@
         matrices.append((row == target).astype(BF16))
     both = jnp.concatenate(matrices, axis=1)
     for g in range(EXPERTS // 2):
-        rows = slice(g * 16, (g + 1) * 16)
+        rows = slice(256 + g * 16, 272 + g * 16)
         data = jnp.concatenate(
             [near[:, rows, :].reshape(256, RANK), far[:, rows, :].reshape(256, RANK)], axis=0
         )
@@ -278,12 +281,13 @@
 
 def finish_state(place, state, near, far, low, out, matrix, wide):
     c = place[2]
-    matrix[:, :256] = unpermute_matrix(place, c)
-    matrix[:, 256:] = unpermute_matrix(place, 1 - c)
+    matrix[:, :256] = unpermute_matrix(place, c, False)
+    matrix[:, 256:] = unpermute_matrix(place, 1 - c, False)
 
     def block(z, _):
+        tile = pl.ds(pl.multiple_of(z * 16, 16), 16)
         both = jnp.concatenate(
-            [near[:, z].reshape(256, RANK), far[:, z].reshape(256, RANK)], axis=0
+            [near[:, tile, :].reshape(256, RANK), far[:, tile, :].reshape(256, RANK)], axis=0
         )
         value = dot(matrix[...], both).astype(BF16)
         rows = pl.ds(pl.multiple_of(z * BLOCK, BLOCK), BLOCK)
@@ -362,18 +366,17 @@
         flops=100_000_000,
     )(panel, inverse)
     back = exchange(tiles, "z")
-    near, far = gather_slices(tiles)
     chosen = call(
         select,
-        sds((16, 80, RANK), BF16),
-        tables + [pltpu.VMEM((EXPERTS + 1, 8, RANK), F32), pltpu.VMEM((80, RANK), BF16)],
-        specs=[SMEM, VMEM],
-    )(owners, back)
-    chosen = exchange(chosen, XY)
-    other = lax.ppermute(chosen, "c", SWAP)
+        sds((16, 336, RANK), BF16),
+        tables + [pltpu.VMEM((EXPERTS + 1, 8, RANK), F32), pltpu.VMEM((336, RANK), BF16)],
+        specs=[SMEM, VMEM, VMEM],
+    )(owners, tiles, back)
+    near = exchange(chosen, XY)
+    far = lax.ppermute(near, "c", SWAP)
     right_out = call(
         finish_right, sds((EXPERTS, 2, BLOCK, RANK), F32), specs=[SMEM, VMEM, VMEM], flops=300_000_000
-    )(place, chosen, other)
+    )(place, near, far)
     state_out = call(
         finish_state,
         sds((n, 128, HID), BF16),

time: 280 us -> 256 us (0.914)
  starting transfers between devices: 92.9 us -> 69.8 us
  blocking collectives: 43.6 us -> 56.1 us
  waiting for transfers between devices: 69.7 us -> 60.9 us
  Pallas kernels: 60.4 us -> 57.3 us
    ppermute x12 -> x6, starting transfers between devices: 38.1 us -> 20 us  [gather_slices(): x = jnp.stack([x] + [lax.ppermute(x, axis, ring(d)) for d in (1, 3, 2)])]
    all_to_all x3, blocking collectives: 43.6 us -> 56.1 us  [exchange(): return lax.all_to_all(x, axis, split_axis=0, concat_axis=0, tiled=True)]
    ppermute x12 -> x6, waiting for transfers between devices: 20.2 us -> 9.98 us  [gather_slices(): x = jnp.stack([x] + [lax.ppermute(x, axis, ring(d)) for d in (1, 3, 2)])]
    ppermute x2 -> x1, starting transfers between devices: 12.5 us -> 6.25 us  [gather_slices(): return (x, lax.ppermute(x, 'c', SWAP))]
    pallas_call x1, Pallas kernels: 14.6 us -> 11.4 us  [shards(): call(weigh, (half, half), specs=[SMEM, VMEM, VMEM], flops=2000000000)]
  transfers between devices with their start and end apart: 20 -> 13, of which waited for: 11 -> 9; matrix products, arithmetic and copies ran while one was open for 2% -> 2% of each run, Pallas kernels for 11% -> 11%
where the time goes in v2:
time: 256 us
  starting transfers between devices  69.8 us (27%)
  waiting for transfers between devices  60.9 us (24%)
  Pallas kernels  57.3 us (22%)
  blocking collectives  56.1 us (22%)
  local copies, waits for them, and re-layouts  6.45 us (3%)
  other arithmetic  4.17 us (2%)
    all_to_all x3, blocking collectives, exchange(): return lax.all_to_all(x, axis, split_axis=0, concat_axis=0, tiled=True)  56.1 us
    all_to_all x4, waiting for transfers between devices, exchange(): return lax.all_to_all(x, axis, split_axis=0, concat_axis=0, tiled=True)  47.3 us
    all_to_all x4, starting transfers between devices, exchange(): return lax.all_to_all(x, axis, split_axis=0, concat_axis=0, tiled=True)  29.2 us
    ppermute x6, starting transfers between devices, gather_slices(): x = jnp.stack([x] + [lax.ppermute(x, axis, ring(d)) for d in (1, 3, 2)])  20 us
    pallas_call x1, Pallas kernels, shards(): call(functools.partial(invert, count=n, size=8), sds((n, RANK, RANK), F32...  18.7 us
    pallas_call x1, Pallas kernels, shards(): call(weigh, (half, half), specs=[SMEM, VMEM, VMEM], flops=2000000000)  11.4 us
    ppermute x6, waiting for transfers between devices, gather_slices(): x = jnp.stack([x] + [lax.ppermute(x, axis, ring(d)) for d in (1, 3, 2)])  9.98 us
    ppermute x1, starting transfers between devices, shards(): parts = keep + lax.ppermute(send, 'c', SWAP)  7.96 us
  transfers between devices with their start and end apart: 13, of which 9 were waited for; matrix products, arithmetic and copies ran while one was open for 2% of the time, Pallas kernels for 11%

profile of v2, /device:TPU:1, one launch (start us, length us, event | category | flops | bytes accessed | tf_op | source)
XLA Modules:
  0.0 255.6 jit_solution(6088195038701011386)
XLA Ops:
  0.6 0.1 pad_add_fusion.place
  0.7 1.0 copy-done.1
  1.7 0.7 copy-done.4
  2.4 1.5 shard_map.68
  3.9 15.7 %all-to-all-start = ((bf16[16,16,128]{2,1,0:T(8,128)(2,1)}), bf16[16,16,128]{2,1,0:T(8,128)(2,1)S(1)}, u32[]{:S(2)}, u32[]{:S(2)}) async-start(bf16[16,16,128]{2,1,0:T(8,128)(2,1)} %shard_map.68), calls=%async_computation | async-start | bytes 131072 | tf_op jit(solution)/shard_map/all_to_all | solution.py:315
  19.7 0.0 copy-start.2
  19.7 1.0 copy-done.2
  20.7 1.0 copy-done.3
  21.7 0.7 copy-done.5
  22.4 2.6 %shard_map.67 = bf16[32,192,128]{2,1,0:T(8,128)(2,1)} custom-call(s32[10]{0:T(128)S(1)} %copy-done.5, bf16[10,2,96,128]{3,2,1,0:T(8,128)(2,1)S(1)} %bitcast.24, bf16[10,2,96,128]{3,2,1,0:T(8,128)(2,1)S(1)} %bitcast.25), custom_call_target="tpu_custom_call" | custom-call | bytes 4000000 | tf_op jit(solution)/shard_map/pallas_call | solution.py:332
  24.9 6.3 %all-to-all-done = bf16[16,16,128]{2,1,0:T(8,128)(2,1)S(1)} async-done(((bf16[16,16,128]{2,1,0:T(8,128)(2,1)}), bf16[16,16,128]{2,1,0:T(8,128)(2,1)S(1)}, u32[]{:S(2)}, u32[]{:S(2)}) %all-to-all-start) | async-done | bytes 65568 | tf_op jit(solution)/shard_map/all_to_all | solution.py:315
  31.2 5.2 %all-to-all-start.1 = ((bf16[16,384,128]{2,1,0:T(8,128)(2,1)}), bf16[16,384,128]{2,1,0:T(8,128)(2,1)S(1)}, u32[]{:S(2)}, u32[]{:S(2)}) async-start(bf16[16,384,128]{2,1,0:T(8,128)(2,1)} %bitcast.5), calls=%async_computation.1 | async-start | bytes 3145728 | tf_op jit(solution)/shard_map/all_to_all | solution.py:315
  36.4 4.7 %collective-permute-start.2 = (bf16[16,16,128]{2,1,0:T(8,128)(2,1)S(1)}, bf16[16,16,128]{2,1,0:T(8,128)(2,1)S(1)}, u32[]{:S(2)}, u32[]{:S(2)}) collective-permute-start(bf16[16,16,128]{2,1,0:T(8,128)(2,1)S(1)} %all-to-all-done), channel_id=1, source_target_pairs={{0,256},{128,384},{256,0},{384,128},{1,257},{129,385},{257,1},{385... | collective-permute-start | bytes 196616 | tf_op jit(solution)/shard_map/ppermute | solution.py:309
  41.1 2.8 %collective-permute-start.1 = (bf16[16,16,128]{2,1,0:T(8,128)(2,1)S(1)}, bf16[16,16,128]{2,1,0:T(8,128)(2,1)S(1)}, u32[]{:S(2)}, u32[]{:S(2)}) collective-permute-start(bf16[16,16,128]{2,1,0:T(8,128)(2,1)S(1)} %all-to-all-done), channel_id=1, source_target_pairs={{0,384},{128,0},{256,128},{384,256},{1,385},{129,1},{257,129},{385... | collective-permute-start | bytes 196616 | tf_op jit(solution)/shard_map/ppermute | solution.py:309
  43.9 2.5 collective-permute-start
  46.4 0.0 collective-permute-done.2
  46.4 4.0 %collective-permute-done = bf16[16,16,128]{2,1,0:T(8,128)(2,1)S(1)} collective-permute-done((bf16[16,16,128]{2,1,0:T(8,128)(2,1)S(1)}, bf16[16,16,128]{2,1,0:T(8,128)(2,1)S(1)}, u32[]{:S(2)}, u32[]{:S(2)}) %collective-permute-start) | collective-permute-done | bytes 65568 | tf_op jit(solution)/shard_map/ppermute | solution.py:309
  50.4 4.8 %collective-permute-start.5 = (bf16[4,16,16,128]{3,2,1,0:T(8,128)(2,1)S(1)}, bf16[4,16,16,128]{3,2,1,0:T(8,128)(2,1)S(1)}, u32[]{:S(2)}, u32[]{:S(2)}) collective-permute-start(bf16[4,16,16,128]{3,2,1,0:T(8,128)(2,1)S(1)} %get-tuple-element.20), channel_id=1, source_target_pairs={{0,64},{32,96},{64,0},{96,32},{1,65},{33,97},{65,1},{97,33},{2,66}... | collective-permute-start | bytes 786440 | tf_op jit(solution)/shard_map/ppermute | solution.py:309
  55.3 2.7 %collective-permute-start.4 = (bf16[4,16,16,128]{3,2,1,0:T(8,128)(2,1)S(1)}, bf16[4,16,16,128]{3,2,1,0:T(8,128)(2,1)S(1)}, u32[]{:S(2)}, u32[]{:S(2)}) collective-permute-start(bf16[4,16,16,128]{3,2,1,0:T(8,128)(2,1)S(1)} %get-tuple-element.20), channel_id=1, source_target_pairs={{0,96},{32,0},{64,32},{96,64},{1,97},{33,1},{65,33},{97,65},{2,98}... | collective-permute-start | bytes 786440 | tf_op jit(solution)/shard_map/ppermute | solution.py:309
  57.9 2.6 %collective-permute-start.3 = (bf16[4,16,16,128]{3,2,1,0:T(8,128)(2,1)S(1)}, bf16[4,16,16,128]{3,2,1,0:T(8,128)(2,1)S(1)}, u32[]{:S(2)}, u32[]{:S(2)}) collective-permute-start(bf16[4,16,16,128]{3,2,1,0:T(8,128)(2,1)S(1)} %get-tuple-element.20), channel_id=1, source_target_pairs={{0,32},{32,64},{64,96},{96,0},{1,33},{33,65},{65,97},{97,1},{2,34}... | collective-permute-start | bytes 786440 | tf_op jit(solution)/shard_map/ppermute | solution.py:309
  60.6 4.6 %collective-permute-done.4 = bf16[4,16,16,128]{3,2,1,0:T(8,128)(2,1)S(1)} collective-permute-done((bf16[4,16,16,128]{3,2,1,0:T(8,128)(2,1)S(1)}, bf16[4,16,16,128]{3,2,1,0:T(8,128)(2,1)S(1)}, u32[]{:S(2)}, u32[]{:S(2)}) %collective-permute-start.4) | collective-permute-done | bytes 262176 | tf_op jit(solution)/shard_map/ppermute | solution.py:309
  65.2 1.4 collective-permute-done.3
  66.6 0.1 pad_maximum_fusion
  66.7 6.3 %collective-permute-start.6 = (bf16[16,16,16,128]{3,2,1,0:T(8,128)(2,1)S(1)}, bf16[16,16,16,128]{3,2,1,0:T(8,128)(2,1)S(1)}, u32[]{:S(2)}, u32[]{:S(2)}) collective-permute-start(bf16[16,16,16,128]{3,2,1,0:T(8,128)(2,1)S(1)} %bitcast.22), channel_id=1, source_target_pairs={{0,16},{16,0},{1,17},{17,1},{2,18},{18,2},{3,19},{19,3},{4,20},{20... | collective-permute-start | bytes 3145736 | tf_op jit(solution)/shard_map/ppermute | solution.py:311
  73.0 2.3 collective-permute-done.6.far
  75.2 4.9 %shard_map.69.right = bf16[16,384,128]{2,1,0:T(8,128)(2,1)S(1)} custom-call(s32[3]{0:T(128)S(1)} %pad_add_fusion.place, bf16[16,16,16,128]{3,2,1,0:T(8,128)(2,1)S(1)} %bitcast.23, bf16[16,16,16,128]{3,2,1,0:T(8,128)(2,1)S(1)} %collective-permute-done.6.far), custom_call_target="tpu_custom_call" | custom-call | flops 800000000 | bytes 4000000 | tf_op jit(solution)/shard_map/pallas_call | solution.py:339
  80.1 25.4 %all-to-all-done.1.state = bf16[16,384,128]{2,1,0:T(8,128)(2,1)S(1)} async-done(((bf16[16,384,128]{2,1,0:T(8,128)(2,1)}), bf16[16,384,128]{2,1,0:T(8,128)(2,1)S(1)}, u32[]{:S(2)}, u32[]{:S(2)}) %all-to-all-start.1) | async-done | bytes 1572896 | tf_op jit(solution)/shard_map/all_to_all | solution.py:315
  105.5 4.4 %shard_map.70 = (f32[4,128,128]{2,1,0:T(8,128)S(1)}, f32[4,128,128]{2,1,0:T(8,128)S(1)}) custom-call(bf16[16,384,128]{2,1,0:T(8,128)(2,1)S(1)} %all-to-all-done.1.state, bf16[16,384,128]{2,1,0:T(8,128)(2,1)S(1)} %shard_map.69.right), custom_call_target="tpu_custom_call" | custom-call | flops 500000000 | bytes 4000000 | tf_op jit(solution)/shard_map/pallas_call | solution.py:342
  109.9 11.4 %shard_map.71 = (f32[16,16,16,128]{3,2,1,0:T(8,128)S(1)}, f32[16,16,16,128]{3,2,1,0:T(8,128)}) custom-call(s32[3]{0:T(128)S(1)} %pad_add_fusion.place, bf16[16,384,128]{2,1,0:T(8,128)(2,1)S(1)} %all-to-all-done.1.state, f32[4,128,128]{2,1,0:T(8,128)S(1)} %get-tuple-element.13.panel), custom_call_target="tpu_custom_call" | custom-call | flops 2000000000 | bytes 4000000 | tf_op jit(solution)/shard_map/pallas_call | solution.py:349
  121.3 1.3 copy-done
  122.6 8.0 %collective-permute-start.7 = (f32[16,16,16,128]{3,2,1,0:T(8,128)}, f32[16,16,16,128]{3,2,1,0:T(8,128)}, u32[]{:S(2)}, u32[]{:S(2)}) collective-permute-start(f32[16,16,16,128]{3,2,1,0:T(8,128)} %get-tuple-element.15), channel_id=1, source_target_pairs={{0,16},{16,0},{1,17},{17,1},{2,18},{18,2},{3,19},{19,3},{4,20},{20... | collective-permute-start | bytes 6291464 | tf_op jit(solution)/shard_map/ppermute | solution.py:352
  130.6 16.0 %all_to_all.35 = f32[32,16,128]{2,1,0:T(8,128)S(1)} all-to-all(f32[32,16,128]{2,1,0:T(8,128)S(1)} %bitcast.27), channel_id=1, replica_groups=mesh['x'=4,'y'=4,'c'=2,'z'=16] {'x','y','c'}, dimensions={0} | all-to-all | bytes 524288 | tf_op jit(solution)/shard_map/all_to_all | solution.py:315
  146.6 0.7 broadcast_in_dim.2
  147.3 3.7 %all-to-all-start.4 = ((f32[32,16,128]{2,1,0:T(8,128)}), f32[32,16,128]{2,1,0:T(8,128)S(1)}, u32[]{:S(2)}, u32[]{:S(2)}) async-start(f32[32,16,128]{2,1,0:T(8,128)} %broadcast_in_dim.2), calls=%async_computation.4 | async-start | bytes 524288 | tf_op jit(solution)/shard_map/all_to_all | solution.py:315
  151.0 3.9 %add.3 = f32[16,16,16,128]{3,2,1,0:T(8,128)} add(f32[16,16,16,128]{3,2,1,0:T(8,128)} %copy-done, f32[16,16,16,128]{3,2,1,0:T(8,128)} %collective-permute-done.7) | non-fusion elementwise | flops 524288 | bytes 6291456 | tf_op jit(solution)/shard_map/add | solution.py:352
  154.9 5.2 %all-to-all-done.4 = f32[32,16,128]{2,1,0:T(8,128)S(1)} async-done(((f32[32,16,128]{2,1,0:T(8,128)}), f32[32,16,128]{2,1,0:T(8,128)S(1)}, u32[]{:S(2)}, u32[]{:S(2)}) %all-to-all-start.4) | async-done | bytes 262176 | tf_op jit(solution)/shard_map/all_to_all | solution.py:315
  160.1 4.6 %all-to-all-start.2 = ((f32[16,256,128]{2,1,0:T(8,128)}), f32[16,256,128]{2,1,0:T(8,128)}, u32[]{:S(2)}, u32[]{:S(2)}) async-start(f32[16,256,128]{2,1,0:T(8,128)} %bitcast.28), calls=%async_computation.2 | async-start | bytes 4194304 | tf_op jit(solution)/shard_map/all_to_all | solution.py:315
  164.8 18.7 %shard_map.72.inverse = f32[4,128,128]{2,1,0:T(8,128)S(1)} custom-call(f32[4,128,128]{2,1,0:T(8,128)S(1)} %bitcast.26), custom_call_target="tpu_custom_call" | custom-call | flops 8000000000 | bytes 4000000 | tf_op jit(solution)/shard_map/pallas_call | solution.py:354
  183.5 10.4 %all-to-all-done.2 = f32[16,256,128]{2,1,0:T(8,128)} async-done(((f32[16,256,128]{2,1,0:T(8,128)}), f32[16,256,128]{2,1,0:T(8,128)}, u32[]{:S(2)}, u32[]{:S(2)}) %all-to-all-start.2) | async-done | bytes 2097184 | tf_op jit(solution)/shard_map/all_to_all | solution.py:315
  193.9 2.3 shard_map.73.mine
  196.2 17.3 %all_to_all.36.tiles = bf16[16,16,128]{2,1,0:T(8,128)(2,1)S(1)} all-to-all(bf16[16,16,128]{2,1,0:T(8,128)(2,1)S(1)} %shard_map.73.mine), channel_id=1, replica_groups=mesh['x'=4,'y'=4,'c'=2,'z'=16] {'z'}, dimensions={0} | all-to-all | bytes 131072 | tf_op jit(solution)/shard_map/all_to_all | solution.py:315
  213.5 0.8 shard_map.74
  214.2 22.9 %all_to_all.37.near = bf16[16,336,128]{2,1,0:T(8,128)(2,1)S(1)} all-to-all(bf16[16,336,128]{2,1,0:T(8,128)(2,1)S(1)} %shard_map.74), channel_id=1, replica_groups=mesh['x'=4,'y'=4,'c'=2,'z'=16] {'x','y'}, dimensions={0} | all-to-all | bytes 2752512 | tf_op jit(solution)/shard_map/all_to_all | solution.py:315
  237.1 6.3 %collective-permute-start.8 = (bf16[16,336,128]{2,1,0:T(8,128)(2,1)S(1)}, bf16[16,336,128]{2,1,0:T(8,128)(2,1)S(1)}, u32[]{:S(2)}, u32[]{:S(2)}) collective-permute-start(bf16[16,336,128]{2,1,0:T(8,128)(2,1)S(1)} %all_to_all.37.near), channel_id=1, source_target_pairs={{0,16},{16,0},{1,17},{17,1},{2,18},{18,2},{3,19},{19,3},{4,20},{20... | collective-permute-start | bytes 4128776 | tf_op jit(solution)/shard_map/ppermute | solution.py:376
  243.4 1.4 shard_map.75
  244.8 1.4 collective-permute-done.8.far
  246.2 2.2 shard_map.77
  248.4 7.2 %shard_map.76 = bf16[4,128,1536]{2,1,0:T(8,128)(2,1)} custom-call(s32[3]{0:T(128)S(1)} %pad_add_fusion.place, bf16[16,384,128]{2,1,0:T(8,128)(2,1)S(1)} %all-to-all-done.1.state, bf16[16,336,128]{2,1,0:T(8,128)(2,1)S(1)} %all_to_all.37.near, bf16[16,336,128]{2,1,0:T(8,128)(2,1)S(1)} %collective-permute-done.8.far, bf16[4,128,128]{2,1,0:T(8,128)(2,1)S(1)} %get-tuple-element.17.low), custom_call_target="tpu_custom_call" | custom-call | flops 1200000000 | bytes 4000000 | tf_op jit(solution)/shard_map/pallas_call | solution.py:380
  (12 shorter events, 0.1 us)
Async XLA Ops:
  0.7 1.0 copy-start.1
  1.7 0.7 copy-start.4
  3.9 27.3 %all-to-all-start = ((bf16[16,16,128]{2,1,0:T(8,128)(2,1)}), bf16[16,16,128]{2,1,0:T(8,128)(2,1)S(1)}, u32[]{:S(2)}, u32[]{:S(2)}) async-start(bf16[16,16,128]{2,1,0:T(8,128)(2,1)} %shard_map.68), calls=%async_computation | async-start | bytes 131072 | tf_op jit(solution)/shard_map/all_to_all | solution.py:315
  19.7 1.0 copy-start.2
  20.7 1.0 copy-start.3
  21.7 0.7 copy-start.5
  31.2 74.2 %all-to-all-start.1 = ((bf16[16,384,128]{2,1,0:T(8,128)(2,1)}), bf16[16,384,128]{2,1,0:T(8,128)(2,1)S(1)}, u32[]{:S(2)}, u32[]{:S(2)}) async-start(bf16[16,384,128]{2,1,0:T(8,128)(2,1)} %bitcast.5), calls=%async_computation.1 | async-start | bytes 3145728 | tf_op jit(solution)/shard_map/all_to_all | solution.py:315
  36.4 10.0 %collective-permute-start.2 = (bf16[16,16,128]{2,1,0:T(8,128)(2,1)S(1)}, bf16[16,16,128]{2,1,0:T(8,128)(2,1)S(1)}, u32[]{:S(2)}, u32[]{:S(2)}) collective-permute-start(bf16[16,16,128]{2,1,0:T(8,128)(2,1)S(1)} %all-to-all-done), channel_id=1, source_target_pairs={{0,256},{128,384},{256,0},{384,128},{1,257},{129,385},{257,1},{385... | collective-permute-start | bytes 196616 | tf_op jit(solution)/shard_map/ppermute | solution.py:309
  41.1 5.3 %collective-permute-start.1 = (bf16[16,16,128]{2,1,0:T(8,128)(2,1)S(1)}, bf16[16,16,128]{2,1,0:T(8,128)(2,1)S(1)}, u32[]{:S(2)}, u32[]{:S(2)}) collective-permute-start(bf16[16,16,128]{2,1,0:T(8,128)(2,1)S(1)} %all-to-all-done), channel_id=1, source_target_pairs={{0,384},{128,0},{256,128},{384,256},{1,385},{129,1},{257,129},{385... | collective-permute-start | bytes 196616 | tf_op jit(solution)/shard_map/ppermute | solution.py:309
  43.9 6.5 %collective-permute-start = (bf16[16,16,128]{2,1,0:T(8,128)(2,1)S(1)}, bf16[16,16,128]{2,1,0:T(8,128)(2,1)S(1)}, u32[]{:S(2)}, u32[]{:S(2)}) collective-permute-start(bf16[16,16,128]{2,1,0:T(8,128)(2,1)S(1)} %all-to-all-done), channel_id=1, source_target_pairs={{0,128},{128,256},{256,384},{384,0},{1,129},{129,257},{257,385},{3... | collective-permute-start | bytes 196616 | tf_op jit(solution)/shard_map/ppermute | solution.py:309
  50.4 10.1 %collective-permute-start.5 = (bf16[4,16,16,128]{3,2,1,0:T(8,128)(2,1)S(1)}, bf16[4,16,16,128]{3,2,1,0:T(8,128)(2,1)S(1)}, u32[]{:S(2)}, u32[]{:S(2)}) collective-permute-start(bf16[4,16,16,128]{3,2,1,0:T(8,128)(2,1)S(1)} %get-tuple-element.20), channel_id=1, source_target_pairs={{0,64},{32,96},{64,0},{96,32},{1,65},{33,97},{65,1},{97,33},{2,66}... | collective-permute-start | bytes 786440 | tf_op jit(solution)/shard_map/ppermute | solution.py:309
  55.3 9.9 %collective-permute-start.4 = (bf16[4,16,16,128]{3,2,1,0:T(8,128)(2,1)S(1)}, bf16[4,16,16,128]{3,2,1,0:T(8,128)(2,1)S(1)}, u32[]{:S(2)}, u32[]{:S(2)}) collective-permute-start(bf16[4,16,16,128]{3,2,1,0:T(8,128)(2,1)S(1)} %get-tuple-element.20), channel_id=1, source_target_pairs={{0,96},{32,0},{64,32},{96,64},{1,97},{33,1},{65,33},{97,65},{2,98}... | collective-permute-start | bytes 786440 | tf_op jit(solution)/shard_map/ppermute | solution.py:309
  57.9 8.6 %collective-permute-start.3 = (bf16[4,16,16,128]{3,2,1,0:T(8,128)(2,1)S(1)}, bf16[4,16,16,128]{3,2,1,0:T(8,128)(2,1)S(1)}, u32[]{:S(2)}, u32[]{:S(2)}) collective-permute-start(bf16[4,16,16,128]{3,2,1,0:T(8,128)(2,1)S(1)} %get-tuple-element.20), channel_id=1, source_target_pairs={{0,32},{32,64},{64,96},{96,0},{1,33},{33,65},{65,97},{97,1},{2,34}... | collective-permute-start | bytes 786440 | tf_op jit(solution)/shard_map/ppermute | solution.py:309
  66.7 8.5 %collective-permute-start.6 = (bf16[16,16,16,128]{3,2,1,0:T(8,128)(2,1)S(1)}, bf16[16,16,16,128]{3,2,1,0:T(8,128)(2,1)S(1)}, u32[]{:S(2)}, u32[]{:S(2)}) collective-permute-start(bf16[16,16,16,128]{3,2,1,0:T(8,128)(2,1)S(1)} %bitcast.22), channel_id=1, source_target_pairs={{0,16},{16,0},{1,17},{17,1},{2,18},{18,2},{3,19},{19,3},{4,20},{20... | collective-permute-start | bytes 3145736 | tf_op jit(solution)/shard_map/ppermute | solution.py:311
  121.3 1.3 copy-start
  122.6 28.4 %collective-permute-start.7 = (f32[16,16,16,128]{3,2,1,0:T(8,128)}, f32[16,16,16,128]{3,2,1,0:T(8,128)}, u32[]{:S(2)}, u32[]{:S(2)}) collective-permute-start(f32[16,16,16,128]{3,2,1,0:T(8,128)} %get-tuple-element.15), channel_id=1, source_target_pairs={{0,16},{16,0},{1,17},{17,1},{2,18},{18,2},{3,19},{19,3},{4,20},{20... | collective-permute-start | bytes 6291464 | tf_op jit(solution)/shard_map/ppermute | solution.py:352
  147.3 12.8 %all-to-all-start.4 = ((f32[32,16,128]{2,1,0:T(8,128)}), f32[32,16,128]{2,1,0:T(8,128)S(1)}, u32[]{:S(2)}, u32[]{:S(2)}) async-start(f32[32,16,128]{2,1,0:T(8,128)} %broadcast_in_dim.2), calls=%async_computation.4 | async-start | bytes 524288 | tf_op jit(solution)/shard_map/all_to_all | solution.py:315
  160.1 33.8 %all-to-all-start.2 = ((f32[16,256,128]{2,1,0:T(8,128)}), f32[16,256,128]{2,1,0:T(8,128)}, u32[]{:S(2)}, u32[]{:S(2)}) async-start(f32[16,256,128]{2,1,0:T(8,128)} %bitcast.28), calls=%async_computation.2 | async-start | bytes 4194304 | tf_op jit(solution)/shard_map/all_to_all | solution.py:315
  183.5 30.0 %copy-start.6 = (s32[10]{0:T(128)S(1)}, s32[10]{0:T(128)}, u32[]{:S(2)}) copy-start(s32[10]{0:T(128)} %own.5) | copy-start | bytes 124
  237.1 9.1 %collective-permute-start.8 = (bf16[16,336,128]{2,1,0:T(8,128)(2,1)S(1)}, bf16[16,336,128]{2,1,0:T(8,128)(2,1)S(1)}, u32[]{:S(2)}, u32[]{:S(2)}) collective-permute-start(bf16[16,336,128]{2,1,0:T(8,128)(2,1)S(1)} %all_to_all.37.near), channel_id=1, source_target_pairs={{0,16},{16,0},{1,17},{17,1},{2,18},{18,2},{3,19},{19,3},{4,20},{20... | collective-permute-start | bytes 4128776 | tf_op jit(solution)/shard_map/ppermute | solution.py:376

commit v3 on v2

v3 whole, which is shorter than its diff:
```python
import functools
import math

import jax
import jax.numpy as jnp
from jax import lax
from jax.experimental import pallas as pl
from jax.experimental.pallas import tpu as pltpu
from jax.sharding import Mesh
from jax.sharding import PartitionSpec as P

D = 4096
HID = 1536
CAP = 2
EXPERTS = 10
GROUPS = 16
BLOCK = 96
RANK = 128

ridge_term = 0.001
feedback = 0.1
epsilon = 1e-06

F32 = jnp.float32
BF16 = jnp.bfloat16
HIGHEST = lax.Precision.HIGHEST
XY = ("x", "y")
FSDP = ("x", "y", "c")
SWAP = [(0, 1), (1, 0)]
VMEM = pl.BlockSpec(memory_space=pltpu.VMEM)
SMEM = pl.BlockSpec(memory_space=pltpu.SMEM)


def call(body, outs, scratch=(), flops=0, specs=None, n_in=0):
    return pl.pallas_call(
        body,
        out_shape=outs,
        in_specs=specs if specs is not None else [VMEM] * n_in,
        out_specs=jax.tree.map(lambda _: VMEM, outs),
        scratch_shapes=list(scratch),
        compiler_params=pltpu.CompilerParams(vmem_limit_bytes=48 * 1024 * 1024),
        cost_estimate=pl.CostEstimate(flops=flops, bytes_accessed=4_000_000, transcendentals=0),
    )


def dot(a, b, contract=((1,), (0,)), precision=None):
    return lax.dot_general(
        a, b, (contract, ((), ())), precision=precision, preferred_element_type=F32
    )


def iota(shape, dim):
    return lax.broadcasted_iota(jnp.int32, shape, dim)


COUNT, WORK, SECOND, HELPER, WHERE, FREE, TABLE = 0, 17, 34, 51, 68, 80, 97
NONE = GROUPS


def fill_table(own, table):
    for g in range(GROUPS + 1):
        table[COUNT + g] = 0
        table[WORK + g] = EXPERTS
        table[SECOND + g] = EXPERTS
        table[HELPER + g] = 0
    for e in range(EXPERTS):
        g = own[e]
        p = table[COUNT + g]
        table[COUNT + g] = p + 1
        table[WORK + jnp.where(p == 0, g, NONE)] = e
        table[SECOND + jnp.where(p == 0, NONE, g)] = e
    free = jnp.int32(0)
    for g in range(GROUPS):
        table[FREE + free] = g
        free = free + jnp.where(table[COUNT + g] == 0, 1, 0)
    used = jnp.int32(0)
    for e in range(EXPERTS):
        g = own[e]
        second = table[SECOND + g] == e
        h = table[FREE + used]
        table[WORK + jnp.where(second, h, NONE)] = e
        table[HELPER + jnp.where(second, g, NONE)] = h
        table[WHERE + e] = jnp.where(second, h, g)
        used = used + jnp.where(second, 1, 0)


def slice_right(own, place, right, out, table, held):
    fill_table(own, table)
    f = place[0] * 8 + place[1] * 2 + place[2]
    pick = (iota((8, 192), 1) == iota((8, 192), 0) + 8 * f).astype(BF16)
    for e in range(EXPERTS):
        held[e] = dot(pick, right[e].reshape(192, RANK))
    held[EXPERTS] = jnp.zeros((8, RANK), F32)

    def group(g, _):
        pair = jnp.concatenate([held[table[WORK + g]], held[table[SECOND + g]]], axis=0)
        out[g] = pair.astype(BF16)
        return 0

    lax.fori_loop(0, GROUPS, group, 0)


def place_state(table, momentum, gradient, first, other):
    def slot(g, _):
        for base, out in ((WORK, first), (SECOND, other)):
            e = table[base + g]

            @pl.when(e < EXPERTS)
            def _():
                total = momentum[e].astype(F32) + gradient[e].astype(F32)
                out[g] = total.astype(BF16).reshape(192, 128)

            @pl.when(e >= EXPERTS)
            def _():
                out[g] = jnp.zeros((192, 128), BF16)

        return 0

    lax.fori_loop(0, GROUPS, slot, 0)


def offset(i):
    return jnp.where(i == 1, 3, jnp.where(i == 2, 1, jnp.where(i == 3, 2, 0)))


def join_matrix(place, core, relative, chips):
    col = iota((384, 16 * chips), 1)
    chip = col >> 4
    if relative:
        x = (place[0] + offset(chip & 3)) & 3
        y = (place[1] + offset(chip >> 2)) & 3
        chip = x * 4 + y
    f = chip * 2 + core
    target = ((col >> 3) & 1) * 192 + 8 * f + (col & 7)
    return ((iota((384, 16 * chips), 0) == target) & (f < 24)).astype(BF16)


def join_right(place, near, far, out, matrix):
    c = place[2]
    matrix[:, :256] = join_matrix(place, c, True, 16)
    matrix[:, 256:] = join_matrix(place, 1 - c, True, 16)

    def block(z, _):
        a = near[:, z].reshape(256, RANK)
        b = far[:, z].reshape(256, RANK)
        both = jnp.concatenate([a, b], axis=0)
        out[z] = dot(matrix[...], both).astype(BF16)
        return 0

    lax.fori_loop(0, GROUPS, block, 0)


def split3(value):
    high = value.astype(BF16)
    rest = value - high.astype(F32)
    middle = rest.astype(BF16)
    low = (rest - middle.astype(F32)).astype(BF16)
    return high, middle, low


def panel_of(state, right, kind, slot):
    def block(z, total):
        a = state[z, kind * BLOCK : (kind + 1) * BLOCK, :]
        b = right[z, pl.ds(slot * 192 + kind * BLOCK, BLOCK), :]
        return total + dot(a, b, ((0,), (0,)))

    return lax.fori_loop(0, GROUPS, block, jnp.zeros((128, RANK), F32), unroll=4)


def panels(place, state, right, panel, keep, send):
    grams = []
    for k in range(2):
        value = panel_of(state, right, k, 0)
        panel[k] = value
        grams.append(dot(value, value, ((0,), (0,)), HIGHEST))
    mine = place[2] == 0
    keep[...] = jnp.where(mine, grams[0], grams[1])
    send[...] = jnp.where(mine, grams[1], grams[0])


def second_panels(state, right, panel):
    for k in range(2):
        panel[k] = panel_of(state, right, k, 1)


def weigh(place, state, panel, keep, send, rows):
    weights = [jnp.concatenate(split3(panel[k]), axis=1) for k in range(2)]
    rows[192:, :] = jnp.zeros((64, RANK), F32)

    def block(z, _):
        for k in range(2):
            value = dot(state[z, k * BLOCK : (k + 1) * BLOCK, :], weights[k])
            total = value[:, :128] + (value[:, 128:256] + value[:, 256:])
            rows[k * BLOCK : (k + 1) * BLOCK, :] = total
        for i in range(16):
            x = (place[0] + offset(i & 3)) & 3
            y = (place[1] + offset(i >> 2)) & 3
            base = (x * 4 + y) * 16
            near = pl.multiple_of(base + 8 * place[2], 8)
            far = pl.multiple_of(base + 8 - 8 * place[2], 8)
            keep[i, z] = rows[pl.ds(near, 8), :]
            send[i, z] = rows[pl.ds(far, 8), :]
        return 0

    lax.fori_loop(0, GROUPS, block, 0, unroll=2)


def invert(place, near, far, out, work, *, size):
    n = RANK
    eye = (iota((n, n), 0) == iota((n, n), 1)).astype(F32)
    mine = place[2] == 0
    first, other = near[...], far[...]
    work[0, :, :n] = jnp.where(mine, first, other) + ridge_term * eye
    work[1, :, :n] = jnp.where(mine, other, first) + ridge_term * eye
    for m in range(2):
        work[m, :, n:] = eye
    row = iota((size, 2 * n), 0)
    lane = iota((size, n), 1)
    for k in range(0, n, size):
        blocks = [work[m, k : k + size, :] for m in range(2)]
        for i in range(size):
            for m in range(2):
                b = blocks[m]
                scale = lax.rsqrt(b[i : i + 1, k + i : k + i + 1])
                line = b[i : i + 1, :] * scale
                column = jnp.where(row > i, b[:, k + i : k + i + 1] * scale, 0.0)
                blocks[m] = jnp.where(row == i, line, b - column * line)
        for m in range(2):
            b = blocks[m]
            out[m, k : k + size, :] = b[:, n:]
            if k + size < n:
                left = jnp.where(lane >= k + size, b[:, :n], 0.0)
                change = dot(left, b, ((0,), (0,)), HIGHEST)
                work[m, k + size :, :] -= change[k + size :, :]


def scale_factor(place, inverse, a, b, c, d, out):
    f = place[0] * 8 + place[1] * 2 + place[2]
    total = ((a[...] + b[...]) + (c[...] + d[...])).reshape(128, RANK)
    kind = jnp.where(f >= 12, 1, 0)
    out[:128] = dot(total, inverse[kind], ((1,), (1,)), HIGHEST).astype(BF16)
    half = jnp.where(f >= 16, 1, 0)
    start = pl.multiple_of(8 * f - 128 * half, 8)
    rows = inverse[half, pl.ds(start, 8), :]
    high = rows.astype(BF16).astype(F32)
    out[128:] = jnp.concatenate([high, rows - high], axis=0).astype(BF16)


def orthonormal(table, place, panel, inverse, left, low):
    owned = table[COUNT + place[3]] > 0
    for k in range(2):
        ortho = dot(panel[k], inverse[k], ((1,), (1,)), HIGHEST)
        ortho = jnp.where(owned, ortho, 0.0)
        left[k] = ortho * math.sqrt(D)
        low[k] = (ortho * (-feedback)).astype(BF16)


def turn(table, place, first, second, out):
    owned = table[COUNT + place[3]] > 0
    eye = (iota((128, 128), 0) == iota((128, 128), 1)).astype(BF16)
    some = jnp.where(owned, eye, jnp.zeros_like(eye))
    for s, (state, unit) in enumerate(((first, some), (second, eye))):
        for k in range(2):
            rows = state[:, k * BLOCK : (k + 1) * BLOCK, :].reshape(HID, 128)
            out[2 * s + k] = dot(unit, rows, ((1,), (1,))).astype(BF16)


ROWS = 368


def select(table, place, mine, tiles, out, packed):
    z = place[3]
    packed[:128, :] = mine[:128, :]
    packed[128:272, :] = tiles[table[HELPER + z]]
    start = pl.multiple_of((z >> 1) * 16, 16)
    upper = (z & 1) == 1
    sums = []
    for e in range(0, EXPERTS, 2):
        pair = []
        for i in range(2):
            p = table[WHERE + e + i]
            value = tiles[p, pl.ds(start, 16), :].astype(F32)
            pair.append(jnp.where(upper, value[8:], value[:8]))
            whole = tiles[p, :128, :].astype(F32)
            sums.append(jnp.sum(whole * whole, axis=0, keepdims=True))
        packed[272 + e * 8 : 288 + e * 8, :] = jnp.concatenate(pair, axis=0).astype(BF16)
    sums.append(jnp.zeros((16 - EXPERTS, RANK), F32))
    packed[352:, :] = jnp.concatenate(sums, axis=0).astype(BF16)
    value = packed[...]
    for i in range(16):
        out[i] = value


def finish_right(place, near, far, out):
    c = place[2]
    matrix = jnp.concatenate(
        [join_matrix(place, c, False, 12), join_matrix(place, 1 - c, False, 12)], axis=1
    )
    parts = near[:, 352:, :].astype(F32) + far[:, 352:, :].astype(F32)
    sums = [jnp.sum(parts[6 * k : 6 * k + 6], axis=0) for k in range(2)]
    scales = [lax.rsqrt(s * (1.0 / HID) + epsilon) for s in sums]
    for g in range(EXPERTS // 2):
        rows = slice(272 + g * 16, 288 + g * 16)
        data = jnp.concatenate(
            [near[:12, rows, :].reshape(192, RANK), far[:12, rows, :].reshape(192, RANK)], axis=0
        )
        value = dot(matrix, data)
        for s in range(2):
            e = 2 * g + s
            for k in range(2):
                i = 2 * s + k
                out[e, k] = value[i * BLOCK : (i + 1) * BLOCK, :] * scales[k][e : e + 1, :]


def finish_state(table, place, turned, near, far, low, panel, left, out, left_out, inverse, wide):
    c = place[2]
    matrix = jnp.concatenate(
        [join_matrix(place, c, False, 12), join_matrix(place, 1 - c, False, 12)], axis=1
    )
    for part, core in ((near, c), (far, 1 - c)):
        for chip in range(16):
            value = part[chip, 256:272, :].astype(F32)
            row = pl.multiple_of(16 * chip + 8 * core, 8)
            inverse[pl.ds(row, 8), :] = value[:8] + value[8:]
    some = table[SECOND + place[3]] < EXPERTS
    lows = [low[0], low[1]]
    for k in range(2):
        ortho = dot(panel[k], inverse[k * RANK : (k + 1) * RANK, :], ((1,), (1,)), HIGHEST)
        ortho = jnp.where(some, ortho, 0.0)
        left_out[k] = left[k]
        left_out[2 + k] = ortho * math.sqrt(D)
        lows.append((ortho * (-feedback)).astype(BF16))
    for s in range(2):
        for g in range(8):
            rows = slice(s * 128 + g * 16, s * 128 + g * 16 + 16)
            data = jnp.concatenate(
                [near[:12, rows, :].reshape(192, RANK), far[:12, rows, :].reshape(192, RANK)],
                axis=0,
            )
            value = dot(matrix, data).astype(BF16)
            for p in range(2):
                for k in range(2):
                    i = 2 * p + k
                    first = (2 * g + p) * BLOCK
                    wide[2 * s + k, first : first + BLOCK, :] = value[i * BLOCK : (i + 1) * BLOCK]
    for i in range(4):
        change = dot(lows[i], wide[i], ((1,), (1,)))
        out[i] = (turned[i].astype(F32) + change).astype(BF16)


def ring(shift):
    return [(i, (i + shift) % 4) for i in range(4)]


SHIFTS = (3, 1, 2)


def gather_slices(x):
    for axis in ("x", "y"):
        x = jnp.stack([x] + [lax.ppermute(x, axis, ring((4 - d) % 4)) for d in SHIFTS])
    x = x.reshape((16,) + x.shape[2:])
    return x, lax.ppermute(x, "c", SWAP)


def spread_sum(x, axis):
    parts = [lax.ppermute(x, axis, ring(d)) for d in SHIFTS]
    return (x + parts[0]) + (parts[1] + parts[2])


def exchange(x, axis):
    return lax.all_to_all(x, axis, split_axis=0, concat_axis=0, tiled=True)


def shards(momentum, gradient, right_in, owners):
    sds = jax.ShapeDtypeStruct
    barrier = lax.optimization_barrier
    place = jnp.stack([lax.axis_index(a) for a in ("x", "y", "c", "z")]).astype(jnp.int32)
    slices, table = pl.pallas_call(
        slice_right,
        out_shape=(sds((16, 16, RANK), BF16), sds((TABLE,), jnp.int32)),
        in_specs=[SMEM, SMEM, VMEM],
        out_specs=(VMEM, SMEM),
        scratch_shapes=[pltpu.VMEM((EXPERTS + 1, 8, RANK), F32)],
    )(owners, place, right_in)
    slices = exchange(slices, "z")
    block = sds((16, 192, 128), BF16)
    sent, late = call(place_state, (block, block), specs=[SMEM, VMEM, VMEM])(
        table, jnp.swapaxes(momentum, 2, 3), jnp.swapaxes(gradient, 2, 3)
    )
    sent, slices = barrier((sent, slices))
    state = exchange(sent, "z")
    near, far = gather_slices(slices)
    right = call(
        join_right,
        sds((16, 384, RANK), BF16),
        [pltpu.VMEM((384, 512), BF16)],
        flops=800_000_000,
        specs=[SMEM, VMEM, VMEM],
    )(place, near, far)
    square = sds((RANK, RANK), F32)
    two = sds((2, 128, RANK), F32)
    panel, keep, send = call(
        panels, (two, square, square), specs=[SMEM, VMEM, VMEM], flops=300_000_000
    )(place, state, right)
    late, send = barrier((late, send))
    second = exchange(late, "z")
    gram = keep + lax.ppermute(send, "c", SWAP)
    half = sds((16, 16, 8, RANK), F32)
    keep, send = call(
        weigh, (half, half), [pltpu.VMEM((256, RANK), F32)], specs=[SMEM, VMEM, VMEM], flops=400_000_000
    )(place, state, panel)
    gram = spread_sum(spread_sum(gram, "x"), "y")
    other = lax.ppermute(gram, "c", SWAP)
    parts = keep + lax.ppermute(send, "c", SWAP)
    parts = parts.reshape(4, 4, 16, 8, RANK)
    moved = [lax.ppermute(parts[:, i + 1], "x", ring(SHIFTS[i])) for i in range(3)]
    parts = (parts[:, 0] + moved[0]) + (moved[1] + moved[2])
    parts = [parts[0]] + [lax.ppermute(parts[i + 1], "y", ring(SHIFTS[i])) for i in range(3)]
    inverse = call(
        functools.partial(invert, size=8),
        sds((2, RANK, RANK), F32),
        [pltpu.VMEM((2, RANK, 2 * RANK), F32)],
        specs=[SMEM, VMEM, VMEM],
        flops=4_000_000_000,
    )(place, gram, other)
    mine = call(
        scale_factor, sds((144, RANK), BF16), specs=[SMEM] + [VMEM] * 5, flops=100_000_000
    )(place, inverse, *parts)
    left, low = call(
        orthonormal, (two, sds((2, 128, RANK), BF16)), specs=[SMEM, SMEM, VMEM, VMEM], flops=100_000_000
    )(table, place, panel, inverse)
    tiles = lax.all_gather(mine, "z")
    second_panel = call(second_panels, two, n_in=2, flops=200_000_000)(second, right)
    turned = call(
        turn, sds((4, 128, HID), BF16), specs=[SMEM, SMEM, VMEM, VMEM], flops=200_000_000
    )(table, place, state, second)
    chosen = call(
        select,
        sds((16, ROWS, RANK), BF16),
        [pltpu.VMEM((ROWS, RANK), BF16)],
        specs=[SMEM, SMEM, VMEM, VMEM],
    )(table, place, mine, tiles)
    near = exchange(chosen, XY)
    far = lax.ppermute(near, "c", SWAP)
    right_out = call(
        finish_right, sds((EXPERTS, 2, BLOCK, RANK), F32), specs=[SMEM, VMEM, VMEM], flops=300_000_000
    )(place, near, far)
    state_out, left_out = call(
        finish_state,
        (sds((4, 128, HID), BF16), sds((4, 128, RANK), F32)),
        [pltpu.VMEM((2 * RANK, RANK), F32), pltpu.VMEM((4, HID, RANK), BF16)],
        specs=[SMEM, SMEM] + [VMEM] * 6,
        flops=1_200_000_000,
    )(table, place, turned, near, far, low, second_panel, left)
    return (
        state_out.reshape(CAP, 2, 128, HID),
        left_out.reshape(CAP, 2, 128, RANK),
        right_out,
    )


def solution(mesh):
    fine = Mesh(mesh.devices.reshape(4, 4, 2, 16), ("x", "y", "c", "z"))
    return jax.shard_map(
        shards,
        mesh=fine,
        in_specs=(
            P(None, None, FSDP, "z"),
            P(None, None, FSDP, "z"),
            P(None, None, "z", None),
            P(),
        ),
        out_specs=(
            P("z", None, FSDP, None),
            P("z", None, FSDP, None),
            P(None, None, "z", None),
        ),
        check_vma=False,
    )
```

time: 256 us -> 260 us (1.016)
  the two profiles are of different devices: /device:TPU:1 before, /device:TPU:32 now
where the time goes in v3:
time: 260 us; the launch traced here: 259 us
  starting transfers between devices  105 us (40%)
  blocking collectives  51.2 us (20%)
  waiting for transfers between devices  51.1 us (20%)
  Pallas kernels  45.9 us (18%)
  local copies, waits for them, and re-layouts  3.6 us (1%)
    all_to_all x3, starting transfers between devices, exchange(): return lax.all_to_all(x, axis, split_axis=0, concat_axis=0, tiled=True)  32.1 us
    all_gather x1, blocking collectives, shards(): tiles = lax.all_gather(mine, 'z')  31.2 us
    all_to_all x3, waiting for transfers between devices, exchange(): return lax.all_to_all(x, axis, split_axis=0, concat_axis=0, tiled=True)  30 us
    ppermute x6, starting transfers between devices, gather_slices(): lax.ppermute(x, axis, ring((4 - d) % 4))  21.7 us
    all_to_all x1, blocking collectives, exchange(): return lax.all_to_all(x, axis, split_axis=0, concat_axis=0, tiled=True)  20 us
    ppermute x6, starting transfers between devices, spread_sum(): parts = [lax.ppermute(x, axis, ring(d)) for d in SHIFTS]  19.6 us
    pallas_call x1, Pallas kernels, shards(): call(functools.partial(invert, size=8), sds((2, RANK, RANK), F32), [pltpu...  16.6 us
    ppermute x6, waiting for transfers between devices, gather_slices(): lax.ppermute(x, axis, ring((4 - d) % 4))  12.5 us
  transfers between devices with their start and end apart: 26, of which 11 were waited for; matrix products, arithmetic and copies ran while one was open for 0% of the time, Pallas kernels for 11%

profile of v3, /device:TPU:32, one launch (start us, length us, event | category | flops | bytes accessed | tf_op | source)
XLA Modules:
  0.0 258.9 jit_solution(4222342006470322823)
XLA Ops:
  1.3 2.1 shard_map.67
  3.4 15.2 %all-to-all-start = ((bf16[16,16,128]{2,1,0:T(8,128)(2,1)}), bf16[16,16,128]{2,1,0:T(8,128)(2,1)S(1)}, u32[]{:S(2)}, u32[]{:S(2)}) async-start(bf16[16,16,128]{2,1,0:T(8,128)(2,1)} %get-tuple-element.22), calls=%async_computation | async-start | bytes 131072 | tf_op jit(solution)/shard_map/all_to_all | solution.py:371
  18.6 1.0 copy-done.3
  19.6 1.0 copy-done.4
  21.2 2.2 shard_map.68
  24.3 5.9 %all-to-all-done = bf16[16,16,128]{2,1,0:T(8,128)(2,1)S(1)} async-done(((bf16[16,16,128]{2,1,0:T(8,128)(2,1)}), bf16[16,16,128]{2,1,0:T(8,128)(2,1)S(1)}, u32[]{:S(2)}, u32[]{:S(2)}) %all-to-all-start) | async-done | bytes 65568 | tf_op jit(solution)/shard_map/all_to_all | solution.py:371
  30.1 6.2 %all-to-all-start.1 = ((bf16[16,192,128]{2,1,0:T(8,128)(2,1)}), bf16[16,192,128]{2,1,0:T(8,128)(2,1)S(1)}, u32[]{:S(2)}, u32[]{:S(2)}) async-start(bf16[16,192,128]{2,1,0:T(8,128)(2,1)} %get-tuple-element.23), calls=%async_computation.1 | async-start | bytes 1572864 | tf_op jit(solution)/shard_map/all_to_all | solution.py:371
  36.3 4.9 %collective-permute-start.2 = (bf16[16,16,128]{2,1,0:T(8,128)(2,1)S(1)}, bf16[16,16,128]{2,1,0:T(8,128)(2,1)S(1)}, u32[]{:S(2)}, u32[]{:S(2)}) collective-permute-start(bf16[16,16,128]{2,1,0:T(8,128)(2,1)S(1)} %all-to-all-done), channel_id=1, source_target_pairs={{0,256},{128,384},{256,0},{384,128},{1,257},{129,385},{257,1},{385... | collective-permute-start | bytes 196616 | tf_op jit(solution)/shard_map/ppermute | solution.py:360
  41.2 3.0 %collective-permute-start.1 = (bf16[16,16,128]{2,1,0:T(8,128)(2,1)S(1)}, bf16[16,16,128]{2,1,0:T(8,128)(2,1)S(1)}, u32[]{:S(2)}, u32[]{:S(2)}) collective-permute-start(bf16[16,16,128]{2,1,0:T(8,128)(2,1)S(1)} %all-to-all-done), channel_id=1, source_target_pairs={{0,384},{128,0},{256,128},{384,256},{1,385},{129,1},{257,129},{385... | collective-permute-start | bytes 196616 | tf_op jit(solution)/shard_map/ppermute | solution.py:360
  44.3 2.8 %collective-permute-start = (bf16[16,16,128]{2,1,0:T(8,128)(2,1)S(1)}, bf16[16,16,128]{2,1,0:T(8,128)(2,1)S(1)}, u32[]{:S(2)}, u32[]{:S(2)}) collective-permute-start(bf16[16,16,128]{2,1,0:T(8,128)(2,1)S(1)} %all-to-all-done), channel_id=1, source_target_pairs={{0,128},{128,256},{256,384},{384,0},{1,129},{129,257},{257,385},{3... | collective-permute-start | bytes 196616 | tf_op jit(solution)/shard_map/ppermute | solution.py:360
  47.4 4.3 %collective-permute-done = bf16[16,16,128]{2,1,0:T(8,128)(2,1)S(1)} collective-permute-done((bf16[16,16,128]{2,1,0:T(8,128)(2,1)S(1)}, bf16[16,16,128]{2,1,0:T(8,128)(2,1)S(1)}, u32[]{:S(2)}, u32[]{:S(2)}) %collective-permute-start) | collective-permute-done | bytes 65568 | tf_op jit(solution)/shard_map/ppermute | solution.py:360
  51.7 4.9 %collective-permute-start.4 = (bf16[4,16,16,128]{3,2,1,0:T(8,128)(2,1)S(1)}, bf16[4,16,16,128]{3,2,1,0:T(8,128)(2,1)S(1)}, u32[]{:S(2)}, u32[]{:S(2)}) collective-permute-start(bf16[4,16,16,128]{3,2,1,0:T(8,128)(2,1)S(1)} %get-tuple-element.45), channel_id=1, source_target_pairs={{0,96},{32,0},{64,32},{96,64},{1,97},{33,1},{65,33},{97,65},{2,98}... | collective-permute-start | bytes 786440 | tf_op jit(solution)/shard_map/ppermute | solution.py:360
  56.6 1.9 collective-permute-start.3
  58.6 4.1 %collective-permute-start.5 = (bf16[4,16,16,128]{3,2,1,0:T(8,128)(2,1)S(1)}, bf16[4,16,16,128]{3,2,1,0:T(8,128)(2,1)S(1)}, u32[]{:S(2)}, u32[]{:S(2)}) collective-permute-start(bf16[4,16,16,128]{3,2,1,0:T(8,128)(2,1)S(1)} %get-tuple-element.45), channel_id=1, source_target_pairs={{0,64},{32,96},{64,0},{96,32},{1,65},{33,97},{65,1},{97,33},{2,66}... | collective-permute-start | bytes 786440 | tf_op jit(solution)/shard_map/ppermute | solution.py:360
  62.7 7.9 %collective-permute-done.3 = bf16[4,16,16,128]{3,2,1,0:T(8,128)(2,1)S(1)} collective-permute-done((bf16[4,16,16,128]{3,2,1,0:T(8,128)(2,1)S(1)}, bf16[4,16,16,128]{3,2,1,0:T(8,128)(2,1)S(1)}, u32[]{:S(2)}, u32[]{:S(2)}) %collective-permute-start.3) | collective-permute-done | bytes 262176 | tf_op jit(solution)/shard_map/ppermute | solution.py:360
  70.7 1.9 collective-permute-start.6
  72.7 2.6 %collective-permute-done.6.far = bf16[16,16,16,128]{3,2,1,0:T(8,128)(2,1)S(1)} collective-permute-done((bf16[16,16,16,128]{3,2,1,0:T(8,128)(2,1)S(1)}, bf16[16,16,16,128]{3,2,1,0:T(8,128)(2,1)S(1)}, u32[]{:S(2)}, u32[]{:S(2)}) %collective-permute-start.6) | collective-permute-done | bytes 1048608 | tf_op jit(solution)/shard_map/ppermute | solution.py:362
  75.3 4.9 %shard_map.69.right = bf16[16,384,128]{2,1,0:T(8,128)(2,1)S(1)} custom-call(s32[4]{0:T(128)S(1)} %copy-done.5, bf16[16,16,16,128]{3,2,1,0:T(8,128)(2,1)S(1)} %bitcast.49, bf16[16,16,16,128]{3,2,1,0:T(8,128)(2,1)S(1)} %collective-permute-done.6.far), custom_call_target="tpu_custom_call" | custom-call | flops 800000000 | bytes 4000000 | tf_op jit(solution)/shard_map/pallas_call | solution.py:393
  80.2 2.8 %shard_map.70 = (f32[2,128,128]{2,1,0:T(8,128)S(1)}, f32[128,128]{1,0:T(8,128)S(1)}, f32[128,128]{1,0:T(8,128)S(1)}) custom-call(s32[4]{0:T(128)S(1)} %copy-done.5, bf16[16,192,128]{2,1,0:T(8,128)(2,1)S(1)} %all-to-all-done.1.state.first, bf16[16,384,128]{2,1,0:T(8,128)(2,1)S(1)} %shard_map.69.right), custom_call_target="tpu_custom_call" | custom-call | flops 300000000 | bytes 4000000 | tf_op jit(solution)/shard_map/pallas_call | solution.py:402
  83.0 2.6 %shard_map.73 = (f32[16,16,8,128]{3,2,1,0:T(8,128)S(1)}, f32[16,16,8,128]{3,2,1,0:T(8,128)S(1)}) custom-call(s32[4]{0:T(128)S(1)} %copy-done.5, bf16[16,192,128]{2,1,0:T(8,128)(2,1)S(1)} %all-to-all-done.1.state.first, f32[2,128,128]{2,1,0:T(8,128)S(1)} %get-tuple-element.30.panel), custom_call_target="tpu_custom_call" | custom-call | flops 400000000 | bytes 4000000 | tf_op jit(solution)/shard_map/pallas_call | solution.py:409
  85.6 2.0 collective-permute-start.15
  87.6 2.3 collective-permute-start.7
  90.8 2.2 collective-permute-start.10
  93.1 2.1 collective-permute-start.9
  95.2 4.9 %collective-permute-start.8 = (f32[128,128]{1,0:T(8,128)S(1)}, f32[128,128]{1,0:T(8,128)S(1)}, u32[]{:S(2)}, u32[]{:S(2)}) collective-permute-start(f32[128,128]{1,0:T(8,128)S(1)} %add.33), channel_id=1, source_target_pairs={{0,384},{128,0},{256,128},{384,256},{1,385},{129,1},{257,129},{385... | collective-permute-start | bytes 196616 | tf_op jit(solution)/shard_map/ppermute | solution.py:366
  100.4 1.9 collective-permute-done.8
  102.3 3.2 %collective-permute-start.13 = (f32[128,128]{1,0:T(8,128)S(1)}, f32[128,128]{1,0:T(8,128)S(1)}, u32[]{:S(2)}, u32[]{:S(2)}) collective-permute-start(f32[128,128]{1,0:T(8,128)S(1)} %add_add_fusion.1), channel_id=1, source_target_pairs={{0,64},{32,96},{64,0},{96,32},{1,65},{33,97},{65,1},{97,33},{2,66}... | collective-permute-start | bytes 196616 | tf_op jit(solution)/shard_map/ppermute | solution.py:366
  105.6 2.4 collective-permute-start.12
  108.0 4.6 %collective-permute-start.11 = (f32[128,128]{1,0:T(8,128)S(1)}, f32[128,128]{1,0:T(8,128)S(1)}, u32[]{:S(2)}, u32[]{:S(2)}) collective-permute-start(f32[128,128]{1,0:T(8,128)S(1)} %add_add_fusion.1), channel_id=1, source_target_pairs={{0,96},{32,0},{64,32},{96,64},{1,97},{33,1},{65,33},{97,65},{2,98}... | collective-permute-start | bytes 196616 | tf_op jit(solution)/shard_map/ppermute | solution.py:366
  112.8 4.2 %collective-permute-start.18 = (f32[4,16,8,128]{3,2,1,0:T(8,128)S(1)}, f32[4,16,8,128]{3,2,1,0:T(8,128)S(1)}, u32[]{:S(2)}, u32[]{:S(2)}) collective-permute-start(f32[4,16,8,128]{3,2,1,0:T(8,128)S(1)} %get-tuple-element.37), channel_id=1, source_target_pairs={{0,256},{128,384},{256,0},{384,128},{1,257},{129,385},{257,1},{385... | collective-permute-start | bytes 786440 | tf_op jit(solution)/shard_map/ppermute | solution.py:416
  117.1 3.7 %collective-permute-start.17 = (f32[4,16,8,128]{3,2,1,0:T(8,128)S(1)}, f32[4,16,8,128]{3,2,1,0:T(8,128)S(1)}, u32[]{:S(2)}, u32[]{:S(2)}) collective-permute-start(f32[4,16,8,128]{3,2,1,0:T(8,128)S(1)} %get-tuple-element.38), channel_id=1, source_target_pairs={{0,128},{128,256},{256,384},{384,0},{1,129},{129,257},{257,385},{3... | collective-permute-start | bytes 786440 | tf_op jit(solution)/shard_map/ppermute | solution.py:416
  120.8 3.3 %collective-permute-start.16 = (f32[4,16,8,128]{3,2,1,0:T(8,128)S(1)}, f32[4,16,8,128]{3,2,1,0:T(8,128)S(1)}, u32[]{:S(2)}, u32[]{:S(2)}) collective-permute-start(f32[4,16,8,128]{3,2,1,0:T(8,128)S(1)} %get-tuple-element.39), channel_id=1, source_target_pairs={{0,384},{128,0},{256,128},{384,256},{1,385},{129,1},{257,129},{385... | collective-permute-start | bytes 786440 | tf_op jit(solution)/shard_map/ppermute | solution.py:416
  124.2 1.9 collective-permute-start.14
  126.1 2.1 collective-permute-done.17
  129.2 2.9 %collective-permute-start.21 = (f32[16,8,128]{2,1,0:T(8,128)S(1)}, f32[16,8,128]{2,1,0:T(8,128)S(1)}, u32[]{:S(2)}, u32[]{:S(2)}) collective-permute-start(f32[16,8,128]{2,1,0:T(8,128)S(1)} %get-tuple-element.40), channel_id=1, source_target_pairs={{0,64},{32,96},{64,0},{96,32},{1,65},{33,97},{65,1},{97,33},{2,66}... | collective-permute-start | bytes 196616 | tf_op jit(solution)/shard_map/ppermute | solution.py:418
  132.1 1.9 collective-permute-start.20
  134.0 5.1 %collective-permute-start.19 = (f32[16,8,128]{2,1,0:T(8,128)S(1)}, f32[16,8,128]{2,1,0:T(8,128)S(1)}, u32[]{:S(2)}, u32[]{:S(2)}) collective-permute-start(f32[16,8,128]{2,1,0:T(8,128)S(1)} %get-tuple-element.42), channel_id=1, source_target_pairs={{0,96},{32,0},{64,32},{96,64},{1,97},{33,1},{65,33},{97,65},{2,98}... | collective-permute-start | bytes 196616 | tf_op jit(solution)/shard_map/ppermute | solution.py:418
  139.2 16.6 %shard_map.72.inverse = f32[2,128,128]{2,1,0:T(8,128)S(1)} custom-call(s32[4]{0:T(128)S(1)} %copy-done.5, f32[128,128]{1,0:T(8,128)S(1)} %add_add_fusion.near, f32[128,128]{1,0:T(8,128)S(1)} %collective-permute-done.14.far), custom_call_target="tpu_custom_call" | custom-call | flops 4000000000 | bytes 4000000 | tf_op jit(solution)/shard_map/pallas_call | solution.py:419
  156.6 31.2 %all-gather = bf16[2304,128]{1,0:T(8,128)(2,1)S(1)} all-gather(bf16[144,128]{1,0:T(8,128)(2,1)S(1)} %shard_map.74.mine), channel_id=2, replica_groups=mesh['x'=4,'y'=4,'c'=2,'z'=16] {'z'}, dimensions={0}, use_global_device_ids=true | all-gather | bytes 626688 | tf_op jit(solution)/shard_map/all_gather | solution.py:432
  188.7 20.0 %all_to_all.20.near = bf16[16,368,128]{2,1,0:T(8,128)(2,1)S(1)} all-to-all(bf16[16,368,128]{2,1,0:T(8,128)(2,1)S(1)} %shard_map.75), channel_id=1, replica_groups=mesh['x'=4,'y'=4,'c'=2,'z'=16] {'x','y'}, dimensions={0} | all-to-all | bytes 3014656 | tf_op jit(solution)/shard_map/all_to_all | solution.py:371
  208.7 10.7 %all-to-all-start.2 = ((bf16[16,192,128]{2,1,0:T(8,128)(2,1)}), bf16[16,192,128]{2,1,0:T(8,128)(2,1)}, u32[]{:S(2)}, u32[]{:S(2)}) async-start(bf16[16,192,128]{2,1,0:T(8,128)(2,1)} %copy-done.2), calls=%async_computation.2 | async-start | bytes 1572864 | tf_op jit(solution)/shard_map/all_to_all | solution.py:371
  219.4 2.1 collective-permute-start.22
  221.5 0.9 shard_map.76
  222.5 24.2 %all-to-all-done.2.second.state = bf16[16,192,128]{2,1,0:T(8,128)(2,1)} async-done(((bf16[16,192,128]{2,1,0:T(8,128)(2,1)}), bf16[16,192,128]{2,1,0:T(8,128)(2,1)}, u32[]{:S(2)}, u32[]{:S(2)}) %all-to-all-start.2) | async-done | bytes 786464 | tf_op jit(solution)/shard_map/all_to_all | solution.py:371
  246.6 2.9 %shard_map.77.panel = f32[2,128,128]{2,1,0:T(8,128)S(1)} custom-call(bf16[16,192,128]{2,1,0:T(8,128)(2,1)} %all-to-all-done.2.second.state, bf16[16,384,128]{2,1,0:T(8,128)(2,1)S(1)} %shard_map.69.right), custom_call_target="tpu_custom_call" | custom-call | flops 200000000 | bytes 4000000 | tf_op jit(solution)/shard_map/pallas_call | solution.py:433
  249.6 1.7 shard_map.71.turned
  251.3 2.9 %shard_map.79 = f32[10,2,96,128]{3,2,1,0:T(8,128)} custom-call(s32[4]{0:T(128)S(1)} %copy-done.5, bf16[16,368,128]{2,1,0:T(8,128)(2,1)S(1)} %all_to_all.20.near, bf16[16,368,128]{2,1,0:T(8,128)(2,1)} %collective-permute-done.22.far), custom_call_target="tpu_custom_call" | custom-call | flops 300000000 | bytes 4000000 | tf_op jit(solution)/shard_map/pallas_call | solution.py:445
  254.2 4.7 %shard_map.78 = (bf16[4,128,1536]{2,1,0:T(8,128)(2,1)}, f32[4,128,128]{2,1,0:T(8,128)}) custom-call(s32[97]{0:T(128)S(1)} %copy-done.7, s32[4]{0:T(128)S(1)} %copy-done.5, bf16[4,128,1536]{2,1,0:T(8,128)(2,1)S(1)} %shard_map.71.turned, bf16[16,368,128]{2,1,0:T(8,128)(2,1)S(1)} %all_to_all.20.near, bf16[16,368,128]{2,1,0:T(8,128)(2,1)} %collective-permute-done.22.far, ...), custom_call_target="tpu_custom_call" | custom-call | flops 1200000000 | bytes 4000000 | tf_op jit(solution)/shard_map/pallas_call | solution.py:448
  (45 shorter events, 6.6 us)
Async XLA Ops:
  3.4 26.8 %all-to-all-start = ((bf16[16,16,128]{2,1,0:T(8,128)(2,1)}), bf16[16,16,128]{2,1,0:T(8,128)(2,1)S(1)}, u32[]{:S(2)}, u32[]{:S(2)}) async-start(bf16[16,16,128]{2,1,0:T(8,128)(2,1)} %get-tuple-element.22), calls=%async_computation | async-start | bytes 131072 | tf_op jit(solution)/shard_map/all_to_all | solution.py:371
  18.6 1.0 copy-start.3
  19.6 1.0 copy-start.4
  20.6 0.6 copy-start.6
  23.4 0.9 copy-start.2
  30.1 50.1 %all-to-all-start.1 = ((bf16[16,192,128]{2,1,0:T(8,128)(2,1)}), bf16[16,192,128]{2,1,0:T(8,128)(2,1)S(1)}, u32[]{:S(2)}, u32[]{:S(2)}) async-start(bf16[16,192,128]{2,1,0:T(8,128)(2,1)} %get-tuple-element.23), calls=%async_computation.1 | async-start | bytes 1572864 | tf_op jit(solution)/shard_map/all_to_all | solution.py:371
  36.3 39.0 %copy-start.5 = (s32[4]{0:T(128)S(1)}, s32[4]{0:T(128)}, u32[]{:S(2)}) copy-start(s32[4]{0:T(128)} %pad_add_fusion.place) | copy-start | bytes 52
  36.3 10.8 %collective-permute-start.2 = (bf16[16,16,128]{2,1,0:T(8,128)(2,1)S(1)}, bf16[16,16,128]{2,1,0:T(8,128)(2,1)S(1)}, u32[]{:S(2)}, u32[]{:S(2)}) collective-permute-start(bf16[16,16,128]{2,1,0:T(8,128)(2,1)S(1)} %all-to-all-done), channel_id=1, source_target_pairs={{0,256},{128,384},{256,0},{384,128},{1,257},{129,385},{257,1},{385... | collective-permute-start | bytes 196616 | tf_op jit(solution)/shard_map/ppermute | solution.py:360
  41.2 6.2 %collective-permute-start.1 = (bf16[16,16,128]{2,1,0:T(8,128)(2,1)S(1)}, bf16[16,16,128]{2,1,0:T(8,128)(2,1)S(1)}, u32[]{:S(2)}, u32[]{:S(2)}) collective-permute-start(bf16[16,16,128]{2,1,0:T(8,128)(2,1)S(1)} %all-to-all-done), channel_id=1, source_target_pairs={{0,384},{128,0},{256,128},{384,256},{1,385},{129,1},{257,129},{385... | collective-permute-start | bytes 196616 | tf_op jit(solution)/shard_map/ppermute | solution.py:360
  44.3 7.4 %collective-permute-start = (bf16[16,16,128]{2,1,0:T(8,128)(2,1)S(1)}, bf16[16,16,128]{2,1,0:T(8,128)(2,1)S(1)}, u32[]{:S(2)}, u32[]{:S(2)}) collective-permute-start(bf16[16,16,128]{2,1,0:T(8,128)(2,1)S(1)} %all-to-all-done), channel_id=1, source_target_pairs={{0,128},{128,256},{256,384},{384,0},{1,129},{129,257},{257,385},{3... | collective-permute-start | bytes 196616 | tf_op jit(solution)/shard_map/ppermute | solution.py:360
  51.7 11.0 %collective-permute-start.4 = (bf16[4,16,16,128]{3,2,1,0:T(8,128)(2,1)S(1)}, bf16[4,16,16,128]{3,2,1,0:T(8,128)(2,1)S(1)}, u32[]{:S(2)}, u32[]{:S(2)}) collective-permute-start(bf16[4,16,16,128]{3,2,1,0:T(8,128)(2,1)S(1)} %get-tuple-element.45), channel_id=1, source_target_pairs={{0,96},{32,0},{64,32},{96,64},{1,97},{33,1},{65,33},{97,65},{2,98}... | collective-permute-start | bytes 786440 | tf_op jit(solution)/shard_map/ppermute | solution.py:360
  56.6 14.0 %collective-permute-start.3 = (bf16[4,16,16,128]{3,2,1,0:T(8,128)(2,1)S(1)}, bf16[4,16,16,128]{3,2,1,0:T(8,128)(2,1)S(1)}, u32[]{:S(2)}, u32[]{:S(2)}) collective-permute-start(bf16[4,16,16,128]{3,2,1,0:T(8,128)(2,1)S(1)} %get-tuple-element.45), channel_id=1, source_target_pairs={{0,32},{32,64},{64,96},{96,0},{1,33},{33,65},{65,97},{97,1},{2,34}... | collective-permute-start | bytes 786440 | tf_op jit(solution)/shard_map/ppermute | solution.py:360
  58.6 12.0 %collective-permute-start.5 = (bf16[4,16,16,128]{3,2,1,0:T(8,128)(2,1)S(1)}, bf16[4,16,16,128]{3,2,1,0:T(8,128)(2,1)S(1)}, u32[]{:S(2)}, u32[]{:S(2)}) collective-permute-start(bf16[4,16,16,128]{3,2,1,0:T(8,128)(2,1)S(1)} %get-tuple-element.45), channel_id=1, source_target_pairs={{0,64},{32,96},{64,0},{96,32},{1,65},{33,97},{65,1},{97,33},{2,66}... | collective-permute-start | bytes 786440 | tf_op jit(solution)/shard_map/ppermute | solution.py:360
  70.7 4.6 %collective-permute-start.6 = (bf16[16,16,16,128]{3,2,1,0:T(8,128)(2,1)S(1)}, bf16[16,16,16,128]{3,2,1,0:T(8,128)(2,1)S(1)}, u32[]{:S(2)}, u32[]{:S(2)}) collective-permute-start(bf16[16,16,16,128]{3,2,1,0:T(8,128)(2,1)S(1)} %bitcast.48), channel_id=1, source_target_pairs={{0,16},{16,0},{1,17},{17,1},{2,18},{18,2},{3,19},{19,3},{4,20},{20... | collective-permute-start | bytes 3145736 | tf_op jit(solution)/shard_map/ppermute | solution.py:362
  80.2 5.4 %copy-start = (bf16[16,192,128]{2,1,0:T(8,128)(2,1)}, bf16[16,192,128]{2,1,0:T(8,128)(2,1)S(1)}, u32[]{:S(2)}) copy-start(bf16[16,192,128]{2,1,0:T(8,128)(2,1)S(1)} %all-to-all-done.1.state.first) | copy-start | bytes 2359300
  85.6 27.0 %collective-permute-start.15 = (f32[16,16,8,128]{3,2,1,0:T(8,128)S(1)}, f32[16,16,8,128]{3,2,1,0:T(8,128)S(1)}, u32[]{:S(2)}, u32[]{:S(2)}) collective-permute-start(f32[16,16,8,128]{3,2,1,0:T(8,128)S(1)} %get-tuple-element.32), channel_id=1, source_target_pairs={{0,16},{16,0},{1,17},{17,1},{2,18},{18,2},{3,19},{19,3},{4,20},{20... | collective-permute-start | bytes 3145736 | tf_op jit(solution)/shard_map/ppermute | solution.py:414
  87.6 3.2 %collective-permute-start.7 = (f32[128,128]{1,0:T(8,128)S(1)}, f32[128,128]{1,0:T(8,128)S(1)}, u32[]{:S(2)}, u32[]{:S(2)}) collective-permute-start(f32[128,128]{1,0:T(8,128)S(1)} %get-tuple-element.29), channel_id=1, source_target_pairs={{0,16},{16,0},{1,17},{17,1},{2,18},{18,2},{3,19},{19,3},{4,20},{20... | collective-permute-start | bytes 196616 | tf_op jit(solution)/shard_map/ppermute | solution.py:407
  90.8 9.3 %collective-permute-start.10 = (f32[128,128]{1,0:T(8,128)S(1)}, f32[128,128]{1,0:T(8,128)S(1)}, u32[]{:S(2)}, u32[]{:S(2)}) collective-permute-start(f32[128,128]{1,0:T(8,128)S(1)} %add.33), channel_id=1, source_target_pairs={{0,256},{128,384},{256,0},{384,128},{1,257},{129,385},{257,1},{385... | collective-permute-start | bytes 196616 | tf_op jit(solution)/shard_map/ppermute | solution.py:366
  93.1 7.4 %collective-permute-start.9 = (f32[128,128]{1,0:T(8,128)S(1)}, f32[128,128]{1,0:T(8,128)S(1)}, u32[]{:S(2)}, u32[]{:S(2)}) collective-permute-start(f32[128,128]{1,0:T(8,128)S(1)} %add.33), channel_id=1, source_target_pairs={{0,128},{128,256},{256,384},{384,0},{1,129},{129,257},{257,385},{3... | collective-permute-start | bytes 196616 | tf_op jit(solution)/shard_map/ppermute | solution.py:366
  95.2 7.1 %collective-permute-start.8 = (f32[128,128]{1,0:T(8,128)S(1)}, f32[128,128]{1,0:T(8,128)S(1)}, u32[]{:S(2)}, u32[]{:S(2)}) collective-permute-start(f32[128,128]{1,0:T(8,128)S(1)} %add.33), channel_id=1, source_target_pairs={{0,384},{128,0},{256,128},{384,256},{1,385},{129,1},{257,129},{385... | collective-permute-start | bytes 196616 | tf_op jit(solution)/shard_map/ppermute | solution.py:366
  102.3 18.5 %collective-permute-start.13 = (f32[128,128]{1,0:T(8,128)S(1)}, f32[128,128]{1,0:T(8,128)S(1)}, u32[]{:S(2)}, u32[]{:S(2)}) collective-permute-start(f32[128,128]{1,0:T(8,128)S(1)} %add_add_fusion.1), channel_id=1, source_target_pairs={{0,64},{32,96},{64,0},{96,32},{1,65},{33,97},{65,1},{97,33},{2,66}... | collective-permute-start | bytes 196616 | tf_op jit(solution)/shard_map/ppermute | solution.py:366
  105.6 18.6 %collective-permute-start.12 = (f32[128,128]{1,0:T(8,128)S(1)}, f32[128,128]{1,0:T(8,128)S(1)}, u32[]{:S(2)}, u32[]{:S(2)}) collective-permute-start(f32[128,128]{1,0:T(8,128)S(1)} %add_add_fusion.1), channel_id=1, source_target_pairs={{0,32},{32,64},{64,96},{96,0},{1,33},{33,65},{65,97},{97,1},{2,34}... | collective-permute-start | bytes 196616 | tf_op jit(solution)/shard_map/ppermute | solution.py:366
  108.0 16.2 %collective-permute-start.11 = (f32[128,128]{1,0:T(8,128)S(1)}, f32[128,128]{1,0:T(8,128)S(1)}, u32[]{:S(2)}, u32[]{:S(2)}) collective-permute-start(f32[128,128]{1,0:T(8,128)S(1)} %add_add_fusion.1), channel_id=1, source_target_pairs={{0,96},{32,0},{64,32},{96,64},{1,97},{33,1},{65,33},{97,65},{2,98}... | collective-permute-start | bytes 196616 | tf_op jit(solution)/shard_map/ppermute | solution.py:366
  112.8 13.3 %collective-permute-start.18 = (f32[4,16,8,128]{3,2,1,0:T(8,128)S(1)}, f32[4,16,8,128]{3,2,1,0:T(8,128)S(1)}, u32[]{:S(2)}, u32[]{:S(2)}) collective-permute-start(f32[4,16,8,128]{3,2,1,0:T(8,128)S(1)} %get-tuple-element.37), channel_id=1, source_target_pairs={{0,256},{128,384},{256,0},{384,128},{1,257},{129,385},{257,1},{385... | collective-permute-start | bytes 786440 | tf_op jit(solution)/shard_map/ppermute | solution.py:416
  117.1 11.1 %collective-permute-start.17 = (f32[4,16,8,128]{3,2,1,0:T(8,128)S(1)}, f32[4,16,8,128]{3,2,1,0:T(8,128)S(1)}, u32[]{:S(2)}, u32[]{:S(2)}) collective-permute-start(f32[4,16,8,128]{3,2,1,0:T(8,128)S(1)} %get-tuple-element.38), channel_id=1, source_target_pairs={{0,128},{128,256},{256,384},{384,0},{1,129},{129,257},{257,385},{3... | collective-permute-start | bytes 786440 | tf_op jit(solution)/shard_map/ppermute | solution.py:416
  120.8 8.3 %collective-permute-start.16 = (f32[4,16,8,128]{3,2,1,0:T(8,128)S(1)}, f32[4,16,8,128]{3,2,1,0:T(8,128)S(1)}, u32[]{:S(2)}, u32[]{:S(2)}) collective-permute-start(f32[4,16,8,128]{3,2,1,0:T(8,128)S(1)} %get-tuple-element.39), channel_id=1, source_target_pairs={{0,384},{128,0},{256,128},{384,256},{1,385},{129,1},{257,129},{385... | collective-permute-start | bytes 786440 | tf_op jit(solution)/shard_map/ppermute | solution.py:416
  124.2 14.9 %collective-permute-start.14 = (f32[128,128]{1,0:T(8,128)S(1)}, f32[128,128]{1,0:T(8,128)S(1)}, u32[]{:S(2)}, u32[]{:S(2)}) collective-permute-start(f32[128,128]{1,0:T(8,128)S(1)} %add_add_fusion.near), channel_id=1, source_target_pairs={{0,16},{16,0},{1,17},{17,1},{2,18},{18,2},{3,19},{19,3},{4,20},{20... | collective-permute-start | bytes 196616 | tf_op jit(solution)/shard_map/ppermute | solution.py:413
  129.2 26.6 %collective-permute-start.21 = (f32[16,8,128]{2,1,0:T(8,128)S(1)}, f32[16,8,128]{2,1,0:T(8,128)S(1)}, u32[]{:S(2)}, u32[]{:S(2)}) collective-permute-start(f32[16,8,128]{2,1,0:T(8,128)S(1)} %get-tuple-element.40), channel_id=1, source_target_pairs={{0,64},{32,96},{64,0},{96,32},{1,65},{33,97},{65,1},{97,33},{2,66}... | collective-permute-start | bytes 196616 | tf_op jit(solution)/shard_map/ppermute | solution.py:418
  132.1 23.7 %collective-permute-start.20 = (f32[16,8,128]{2,1,0:T(8,128)S(1)}, f32[16,8,128]{2,1,0:T(8,128)S(1)}, u32[]{:S(2)}, u32[]{:S(2)}) collective-permute-start(f32[16,8,128]{2,1,0:T(8,128)S(1)} %get-tuple-element.41), channel_id=1, source_target_pairs={{0,32},{32,64},{64,96},{96,0},{1,33},{33,65},{65,97},{97,1},{2,34}... | collective-permute-start | bytes 196616 | tf_op jit(solution)/shard_map/ppermute | solution.py:418
  134.0 53.9 %copy-start.7 = (s32[97]{0:T(128)S(1)}, s32[97]{0:T(128)}, u32[]{:S(2)}) copy-start(s32[97]{0:T(128)} %get-tuple-element.20.table) | copy-start | bytes 1168
  134.0 21.8 %collective-permute-start.19 = (f32[16,8,128]{2,1,0:T(8,128)S(1)}, f32[16,8,128]{2,1,0:T(8,128)S(1)}, u32[]{:S(2)}, u32[]{:S(2)}) collective-permute-start(f32[16,8,128]{2,1,0:T(8,128)S(1)} %get-tuple-element.42), channel_id=1, source_target_pairs={{0,96},{32,0},{64,32},{96,64},{1,97},{33,1},{65,33},{97,65},{2,98}... | collective-permute-start | bytes 196616 | tf_op jit(solution)/shard_map/ppermute | solution.py:418
  208.7 37.9 %all-to-all-start.2 = ((bf16[16,192,128]{2,1,0:T(8,128)(2,1)}), bf16[16,192,128]{2,1,0:T(8,128)(2,1)}, u32[]{:S(2)}, u32[]{:S(2)}) async-start(bf16[16,192,128]{2,1,0:T(8,128)(2,1)} %copy-done.2), calls=%async_computation.2 | async-start | bytes 1572864 | tf_op jit(solution)/shard_map/all_to_all | solution.py:371
  219.4 31.9 %collective-permute-start.22 = (bf16[16,368,128]{2,1,0:T(8,128)(2,1)S(1)}, bf16[16,368,128]{2,1,0:T(8,128)(2,1)}, u32[]{:S(2)}, u32[]{:S(2)}) collective-permute-start(bf16[16,368,128]{2,1,0:T(8,128)(2,1)S(1)} %all_to_all.20.near), channel_id=1, source_target_pairs={{0,16},{16,0},{1,17},{17,1},{2,18},{18,2},{3,19},{19,3},{4,20},{20... | collective-permute-start | bytes 4521992 | tf_op jit(solution)/shard_map/ppermute | solution.py:444
  246.6 2.9 %copy-start.1 = (bf16[16,192,128]{2,1,0:T(8,128)(2,1)S(1)}, bf16[16,192,128]{2,1,0:T(8,128)(2,1)}, u32[]{:S(2)}) copy-start(bf16[16,192,128]{2,1,0:T(8,128)(2,1)} %copy-done) | copy-start | bytes 2359300

commit v4 on v3

--- a/solution.py
+++ b/solution.py
@@ -29,6 +29,7 @@
 SWAP = [(0, 1), (1, 0)]
 VMEM = pl.BlockSpec(memory_space=pltpu.VMEM)
 SMEM = pl.BlockSpec(memory_space=pltpu.SMEM)
+ANY = pl.BlockSpec(memory_space=pl.ANY)
 
 
 def call(body, outs, scratch=(), flops=0, specs=None, n_in=0):
@@ -234,7 +235,7 @@
                 work[m, k + size :, :] -= change[k + size :, :]
 
 
-def scale_factor(place, inverse, a, b, c, d, out):
+def scale_factor(place, inverse, a, b, c, d, _, out):
     f = place[0] * 8 + place[1] * 2 + place[2]
     total = ((a[...] + b[...]) + (c[...] + d[...])).reshape(128, RANK)
     kind = jnp.where(f >= 12, 1, 0)
@@ -409,12 +410,13 @@
     keep, send = call(
         weigh, (half, half), [pltpu.VMEM((256, RANK), F32)], specs=[SMEM, VMEM, VMEM], flops=400_000_000
     )(place, state, panel)
-    gram = spread_sum(spread_sum(gram, "x"), "y")
-    other = lax.ppermute(gram, "c", SWAP)
     parts = keep + lax.ppermute(send, "c", SWAP)
+    parts, gram = barrier((parts, spread_sum(gram, "x")))
     parts = parts.reshape(4, 4, 16, 8, RANK)
     moved = [lax.ppermute(parts[:, i + 1], "x", ring(SHIFTS[i])) for i in range(3)]
     parts = (parts[:, 0] + moved[0]) + (moved[1] + moved[2])
+    parts, gram = barrier((parts, spread_sum(gram, "y")))
+    other = lax.ppermute(gram, "c", SWAP)
     parts = [parts[0]] + [lax.ppermute(parts[i + 1], "y", ring(SHIFTS[i])) for i in range(3)]
     inverse = call(
         functools.partial(invert, size=8),
@@ -424,8 +426,8 @@
         flops=4_000_000_000,
     )(place, gram, other)
     mine = call(
-        scale_factor, sds((144, RANK), BF16), specs=[SMEM] + [VMEM] * 5, flops=100_000_000
-    )(place, inverse, *parts)
+        scale_factor, sds((144, RANK), BF16), specs=[SMEM] + [VMEM] * 5 + [ANY], flops=100_000_000
+    )(place, inverse, *parts, second)
     left, low = call(
         orthonormal, (two, sds((2, 128, RANK), BF16)), specs=[SMEM, SMEM, VMEM, VMEM], flops=100_000_000
     )(table, place, panel, inverse)

time: 260 us -> 239 us (0.919)
  the two profiles are of different devices: /device:TPU:32 before, /device:TPU:1 now
where the time goes in v4:
time: 239 us; the launch traced here: 238 us
  starting transfers between devices  116 us (49%)
  blocking collectives  45.3 us (19%)
  Pallas kernels  42.4 us (18%)
  waiting for transfers between devices  28.8 us (12%)
  local copies, waits for them, and re-layouts  3.6 us (2%)
    all_to_all x3, starting transfers between devices, exchange(): return lax.all_to_all(x, axis, split_axis=0, concat_axis=0, tiled=True)  32.8 us
    all_gather x1, blocking collectives, shards(): tiles = lax.all_gather(mine, 'z')  26.4 us
    ppermute x6, starting transfers between devices, gather_slices(): lax.ppermute(x, axis, ring((4 - d) % 4))  20 us
    all_to_all x1, blocking collectives, exchange(): return lax.all_to_all(x, axis, split_axis=0, concat_axis=0, tiled=True)  18.9 us
    ppermute x6, starting transfers between devices, spread_sum(): parts = [lax.ppermute(x, axis, ring(d)) for d in SHIFTS]  17.9 us
    pallas_call x1, Pallas kernels, shards(): call(functools.partial(invert, size=8), sds((2, RANK, RANK), F32), [pltpu...  16.6 us
    ppermute x6, waiting for transfers between devices, gather_slices(): lax.ppermute(x, axis, ring((4 - d) % 4))  11.8 us
    ppermute x1, starting transfers between devices, shards(): far = lax.ppermute(near, 'c', SWAP)  10.7 us
  transfers between devices with their start and end apart: 26, of which 8 were waited for; matrix products, arithmetic and copies ran while one was open for 0% of the time, Pallas kernels for 13%

profile of v4, /device:TPU:1, one launch (start us, length us, event | category | flops | bytes accessed | tf_op | source)
XLA Modules:
  0.0 237.9 jit_solution(15961664647676664482)
XLA Ops:
  1.3 2.1 shard_map.67
  3.4 15.8 %all-to-all-start = ((bf16[16,16,128]{2,1,0:T(8,128)(2,1)}), bf16[16,16,128]{2,1,0:T(8,128)(2,1)S(1)}, u32[]{:S(2)}, u32[]{:S(2)}) async-start(bf16[16,16,128]{2,1,0:T(8,128)(2,1)} %get-tuple-element.26), calls=%async_computation | async-start | bytes 131072 | tf_op jit(solution)/shard_map/all_to_all | solution.py:372
  19.1 1.0 copy-done.1
  20.2 1.0 copy-done.2
  21.8 2.2 shard_map.68
  24.8 5.9 %all-to-all-done = bf16[16,16,128]{2,1,0:T(8,128)(2,1)S(1)} async-done(((bf16[16,16,128]{2,1,0:T(8,128)(2,1)}), bf16[16,16,128]{2,1,0:T(8,128)(2,1)S(1)}, u32[]{:S(2)}, u32[]{:S(2)}) %all-to-all-start) | async-done | bytes 65568 | tf_op jit(solution)/shard_map/all_to_all | solution.py:372
  30.7 5.6 %all-to-all-start.1 = ((bf16[16,192,128]{2,1,0:T(8,128)(2,1)}), bf16[16,192,128]{2,1,0:T(8,128)(2,1)S(1)}, u32[]{:S(2)}, u32[]{:S(2)}) async-start(bf16[16,192,128]{2,1,0:T(8,128)(2,1)} %get-tuple-element.27), calls=%async_computation.1 | async-start | bytes 1572864 | tf_op jit(solution)/shard_map/all_to_all | solution.py:372
  36.3 4.7 %collective-permute-start.2 = (bf16[16,16,128]{2,1,0:T(8,128)(2,1)S(1)}, bf16[16,16,128]{2,1,0:T(8,128)(2,1)S(1)}, u32[]{:S(2)}, u32[]{:S(2)}) collective-permute-start(bf16[16,16,128]{2,1,0:T(8,128)(2,1)S(1)} %all-to-all-done), channel_id=1, source_target_pairs={{0,256},{128,384},{256,0},{384,128},{1,257},{129,385},{257,1},{385... | collective-permute-start | bytes 196616 | tf_op jit(solution)/shard_map/ppermute | solution.py:361
  41.0 2.8 %collective-permute-start.1 = (bf16[16,16,128]{2,1,0:T(8,128)(2,1)S(1)}, bf16[16,16,128]{2,1,0:T(8,128)(2,1)S(1)}, u32[]{:S(2)}, u32[]{:S(2)}) collective-permute-start(bf16[16,16,128]{2,1,0:T(8,128)(2,1)S(1)} %all-to-all-done), channel_id=1, source_target_pairs={{0,384},{128,0},{256,128},{384,256},{1,385},{129,1},{257,129},{385... | collective-permute-start | bytes 196616 | tf_op jit(solution)/shard_map/ppermute | solution.py:361
  43.7 2.5 %collective-permute-start = (bf16[16,16,128]{2,1,0:T(8,128)(2,1)S(1)}, bf16[16,16,128]{2,1,0:T(8,128)(2,1)S(1)}, u32[]{:S(2)}, u32[]{:S(2)}) collective-permute-start(bf16[16,16,128]{2,1,0:T(8,128)(2,1)S(1)} %all-to-all-done), channel_id=1, source_target_pairs={{0,128},{128,256},{256,384},{384,0},{1,129},{129,257},{257,385},{3... | collective-permute-start | bytes 196616 | tf_op jit(solution)/shard_map/ppermute | solution.py:361
  46.3 4.0 %collective-permute-done = bf16[16,16,128]{2,1,0:T(8,128)(2,1)S(1)} collective-permute-done((bf16[16,16,128]{2,1,0:T(8,128)(2,1)S(1)}, bf16[16,16,128]{2,1,0:T(8,128)(2,1)S(1)}, u32[]{:S(2)}, u32[]{:S(2)}) %collective-permute-start) | collective-permute-done | bytes 65568 | tf_op jit(solution)/shard_map/ppermute | solution.py:361
  50.3 4.6 %collective-permute-start.4 = (bf16[4,16,16,128]{3,2,1,0:T(8,128)(2,1)S(1)}, bf16[4,16,16,128]{3,2,1,0:T(8,128)(2,1)S(1)}, u32[]{:S(2)}, u32[]{:S(2)}) collective-permute-start(bf16[4,16,16,128]{3,2,1,0:T(8,128)(2,1)S(1)} %get-tuple-element.53), channel_id=1, source_target_pairs={{0,96},{32,0},{64,32},{96,64},{1,97},{33,1},{65,33},{97,65},{2,98}... | collective-permute-start | bytes 786440 | tf_op jit(solution)/shard_map/ppermute | solution.py:361
  54.9 1.9 collective-permute-start.3
  56.9 3.5 %collective-permute-start.5 = (bf16[4,16,16,128]{3,2,1,0:T(8,128)(2,1)S(1)}, bf16[4,16,16,128]{3,2,1,0:T(8,128)(2,1)S(1)}, u32[]{:S(2)}, u32[]{:S(2)}) collective-permute-start(bf16[4,16,16,128]{3,2,1,0:T(8,128)(2,1)S(1)} %get-tuple-element.53), channel_id=1, source_target_pairs={{0,64},{32,96},{64,0},{96,32},{1,65},{33,97},{65,1},{97,33},{2,66}... | collective-permute-start | bytes 786440 | tf_op jit(solution)/shard_map/ppermute | solution.py:361
  60.4 4.0 %collective-permute-done.3 = bf16[4,16,16,128]{3,2,1,0:T(8,128)(2,1)S(1)} collective-permute-done((bf16[4,16,16,128]{3,2,1,0:T(8,128)(2,1)S(1)}, bf16[4,16,16,128]{3,2,1,0:T(8,128)(2,1)S(1)}, u32[]{:S(2)}, u32[]{:S(2)}) %collective-permute-start.3) | collective-permute-done | bytes 262176 | tf_op jit(solution)/shard_map/ppermute | solution.py:361
  64.5 3.8 %collective-permute-done.5 = bf16[4,16,16,128]{3,2,1,0:T(8,128)(2,1)S(1)} collective-permute-done((bf16[4,16,16,128]{3,2,1,0:T(8,128)(2,1)S(1)}, bf16[4,16,16,128]{3,2,1,0:T(8,128)(2,1)S(1)}, u32[]{:S(2)}, u32[]{:S(2)}) %collective-permute-start.5) | collective-permute-done | bytes 262176 | tf_op jit(solution)/shard_map/ppermute | solution.py:361
  68.4 6.0 %collective-permute-start.6 = (bf16[16,16,16,128]{3,2,1,0:T(8,128)(2,1)S(1)}, bf16[16,16,16,128]{3,2,1,0:T(8,128)(2,1)S(1)}, u32[]{:S(2)}, u32[]{:S(2)}) collective-permute-start(bf16[16,16,16,128]{3,2,1,0:T(8,128)(2,1)S(1)} %bitcast.48), channel_id=1, source_target_pairs={{0,16},{16,0},{1,17},{17,1},{2,18},{18,2},{3,19},{19,3},{4,20},{20... | collective-permute-start | bytes 3145736 | tf_op jit(solution)/shard_map/ppermute | solution.py:363
  74.4 2.3 collective-permute-done.6.far
  76.7 4.9 %shard_map.69.right = bf16[16,384,128]{2,1,0:T(8,128)(2,1)S(1)} custom-call(s32[4]{0:T(128)S(1)} %copy-done.3, bf16[16,16,16,128]{3,2,1,0:T(8,128)(2,1)S(1)} %bitcast.49, bf16[16,16,16,128]{3,2,1,0:T(8,128)(2,1)S(1)} %collective-permute-done.6.far), custom_call_target="tpu_custom_call" | custom-call | flops 800000000 | bytes 4000000 | tf_op jit(solution)/shard_map/pallas_call | solution.py:394
  81.6 2.8 %shard_map.70 = (f32[2,128,128]{2,1,0:T(8,128)S(1)}, f32[128,128]{1,0:T(8,128)S(1)}, f32[128,128]{1,0:T(8,128)S(1)}) custom-call(s32[4]{0:T(128)S(1)} %copy-done.3, bf16[16,192,128]{2,1,0:T(8,128)(2,1)S(1)} %all-to-all-done.1.state.first, bf16[16,384,128]{2,1,0:T(8,128)(2,1)S(1)} %shard_map.69.right), custom_call_target="tpu_custom_call" | custom-call | flops 300000000 | bytes 4000000 | tf_op jit(solution)/shard_map/pallas_call | solution.py:403
  84.4 11.5 %all-to-all-start.2 = ((bf16[16,192,128]{2,1,0:T(8,128)(2,1)}), bf16[16,192,128]{2,1,0:T(8,128)(2,1)S(1)}, u32[]{:S(2)}, u32[]{:S(2)}) async-start(bf16[16,192,128]{2,1,0:T(8,128)(2,1)} %copy-done), calls=%async_computation.2 | async-start | bytes 1572864 | tf_op jit(solution)/shard_map/all_to_all | solution.py:372
  95.9 2.6 %shard_map.72 = (f32[16,16,8,128]{3,2,1,0:T(8,128)S(1)}, f32[16,16,8,128]{3,2,1,0:T(8,128)S(1)}) custom-call(s32[4]{0:T(128)S(1)} %copy-done.3, bf16[16,192,128]{2,1,0:T(8,128)(2,1)S(1)} %all-to-all-done.1.state.first, f32[2,128,128]{2,1,0:T(8,128)S(1)} %get-tuple-element.32.panel), custom_call_target="tpu_custom_call" | custom-call | flops 400000000 | bytes 4000000 | tf_op jit(solution)/shard_map/pallas_call | solution.py:410
  98.5 2.6 %collective-permute-start.7 = (f32[16,16,8,128]{3,2,1,0:T(8,128)S(1)}, f32[16,16,8,128]{3,2,1,0:T(8,128)S(1)}, u32[]{:S(2)}, u32[]{:S(2)}) collective-permute-start(f32[16,16,8,128]{3,2,1,0:T(8,128)S(1)} %get-tuple-element.34), channel_id=1, source_target_pairs={{0,16},{16,0},{1,17},{17,1},{2,18},{18,2},{3,19},{19,3},{4,20},{20... | collective-permute-start | bytes 3145736 | tf_op jit(solution)/shard_map/ppermute | solution.py:413
  101.0 1.9 collective-permute-start.8
  103.0 1.2 collective-permute-done.8
  104.2 1.9 collective-permute-start.11
  106.2 1.9 collective-permute-start.10
  108.1 4.6 %collective-permute-start.9 = (f32[128,128]{1,0:T(8,128)S(1)}, f32[128,128]{1,0:T(8,128)S(1)}, u32[]{:S(2)}, u32[]{:S(2)}) collective-permute-start(f32[128,128]{1,0:T(8,128)S(1)} %add.34), channel_id=1, source_target_pairs={{0,384},{128,0},{256,128},{384,256},{1,385},{129,1},{257,129},{385... | collective-permute-start | bytes 196616 | tf_op jit(solution)/shard_map/ppermute | solution.py:367
  112.7 1.9 collective-permute-done.9
  114.7 2.9 %collective-permute-start.17 = (f32[128,128]{1,0:T(8,128)S(1)}, f32[128,128]{1,0:T(8,128)S(1)}, u32[]{:S(2)}, u32[]{:S(2)}) collective-permute-start(f32[128,128]{1,0:T(8,128)S(1)} %add_add_fusion.1), channel_id=1, source_target_pairs={{0,64},{32,96},{64,0},{96,32},{1,65},{33,97},{65,1},{97,33},{2,66}... | collective-permute-start | bytes 196616 | tf_op jit(solution)/shard_map/ppermute | solution.py:367
  117.7 2.1 collective-permute-start.16
  119.8 4.3 %collective-permute-start.15 = (f32[128,128]{1,0:T(8,128)S(1)}, f32[128,128]{1,0:T(8,128)S(1)}, u32[]{:S(2)}, u32[]{:S(2)}) collective-permute-start(f32[128,128]{1,0:T(8,128)S(1)} %add_add_fusion.1), channel_id=1, source_target_pairs={{0,96},{32,0},{64,32},{96,64},{1,97},{33,1},{65,33},{97,65},{2,98}... | collective-permute-start | bytes 196616 | tf_op jit(solution)/shard_map/ppermute | solution.py:367
  124.2 3.7 %collective-permute-start.14 = (f32[4,16,8,128]{3,2,1,0:T(8,128)S(1)}, f32[4,16,8,128]{3,2,1,0:T(8,128)S(1)}, u32[]{:S(2)}, u32[]{:S(2)}) collective-permute-start(f32[4,16,8,128]{3,2,1,0:T(8,128)S(1)} %get-tuple-element.45), channel_id=1, source_target_pairs={{0,256},{128,384},{256,0},{384,128},{1,257},{129,385},{257,1},{385... | collective-permute-start | bytes 786440 | tf_op jit(solution)/shard_map/ppermute | solution.py:416
  127.9 3.4 %collective-permute-start.13 = (f32[4,16,8,128]{3,2,1,0:T(8,128)S(1)}, f32[4,16,8,128]{3,2,1,0:T(8,128)S(1)}, u32[]{:S(2)}, u32[]{:S(2)}) collective-permute-start(f32[4,16,8,128]{3,2,1,0:T(8,128)S(1)} %get-tuple-element.46), channel_id=1, source_target_pairs={{0,128},{128,256},{256,384},{384,0},{1,129},{129,257},{257,385},{3... | collective-permute-start | bytes 786440 | tf_op jit(solution)/shard_map/ppermute | solution.py:416
  131.4 3.1 %collective-permute-start.12 = (f32[4,16,8,128]{3,2,1,0:T(8,128)S(1)}, f32[4,16,8,128]{3,2,1,0:T(8,128)S(1)}, u32[]{:S(2)}, u32[]{:S(2)}) collective-permute-start(f32[4,16,8,128]{3,2,1,0:T(8,128)S(1)} %get-tuple-element.47), channel_id=1, source_target_pairs={{0,384},{128,0},{256,128},{384,256},{1,385},{129,1},{257,129},{385... | collective-permute-start | bytes 786440 | tf_op jit(solution)/shard_map/ppermute | solution.py:416
  134.5 5.7 %collective-permute-done.13 = f32[4,16,8,128]{3,2,1,0:T(8,128)S(1)} collective-permute-done((f32[4,16,8,128]{3,2,1,0:T(8,128)S(1)}, f32[4,16,8,128]{3,2,1,0:T(8,128)S(1)}, u32[]{:S(2)}, u32[]{:S(2)}) %collective-permute-start.13) | collective-permute-done | bytes 262176 | tf_op jit(solution)/shard_map/ppermute | solution.py:416
  140.3 4.3 %collective-permute-start.18 = (f32[128,128]{1,0:T(8,128)S(1)}, f32[128,128]{1,0:T(8,128)S(1)}, u32[]{:S(2)}, u32[]{:S(2)}) collective-permute-start(f32[128,128]{1,0:T(8,128)S(1)} %add_add_fusion.near), channel_id=1, source_target_pairs={{0,16},{16,0},{1,17},{17,1},{2,18},{18,2},{3,19},{19,3},{4,20},{20... | collective-permute-start | bytes 196616 | tf_op jit(solution)/shard_map/ppermute | solution.py:419
  144.6 2.6 %collective-permute-start.21 = (f32[16,8,128]{2,1,0:T(8,128)S(1)}, f32[16,8,128]{2,1,0:T(8,128)S(1)}, u32[]{:S(2)}, u32[]{:S(2)}) collective-permute-start(f32[16,8,128]{2,1,0:T(8,128)S(1)} %get-tuple-element.48), channel_id=1, source_target_pairs={{0,64},{32,96},{64,0},{96,32},{1,65},{33,97},{65,1},{97,33},{2,66}... | collective-permute-start | bytes 196616 | tf_op jit(solution)/shard_map/ppermute | solution.py:420
  147.3 1.9 collective-permute-start.20
  149.2 4.6 %collective-permute-start.19 = (f32[16,8,128]{2,1,0:T(8,128)S(1)}, f32[16,8,128]{2,1,0:T(8,128)S(1)}, u32[]{:S(2)}, u32[]{:S(2)}) collective-permute-start(f32[16,8,128]{2,1,0:T(8,128)S(1)} %get-tuple-element.50), channel_id=1, source_target_pairs={{0,96},{32,0},{64,32},{96,64},{1,97},{33,1},{65,33},{97,65},{2,98}... | collective-permute-start | bytes 196616 | tf_op jit(solution)/shard_map/ppermute | solution.py:420
  153.8 16.6 %shard_map.73.inverse = f32[2,128,128]{2,1,0:T(8,128)S(1)} custom-call(s32[4]{0:T(128)S(1)} %copy-done.3, f32[128,128]{1,0:T(8,128)S(1)} %add_add_fusion.near, f32[128,128]{1,0:T(8,128)S(1)} %collective-permute-done.18.far), custom_call_target="tpu_custom_call" | custom-call | flops 4000000000 | bytes 4000000 | tf_op jit(solution)/shard_map/pallas_call | solution.py:421
  171.3 26.4 %all-gather = bf16[2304,128]{1,0:T(8,128)(2,1)S(1)} all-gather(bf16[144,128]{1,0:T(8,128)(2,1)S(1)} %shard_map.74.mine), channel_id=2, replica_groups=mesh['x'=4,'y'=4,'c'=2,'z'=16] {'z'}, dimensions={0}, use_global_device_ids=true | all-gather | bytes 626688 | tf_op jit(solution)/shard_map/all_gather | solution.py:434
  198.5 18.9 %all_to_all.20.near = bf16[16,368,128]{2,1,0:T(8,128)(2,1)S(1)} all-to-all(bf16[16,368,128]{2,1,0:T(8,128)(2,1)S(1)} %shard_map.75), channel_id=1, replica_groups=mesh['x'=4,'y'=4,'c'=2,'z'=16] {'x','y'}, dimensions={0} | all-to-all | bytes 3014656 | tf_op jit(solution)/shard_map/all_to_all | solution.py:372
  217.4 10.7 %collective-permute-start.22 = (bf16[16,368,128]{2,1,0:T(8,128)(2,1)S(1)}, bf16[16,368,128]{2,1,0:T(8,128)(2,1)S(1)}, u32[]{:S(2)}, u32[]{:S(2)}) collective-permute-start(bf16[16,368,128]{2,1,0:T(8,128)(2,1)S(1)} %all_to_all.20.near), channel_id=1, source_target_pairs={{0,16},{16,0},{1,17},{17,1},{2,18},{18,2},{3,19},{19,3},{4,20},{20... | collective-permute-start | bytes 4521992 | tf_op jit(solution)/shard_map/ppermute | solution.py:446
  229.1 1.7 shard_map.77.panel
  230.9 1.1 shard_map.71.turned
  232.0 2.1 shard_map.79
  234.1 3.8 %shard_map.78 = (bf16[4,128,1536]{2,1,0:T(8,128)(2,1)}, f32[4,128,128]{2,1,0:T(8,128)}) custom-call(s32[97]{0:T(128)S(1)} %copy-done.5, s32[4]{0:T(128)S(1)} %copy-done.3, bf16[4,128,1536]{2,1,0:T(8,128)(2,1)S(1)} %shard_map.71.turned, bf16[16,368,128]{2,1,0:T(8,128)(2,1)S(1)} %all_to_all.20.near, bf16[16,368,128]{2,1,0:T(8,128)(2,1)S(1)} %collective-permute-done.22.far, ...), custom_call_target="tpu_custom_call" | custom-call | flops 1200000000 | bytes 4000000 | tf_op jit(solution)/shard_map/pallas_call | solution.py:450
  (45 shorter events, 5.2 us)
Async XLA Ops:
  3.4 27.3 %all-to-all-start = ((bf16[16,16,128]{2,1,0:T(8,128)(2,1)}), bf16[16,16,128]{2,1,0:T(8,128)(2,1)S(1)}, u32[]{:S(2)}, u32[]{:S(2)}) async-start(bf16[16,16,128]{2,1,0:T(8,128)(2,1)} %get-tuple-element.26), calls=%async_computation | async-start | bytes 131072 | tf_op jit(solution)/shard_map/all_to_all | solution.py:372
  19.1 1.0 copy-start.1
  20.2 1.0 copy-start.2
  21.2 0.6 copy-start.4
  23.9 0.9 copy-start
  30.7 50.9 %all-to-all-start.1 = ((bf16[16,192,128]{2,1,0:T(8,128)(2,1)}), bf16[16,192,128]{2,1,0:T(8,128)(2,1)S(1)}, u32[]{:S(2)}, u32[]{:S(2)}) async-start(bf16[16,192,128]{2,1,0:T(8,128)(2,1)} %get-tuple-element.27), calls=%async_computation.1 | async-start | bytes 1572864 | tf_op jit(solution)/shard_map/all_to_all | solution.py:372
  36.3 40.4 %copy-start.3 = (s32[4]{0:T(128)S(1)}, s32[4]{0:T(128)}, u32[]{:S(2)}) copy-start(s32[4]{0:T(128)} %pad_add_fusion.place) | copy-start | bytes 52
  36.3 10.0 %collective-permute-start.2 = (bf16[16,16,128]{2,1,0:T(8,128)(2,1)S(1)}, bf16[16,16,128]{2,1,0:T(8,128)(2,1)S(1)}, u32[]{:S(2)}, u32[]{:S(2)}) collective-permute-start(bf16[16,16,128]{2,1,0:T(8,128)(2,1)S(1)} %all-to-all-done), channel_id=1, source_target_pairs={{0,256},{128,384},{256,0},{384,128},{1,257},{129,385},{257,1},{385... | collective-permute-start | bytes 196616 | tf_op jit(solution)/shard_map/ppermute | solution.py:361
  41.0 5.3 %collective-permute-start.1 = (bf16[16,16,128]{2,1,0:T(8,128)(2,1)S(1)}, bf16[16,16,128]{2,1,0:T(8,128)(2,1)S(1)}, u32[]{:S(2)}, u32[]{:S(2)}) collective-permute-start(bf16[16,16,128]{2,1,0:T(8,128)(2,1)S(1)} %all-to-all-done), channel_id=1, source_target_pairs={{0,384},{128,0},{256,128},{384,256},{1,385},{129,1},{257,129},{385... | collective-permute-start | bytes 196616 | tf_op jit(solution)/shard_map/ppermute | solution.py:361
  43.7 6.5 %collective-permute-start = (bf16[16,16,128]{2,1,0:T(8,128)(2,1)S(1)}, bf16[16,16,128]{2,1,0:T(8,128)(2,1)S(1)}, u32[]{:S(2)}, u32[]{:S(2)}) collective-permute-start(bf16[16,16,128]{2,1,0:T(8,128)(2,1)S(1)} %all-to-all-done), channel_id=1, source_target_pairs={{0,128},{128,256},{256,384},{384,0},{1,129},{129,257},{257,385},{3... | collective-permute-start | bytes 196616 | tf_op jit(solution)/shard_map/ppermute | solution.py:361
  50.3 10.1 %collective-permute-start.4 = (bf16[4,16,16,128]{3,2,1,0:T(8,128)(2,1)S(1)}, bf16[4,16,16,128]{3,2,1,0:T(8,128)(2,1)S(1)}, u32[]{:S(2)}, u32[]{:S(2)}) collective-permute-start(bf16[4,16,16,128]{3,2,1,0:T(8,128)(2,1)S(1)} %get-tuple-element.53), channel_id=1, source_target_pairs={{0,96},{32,0},{64,32},{96,64},{1,97},{33,1},{65,33},{97,65},{2,98}... | collective-permute-start | bytes 786440 | tf_op jit(solution)/shard_map/ppermute | solution.py:361
  54.9 9.5 %collective-permute-start.3 = (bf16[4,16,16,128]{3,2,1,0:T(8,128)(2,1)S(1)}, bf16[4,16,16,128]{3,2,1,0:T(8,128)(2,1)S(1)}, u32[]{:S(2)}, u32[]{:S(2)}) collective-permute-start(bf16[4,16,16,128]{3,2,1,0:T(8,128)(2,1)S(1)} %get-tuple-element.53), channel_id=1, source_target_pairs={{0,32},{32,64},{64,96},{96,0},{1,33},{33,65},{65,97},{97,1},{2,34}... | collective-permute-start | bytes 786440 | tf_op jit(solution)/shard_map/ppermute | solution.py:361
  56.9 11.4 %collective-permute-start.5 = (bf16[4,16,16,128]{3,2,1,0:T(8,128)(2,1)S(1)}, bf16[4,16,16,128]{3,2,1,0:T(8,128)(2,1)S(1)}, u32[]{:S(2)}, u32[]{:S(2)}) collective-permute-start(bf16[4,16,16,128]{3,2,1,0:T(8,128)(2,1)S(1)} %get-tuple-element.53), channel_id=1, source_target_pairs={{0,64},{32,96},{64,0},{96,32},{1,65},{33,97},{65,1},{97,33},{2,66}... | collective-permute-start | bytes 786440 | tf_op jit(solution)/shard_map/ppermute | solution.py:361
  68.4 8.3 %collective-permute-start.6 = (bf16[16,16,16,128]{3,2,1,0:T(8,128)(2,1)S(1)}, bf16[16,16,16,128]{3,2,1,0:T(8,128)(2,1)S(1)}, u32[]{:S(2)}, u32[]{:S(2)}) collective-permute-start(bf16[16,16,16,128]{3,2,1,0:T(8,128)(2,1)S(1)} %bitcast.48), channel_id=1, source_target_pairs={{0,16},{16,0},{1,17},{17,1},{2,18},{18,2},{3,19},{19,3},{4,20},{20... | collective-permute-start | bytes 3145736 | tf_op jit(solution)/shard_map/ppermute | solution.py:363
  84.4 19.8 %copy-start.6 = (f32[2,128,128]{2,1,0:T(8,128)}, f32[2,128,128]{2,1,0:T(8,128)S(1)}, u32[]{:S(2)}) copy-start(f32[2,128,128]{2,1,0:T(8,128)S(1)} %get-tuple-element.32.panel) | copy-start | bytes 393220
  84.4 86.1 %all-to-all-start.2 = ((bf16[16,192,128]{2,1,0:T(8,128)(2,1)}), bf16[16,192,128]{2,1,0:T(8,128)(2,1)S(1)}, u32[]{:S(2)}, u32[]{:S(2)}) async-start(bf16[16,192,128]{2,1,0:T(8,128)(2,1)} %copy-done), calls=%async_computation.2 | async-start | bytes 1572864 | tf_op jit(solution)/shard_map/all_to_all | solution.py:372
  98.5 16.1 %collective-permute-start.7 = (f32[16,16,8,128]{3,2,1,0:T(8,128)S(1)}, f32[16,16,8,128]{3,2,1,0:T(8,128)S(1)}, u32[]{:S(2)}, u32[]{:S(2)}) collective-permute-start(f32[16,16,8,128]{3,2,1,0:T(8,128)S(1)} %get-tuple-element.34), channel_id=1, source_target_pairs={{0,16},{16,0},{1,17},{17,1},{2,18},{18,2},{3,19},{19,3},{4,20},{20... | collective-permute-start | bytes 3145736 | tf_op jit(solution)/shard_map/ppermute | solution.py:413
  101.0 3.1 %collective-permute-start.8 = (f32[128,128]{1,0:T(8,128)S(1)}, f32[128,128]{1,0:T(8,128)S(1)}, u32[]{:S(2)}, u32[]{:S(2)}) collective-permute-start(f32[128,128]{1,0:T(8,128)S(1)} %get-tuple-element.36), channel_id=1, source_target_pairs={{0,16},{16,0},{1,17},{17,1},{2,18},{18,2},{3,19},{19,3},{4,20},{20... | collective-permute-start | bytes 196616 | tf_op jit(solution)/shard_map/ppermute | solution.py:408
  104.2 8.5 %collective-permute-start.11 = (f32[128,128]{1,0:T(8,128)S(1)}, f32[128,128]{1,0:T(8,128)S(1)}, u32[]{:S(2)}, u32[]{:S(2)}) collective-permute-start(f32[128,128]{1,0:T(8,128)S(1)} %add.34), channel_id=1, source_target_pairs={{0,256},{128,384},{256,0},{384,128},{1,257},{129,385},{257,1},{385... | collective-permute-start | bytes 196616 | tf_op jit(solution)/shard_map/ppermute | solution.py:367
  106.2 6.5 %collective-permute-start.10 = (f32[128,128]{1,0:T(8,128)S(1)}, f32[128,128]{1,0:T(8,128)S(1)}, u32[]{:S(2)}, u32[]{:S(2)}) collective-permute-start(f32[128,128]{1,0:T(8,128)S(1)} %add.34), channel_id=1, source_target_pairs={{0,128},{128,256},{256,384},{384,0},{1,129},{129,257},{257,385},{3... | collective-permute-start | bytes 196616 | tf_op jit(solution)/shard_map/ppermute | solution.py:367
  108.1 6.5 %collective-permute-start.9 = (f32[128,128]{1,0:T(8,128)S(1)}, f32[128,128]{1,0:T(8,128)S(1)}, u32[]{:S(2)}, u32[]{:S(2)}) collective-permute-start(f32[128,128]{1,0:T(8,128)S(1)} %add.34), channel_id=1, source_target_pairs={{0,384},{128,0},{256,128},{384,256},{1,385},{129,1},{257,129},{385... | collective-permute-start | bytes 196616 | tf_op jit(solution)/shard_map/ppermute | solution.py:367
  114.7 16.7 %collective-permute-start.17 = (f32[128,128]{1,0:T(8,128)S(1)}, f32[128,128]{1,0:T(8,128)S(1)}, u32[]{:S(2)}, u32[]{:S(2)}) collective-permute-start(f32[128,128]{1,0:T(8,128)S(1)} %add_add_fusion.1), channel_id=1, source_target_pairs={{0,64},{32,96},{64,0},{96,32},{1,65},{33,97},{65,1},{97,33},{2,66}... | collective-permute-start | bytes 196616 | tf_op jit(solution)/shard_map/ppermute | solution.py:367
  117.7 16.8 %collective-permute-start.16 = (f32[128,128]{1,0:T(8,128)S(1)}, f32[128,128]{1,0:T(8,128)S(1)}, u32[]{:S(2)}, u32[]{:S(2)}) collective-permute-start(f32[128,128]{1,0:T(8,128)S(1)} %add_add_fusion.1), channel_id=1, source_target_pairs={{0,32},{32,64},{64,96},{96,0},{1,33},{33,65},{65,97},{97,1},{2,34}... | collective-permute-start | bytes 196616 | tf_op jit(solution)/shard_map/ppermute | solution.py:367
  119.8 14.7 %collective-permute-start.15 = (f32[128,128]{1,0:T(8,128)S(1)}, f32[128,128]{1,0:T(8,128)S(1)}, u32[]{:S(2)}, u32[]{:S(2)}) collective-permute-start(f32[128,128]{1,0:T(8,128)S(1)} %add_add_fusion.1), channel_id=1, source_target_pairs={{0,96},{32,0},{64,32},{96,64},{1,97},{33,1},{65,33},{97,65},{2,98}... | collective-permute-start | bytes 196616 | tf_op jit(solution)/shard_map/ppermute | solution.py:367
  124.2 10.3 %collective-permute-start.14 = (f32[4,16,8,128]{3,2,1,0:T(8,128)S(1)}, f32[4,16,8,128]{3,2,1,0:T(8,128)S(1)}, u32[]{:S(2)}, u32[]{:S(2)}) collective-permute-start(f32[4,16,8,128]{3,2,1,0:T(8,128)S(1)} %get-tuple-element.45), channel_id=1, source_target_pairs={{0,256},{128,384},{256,0},{384,128},{1,257},{129,385},{257,1},{385... | collective-permute-start | bytes 786440 | tf_op jit(solution)/shard_map/ppermute | solution.py:416
  127.9 12.3 %collective-permute-start.13 = (f32[4,16,8,128]{3,2,1,0:T(8,128)S(1)}, f32[4,16,8,128]{3,2,1,0:T(8,128)S(1)}, u32[]{:S(2)}, u32[]{:S(2)}) collective-permute-start(f32[4,16,8,128]{3,2,1,0:T(8,128)S(1)} %get-tuple-element.46), channel_id=1, source_target_pairs={{0,128},{128,256},{256,384},{384,0},{1,129},{129,257},{257,385},{3... | collective-permute-start | bytes 786440 | tf_op jit(solution)/shard_map/ppermute | solution.py:416
  131.4 8.9 %collective-permute-start.12 = (f32[4,16,8,128]{3,2,1,0:T(8,128)S(1)}, f32[4,16,8,128]{3,2,1,0:T(8,128)S(1)}, u32[]{:S(2)}, u32[]{:S(2)}) collective-permute-start(f32[4,16,8,128]{3,2,1,0:T(8,128)S(1)} %get-tuple-element.47), channel_id=1, source_target_pairs={{0,384},{128,0},{256,128},{384,256},{1,385},{129,1},{257,129},{385... | collective-permute-start | bytes 786440 | tf_op jit(solution)/shard_map/ppermute | solution.py:416
  140.3 13.5 %collective-permute-start.18 = (f32[128,128]{1,0:T(8,128)S(1)}, f32[128,128]{1,0:T(8,128)S(1)}, u32[]{:S(2)}, u32[]{:S(2)}) collective-permute-start(f32[128,128]{1,0:T(8,128)S(1)} %add_add_fusion.near), channel_id=1, source_target_pairs={{0,16},{16,0},{1,17},{17,1},{2,18},{18,2},{3,19},{19,3},{4,20},{20... | collective-permute-start | bytes 196616 | tf_op jit(solution)/shard_map/ppermute | solution.py:419
  144.6 25.8 %collective-permute-start.21 = (f32[16,8,128]{2,1,0:T(8,128)S(1)}, f32[16,8,128]{2,1,0:T(8,128)S(1)}, u32[]{:S(2)}, u32[]{:S(2)}) collective-permute-start(f32[16,8,128]{2,1,0:T(8,128)S(1)} %get-tuple-element.48), channel_id=1, source_target_pairs={{0,64},{32,96},{64,0},{96,32},{1,65},{33,97},{65,1},{97,33},{2,66}... | collective-permute-start | bytes 196616 | tf_op jit(solution)/shard_map/ppermute | solution.py:420
  147.3 23.2 %collective-permute-start.20 = (f32[16,8,128]{2,1,0:T(8,128)S(1)}, f32[16,8,128]{2,1,0:T(8,128)S(1)}, u32[]{:S(2)}, u32[]{:S(2)}) collective-permute-start(f32[16,8,128]{2,1,0:T(8,128)S(1)} %get-tuple-element.49), channel_id=1, source_target_pairs={{0,32},{32,64},{64,96},{96,0},{1,33},{33,65},{65,97},{97,1},{2,34}... | collective-permute-start | bytes 196616 | tf_op jit(solution)/shard_map/ppermute | solution.py:420
  149.2 21.3 %collective-permute-start.19 = (f32[16,8,128]{2,1,0:T(8,128)S(1)}, f32[16,8,128]{2,1,0:T(8,128)S(1)}, u32[]{:S(2)}, u32[]{:S(2)}) collective-permute-start(f32[16,8,128]{2,1,0:T(8,128)S(1)} %get-tuple-element.50), channel_id=1, source_target_pairs={{0,96},{32,0},{64,32},{96,64},{1,97},{33,1},{65,33},{97,65},{2,98}... | collective-permute-start | bytes 196616 | tf_op jit(solution)/shard_map/ppermute | solution.py:420
  170.4 27.3 %copy-start.5 = (s32[97]{0:T(128)S(1)}, s32[97]{0:T(128)}, u32[]{:S(2)}) copy-start(s32[97]{0:T(128)} %get-tuple-element.24.table) | copy-start | bytes 1168
  198.5 29.7 %copy-start.7 = (f32[2,128,128]{2,1,0:T(8,128)S(1)}, f32[2,128,128]{2,1,0:T(8,128)}, u32[]{:S(2)}) copy-start(f32[2,128,128]{2,1,0:T(8,128)} %copy-done.6) | copy-start | bytes 393220
  217.4 14.6 %collective-permute-start.22 = (bf16[16,368,128]{2,1,0:T(8,128)(2,1)S(1)}, bf16[16,368,128]{2,1,0:T(8,128)(2,1)S(1)}, u32[]{:S(2)}, u32[]{:S(2)}) collective-permute-start(bf16[16,368,128]{2,1,0:T(8,128)(2,1)S(1)} %all_to_all.20.near), channel_id=1, source_target_pairs={{0,16},{16,0},{1,17},{17,1},{2,18},{18,2},{3,19},{19,3},{4,20},{20... | collective-permute-start | bytes 4521992 | tf_op jit(solution)/shard_map/ppermute | solution.py:446

commit v5 on v3

--- a/solution.py
+++ b/solution.py
@@ -29,6 +29,7 @@
 SWAP = [(0, 1), (1, 0)]
 VMEM = pl.BlockSpec(memory_space=pltpu.VMEM)
 SMEM = pl.BlockSpec(memory_space=pltpu.SMEM)
+ANY = pl.BlockSpec(memory_space=pl.ANY)
 
 
 def call(body, outs, scratch=(), flops=0, specs=None, n_in=0):
@@ -147,7 +148,7 @@
         out[z] = dot(matrix[...], both).astype(BF16)
         return 0
 
-    lax.fori_loop(0, GROUPS, block, 0)
+    lax.fori_loop(0, GROUPS, block, 0, unroll=4)
 
 
 def split3(value):
@@ -193,16 +194,13 @@
             total = value[:, :128] + (value[:, 128:256] + value[:, 256:])
             rows[k * BLOCK : (k + 1) * BLOCK, :] = total
         for i in range(16):
-            x = (place[0] + offset(i & 3)) & 3
-            y = (place[1] + offset(i >> 2)) & 3
-            base = (x * 4 + y) * 16
-            near = pl.multiple_of(base + 8 * place[2], 8)
-            far = pl.multiple_of(base + 8 - 8 * place[2], 8)
+            near = pl.multiple_of(16 * i + 8 * place[2], 8)
+            far = pl.multiple_of(16 * i + 8 - 8 * place[2], 8)
             keep[i, z] = rows[pl.ds(near, 8), :]
             send[i, z] = rows[pl.ds(far, 8), :]
         return 0
 
-    lax.fori_loop(0, GROUPS, block, 0, unroll=2)
+    lax.fori_loop(0, GROUPS, block, 0, unroll=4)
 
 
 def invert(place, near, far, out, work, *, size):
@@ -234,16 +232,22 @@
                 work[m, k + size :, :] -= change[k + size :, :]
 
 
-def scale_factor(place, inverse, a, b, c, d, out):
+def scale_factor(place, inverse, parts, _panel, _turned, mine, out):
     f = place[0] * 8 + place[1] * 2 + place[2]
-    total = ((a[...] + b[...]) + (c[...] + d[...])).reshape(128, RANK)
+    total = parts[0]
+    for i in range(1, 16):
+        total = total + parts[i]
     kind = jnp.where(f >= 12, 1, 0)
-    out[:128] = dot(total, inverse[kind], ((1,), (1,)), HIGHEST).astype(BF16)
+    factor = dot(total, inverse[kind], ((1,), (1,)), HIGHEST).astype(BF16)
+    mine[...] = factor
     half = jnp.where(f >= 16, 1, 0)
     start = pl.multiple_of(8 * f - 128 * half, 8)
     rows = inverse[half, pl.ds(start, 8), :]
     high = rows.astype(BF16).astype(F32)
-    out[128:] = jnp.concatenate([high, rows - high], axis=0).astype(BF16)
+    both = jnp.concatenate([high, rows - high], axis=0).astype(BF16)
+    for i in range(GROUPS):
+        out[i, :128] = factor
+        out[i, 128:] = both
 
 
 def orthonormal(table, place, panel, inverse, left, low):
@@ -265,13 +269,12 @@
             out[2 * s + k] = dot(unit, rows, ((1,), (1,))).astype(BF16)
 
 
-ROWS = 368
-
-
-def select(table, place, mine, tiles, out, packed):
+ROWS = 240
+
+
+def select(table, place, tiles, out, packed):
     z = place[3]
-    packed[:128, :] = mine[:128, :]
-    packed[128:272, :] = tiles[table[HELPER + z]]
+    packed[:144, :] = tiles[table[HELPER + z]]
     start = pl.multiple_of((z >> 1) * 16, 16)
     upper = (z & 1) == 1
     sums = []
@@ -283,9 +286,9 @@
             pair.append(jnp.where(upper, value[8:], value[:8]))
             whole = tiles[p, :128, :].astype(F32)
             sums.append(jnp.sum(whole * whole, axis=0, keepdims=True))
-        packed[272 + e * 8 : 288 + e * 8, :] = jnp.concatenate(pair, axis=0).astype(BF16)
+        packed[144 + e * 8 : 160 + e * 8, :] = jnp.concatenate(pair, axis=0).astype(BF16)
     sums.append(jnp.zeros((16 - EXPERTS, RANK), F32))
-    packed[352:, :] = jnp.concatenate(sums, axis=0).astype(BF16)
+    packed[224:, :] = jnp.concatenate(sums, axis=0).astype(BF16)
     value = packed[...]
     for i in range(16):
         out[i] = value
@@ -296,11 +299,11 @@
     matrix = jnp.concatenate(
         [join_matrix(place, c, False, 12), join_matrix(place, 1 - c, False, 12)], axis=1
     )
-    parts = near[:, 352:, :].astype(F32) + far[:, 352:, :].astype(F32)
+    parts = near[:, 224:, :].astype(F32) + far[:, 224:, :].astype(F32)
     sums = [jnp.sum(parts[6 * k : 6 * k + 6], axis=0) for k in range(2)]
     scales = [lax.rsqrt(s * (1.0 / HID) + epsilon) for s in sums]
     for g in range(EXPERTS // 2):
-        rows = slice(272 + g * 16, 288 + g * 16)
+        rows = slice(144 + g * 16, 160 + g * 16)
         data = jnp.concatenate(
             [near[:12, rows, :].reshape(192, RANK), far[:12, rows, :].reshape(192, RANK)], axis=0
         )
@@ -312,40 +315,51 @@
                 out[e, k] = value[i * BLOCK : (i + 1) * BLOCK, :] * scales[k][e : e + 1, :]
 
 
-def finish_state(table, place, turned, near, far, low, panel, left, out, left_out, inverse, wide):
+def update(matrix, chips, near, far, wide):
+    for g in range(8):
+        rows = slice(g * 16, g * 16 + 16)
+        data = jnp.concatenate(
+            [part[:chips, rows, :].reshape(16 * chips, RANK) for part in (near, far)], axis=0
+        )
+        value = dot(matrix, data).astype(BF16)
+        for p in range(2):
+            for k in range(2):
+                i = 2 * p + k
+                first = (2 * g + p) * BLOCK
+                wide[k, first : first + BLOCK, :] = value[i * BLOCK : (i + 1) * BLOCK]
+
+
+def finish_first(place, turned, near, far, low, out, wide):
+    c = place[2]
+    matrix = jnp.concatenate(
+        [join_matrix(place, c, True, 16), join_matrix(place, 1 - c, True, 16)], axis=1
+    )
+    update(matrix, 16, near, far, wide)
+    for k in range(2):
+        change = dot(low[k], wide[k], ((1,), (1,)))
+        out[k] = (turned[k].astype(F32) + change).astype(BF16)
+
+
+def finish_second(table, place, turned, near, far, first, panel, left, out, left_out, inverse, wide):
     c = place[2]
     matrix = jnp.concatenate(
         [join_matrix(place, c, False, 12), join_matrix(place, 1 - c, False, 12)], axis=1
     )
     for part, core in ((near, c), (far, 1 - c)):
         for chip in range(16):
-            value = part[chip, 256:272, :].astype(F32)
+            value = part[chip, 128:144, :].astype(F32)
             row = pl.multiple_of(16 * chip + 8 * core, 8)
             inverse[pl.ds(row, 8), :] = value[:8] + value[8:]
     some = table[SECOND + place[3]] < EXPERTS
-    lows = [low[0], low[1]]
+    update(matrix, 12, near, far, wide)
     for k in range(2):
         ortho = dot(panel[k], inverse[k * RANK : (k + 1) * RANK, :], ((1,), (1,)), HIGHEST)
         ortho = jnp.where(some, ortho, 0.0)
         left_out[k] = left[k]
         left_out[2 + k] = ortho * math.sqrt(D)
-        lows.append((ortho * (-feedback)).astype(BF16))
-    for s in range(2):
-        for g in range(8):
-            rows = slice(s * 128 + g * 16, s * 128 + g * 16 + 16)
-            data = jnp.concatenate(
-                [near[:12, rows, :].reshape(192, RANK), far[:12, rows, :].reshape(192, RANK)],
-                axis=0,
-            )
-            value = dot(matrix, data).astype(BF16)
-            for p in range(2):
-                for k in range(2):
-                    i = 2 * p + k
-                    first = (2 * g + p) * BLOCK
-                    wide[2 * s + k, first : first + BLOCK, :] = value[i * BLOCK : (i + 1) * BLOCK]
-    for i in range(4):
-        change = dot(lows[i], wide[i], ((1,), (1,)))
-        out[i] = (turned[i].astype(F32) + change).astype(BF16)
+        change = dot((ortho * (-feedback)).astype(BF16), wide[k], ((1,), (1,)))
+        out[k] = first[k]
+        out[2 + k] = (turned[2 + k].astype(F32) + change).astype(BF16)
 
 
 def ring(shift):
@@ -412,10 +426,7 @@
     gram = spread_sum(spread_sum(gram, "x"), "y")
     other = lax.ppermute(gram, "c", SWAP)
     parts = keep + lax.ppermute(send, "c", SWAP)
-    parts = parts.reshape(4, 4, 16, 8, RANK)
-    moved = [lax.ppermute(parts[:, i + 1], "x", ring(SHIFTS[i])) for i in range(3)]
-    parts = (parts[:, 0] + moved[0]) + (moved[1] + moved[2])
-    parts = [parts[0]] + [lax.ppermute(parts[i + 1], "y", ring(SHIFTS[i])) for i in range(3)]
+    parts = exchange(parts.reshape(16, 128, RANK), XY)
     inverse = call(
         functools.partial(invert, size=8),
         sds((2, RANK, RANK), F32),
@@ -423,35 +434,46 @@
         specs=[SMEM, VMEM, VMEM],
         flops=4_000_000_000,
     )(place, gram, other)
-    mine = call(
-        scale_factor, sds((144, RANK), BF16), specs=[SMEM] + [VMEM] * 5, flops=100_000_000
-    )(place, inverse, *parts)
-    left, low = call(
-        orthonormal, (two, sds((2, 128, RANK), BF16)), specs=[SMEM, SMEM, VMEM, VMEM], flops=100_000_000
-    )(table, place, panel, inverse)
-    tiles = lax.all_gather(mine, "z")
     second_panel = call(second_panels, two, n_in=2, flops=200_000_000)(second, right)
     turned = call(
         turn, sds((4, 128, HID), BF16), specs=[SMEM, SMEM, VMEM, VMEM], flops=200_000_000
     )(table, place, state, second)
+    mine, copies = call(
+        scale_factor,
+        (sds((128, RANK), BF16), sds((16, 144, RANK), BF16)),
+        specs=[SMEM, VMEM, VMEM, ANY, ANY],
+        flops=100_000_000,
+    )(place, inverse, parts, second_panel, turned)
+    tiles = exchange(copies, "z")
+    left, low = call(
+        orthonormal, (two, sds((2, 128, RANK), BF16)), specs=[SMEM, SMEM, VMEM, VMEM], flops=100_000_000
+    )(table, place, panel, inverse)
+    near, far = gather_slices(mine)
+    first = call(
+        finish_first,
+        sds((2, 128, HID), BF16),
+        [pltpu.VMEM((2, HID, RANK), BF16)],
+        specs=[SMEM] + [VMEM] * 4,
+        flops=600_000_000,
+    )(place, turned, near, far, low)
     chosen = call(
         select,
         sds((16, ROWS, RANK), BF16),
         [pltpu.VMEM((ROWS, RANK), BF16)],
-        specs=[SMEM, SMEM, VMEM, VMEM],
-    )(table, place, mine, tiles)
+        specs=[SMEM, SMEM, VMEM],
+    )(table, place, tiles)
     near = exchange(chosen, XY)
     far = lax.ppermute(near, "c", SWAP)
     right_out = call(
         finish_right, sds((EXPERTS, 2, BLOCK, RANK), F32), specs=[SMEM, VMEM, VMEM], flops=300_000_000
     )(place, near, far)
     state_out, left_out = call(
-        finish_state,
+        finish_second,
         (sds((4, 128, HID), BF16), sds((4, 128, RANK), F32)),
-        [pltpu.VMEM((2 * RANK, RANK), F32), pltpu.VMEM((4, HID, RANK), BF16)],
+        [pltpu.VMEM((2 * RANK, RANK), F32), pltpu.VMEM((2, HID, RANK), BF16)],
         specs=[SMEM, SMEM] + [VMEM] * 6,
-        flops=1_200_000_000,
-    )(table, place, turned, near, far, low, second_panel, left)
+        flops=600_000_000,
+    )(table, place, turned, near, far, first, second_panel, left)
     return (
         state_out.reshape(CAP, 2, 128, HID),
         left_out.reshape(CAP, 2, 128, RANK),

time: 260 us -> 275 us (1.058)
  the two profiles are of different devices: /device:TPU:32 before, /device:TPU:1 now
where the time goes in v5:
time: 275 us; the launch traced here: 273 us
  starting transfers between devices  126 us (46%)
  waiting for transfers between devices  54.2 us (20%)
  blocking collectives  43.9 us (16%)
  Pallas kernels  42.7 us (16%)
  local copies, waits for them, and re-layouts  3.56 us (1%)
    all_to_all x1, blocking collectives, exchange(): return lax.all_to_all(x, axis, split_axis=0, concat_axis=0, tiled=True)  43.9 us
    all_to_all x5, starting transfers between devices, exchange(): return lax.all_to_all(x, axis, split_axis=0, concat_axis=0, tiled=True)  43.5 us
    ppermute x12, starting transfers between devices, gather_slices(): lax.ppermute(x, axis, ring((4 - d) % 4))  38.9 us
    all_to_all x5, waiting for transfers between devices, exchange(): return lax.all_to_all(x, axis, split_axis=0, concat_axis=0, tiled=True)  26.8 us
    ppermute x6, starting transfers between devices, spread_sum(): parts = [lax.ppermute(x, axis, ring(d)) for d in SHIFTS]  19.5 us
    pallas_call x1, Pallas kernels, shards(): call(functools.partial(invert, size=8), sds((2, RANK, RANK), F32), [pltpu...  16.6 us
    ppermute x12, waiting for transfers between devices, gather_slices(): lax.ppermute(x, axis, ring((4 - d) % 4))  16.3 us
    ppermute x2, starting transfers between devices, gather_slices(): return (x, lax.ppermute(x, 'c', SWAP))  9.41 us
  transfers between devices with their start and end apart: 29, of which 14 were waited for; matrix products, arithmetic and copies ran while one was open for 1% of the time, Pallas kernels for 11%

profile of v5, /device:TPU:1, one launch (start us, length us, event | category | flops | bytes accessed | tf_op | source)
XLA Modules:
  0.0 273.3 jit_solution(9807353464343388649)
XLA Ops:
  1.3 2.1 shard_map.67
  3.4 15.8 %all-to-all-start = ((bf16[16,16,128]{2,1,0:T(8,128)(2,1)}), bf16[16,16,128]{2,1,0:T(8,128)(2,1)S(1)}, u32[]{:S(2)}, u32[]{:S(2)}) async-start(bf16[16,16,128]{2,1,0:T(8,128)(2,1)} %get-tuple-element.24), calls=%async_computation | async-start | bytes 131072 | tf_op jit(solution)/shard_map/all_to_all | solution.py:385
  21.8 2.2 shard_map.68
  24.9 5.9 %all-to-all-done = bf16[16,16,128]{2,1,0:T(8,128)(2,1)S(1)} async-done(((bf16[16,16,128]{2,1,0:T(8,128)(2,1)}), bf16[16,16,128]{2,1,0:T(8,128)(2,1)S(1)}, u32[]{:S(2)}, u32[]{:S(2)}) %all-to-all-start) | async-done | bytes 65568 | tf_op jit(solution)/shard_map/all_to_all | solution.py:385
  30.7 5.6 %all-to-all-start.1 = ((bf16[16,192,128]{2,1,0:T(8,128)(2,1)}), bf16[16,192,128]{2,1,0:T(8,128)(2,1)S(1)}, u32[]{:S(2)}, u32[]{:S(2)}) async-start(bf16[16,192,128]{2,1,0:T(8,128)(2,1)} %get-tuple-element.25), calls=%async_computation.1 | async-start | bytes 1572864 | tf_op jit(solution)/shard_map/all_to_all | solution.py:385
  36.3 4.7 %collective-permute-start.2 = (bf16[16,16,128]{2,1,0:T(8,128)(2,1)S(1)}, bf16[16,16,128]{2,1,0:T(8,128)(2,1)S(1)}, u32[]{:S(2)}, u32[]{:S(2)}) collective-permute-start(bf16[16,16,128]{2,1,0:T(8,128)(2,1)S(1)} %all-to-all-done), channel_id=1, source_target_pairs={{0,256},{128,384},{256,0},{384,128},{1,257},{129,385},{257,1},{385... | collective-permute-start | bytes 196616 | tf_op jit(solution)/shard_map/ppermute | solution.py:374
  41.0 2.8 %collective-permute-start.1 = (bf16[16,16,128]{2,1,0:T(8,128)(2,1)S(1)}, bf16[16,16,128]{2,1,0:T(8,128)(2,1)S(1)}, u32[]{:S(2)}, u32[]{:S(2)}) collective-permute-start(bf16[16,16,128]{2,1,0:T(8,128)(2,1)S(1)} %all-to-all-done), channel_id=1, source_target_pairs={{0,384},{128,0},{256,128},{384,256},{1,385},{129,1},{257,129},{385... | collective-permute-start | bytes 196616 | tf_op jit(solution)/shard_map/ppermute | solution.py:374
  43.8 2.5 collective-permute-start
  46.3 4.0 %collective-permute-done = bf16[16,16,128]{2,1,0:T(8,128)(2,1)S(1)} collective-permute-done((bf16[16,16,128]{2,1,0:T(8,128)(2,1)S(1)}, bf16[16,16,128]{2,1,0:T(8,128)(2,1)S(1)}, u32[]{:S(2)}, u32[]{:S(2)}) %collective-permute-start) | collective-permute-done | bytes 65568 | tf_op jit(solution)/shard_map/ppermute | solution.py:374
  50.3 4.6 %collective-permute-start.4 = (bf16[4,16,16,128]{3,2,1,0:T(8,128)(2,1)S(1)}, bf16[4,16,16,128]{3,2,1,0:T(8,128)(2,1)S(1)}, u32[]{:S(2)}, u32[]{:S(2)}) collective-permute-start(bf16[4,16,16,128]{3,2,1,0:T(8,128)(2,1)S(1)} %get-tuple-element.42), channel_id=1, source_target_pairs={{0,96},{32,0},{64,32},{96,64},{1,97},{33,1},{65,33},{97,65},{2,98}... | collective-permute-start | bytes 786440 | tf_op jit(solution)/shard_map/ppermute | solution.py:374
  55.0 1.9 collective-permute-start.3
  56.9 3.5 %collective-permute-start.5 = (bf16[4,16,16,128]{3,2,1,0:T(8,128)(2,1)S(1)}, bf16[4,16,16,128]{3,2,1,0:T(8,128)(2,1)S(1)}, u32[]{:S(2)}, u32[]{:S(2)}) collective-permute-start(bf16[4,16,16,128]{3,2,1,0:T(8,128)(2,1)S(1)} %get-tuple-element.42), channel_id=1, source_target_pairs={{0,64},{32,96},{64,0},{96,32},{1,65},{33,97},{65,1},{97,33},{2,66}... | collective-permute-start | bytes 786440 | tf_op jit(solution)/shard_map/ppermute | solution.py:374
  60.5 4.0 %collective-permute-done.3 = bf16[4,16,16,128]{3,2,1,0:T(8,128)(2,1)S(1)} collective-permute-done((bf16[4,16,16,128]{3,2,1,0:T(8,128)(2,1)S(1)}, bf16[4,16,16,128]{3,2,1,0:T(8,128)(2,1)S(1)}, u32[]{:S(2)}, u32[]{:S(2)}) %collective-permute-start.3) | collective-permute-done | bytes 262176 | tf_op jit(solution)/shard_map/ppermute | solution.py:374
  64.5 3.8 %collective-permute-done.5 = bf16[4,16,16,128]{3,2,1,0:T(8,128)(2,1)S(1)} collective-permute-done((bf16[4,16,16,128]{3,2,1,0:T(8,128)(2,1)S(1)}, bf16[4,16,16,128]{3,2,1,0:T(8,128)(2,1)S(1)}, u32[]{:S(2)}, u32[]{:S(2)}) %collective-permute-start.5) | collective-permute-done | bytes 262176 | tf_op jit(solution)/shard_map/ppermute | solution.py:374
  68.4 6.0 %collective-permute-start.6 = (bf16[16,16,16,128]{3,2,1,0:T(8,128)(2,1)S(1)}, bf16[16,16,16,128]{3,2,1,0:T(8,128)(2,1)S(1)}, u32[]{:S(2)}, u32[]{:S(2)}) collective-permute-start(bf16[16,16,16,128]{3,2,1,0:T(8,128)(2,1)S(1)} %bitcast.30), channel_id=1, source_target_pairs={{0,16},{16,0},{1,17},{17,1},{2,18},{18,2},{3,19},{19,3},{4,20},{20... | collective-permute-start | bytes 3145736 | tf_op jit(solution)/shard_map/ppermute | solution.py:376
  74.5 2.3 collective-permute-done.6.far
  76.8 2.9 %shard_map.69.right = bf16[16,384,128]{2,1,0:T(8,128)(2,1)S(1)} custom-call(s32[4]{0:T(128)S(1)} %copy-done.5, bf16[16,16,16,128]{3,2,1,0:T(8,128)(2,1)S(1)} %bitcast.31, bf16[16,16,16,128]{3,2,1,0:T(8,128)(2,1)S(1)} %collective-permute-done.6.far), custom_call_target="tpu_custom_call" | custom-call | flops 800000000 | bytes 4000000 | tf_op jit(solution)/shard_map/pallas_call | solution.py:407
  79.7 2.8 %shard_map.70 = (f32[2,128,128]{2,1,0:T(8,128)S(1)}, f32[128,128]{1,0:T(8,128)S(1)}, f32[128,128]{1,0:T(8,128)S(1)}) custom-call(s32[4]{0:T(128)S(1)} %copy-done.5, bf16[16,192,128]{2,1,0:T(8,128)(2,1)S(1)} %all-to-all-done.1.state.first, bf16[16,384,128]{2,1,0:T(8,128)(2,1)S(1)} %shard_map.69.right), custom_call_target="tpu_custom_call" | custom-call | flops 300000000 | bytes 4000000 | tf_op jit(solution)/shard_map/pallas_call | solution.py:416
  82.5 11.5 %all-to-all-start.2 = ((bf16[16,192,128]{2,1,0:T(8,128)(2,1)}), bf16[16,192,128]{2,1,0:T(8,128)(2,1)S(1)}, u32[]{:S(2)}, u32[]{:S(2)}) async-start(bf16[16,192,128]{2,1,0:T(8,128)(2,1)} %copy-done), calls=%async_computation.2 | async-start | bytes 1572864 | tf_op jit(solution)/shard_map/all_to_all | solution.py:385
  94.0 2.0 shard_map.73
  95.9 2.6 collective-permute-start.15
  98.5 1.9 collective-permute-start.7
  101.7 1.9 collective-permute-start.10
  103.6 1.9 collective-permute-start.9
  105.6 4.6 %collective-permute-start.8 = (f32[128,128]{1,0:T(8,128)S(1)}, f32[128,128]{1,0:T(8,128)S(1)}, u32[]{:S(2)}, u32[]{:S(2)}) collective-permute-start(f32[128,128]{1,0:T(8,128)S(1)} %add.24), channel_id=1, source_target_pairs={{0,384},{128,0},{256,128},{384,256},{1,385},{129,1},{257,129},{385... | collective-permute-start | bytes 196616 | tf_op jit(solution)/shard_map/ppermute | solution.py:380
  111.3 16.9 %all-to-all-done.2.second.state = bf16[16,192,128]{2,1,0:T(8,128)(2,1)S(1)} async-done(((bf16[16,192,128]{2,1,0:T(8,128)(2,1)}), bf16[16,192,128]{2,1,0:T(8,128)(2,1)S(1)}, u32[]{:S(2)}, u32[]{:S(2)}) %all-to-all-start.2) | async-done | bytes 786464 | tf_op jit(solution)/shard_map/all_to_all | solution.py:385
  128.2 4.3 %all-to-all-start.3 = ((f32[16,128,128]{2,1,0:T(8,128)}), f32[16,128,128]{2,1,0:T(8,128)}, u32[]{:S(2)}, u32[]{:S(2)}) async-start(f32[16,128,128]{2,1,0:T(8,128)} %add_bitcast_fusion), calls=%async_computation.3 | async-start | bytes 2097152 | tf_op jit(solution)/shard_map/all_to_all | solution.py:385
  132.6 4.6 %collective-permute-start.13 = (f32[128,128]{1,0:T(8,128)S(1)}, f32[128,128]{1,0:T(8,128)S(1)}, u32[]{:S(2)}, u32[]{:S(2)}) collective-permute-start(f32[128,128]{1,0:T(8,128)S(1)} %add_add_fusion.1), channel_id=1, source_target_pairs={{0,64},{32,96},{64,0},{96,32},{1,65},{33,97},{65,1},{97,33},{2,66}... | collective-permute-start | bytes 196616 | tf_op jit(solution)/shard_map/ppermute | solution.py:380
  137.2 2.2 collective-permute-start.12
  139.4 4.3 %collective-permute-start.11 = (f32[128,128]{1,0:T(8,128)S(1)}, f32[128,128]{1,0:T(8,128)S(1)}, u32[]{:S(2)}, u32[]{:S(2)}) collective-permute-start(f32[128,128]{1,0:T(8,128)S(1)} %add_add_fusion.1), channel_id=1, source_target_pairs={{0,96},{32,0},{64,32},{96,64},{1,97},{33,1},{65,33},{97,65},{2,98}... | collective-permute-start | bytes 196616 | tf_op jit(solution)/shard_map/ppermute | solution.py:380
  143.7 4.4 %collective-permute-done.12 = f32[128,128]{1,0:T(8,128)S(1)} collective-permute-done((f32[128,128]{1,0:T(8,128)S(1)}, f32[128,128]{1,0:T(8,128)S(1)}, u32[]{:S(2)}, u32[]{:S(2)}) %collective-permute-start.12) | collective-permute-done | bytes 65568 | tf_op jit(solution)/shard_map/ppermute | solution.py:380
  149.8 4.8 %collective-permute-start.14 = (f32[128,128]{1,0:T(8,128)S(1)}, f32[128,128]{1,0:T(8,128)S(1)}, u32[]{:S(2)}, u32[]{:S(2)}) collective-permute-start(f32[128,128]{1,0:T(8,128)S(1)} %add_add_fusion.near), channel_id=1, source_target_pairs={{0,16},{16,0},{1,17},{17,1},{2,18},{18,2},{3,19},{19,3},{4,20},{20... | collective-permute-start | bytes 196616 | tf_op jit(solution)/shard_map/ppermute | solution.py:427
  155.5 16.6 %shard_map.72.inverse = f32[2,128,128]{2,1,0:T(8,128)S(1)} custom-call(s32[4]{0:T(128)S(1)} %copy-done.5, f32[128,128]{1,0:T(8,128)S(1)} %add_add_fusion.near, f32[128,128]{1,0:T(8,128)S(1)} %collective-permute-done.14.far), custom_call_target="tpu_custom_call" | custom-call | flops 4000000000 | bytes 4000000 | tf_op jit(solution)/shard_map/pallas_call | solution.py:430
  176.5 43.9 %all_to_all.30.tiles = bf16[16,144,128]{2,1,0:T(8,128)(2,1)S(1)} all-to-all(bf16[16,144,128]{2,1,0:T(8,128)(2,1)S(1)} %get-tuple-element.35), channel_id=1, replica_groups=mesh['x'=4,'y'=4,'c'=2,'z'=16] {'z'}, dimensions={0} | all-to-all | bytes 1179648 | tf_op jit(solution)/shard_map/all_to_all | solution.py:385
  222.1 6.3 %all-to-all-start.5 = ((bf16[16,240,128]{2,1,0:T(8,128)(2,1)}), bf16[16,240,128]{2,1,0:T(8,128)(2,1)S(1)}, u32[]{:S(2)}, u32[]{:S(2)}) async-start(bf16[16,240,128]{2,1,0:T(8,128)(2,1)} %shard_map.76), calls=%async_computation.5 | async-start | bytes 1966080 | tf_op jit(solution)/shard_map/all_to_all | solution.py:385
  228.4 4.8 %collective-permute-start.19 = (bf16[128,128]{1,0:T(8,128)(2,1)S(1)}, bf16[128,128]{1,0:T(8,128)(2,1)S(1)}, u32[]{:S(2)}, u32[]{:S(2)}) collective-permute-start(bf16[128,128]{1,0:T(8,128)(2,1)S(1)} %get-tuple-element.36), channel_id=1, source_target_pairs={{0,256},{128,384},{256,0},{384,128},{1,257},{129,385},{257,1},{385... | collective-permute-start | bytes 98312 | tf_op jit(solution)/shard_map/ppermute | solution.py:374
  233.2 2.8 %collective-permute-start.18 = (bf16[128,128]{1,0:T(8,128)(2,1)S(1)}, bf16[128,128]{1,0:T(8,128)(2,1)S(1)}, u32[]{:S(2)}, u32[]{:S(2)}) collective-permute-start(bf16[128,128]{1,0:T(8,128)(2,1)S(1)} %get-tuple-element.36), channel_id=1, source_target_pairs={{0,384},{128,0},{256,128},{384,256},{1,385},{129,1},{257,129},{385... | collective-permute-start | bytes 98312 | tf_op jit(solution)/shard_map/ppermute | solution.py:374
  236.0 2.5 collective-permute-start.17
  238.5 4.0 %all-to-all-done.5.near = bf16[16,240,128]{2,1,0:T(8,128)(2,1)S(1)} async-done(((bf16[16,240,128]{2,1,0:T(8,128)(2,1)}), bf16[16,240,128]{2,1,0:T(8,128)(2,1)S(1)}, u32[]{:S(2)}, u32[]{:S(2)}) %all-to-all-start.5) | async-done | bytes 983072 | tf_op jit(solution)/shard_map/all_to_all | solution.py:385
  242.5 5.1 %collective-permute-start.16 = (bf16[16,240,128]{2,1,0:T(8,128)(2,1)S(1)}, bf16[16,240,128]{2,1,0:T(8,128)(2,1)S(1)}, u32[]{:S(2)}, u32[]{:S(2)}) collective-permute-start(bf16[16,240,128]{2,1,0:T(8,128)(2,1)S(1)} %all-to-all-done.5.near), channel_id=1, source_target_pairs={{0,16},{16,0},{1,17},{17,1},{2,18},{18,2},{3,19},{19,3},{4,20},{20... | collective-permute-start | bytes 2949128 | tf_op jit(solution)/shard_map/ppermute | solution.py:466
  247.7 3.0 %collective-permute-start.21 = (bf16[4,128,128]{2,1,0:T(8,128)(2,1)S(1)}, bf16[4,128,128]{2,1,0:T(8,128)(2,1)S(1)}, u32[]{:S(2)}, u32[]{:S(2)}) collective-permute-start(bf16[4,128,128]{2,1,0:T(8,128)(2,1)S(1)} %get-tuple-element.44), channel_id=1, source_target_pairs={{0,96},{32,0},{64,32},{96,64},{1,97},{33,1},{65,33},{97,65},{2,98}... | collective-permute-start | bytes 393224 | tf_op jit(solution)/shard_map/ppermute | solution.py:374
  250.7 2.2 collective-permute-start.20
  253.0 3.6 %collective-permute-start.22 = (bf16[4,128,128]{2,1,0:T(8,128)(2,1)S(1)}, bf16[4,128,128]{2,1,0:T(8,128)(2,1)S(1)}, u32[]{:S(2)}, u32[]{:S(2)}) collective-permute-start(bf16[4,128,128]{2,1,0:T(8,128)(2,1)S(1)} %get-tuple-element.44), channel_id=1, source_target_pairs={{0,64},{32,96},{64,0},{96,32},{1,65},{33,97},{65,1},{97,33},{2,66}... | collective-permute-start | bytes 393224 | tf_op jit(solution)/shard_map/ppermute | solution.py:374
  256.6 2.1 collective-permute-done.20
  258.6 2.5 collective-permute-done.22
  261.2 3.4 %collective-permute-start.23 = (bf16[16,128,128]{2,1,0:T(8,128)(2,1)S(1)}, bf16[16,128,128]{2,1,0:T(8,128)(2,1)S(1)}, u32[]{:S(2)}, u32[]{:S(2)}) collective-permute-start(bf16[16,128,128]{2,1,0:T(8,128)(2,1)S(1)} %bitcast.32), channel_id=1, source_target_pairs={{0,16},{16,0},{1,17},{17,1},{2,18},{18,2},{3,19},{19,3},{4,20},{20... | collective-permute-start | bytes 1572872 | tf_op jit(solution)/shard_map/ppermute | solution.py:376
  267.9 2.1 shard_map.80
  270.0 3.3 %shard_map.79 = (bf16[4,128,1536]{2,1,0:T(8,128)(2,1)}, f32[4,128,128]{2,1,0:T(8,128)}) custom-call(s32[97]{0:T(128)S(1)} %copy-done.7, s32[4]{0:T(128)S(1)} %copy-done.5, bf16[4,128,1536]{2,1,0:T(8,128)(2,1)S(1)} %shard_map.71._turned.turned, bf16[16,240,128]{2,1,0:T(8,128)(2,1)S(1)} %all-to-all-done.5.near, ...), custom_call_target="tpu_custom_call" | custom-call | flops 600000000 | bytes 4000000 | tf_op jit(solution)/shard_map/pallas_call | solution.py:470
  (54 shorter events, 18.8 us)
Async XLA Ops:
  3.4 27.3 %all-to-all-start = ((bf16[16,16,128]{2,1,0:T(8,128)(2,1)}), bf16[16,16,128]{2,1,0:T(8,128)(2,1)S(1)}, u32[]{:S(2)}, u32[]{:S(2)}) async-start(bf16[16,16,128]{2,1,0:T(8,128)(2,1)} %get-tuple-element.24), calls=%async_computation | async-start | bytes 131072 | tf_op jit(solution)/shard_map/all_to_all | solution.py:385
  19.1 1.0 copy-start.1
  20.2 1.0 copy-start.2
  21.2 0.6 copy-start.6
  24.0 0.9 copy-start
  30.7 49.0 %all-to-all-start.1 = ((bf16[16,192,128]{2,1,0:T(8,128)(2,1)}), bf16[16,192,128]{2,1,0:T(8,128)(2,1)S(1)}, u32[]{:S(2)}, u32[]{:S(2)}) async-start(bf16[16,192,128]{2,1,0:T(8,128)(2,1)} %get-tuple-element.25), calls=%async_computation.1 | async-start | bytes 1572864 | tf_op jit(solution)/shard_map/all_to_all | solution.py:385
  36.3 40.4 %copy-start.5 = (s32[4]{0:T(128)S(1)}, s32[4]{0:T(128)}, u32[]{:S(2)}) copy-start(s32[4]{0:T(128)} %pad_add_fusion.place) | copy-start | bytes 52
  36.3 10.0 %collective-permute-start.2 = (bf16[16,16,128]{2,1,0:T(8,128)(2,1)S(1)}, bf16[16,16,128]{2,1,0:T(8,128)(2,1)S(1)}, u32[]{:S(2)}, u32[]{:S(2)}) collective-permute-start(bf16[16,16,128]{2,1,0:T(8,128)(2,1)S(1)} %all-to-all-done), channel_id=1, source_target_pairs={{0,256},{128,384},{256,0},{384,128},{1,257},{129,385},{257,1},{385... | collective-permute-start | bytes 196616 | tf_op jit(solution)/shard_map/ppermute | solution.py:374
  41.0 5.3 %collective-permute-start.1 = (bf16[16,16,128]{2,1,0:T(8,128)(2,1)S(1)}, bf16[16,16,128]{2,1,0:T(8,128)(2,1)S(1)}, u32[]{:S(2)}, u32[]{:S(2)}) collective-permute-start(bf16[16,16,128]{2,1,0:T(8,128)(2,1)S(1)} %all-to-all-done), channel_id=1, source_target_pairs={{0,384},{128,0},{256,128},{384,256},{1,385},{129,1},{257,129},{385... | collective-permute-start | bytes 196616 | tf_op jit(solution)/shard_map/ppermute | solution.py:374
  43.8 6.5 %collective-permute-start = (bf16[16,16,128]{2,1,0:T(8,128)(2,1)S(1)}, bf16[16,16,128]{2,1,0:T(8,128)(2,1)S(1)}, u32[]{:S(2)}, u32[]{:S(2)}) collective-permute-start(bf16[16,16,128]{2,1,0:T(8,128)(2,1)S(1)} %all-to-all-done), channel_id=1, source_target_pairs={{0,128},{128,256},{256,384},{384,0},{1,129},{129,257},{257,385},{3... | collective-permute-start | bytes 196616 | tf_op jit(solution)/shard_map/ppermute | solution.py:374
  50.3 10.1 %collective-permute-start.4 = (bf16[4,16,16,128]{3,2,1,0:T(8,128)(2,1)S(1)}, bf16[4,16,16,128]{3,2,1,0:T(8,128)(2,1)S(1)}, u32[]{:S(2)}, u32[]{:S(2)}) collective-permute-start(bf16[4,16,16,128]{3,2,1,0:T(8,128)(2,1)S(1)} %get-tuple-element.42), channel_id=1, source_target_pairs={{0,96},{32,0},{64,32},{96,64},{1,97},{33,1},{65,33},{97,65},{2,98}... | collective-permute-start | bytes 786440 | tf_op jit(solution)/shard_map/ppermute | solution.py:374
  55.0 9.5 %collective-permute-start.3 = (bf16[4,16,16,128]{3,2,1,0:T(8,128)(2,1)S(1)}, bf16[4,16,16,128]{3,2,1,0:T(8,128)(2,1)S(1)}, u32[]{:S(2)}, u32[]{:S(2)}) collective-permute-start(bf16[4,16,16,128]{3,2,1,0:T(8,128)(2,1)S(1)} %get-tuple-element.42), channel_id=1, source_target_pairs={{0,32},{32,64},{64,96},{96,0},{1,33},{33,65},{65,97},{97,1},{2,34}... | collective-permute-start | bytes 786440 | tf_op jit(solution)/shard_map/ppermute | solution.py:374
  56.9 11.4 %collective-permute-start.5 = (bf16[4,16,16,128]{3,2,1,0:T(8,128)(2,1)S(1)}, bf16[4,16,16,128]{3,2,1,0:T(8,128)(2,1)S(1)}, u32[]{:S(2)}, u32[]{:S(2)}) collective-permute-start(bf16[4,16,16,128]{3,2,1,0:T(8,128)(2,1)S(1)} %get-tuple-element.42), channel_id=1, source_target_pairs={{0,64},{32,96},{64,0},{96,32},{1,65},{33,97},{65,1},{97,33},{2,66}... | collective-permute-start | bytes 786440 | tf_op jit(solution)/shard_map/ppermute | solution.py:374
  68.4 8.3 %collective-permute-start.6 = (bf16[16,16,16,128]{3,2,1,0:T(8,128)(2,1)S(1)}, bf16[16,16,16,128]{3,2,1,0:T(8,128)(2,1)S(1)}, u32[]{:S(2)}, u32[]{:S(2)}) collective-permute-start(bf16[16,16,16,128]{3,2,1,0:T(8,128)(2,1)S(1)} %bitcast.30), channel_id=1, source_target_pairs={{0,16},{16,0},{1,17},{17,1},{2,18},{18,2},{3,19},{19,3},{4,20},{20... | collective-permute-start | bytes 3145736 | tf_op jit(solution)/shard_map/ppermute | solution.py:376
  82.5 19.2 %copy-start.8 = (f32[2,128,128]{2,1,0:T(8,128)}, f32[2,128,128]{2,1,0:T(8,128)S(1)}, u32[]{:S(2)}) copy-start(f32[2,128,128]{2,1,0:T(8,128)S(1)} %get-tuple-element.32.panel) | copy-start | bytes 393220
  82.5 45.7 %all-to-all-start.2 = ((bf16[16,192,128]{2,1,0:T(8,128)(2,1)}), bf16[16,192,128]{2,1,0:T(8,128)(2,1)S(1)}, u32[]{:S(2)}, u32[]{:S(2)}) async-start(bf16[16,192,128]{2,1,0:T(8,128)(2,1)} %copy-done), calls=%async_computation.2 | async-start | bytes 1572864 | tf_op jit(solution)/shard_map/all_to_all | solution.py:385
  95.9 14.2 %collective-permute-start.15 = (f32[16,16,8,128]{3,2,1,0:T(8,128)S(1)}, f32[16,16,8,128]{3,2,1,0:T(8,128)S(1)}, u32[]{:S(2)}, u32[]{:S(2)}) collective-permute-start(f32[16,16,8,128]{3,2,1,0:T(8,128)S(1)} %get-tuple-element.34), channel_id=1, source_target_pairs={{0,16},{16,0},{1,17},{17,1},{2,18},{18,2},{3,19},{19,3},{4,20},{20... | collective-permute-start | bytes 3145736 | tf_op jit(solution)/shard_map/ppermute | solution.py:428
  98.5 3.1 %collective-permute-start.7 = (f32[128,128]{1,0:T(8,128)S(1)}, f32[128,128]{1,0:T(8,128)S(1)}, u32[]{:S(2)}, u32[]{:S(2)}) collective-permute-start(f32[128,128]{1,0:T(8,128)S(1)} %get-tuple-element.31), channel_id=1, source_target_pairs={{0,16},{16,0},{1,17},{17,1},{2,18},{18,2},{3,19},{19,3},{4,20},{20... | collective-permute-start | bytes 196616 | tf_op jit(solution)/shard_map/ppermute | solution.py:421
  101.7 30.9 %collective-permute-start.10 = (f32[128,128]{1,0:T(8,128)S(1)}, f32[128,128]{1,0:T(8,128)S(1)}, u32[]{:S(2)}, u32[]{:S(2)}) collective-permute-start(f32[128,128]{1,0:T(8,128)S(1)} %add.24), channel_id=1, source_target_pairs={{0,256},{128,384},{256,0},{384,128},{1,257},{129,385},{257,1},{385... | collective-permute-start | bytes 196616 | tf_op jit(solution)/shard_map/ppermute | solution.py:380
  103.6 28.9 %collective-permute-start.9 = (f32[128,128]{1,0:T(8,128)S(1)}, f32[128,128]{1,0:T(8,128)S(1)}, u32[]{:S(2)}, u32[]{:S(2)}) collective-permute-start(f32[128,128]{1,0:T(8,128)S(1)} %add.24), channel_id=1, source_target_pairs={{0,128},{128,256},{256,384},{384,0},{1,129},{129,257},{257,385},{3... | collective-permute-start | bytes 196616 | tf_op jit(solution)/shard_map/ppermute | solution.py:380
  105.6 27.0 %collective-permute-start.8 = (f32[128,128]{1,0:T(8,128)S(1)}, f32[128,128]{1,0:T(8,128)S(1)}, u32[]{:S(2)}, u32[]{:S(2)}) collective-permute-start(f32[128,128]{1,0:T(8,128)S(1)} %add.24), channel_id=1, source_target_pairs={{0,384},{128,0},{256,128},{384,256},{1,385},{129,1},{257,129},{385... | collective-permute-start | bytes 196616 | tf_op jit(solution)/shard_map/ppermute | solution.py:380
  128.2 46.8 %all-to-all-start.3 = ((f32[16,128,128]{2,1,0:T(8,128)}), f32[16,128,128]{2,1,0:T(8,128)}, u32[]{:S(2)}, u32[]{:S(2)}) async-start(f32[16,128,128]{2,1,0:T(8,128)} %add_bitcast_fusion), calls=%async_computation.3 | async-start | bytes 2097152 | tf_op jit(solution)/shard_map/all_to_all | solution.py:385
  132.6 11.1 %collective-permute-start.13 = (f32[128,128]{1,0:T(8,128)S(1)}, f32[128,128]{1,0:T(8,128)S(1)}, u32[]{:S(2)}, u32[]{:S(2)}) collective-permute-start(f32[128,128]{1,0:T(8,128)S(1)} %add_add_fusion.1), channel_id=1, source_target_pairs={{0,64},{32,96},{64,0},{96,32},{1,65},{33,97},{65,1},{97,33},{2,66}... | collective-permute-start | bytes 196616 | tf_op jit(solution)/shard_map/ppermute | solution.py:380
  137.2 10.9 %collective-permute-start.12 = (f32[128,128]{1,0:T(8,128)S(1)}, f32[128,128]{1,0:T(8,128)S(1)}, u32[]{:S(2)}, u32[]{:S(2)}) collective-permute-start(f32[128,128]{1,0:T(8,128)S(1)} %add_add_fusion.1), channel_id=1, source_target_pairs={{0,32},{32,64},{64,96},{96,0},{1,33},{33,65},{65,97},{97,1},{2,34}... | collective-permute-start | bytes 196616 | tf_op jit(solution)/shard_map/ppermute | solution.py:380
  139.4 10.4 %collective-permute-start.11 = (f32[128,128]{1,0:T(8,128)S(1)}, f32[128,128]{1,0:T(8,128)S(1)}, u32[]{:S(2)}, u32[]{:S(2)}) collective-permute-start(f32[128,128]{1,0:T(8,128)S(1)} %add_add_fusion.1), channel_id=1, source_target_pairs={{0,96},{32,0},{64,32},{96,64},{1,97},{33,1},{65,33},{97,65},{2,98}... | collective-permute-start | bytes 196616 | tf_op jit(solution)/shard_map/ppermute | solution.py:380
  149.8 5.6 %collective-permute-start.14 = (f32[128,128]{1,0:T(8,128)S(1)}, f32[128,128]{1,0:T(8,128)S(1)}, u32[]{:S(2)}, u32[]{:S(2)}) collective-permute-start(f32[128,128]{1,0:T(8,128)S(1)} %add_add_fusion.near), channel_id=1, source_target_pairs={{0,16},{16,0},{1,17},{17,1},{2,18},{18,2},{3,19},{19,3},{4,20},{20... | collective-permute-start | bytes 196616 | tf_op jit(solution)/shard_map/ppermute | solution.py:427
  172.1 2.9 %copy-start.3 = (f32[2,128,128]{2,1,0:T(8,128)}, f32[2,128,128]{2,1,0:T(8,128)S(1)}, u32[]{:S(2)}) copy-start(f32[2,128,128]{2,1,0:T(8,128)S(1)} %shard_map.72.inverse) | copy-start | bytes 393220
  172.1 1.8 copy-start.7
  222.1 42.5 %copy-start.4 = (f32[2,128,128]{2,1,0:T(8,128)S(1)}, f32[2,128,128]{2,1,0:T(8,128)}, u32[]{:S(2)}) copy-start(f32[2,128,128]{2,1,0:T(8,128)} %copy-done.3) | copy-start | bytes 393220
  222.1 42.5 %copy-start.9 = (f32[2,128,128]{2,1,0:T(8,128)S(1)}, f32[2,128,128]{2,1,0:T(8,128)}, u32[]{:S(2)}) copy-start(f32[2,128,128]{2,1,0:T(8,128)} %copy-done.8) | copy-start | bytes 393220
  222.1 20.5 %all-to-all-start.5 = ((bf16[16,240,128]{2,1,0:T(8,128)(2,1)}), bf16[16,240,128]{2,1,0:T(8,128)(2,1)S(1)}, u32[]{:S(2)}, u32[]{:S(2)}) async-start(bf16[16,240,128]{2,1,0:T(8,128)(2,1)} %shard_map.76), calls=%async_computation.5 | async-start | bytes 1966080 | tf_op jit(solution)/shard_map/all_to_all | solution.py:385
  228.4 19.2 %collective-permute-start.19 = (bf16[128,128]{1,0:T(8,128)(2,1)S(1)}, bf16[128,128]{1,0:T(8,128)(2,1)S(1)}, u32[]{:S(2)}, u32[]{:S(2)}) collective-permute-start(bf16[128,128]{1,0:T(8,128)(2,1)S(1)} %get-tuple-element.36), channel_id=1, source_target_pairs={{0,256},{128,384},{256,0},{384,128},{1,257},{129,385},{257,1},{385... | collective-permute-start | bytes 98312 | tf_op jit(solution)/shard_map/ppermute | solution.py:374
  233.2 14.4 %collective-permute-start.18 = (bf16[128,128]{1,0:T(8,128)(2,1)S(1)}, bf16[128,128]{1,0:T(8,128)(2,1)S(1)}, u32[]{:S(2)}, u32[]{:S(2)}) collective-permute-start(bf16[128,128]{1,0:T(8,128)(2,1)S(1)} %get-tuple-element.36), channel_id=1, source_target_pairs={{0,384},{128,0},{256,128},{384,256},{1,385},{129,1},{257,129},{385... | collective-permute-start | bytes 98312 | tf_op jit(solution)/shard_map/ppermute | solution.py:374
  236.0 11.7 %collective-permute-start.17 = (bf16[128,128]{1,0:T(8,128)(2,1)S(1)}, bf16[128,128]{1,0:T(8,128)(2,1)S(1)}, u32[]{:S(2)}, u32[]{:S(2)}) collective-permute-start(bf16[128,128]{1,0:T(8,128)(2,1)S(1)} %get-tuple-element.36), channel_id=1, source_target_pairs={{0,128},{128,256},{256,384},{384,0},{1,129},{129,257},{257,385},{3... | collective-permute-start | bytes 98312 | tf_op jit(solution)/shard_map/ppermute | solution.py:374
  242.5 25.3 %collective-permute-start.16 = (bf16[16,240,128]{2,1,0:T(8,128)(2,1)S(1)}, bf16[16,240,128]{2,1,0:T(8,128)(2,1)S(1)}, u32[]{:S(2)}, u32[]{:S(2)}) collective-permute-start(bf16[16,240,128]{2,1,0:T(8,128)(2,1)S(1)} %all-to-all-done.5.near), channel_id=1, source_target_pairs={{0,16},{16,0},{1,17},{17,1},{2,18},{18,2},{3,19},{19,3},{4,20},{20... | collective-permute-start | bytes 2949128 | tf_op jit(solution)/shard_map/ppermute | solution.py:466
  247.7 8.9 %collective-permute-start.21 = (bf16[4,128,128]{2,1,0:T(8,128)(2,1)S(1)}, bf16[4,128,128]{2,1,0:T(8,128)(2,1)S(1)}, u32[]{:S(2)}, u32[]{:S(2)}) collective-permute-start(bf16[4,128,128]{2,1,0:T(8,128)(2,1)S(1)} %get-tuple-element.44), channel_id=1, source_target_pairs={{0,96},{32,0},{64,32},{96,64},{1,97},{33,1},{65,33},{97,65},{2,98}... | collective-permute-start | bytes 393224 | tf_op jit(solution)/shard_map/ppermute | solution.py:374
  250.7 7.9 %collective-permute-start.20 = (bf16[4,128,128]{2,1,0:T(8,128)(2,1)S(1)}, bf16[4,128,128]{2,1,0:T(8,128)(2,1)S(1)}, u32[]{:S(2)}, u32[]{:S(2)}) collective-permute-start(bf16[4,128,128]{2,1,0:T(8,128)(2,1)S(1)} %get-tuple-element.44), channel_id=1, source_target_pairs={{0,32},{32,64},{64,96},{96,0},{1,33},{33,65},{65,97},{97,1},{2,34}... | collective-permute-start | bytes 393224 | tf_op jit(solution)/shard_map/ppermute | solution.py:374
  253.0 8.1 %collective-permute-start.22 = (bf16[4,128,128]{2,1,0:T(8,128)(2,1)S(1)}, bf16[4,128,128]{2,1,0:T(8,128)(2,1)S(1)}, u32[]{:S(2)}, u32[]{:S(2)}) collective-permute-start(bf16[4,128,128]{2,1,0:T(8,128)(2,1)S(1)} %get-tuple-element.44), channel_id=1, source_target_pairs={{0,64},{32,96},{64,0},{96,32},{1,65},{33,97},{65,1},{97,33},{2,66}... | collective-permute-start | bytes 393224 | tf_op jit(solution)/shard_map/ppermute | solution.py:374
  261.2 4.9 %collective-permute-start.23 = (bf16[16,128,128]{2,1,0:T(8,128)(2,1)S(1)}, bf16[16,128,128]{2,1,0:T(8,128)(2,1)S(1)}, u32[]{:S(2)}, u32[]{:S(2)}) collective-permute-start(bf16[16,128,128]{2,1,0:T(8,128)(2,1)S(1)} %bitcast.32), channel_id=1, source_target_pairs={{0,16},{16,0},{1,17},{17,1},{2,18},{18,2},{3,19},{19,3},{4,20},{20... | collective-permute-start | bytes 1572872 | tf_op jit(solution)/shard_map/ppermute | solution.py:376

commit v6 on v4

--- a/solution.py
+++ b/solution.py
@@ -54,7 +54,8 @@
     return lax.broadcasted_iota(jnp.int32, shape, dim)
 
 
-COUNT, WORK, SECOND, HELPER, WHERE, FREE, TABLE = 0, 17, 34, 51, 68, 80, 97
+COUNT, WORK, SECOND, HELPER, WHERE, FREE, SLOT, LIST, TABLE = 0, 17, 34, 51, 68, 80, 97, 114, 128
+SECONDS = EXPERTS // 2
 NONE = GROUPS
 
 
@@ -64,6 +65,9 @@
         table[WORK + g] = EXPERTS
         table[SECOND + g] = EXPERTS
         table[HELPER + g] = 0
+        table[SLOT + g] = 0
+    for j in range(TABLE - LIST):
+        table[LIST + j] = EXPERTS
     for e in range(EXPERTS):
         g = own[e]
         p = table[COUNT + g]
@@ -82,6 +86,8 @@
         table[WORK + jnp.where(second, h, NONE)] = e
         table[HELPER + jnp.where(second, g, NONE)] = h
         table[WHERE + e] = jnp.where(second, h, g)
+        table[SLOT + jnp.where(second, g, NONE)] = used
+        table[LIST + jnp.where(second, used, SECONDS)] = e
         used = used + jnp.where(second, 1, 0)
 
 
@@ -102,22 +108,23 @@
 
 
 def place_state(table, momentum, gradient, first, other):
+    def put(out, i, e):
+        @pl.when(e < EXPERTS)
+        def _():
+            total = momentum[e].astype(F32) + gradient[e].astype(F32)
+            out[i] = total.astype(BF16).reshape(192, 128)
+
+        @pl.when(e >= EXPERTS)
+        def _():
+            out[i] = jnp.zeros((192, 128), BF16)
+
     def slot(g, _):
-        for base, out in ((WORK, first), (SECOND, other)):
-            e = table[base + g]
-
-            @pl.when(e < EXPERTS)
-            def _():
-                total = momentum[e].astype(F32) + gradient[e].astype(F32)
-                out[g] = total.astype(BF16).reshape(192, 128)
-
-            @pl.when(e >= EXPERTS)
-            def _():
-                out[g] = jnp.zeros((192, 128), BF16)
-
+        put(first, g, table[WORK + g])
         return 0
 
     lax.fori_loop(0, GROUPS, slot, 0)
+    for j in range(SECONDS):
+        put(other, j, table[LIST + j])
 
 
 def offset(i):
@@ -148,7 +155,7 @@
         out[z] = dot(matrix[...], both).astype(BF16)
         return 0
 
-    lax.fori_loop(0, GROUPS, block, 0)
+    lax.fori_loop(0, GROUPS, block, 0, unroll=4)
 
 
 def split3(value):
@@ -159,29 +166,34 @@
     return high, middle, low
 
 
-def panel_of(state, right, kind, slot):
+def panel_of(block_of, right, kind, slot):
     def block(z, total):
-        a = state[z, kind * BLOCK : (kind + 1) * BLOCK, :]
         b = right[z, pl.ds(slot * 192 + kind * BLOCK, BLOCK), :]
-        return total + dot(a, b, ((0,), (0,)))
+        return total + dot(block_of(z), b, ((0,), (0,)))
 
     return lax.fori_loop(0, GROUPS, block, jnp.zeros((128, RANK), F32), unroll=4)
 
 
-def panels(place, state, right, panel, keep, send):
-    grams = []
+def panels(state, right, panel, gram):
     for k in range(2):
-        value = panel_of(state, right, k, 0)
+        rows = slice(k * BLOCK, (k + 1) * BLOCK)
+        value = panel_of(lambda z: state[z, rows, :], right, k, 0)
         panel[k] = value
-        grams.append(dot(value, value, ((0,), (0,)), HIGHEST))
-    mine = place[2] == 0
-    keep[...] = jnp.where(mine, grams[0], grams[1])
-    send[...] = jnp.where(mine, grams[1], grams[0])
-
-
-def second_panels(state, right, panel):
+        gram[k] = dot(value, value, ((0,), (0,)), HIGHEST)
+
+
+def unit():
+    return (iota((128, 128), 0) == iota((128, 128), 1)).astype(BF16)
+
+
+def second_panels(table, place, state, right, panel, turned):
+    some = table[SECOND + place[3]] < EXPERTS
+    eye = jnp.where(some, unit(), jnp.zeros((128, 128), BF16))
     for k in range(2):
-        panel[k] = panel_of(state, right, k, 1)
+        rows = slice(k * BLOCK, (k + 1) * BLOCK)
+        panel[k] = panel_of(lambda z: state[z, 0, rows, :], right, k, 1)
+        whole = state[:, 0, rows, :].reshape(HID, 128)
+        turned[k] = dot(eye, whole, ((1,), (1,))).astype(BF16)
 
 
 def weigh(place, state, panel, keep, send, rows):
@@ -194,25 +206,20 @@
             total = value[:, :128] + (value[:, 128:256] + value[:, 256:])
             rows[k * BLOCK : (k + 1) * BLOCK, :] = total
         for i in range(16):
-            x = (place[0] + offset(i & 3)) & 3
-            y = (place[1] + offset(i >> 2)) & 3
-            base = (x * 4 + y) * 16
-            near = pl.multiple_of(base + 8 * place[2], 8)
-            far = pl.multiple_of(base + 8 - 8 * place[2], 8)
+            near = pl.multiple_of(16 * i + 8 * place[2], 8)
+            far = pl.multiple_of(16 * i + 8 - 8 * place[2], 8)
             keep[i, z] = rows[pl.ds(near, 8), :]
             send[i, z] = rows[pl.ds(far, 8), :]
         return 0
 
-    lax.fori_loop(0, GROUPS, block, 0, unroll=2)
-
-
-def invert(place, near, far, out, work, *, size):
+    lax.fori_loop(0, GROUPS, block, 0, unroll=4)
+
+
+def invert(gram, out, work, *, size):
     n = RANK
     eye = (iota((n, n), 0) == iota((n, n), 1)).astype(F32)
-    mine = place[2] == 0
-    first, other = near[...], far[...]
-    work[0, :, :n] = jnp.where(mine, first, other) + ridge_term * eye
-    work[1, :, :n] = jnp.where(mine, other, first) + ridge_term * eye
+    for m in range(2):
+        work[m, :, :n] = gram[m] + ridge_term * eye
     for m in range(2):
         work[m, :, n:] = eye
     row = iota((size, 2 * n), 0)
@@ -235,9 +242,11 @@
                 work[m, k + size :, :] -= change[k + size :, :]
 
 
-def scale_factor(place, inverse, a, b, c, d, _, out):
+def scale_factor(place, inverse, parts, out):
     f = place[0] * 8 + place[1] * 2 + place[2]
-    total = ((a[...] + b[...]) + (c[...] + d[...])).reshape(128, RANK)
+    total = parts[0]
+    for i in range(1, 16):
+        total = total + parts[i]
     kind = jnp.where(f >= 12, 1, 0)
     out[:128] = dot(total, inverse[kind], ((1,), (1,)), HIGHEST).astype(BF16)
     half = jnp.where(f >= 16, 1, 0)
@@ -256,20 +265,18 @@
         low[k] = (ortho * (-feedback)).astype(BF16)
 
 
-def turn(table, place, first, second, out):
+def turn(table, place, state, out):
     owned = table[COUNT + place[3]] > 0
-    eye = (iota((128, 128), 0) == iota((128, 128), 1)).astype(BF16)
-    some = jnp.where(owned, eye, jnp.zeros_like(eye))
-    for s, (state, unit) in enumerate(((first, some), (second, eye))):
-        for k in range(2):
-            rows = state[:, k * BLOCK : (k + 1) * BLOCK, :].reshape(HID, 128)
-            out[2 * s + k] = dot(unit, rows, ((1,), (1,))).astype(BF16)
+    eye = jnp.where(owned, unit(), jnp.zeros((128, 128), BF16))
+    for k in range(2):
+        rows = state[:, k * BLOCK : (k + 1) * BLOCK, :].reshape(HID, 128)
+        out[k] = dot(eye, rows, ((1,), (1,))).astype(BF16)
 
 
 ROWS = 368
 
 
-def select(table, place, mine, tiles, out, packed):
+def select(table, place, mine, tiles, _, out, packed):
     z = place[3]
     packed[:128, :] = mine[:128, :]
     packed[128:272, :] = tiles[table[HELPER + z]]
@@ -313,7 +320,9 @@
                 out[e, k] = value[i * BLOCK : (i + 1) * BLOCK, :] * scales[k][e : e + 1, :]
 
 
-def finish_state(table, place, turned, near, far, low, panel, left, out, left_out, inverse, wide):
+def finish_state(
+    table, place, turned, second, near, far, low, panel, left, out, left_out, inverse, wide
+):
     c = place[2]
     matrix = jnp.concatenate(
         [join_matrix(place, c, False, 12), join_matrix(place, 1 - c, False, 12)], axis=1
@@ -331,7 +340,7 @@
         left_out[k] = left[k]
         left_out[2 + k] = ortho * math.sqrt(D)
         lows.append((ortho * (-feedback)).astype(BF16))
-    for s in range(2):
+    for s, state in enumerate((turned, second)):
         for g in range(8):
             rows = slice(s * 128 + g * 16, s * 128 + g * 16 + 16)
             data = jnp.concatenate(
@@ -344,9 +353,9 @@
                     i = 2 * p + k
                     first = (2 * g + p) * BLOCK
                     wide[2 * s + k, first : first + BLOCK, :] = value[i * BLOCK : (i + 1) * BLOCK]
-    for i in range(4):
-        change = dot(lows[i], wide[i], ((1,), (1,)))
-        out[i] = (turned[i].astype(F32) + change).astype(BF16)
+        for k in range(2):
+            change = dot(lows[2 * s + k], wide[2 * s + k], ((1,), (1,)))
+            out[2 * s + k] = (state[k].astype(F32) + change).astype(BF16)
 
 
 def ring(shift):
@@ -361,11 +370,6 @@
         x = jnp.stack([x] + [lax.ppermute(x, axis, ring((4 - d) % 4)) for d in SHIFTS])
     x = x.reshape((16,) + x.shape[2:])
     return x, lax.ppermute(x, "c", SWAP)
-
-
-def spread_sum(x, axis):
-    parts = [lax.ppermute(x, axis, ring(d)) for d in SHIFTS]
-    return (x + parts[0]) + (parts[1] + parts[2])
 
 
 def exchange(x, axis):
@@ -384,10 +388,11 @@
         scratch_shapes=[pltpu.VMEM((EXPERTS + 1, 8, RANK), F32)],
     )(owners, place, right_in)
     slices = exchange(slices, "z")
-    block = sds((16, 192, 128), BF16)
-    sent, late = call(place_state, (block, block), specs=[SMEM, VMEM, VMEM])(
-        table, jnp.swapaxes(momentum, 2, 3), jnp.swapaxes(gradient, 2, 3)
-    )
+    sent, late = call(
+        place_state,
+        (sds((16, 192, 128), BF16), sds((SECONDS, 192, 128), BF16)),
+        specs=[SMEM, VMEM, VMEM],
+    )(table, jnp.swapaxes(momentum, 2, 3), jnp.swapaxes(gradient, 2, 3))
     sent, slices = barrier((sent, slices))
     state = exchange(sent, "z")
     near, far = gather_slices(slices)
@@ -398,50 +403,62 @@
         flops=800_000_000,
         specs=[SMEM, VMEM, VMEM],
     )(place, near, far)
-    square = sds((RANK, RANK), F32)
+    late, state = barrier((late, state))
+    seconds = lax.all_gather(late, "z")
+    square = sds((2, RANK, RANK), F32)
     two = sds((2, 128, RANK), F32)
-    panel, keep, send = call(
-        panels, (two, square, square), specs=[SMEM, VMEM, VMEM], flops=300_000_000
-    )(place, state, right)
-    late, send = barrier((late, send))
-    second = exchange(late, "z")
-    gram = keep + lax.ppermute(send, "c", SWAP)
+    panel, gram = call(panels, (two, square), n_in=2, flops=300_000_000)(state, right)
+    gram = exchange(gram.reshape(32, 8, RANK), FSDP)
     half = sds((16, 16, 8, RANK), F32)
     keep, send = call(
         weigh, (half, half), [pltpu.VMEM((256, RANK), F32)], specs=[SMEM, VMEM, VMEM], flops=400_000_000
     )(place, state, panel)
     parts = keep + lax.ppermute(send, "c", SWAP)
-    parts, gram = barrier((parts, spread_sum(gram, "x")))
-    parts = parts.reshape(4, 4, 16, 8, RANK)
-    moved = [lax.ppermute(parts[:, i + 1], "x", ring(SHIFTS[i])) for i in range(3)]
-    parts = (parts[:, 0] + moved[0]) + (moved[1] + moved[2])
-    parts, gram = barrier((parts, spread_sum(gram, "y")))
-    other = lax.ppermute(gram, "c", SWAP)
-    parts = [parts[0]] + [lax.ppermute(parts[i + 1], "y", ring(SHIFTS[i])) for i in range(3)]
+    gram = jnp.broadcast_to(jnp.sum(gram, axis=0)[None], gram.shape)
+    gram = exchange(gram, FSDP).reshape(2, RANK, RANK)
+    parts, gram = barrier((parts, gram))
+    parts = exchange(parts.reshape(16, 128, RANK), XY)
     inverse = call(
         functools.partial(invert, size=8),
-        sds((2, RANK, RANK), F32),
+        square,
         [pltpu.VMEM((2, RANK, 2 * RANK), F32)],
-        specs=[SMEM, VMEM, VMEM],
+        n_in=1,
         flops=4_000_000_000,
-    )(place, gram, other)
-    mine = call(
-        scale_factor, sds((144, RANK), BF16), specs=[SMEM] + [VMEM] * 5 + [ANY], flops=100_000_000
-    )(place, inverse, *parts, second)
+    )(gram)
+    mine = call(scale_factor, sds((144, RANK), BF16), specs=[SMEM, VMEM, VMEM], flops=100_000_000)(
+        place, inverse, parts
+    )
+    turned = call(turn, sds((2, 128, HID), BF16), specs=[SMEM, SMEM, VMEM], flops=100_000_000)(
+        table, place, state
+    )
     left, low = call(
         orthonormal, (two, sds((2, 128, RANK), BF16)), specs=[SMEM, SMEM, VMEM, VMEM], flops=100_000_000
     )(table, place, panel, inverse)
     tiles = lax.all_gather(mine, "z")
-    second_panel = call(second_panels, two, n_in=2, flops=200_000_000)(second, right)
-    turned = call(
-        turn, sds((4, 128, HID), BF16), specs=[SMEM, SMEM, VMEM, VMEM], flops=200_000_000
-    )(table, place, state, second)
+    second_panel, second_turned = pl.pallas_call(
+        second_panels,
+        grid_spec=pltpu.PrefetchScalarGridSpec(
+            num_scalar_prefetch=2,
+            grid=(1,),
+            in_specs=[
+                pl.BlockSpec((16, 1, 192, 128), lambda i, t, p: (0, t[SLOT + p[3]], 0, 0)),
+                pl.BlockSpec((16, 384, RANK), lambda i, t, p: (0, 0, 0)),
+            ],
+            out_specs=[
+                pl.BlockSpec((2, 128, RANK), lambda i, t, p: (0, 0, 0)),
+                pl.BlockSpec((2, 128, HID), lambda i, t, p: (0, 0, 0)),
+            ],
+        ),
+        out_shape=[two, sds((2, 128, HID), BF16)],
+        compiler_params=pltpu.CompilerParams(vmem_limit_bytes=24 * 1024 * 1024),
+        cost_estimate=pl.CostEstimate(flops=300_000_000, bytes_accessed=3_000_000, transcendentals=0),
+    )(table, place, seconds, right)
     chosen = call(
         select,
         sds((16, ROWS, RANK), BF16),
         [pltpu.VMEM((ROWS, RANK), BF16)],
-        specs=[SMEM, SMEM, VMEM, VMEM],
-    )(table, place, mine, tiles)
+        specs=[SMEM, SMEM, VMEM, VMEM, ANY],
+    )(table, place, mine, tiles, seconds)
     near = exchange(chosen, XY)
     far = lax.ppermute(near, "c", SWAP)
     right_out = call(
@@ -451,9 +468,9 @@
         finish_state,
         (sds((4, 128, HID), BF16), sds((4, 128, RANK), F32)),
         [pltpu.VMEM((2 * RANK, RANK), F32), pltpu.VMEM((4, HID, RANK), BF16)],
-        specs=[SMEM, SMEM] + [VMEM] * 6,
+        specs=[SMEM, SMEM] + [VMEM] * 7,
         flops=1_200_000_000,
-    )(table, place, turned, near, far, low, second_panel, left)
+    )(table, place, turned, second_turned, near, far, low, second_panel, left)
     return (
         state_out.reshape(CAP, 2, 128, HID),
         left_out.reshape(CAP, 2, 128, RANK),

time: 239 us -> 257 us (1.075)
  blocking collectives: 45.3 us -> 96.8 us
  starting transfers between devices: 116 us -> 68 us
  between operations: 1.14 us -> 14.3 us
  waiting for transfers between devices: 28.8 us -> 25.2 us
  local copies, waits for them, and re-layouts: 3.6 us -> 7.1 us
  other arithmetic: 1.06 us -> 4.04 us
    all_to_all x1 -> x3, blocking collectives: 18.9 us -> 71.7 us  [exchange(): return lax.all_to_all(x, axis, split_axis=0, concat_axis=0, tiled=True)]
    ppermute x14 -> x0, starting transfers between devices: 43.4 us -> none  [the longest x6 17.9 us: spread_sum(): parts = [lax.ppermute(x, axis, ring(d)) for d in SHIFTS]]
    all_to_all x3, starting transfers between devices: 32.8 us -> 23.3 us  [exchange(): return lax.all_to_all(x, axis, split_axis=0, concat_axis=0, tiled=True)]
    ppermute x14 -> x0, waiting for transfers between devices: 8.85 us -> none  [the longest x3 5.73 us: shards(): lax.ppermute(parts[:, i + 1], 'x', ring(SHIFTS[i]))]
    all_to_all x3, waiting for transfers between devices: 5.89 us -> 12.5 us  [exchange(): return lax.all_to_all(x, axis, split_axis=0, concat_axis=0, tiled=True)]
    ppermute x1, starting transfers between devices: 6.04 us -> 11 us  [gather_slices(): return (x, lax.ppermute(x, 'c', SWAP))]
    unnamed x16 -> x24, local copies, waits for them, and re-layouts: 3.53 us -> 6.44 us
  transfers between devices with their start and end apart: 26 -> 13, of which waited for: 8 -> 5; matrix products, arithmetic and copies ran while one was open for 0% -> 2% of each run, Pallas kernels for 13% -> 12%
where the time goes in v6:
time: 257 us; the launch traced here: 256 us
  blocking collectives  96.8 us (38%)
  starting transfers between devices  68 us (26%)
  Pallas kernels  40.3 us (16%)
  waiting for transfers between devices  25.2 us (10%)
  between operations  14.3 us (6%)
  local copies, waits for them, and re-layouts  7.1 us (3%)
  other arithmetic  4.04 us (2%)
    all_to_all x3, blocking collectives, exchange(): return lax.all_to_all(x, axis, split_axis=0, concat_axis=0, tiled=True)  71.7 us
    all_gather x1, blocking collectives, shards(): tiles = lax.all_gather(mine, 'z')  25.1 us
    all_to_all x3, starting transfers between devices, exchange(): return lax.all_to_all(x, axis, split_axis=0, concat_axis=0, tiled=True)  23.3 us
    ppermute x6, starting transfers between devices, gather_slices(): lax.ppermute(x, axis, ring((4 - d) % 4))  20 us
    pallas_call x1, Pallas kernels, shards(): call(functools.partial(invert, size=8), square, [pltpu.VMEM((2, RANK, 2 *...  16.1 us
    all_to_all x3, waiting for transfers between devices, exchange(): return lax.all_to_all(x, axis, split_axis=0, concat_axis=0, tiled=True)  12.5 us
    ppermute x1, starting transfers between devices, shards(): far = lax.ppermute(near, 'c', SWAP)  11.3 us
    ppermute x1, starting transfers between devices, gather_slices(): return (x, lax.ppermute(x, 'c', SWAP))  11 us
  transfers between devices with their start and end apart: 13, of which 5 were waited for; matrix products, arithmetic and copies ran while one was open for 2% of the time, Pallas kernels for 12%

profile of v6, /device:TPU:1, one launch (start us, length us, event | category | flops | bytes accessed | tf_op | source)
XLA Modules:
  0.0 255.8 jit_solution(11597606355893987227)
XLA Ops:
  7.2 0.6 pad_add_fusion.place
  7.8 2.1 shard_map.67
  9.9 15.8 %all-to-all-start = ((bf16[16,16,128]{2,1,0:T(8,128)(2,1)}), bf16[16,16,128]{2,1,0:T(8,128)(2,1)S(1)}, u32[]{:S(2)}, u32[]{:S(2)}) async-start(bf16[16,16,128]{2,1,0:T(8,128)(2,1)} %get-tuple-element.26), calls=%async_computation | async-start | bytes 131072 | tf_op jit(solution)/shard_map/all_to_all | solution.py:376
  25.7 0.0 all-gather.4.cloned.1.call-start
  25.7 0.0 copy-start.2
  25.7 1.0 copy-done.2
  26.8 1.0 copy-done.3
  27.8 0.7 copy-done.8
  28.4 1.8 shard_map.68
  30.2 7.0 %all-to-all-done = bf16[16,16,128]{2,1,0:T(8,128)(2,1)S(1)} async-done(((bf16[16,16,128]{2,1,0:T(8,128)(2,1)}), bf16[16,16,128]{2,1,0:T(8,128)(2,1)S(1)}, u32[]{:S(2)}, u32[]{:S(2)}) %all-to-all-start) | async-done | bytes 65568 | tf_op jit(solution)/shard_map/all_to_all | solution.py:376
  37.2 39.3 %all_to_all.30.state = bf16[16,192,128]{2,1,0:T(8,128)(2,1)S(1)} all-to-all(bf16[16,192,128]{2,1,0:T(8,128)(2,1)S(1)} %get-tuple-element.27), channel_id=1, replica_groups=mesh['x'=4,'y'=4,'c'=2,'z'=16] {'z'}, dimensions={0} | all-to-all | bytes 1572864 | tf_op jit(solution)/shard_map/all_to_all | solution.py:376
  76.6 0.0 all-gather.4.cloned.1.call-update
  76.6 4.7 %collective-permute-start.2 = (bf16[16,16,128]{2,1,0:T(8,128)(2,1)S(1)}, bf16[16,16,128]{2,1,0:T(8,128)(2,1)S(1)}, u32[]{:S(2)}, u32[]{:S(2)}) collective-permute-start(bf16[16,16,128]{2,1,0:T(8,128)(2,1)S(1)} %all-to-all-done), channel_id=1, source_target_pairs={{0,256},{128,384},{256,0},{384,128},{1,257},{129,385},{257,1},{385... | collective-permute-start | bytes 196616 | tf_op jit(solution)/shard_map/ppermute | solution.py:370
  81.3 2.8 %collective-permute-start.1 = (bf16[16,16,128]{2,1,0:T(8,128)(2,1)S(1)}, bf16[16,16,128]{2,1,0:T(8,128)(2,1)S(1)}, u32[]{:S(2)}, u32[]{:S(2)}) collective-permute-start(bf16[16,16,128]{2,1,0:T(8,128)(2,1)S(1)} %all-to-all-done), channel_id=1, source_target_pairs={{0,384},{128,0},{256,128},{384,256},{1,385},{129,1},{257,129},{385... | collective-permute-start | bytes 196616 | tf_op jit(solution)/shard_map/ppermute | solution.py:370
  84.0 2.5 collective-permute-start
  86.6 4.4 %collective-permute-done = bf16[16,16,128]{2,1,0:T(8,128)(2,1)S(1)} collective-permute-done((bf16[16,16,128]{2,1,0:T(8,128)(2,1)S(1)}, bf16[16,16,128]{2,1,0:T(8,128)(2,1)S(1)}, u32[]{:S(2)}, u32[]{:S(2)}) %collective-permute-start) | collective-permute-done | bytes 65568 | tf_op jit(solution)/shard_map/ppermute | solution.py:370
  91.0 4.6 %collective-permute-start.4 = (bf16[4,16,16,128]{3,2,1,0:T(8,128)(2,1)S(1)}, bf16[4,16,16,128]{3,2,1,0:T(8,128)(2,1)S(1)}, u32[]{:S(2)}, u32[]{:S(2)}) collective-permute-start(bf16[4,16,16,128]{3,2,1,0:T(8,128)(2,1)S(1)} %get-tuple-element.44), channel_id=1, source_target_pairs={{0,96},{32,0},{64,32},{96,64},{1,97},{33,1},{65,33},{97,65},{2,98}... | collective-permute-start | bytes 786440 | tf_op jit(solution)/shard_map/ppermute | solution.py:370
  95.7 1.9 collective-permute-start.3
  97.6 3.5 %collective-permute-start.5 = (bf16[4,16,16,128]{3,2,1,0:T(8,128)(2,1)S(1)}, bf16[4,16,16,128]{3,2,1,0:T(8,128)(2,1)S(1)}, u32[]{:S(2)}, u32[]{:S(2)}) collective-permute-start(bf16[4,16,16,128]{3,2,1,0:T(8,128)(2,1)S(1)} %get-tuple-element.44), channel_id=1, source_target_pairs={{0,64},{32,96},{64,0},{96,32},{1,65},{33,97},{65,1},{97,33},{2,66}... | collective-permute-start | bytes 786440 | tf_op jit(solution)/shard_map/ppermute | solution.py:370
  101.2 6.0 %collective-permute-done.3 = bf16[4,16,16,128]{3,2,1,0:T(8,128)(2,1)S(1)} collective-permute-done((bf16[4,16,16,128]{3,2,1,0:T(8,128)(2,1)S(1)}, bf16[4,16,16,128]{3,2,1,0:T(8,128)(2,1)S(1)}, u32[]{:S(2)}, u32[]{:S(2)}) %collective-permute-start.3) | collective-permute-done | bytes 262176 | tf_op jit(solution)/shard_map/ppermute | solution.py:370
  107.2 0.1 pad_maximum_fusion
  107.3 11.0 %collective-permute-start.6 = (bf16[16,16,16,128]{3,2,1,0:T(8,128)(2,1)S(1)}, bf16[16,16,16,128]{3,2,1,0:T(8,128)(2,1)S(1)}, u32[]{:S(2)}, u32[]{:S(2)}) collective-permute-start(bf16[16,16,16,128]{3,2,1,0:T(8,128)(2,1)S(1)} %bitcast.25), channel_id=1, source_target_pairs={{0,16},{16,0},{1,17},{17,1},{2,18},{18,2},{3,19},{19,3},{4,20},{20... | collective-permute-start | bytes 3145736 | tf_op jit(solution)/shard_map/ppermute | solution.py:372
  118.4 2.3 collective-permute-done.6.far
  120.6 2.9 %shard_map.70.right = bf16[16,384,128]{2,1,0:T(8,128)(2,1)S(1)} custom-call(s32[4]{0:T(128)S(1)} %copy-done.7, bf16[16,16,16,128]{3,2,1,0:T(8,128)(2,1)S(1)} %bitcast.26, bf16[16,16,16,128]{3,2,1,0:T(8,128)(2,1)S(1)} %collective-permute-done.6.far), custom_call_target="tpu_custom_call" | custom-call | flops 800000000 | bytes 4000000 | tf_op jit(solution)/shard_map/pallas_call | solution.py:399
  123.6 2.2 shard_map.72
  125.8 2.9 %shard_map.73 = (f32[16,16,8,128]{3,2,1,0:T(8,128)S(1)}, f32[16,16,8,128]{3,2,1,0:T(8,128)}) custom-call(s32[4]{0:T(128)S(1)} %copy-done.7, bf16[16,192,128]{2,1,0:T(8,128)(2,1)S(1)} %all_to_all.30.state, f32[2,128,128]{2,1,0:T(8,128)S(1)} %get-tuple-element.32.panel), custom_call_target="tpu_custom_call" | custom-call | flops 400000000 | bytes 4000000 | tf_op jit(solution)/shard_map/pallas_call | solution.py:413
  128.7 2.3 collective-permute-start.7
  131.0 11.8 %all_to_all.31 = f32[32,8,128]{2,1,0:T(8,128)} all-to-all(f32[32,8,128]{2,1,0:T(8,128)S(1)} %bitcast.31), channel_id=1, replica_groups=mesh['x'=4,'y'=4,'c'=2,'z'=16] {'x','y','c'}, dimensions={0} | all-to-all | bytes 262144 | tf_op jit(solution)/shard_map/all_to_all | solution.py:376
  142.9 0.9 reduce_sum.9
  143.8 0.7 broadcast_in_dim.2
  144.5 3.9 %all-to-all-start.3 = ((f32[32,8,128]{2,1,0:T(8,128)}), f32[32,8,128]{2,1,0:T(8,128)S(1)}, u32[]{:S(2)}, u32[]{:S(2)}) async-start(f32[32,8,128]{2,1,0:T(8,128)} %broadcast_in_dim.2), calls=%async_computation.3 | async-start | bytes 262144 | tf_op jit(solution)/shard_map/all_to_all | solution.py:376
  148.4 2.3 add.3
  150.7 5.5 %all-to-all-done.3 = f32[32,8,128]{2,1,0:T(8,128)S(1)} async-done(((f32[32,8,128]{2,1,0:T(8,128)}), f32[32,8,128]{2,1,0:T(8,128)S(1)}, u32[]{:S(2)}, u32[]{:S(2)}) %all-to-all-start.3) | async-done | bytes 131104 | tf_op jit(solution)/shard_map/all_to_all | solution.py:376
  156.2 3.7 %all-to-all-start.4 = ((f32[16,128,128]{2,1,0:T(8,128)}), f32[16,128,128]{2,1,0:T(8,128)S(1)}, u32[]{:S(2)}, u32[]{:S(2)}) async-start(f32[16,128,128]{2,1,0:T(8,128)} %bitcast.32), calls=%async_computation.4 | async-start | bytes 2097152 | tf_op jit(solution)/shard_map/all_to_all | solution.py:376
  159.9 16.1 %shard_map.74.inverse = f32[2,128,128]{2,1,0:T(8,128)S(1)} custom-call(f32[2,128,128]{2,1,0:T(8,128)S(1)} %bitcast.30), custom_call_target="tpu_custom_call" | custom-call | flops 4000000000 | bytes 4000000 | tf_op jit(solution)/shard_map/pallas_call | solution.py:421
  175.9 0.7 copy-done.4
  176.6 0.9 copy-done.5
  177.5 0.8 shard_map.75.mine
  178.3 25.1 %all-gather.1 = bf16[2304,128]{1,0:T(8,128)(2,1)S(1)} all-gather(bf16[144,128]{1,0:T(8,128)(2,1)S(1)} %shard_map.75.mine), channel_id=3, replica_groups=mesh['x'=4,'y'=4,'c'=2,'z'=16] {'z'}, dimensions={0}, use_global_device_ids=true | all-gather | bytes 626688 | tf_op jit(solution)/shard_map/all_gather | solution.py:437
  203.4 2.1 copy-done
  205.5 0.8 shard_map.76
  206.3 20.5 %all_to_all.32.near = bf16[16,368,128]{2,1,0:T(8,128)(2,1)S(1)} all-to-all(bf16[16,368,128]{2,1,0:T(8,128)(2,1)S(1)} %shard_map.76), channel_id=1, replica_groups=mesh['x'=4,'y'=4,'c'=2,'z'=16] {'x','y'}, dimensions={0} | all-to-all | bytes 3014656 | tf_op jit(solution)/shard_map/all_to_all | solution.py:376
  226.9 11.3 %collective-permute-start.8 = (bf16[16,368,128]{2,1,0:T(8,128)(2,1)S(1)}, bf16[16,368,128]{2,1,0:T(8,128)(2,1)S(1)}, u32[]{:S(2)}, u32[]{:S(2)}) collective-permute-start(bf16[16,368,128]{2,1,0:T(8,128)(2,1)S(1)} %all_to_all.32.near), channel_id=1, source_target_pairs={{0,16},{16,0},{1,17},{17,1},{2,18},{18,2},{3,19},{19,3},{4,20},{20... | collective-permute-start | bytes 4521992 | tf_op jit(solution)/shard_map/ppermute | solution.py:463
  238.2 0.9 shard_map.69.turned
  239.1 0.9 shard_map.77
  240.1 2.9 %shard_map.71 = (f32[2,128,128]{2,1,0:T(8,128)S(1)}, bf16[2,128,1536]{2,1,0:T(8,128)(2,1)S(1)}) custom-call(s32[128]{0:T(128)S(1)} %copy-done.9, s32[4]{0:T(128)S(1)} %copy-done.7, bf16[16,5,192,128]{3,2,1,0:T(8,128)(2,1)S(1)} %bitcast.24, bf16[16,384,128]{2,1,0:T(8,128)(2,1)S(1)} %shard_map.70.right), custom_call_target="tpu_custom_call" | custom-call | flops 300000000 | bytes 3000000 | tf_op jit(solution)/shard_map/pallas_call | solution.py:438
  243.0 2.1 shard_map.79
  245.1 3.9 %shard_map.78 = (bf16[4,128,1536]{2,1,0:T(8,128)(2,1)}, f32[4,128,128]{2,1,0:T(8,128)}) custom-call(s32[128]{0:T(128)S(1)} %copy-done.9, s32[4]{0:T(128)S(1)} %copy-done.7, bf16[2,128,1536]{2,1,0:T(8,128)(2,1)S(1)} %shard_map.69.turned, bf16[2,128,1536]{2,1,0:T(8,128)(2,1)S(1)} %get-tuple-element.31.second, bf16[16,368,128]{2,1,0:T(8,128)(2,1)S(1)} %all_to_all.32.near, ...), custom_call_target="tpu_custom_call" | custom-call | flops 1200000000 | bytes 4000000 | tf_op jit(solution)/shard_map/pallas_call | solution.py:467
  (26 shorter events, 0.1 us)
Async XLA Ops:
  9.9 27.3 %all-to-all-start = ((bf16[16,16,128]{2,1,0:T(8,128)(2,1)}), bf16[16,16,128]{2,1,0:T(8,128)(2,1)S(1)}, u32[]{:S(2)}, u32[]{:S(2)}) async-start(bf16[16,16,128]{2,1,0:T(8,128)(2,1)} %get-tuple-element.26), calls=%async_computation | async-start | bytes 131072 | tf_op jit(solution)/shard_map/all_to_all | solution.py:376
  25.7 177.7 %all-gather.4.cloned.1.call-start = ((), (), s32[]{:S(2)}) async-start(), calls=%async_computation.6 | async-start | bytes 4177920 | tf_op jit(solution)/shard_map/all_gather | solution.py:407
  25.7 1.0 copy-start.2
  26.8 1.0 copy-start.3
  27.8 0.7 copy-start.8
  76.6 44.1 %copy-start.7 = (s32[4]{0:T(128)S(1)}, s32[4]{0:T(128)}, u32[]{:S(2)}) copy-start(s32[4]{0:T(128)} %pad_add_fusion.place) | copy-start | bytes 52
  76.6 10.0 %collective-permute-start.2 = (bf16[16,16,128]{2,1,0:T(8,128)(2,1)S(1)}, bf16[16,16,128]{2,1,0:T(8,128)(2,1)S(1)}, u32[]{:S(2)}, u32[]{:S(2)}) collective-permute-start(bf16[16,16,128]{2,1,0:T(8,128)(2,1)S(1)} %all-to-all-done), channel_id=1, source_target_pairs={{0,256},{128,384},{256,0},{384,128},{1,257},{129,385},{257,1},{385... | collective-permute-start | bytes 196616 | tf_op jit(solution)/shard_map/ppermute | solution.py:370
  81.3 5.3 %collective-permute-start.1 = (bf16[16,16,128]{2,1,0:T(8,128)(2,1)S(1)}, bf16[16,16,128]{2,1,0:T(8,128)(2,1)S(1)}, u32[]{:S(2)}, u32[]{:S(2)}) collective-permute-start(bf16[16,16,128]{2,1,0:T(8,128)(2,1)S(1)} %all-to-all-done), channel_id=1, source_target_pairs={{0,384},{128,0},{256,128},{384,256},{1,385},{129,1},{257,129},{385... | collective-permute-start | bytes 196616 | tf_op jit(solution)/shard_map/ppermute | solution.py:370
  84.0 6.9 %collective-permute-start = (bf16[16,16,128]{2,1,0:T(8,128)(2,1)S(1)}, bf16[16,16,128]{2,1,0:T(8,128)(2,1)S(1)}, u32[]{:S(2)}, u32[]{:S(2)}) collective-permute-start(bf16[16,16,128]{2,1,0:T(8,128)(2,1)S(1)} %all-to-all-done), channel_id=1, source_target_pairs={{0,128},{128,256},{256,384},{384,0},{1,129},{129,257},{257,385},{3... | collective-permute-start | bytes 196616 | tf_op jit(solution)/shard_map/ppermute | solution.py:370
  91.0 10.1 %collective-permute-start.4 = (bf16[4,16,16,128]{3,2,1,0:T(8,128)(2,1)S(1)}, bf16[4,16,16,128]{3,2,1,0:T(8,128)(2,1)S(1)}, u32[]{:S(2)}, u32[]{:S(2)}) collective-permute-start(bf16[4,16,16,128]{3,2,1,0:T(8,128)(2,1)S(1)} %get-tuple-element.44), channel_id=1, source_target_pairs={{0,96},{32,0},{64,32},{96,64},{1,97},{33,1},{65,33},{97,65},{2,98}... | collective-permute-start | bytes 786440 | tf_op jit(solution)/shard_map/ppermute | solution.py:370
  95.7 11.5 %collective-permute-start.3 = (bf16[4,16,16,128]{3,2,1,0:T(8,128)(2,1)S(1)}, bf16[4,16,16,128]{3,2,1,0:T(8,128)(2,1)S(1)}, u32[]{:S(2)}, u32[]{:S(2)}) collective-permute-start(bf16[4,16,16,128]{3,2,1,0:T(8,128)(2,1)S(1)} %get-tuple-element.44), channel_id=1, source_target_pairs={{0,32},{32,64},{64,96},{96,0},{1,33},{33,65},{65,97},{97,1},{2,34}... | collective-permute-start | bytes 786440 | tf_op jit(solution)/shard_map/ppermute | solution.py:370
  97.6 9.6 %collective-permute-start.5 = (bf16[4,16,16,128]{3,2,1,0:T(8,128)(2,1)S(1)}, bf16[4,16,16,128]{3,2,1,0:T(8,128)(2,1)S(1)}, u32[]{:S(2)}, u32[]{:S(2)}) collective-permute-start(bf16[4,16,16,128]{3,2,1,0:T(8,128)(2,1)S(1)} %get-tuple-element.44), channel_id=1, source_target_pairs={{0,64},{32,96},{64,0},{96,32},{1,65},{33,97},{65,1},{97,33},{2,66}... | collective-permute-start | bytes 786440 | tf_op jit(solution)/shard_map/ppermute | solution.py:370
  107.3 13.3 %collective-permute-start.6 = (bf16[16,16,16,128]{3,2,1,0:T(8,128)(2,1)S(1)}, bf16[16,16,16,128]{3,2,1,0:T(8,128)(2,1)S(1)}, u32[]{:S(2)}, u32[]{:S(2)}) collective-permute-start(bf16[16,16,16,128]{3,2,1,0:T(8,128)(2,1)S(1)} %bitcast.25), channel_id=1, source_target_pairs={{0,16},{16,0},{1,17},{17,1},{2,18},{18,2},{3,19},{19,3},{4,20},{20... | collective-permute-start | bytes 3145736 | tf_op jit(solution)/shard_map/ppermute | solution.py:372
  125.8 18.7 %copy-start.10 = (f32[2,128,128]{2,1,0:T(8,128)}, f32[2,128,128]{2,1,0:T(8,128)S(1)}, u32[]{:S(2)}) copy-start(f32[2,128,128]{2,1,0:T(8,128)S(1)} %get-tuple-element.32.panel) | copy-start | bytes 393220
  128.7 19.6 %collective-permute-start.7 = (f32[16,16,8,128]{3,2,1,0:T(8,128)}, f32[16,16,8,128]{3,2,1,0:T(8,128)}, u32[]{:S(2)}, u32[]{:S(2)}) collective-permute-start(f32[16,16,8,128]{3,2,1,0:T(8,128)} %get-tuple-element.34), channel_id=1, source_target_pairs={{0,16},{16,0},{1,17},{17,1},{2,18},{18,2},{3,19},{19,3},{4,20},{20... | collective-permute-start | bytes 3145736 | tf_op jit(solution)/shard_map/ppermute | solution.py:416
  144.5 11.7 %all-to-all-start.3 = ((f32[32,8,128]{2,1,0:T(8,128)}), f32[32,8,128]{2,1,0:T(8,128)S(1)}, u32[]{:S(2)}, u32[]{:S(2)}) async-start(f32[32,8,128]{2,1,0:T(8,128)} %broadcast_in_dim.2), calls=%async_computation.3 | async-start | bytes 262144 | tf_op jit(solution)/shard_map/all_to_all | solution.py:376
  156.2 20.4 %all-to-all-start.4 = ((f32[16,128,128]{2,1,0:T(8,128)}), f32[16,128,128]{2,1,0:T(8,128)S(1)}, u32[]{:S(2)}, u32[]{:S(2)}) async-start(f32[16,128,128]{2,1,0:T(8,128)} %bitcast.32), calls=%async_computation.4 | async-start | bytes 2097152 | tf_op jit(solution)/shard_map/all_to_all | solution.py:376
  175.9 0.7 copy-start.4
  176.6 0.9 copy-start.5
  177.5 25.9 %copy-start.9 = (s32[128]{0:T(128)S(1)}, s32[128]{0:T(128)}, u32[]{:S(2)}) copy-start(s32[128]{0:T(128)} %get-tuple-element.23.table) | copy-start | bytes 1540
  203.4 2.1 copy-start
  206.3 32.8 %copy-start.6 = (f32[2,128,128]{2,1,0:T(8,128)S(1)}, f32[2,128,128]{2,1,0:T(8,128)}, u32[]{:S(2)}) copy-start(f32[2,128,128]{2,1,0:T(8,128)} %copy-done.4) | copy-start | bytes 393220
  206.3 32.8 %copy-start.11 = (f32[2,128,128]{2,1,0:T(8,128)S(1)}, f32[2,128,128]{2,1,0:T(8,128)}, u32[]{:S(2)}) copy-start(f32[2,128,128]{2,1,0:T(8,128)} %copy-done.10) | copy-start | bytes 393220
  206.3 33.8 %copy-start.1 = (bf16[80,192,128]{2,1,0:T(8,128)(2,1)S(1)}, bf16[80,192,128]{2,1,0:T(8,128)(2,1)}, u32[]{:S(2)}) copy-start(bf16[80,192,128]{2,1,0:T(8,128)(2,1)} %all-gather.4.cloned.1.call-done) | copy-start | bytes 11796484
  226.9 16.1 %collective-permute-start.8 = (bf16[16,368,128]{2,1,0:T(8,128)(2,1)S(1)}, bf16[16,368,128]{2,1,0:T(8,128)(2,1)S(1)}, u32[]{:S(2)}, u32[]{:S(2)}) collective-permute-start(bf16[16,368,128]{2,1,0:T(8,128)(2,1)S(1)} %all_to_all.32.near), channel_id=1, source_target_pairs={{0,16},{16,0},{1,17},{17,1},{2,18},{18,2},{3,19},{19,3},{4,20},{20... | collective-permute-start | bytes 4521992 | tf_op jit(solution)/shard_map/ppermute | solution.py:463
Sparse Core Ops, SparseCore 0:
  76.7 70.7 all-gather.3

commit v7 on v6

--- a/solution.py
+++ b/solution.py
@@ -30,6 +30,7 @@
 VMEM = pl.BlockSpec(memory_space=pltpu.VMEM)
 SMEM = pl.BlockSpec(memory_space=pltpu.SMEM)
 ANY = pl.BlockSpec(memory_space=pl.ANY)
+HBM = pl.BlockSpec(memory_space=pltpu.HBM)
 
 
 def call(body, outs, scratch=(), flops=0, specs=None, n_in=0):
@@ -196,7 +197,7 @@
         turned[k] = dot(eye, whole, ((1,), (1,))).astype(BF16)
 
 
-def weigh(place, state, panel, keep, send, rows):
+def weigh(place, state, panel, _, keep, send, rows):
     weights = [jnp.concatenate(split3(panel[k]), axis=1) for k in range(2)]
     rows[192:, :] = jnp.zeros((64, RANK), F32)
 
@@ -403,19 +404,18 @@
         flops=800_000_000,
         specs=[SMEM, VMEM, VMEM],
     )(place, near, far)
-    late, state = barrier((late, state))
-    seconds = lax.all_gather(late, "z")
     square = sds((2, RANK, RANK), F32)
     two = sds((2, 128, RANK), F32)
     panel, gram = call(panels, (two, square), n_in=2, flops=300_000_000)(state, right)
-    gram = exchange(gram.reshape(32, 8, RANK), FSDP)
+    late, gram = barrier((late, gram))
+    seconds = lax.all_gather(late, "z")
+    gram = jnp.sum(exchange(gram.reshape(32, 8, RANK), FSDP), axis=0)
     half = sds((16, 16, 8, RANK), F32)
     keep, send = call(
-        weigh, (half, half), [pltpu.VMEM((256, RANK), F32)], specs=[SMEM, VMEM, VMEM], flops=400_000_000
-    )(place, state, panel)
+        weigh, (half, half), [pltpu.VMEM((256, RANK), F32)], specs=[SMEM, VMEM, VMEM, ANY], flops=400_000_000
+    )(place, state, panel, gram)
     parts = keep + lax.ppermute(send, "c", SWAP)
-    gram = jnp.broadcast_to(jnp.sum(gram, axis=0)[None], gram.shape)
-    gram = exchange(gram, FSDP).reshape(2, RANK, RANK)
+    gram = exchange(jnp.broadcast_to(gram[None], (32, 8, RANK)), FSDP).reshape(2, RANK, RANK)
     parts, gram = barrier((parts, gram))
     parts = exchange(parts.reshape(16, 128, RANK), XY)
     inverse = call(
@@ -457,9 +457,12 @@
         select,
         sds((16, ROWS, RANK), BF16),
         [pltpu.VMEM((ROWS, RANK), BF16)],
-        specs=[SMEM, SMEM, VMEM, VMEM, ANY],
+        specs=[SMEM, SMEM, VMEM, VMEM, HBM],
     )(table, place, mine, tiles, seconds)
     near = exchange(chosen, XY)
+    near, turned, low, left, second_panel, second_turned = barrier(
+        (near, turned, low, left, second_panel, second_turned)
+    )
     far = lax.ppermute(near, "c", SWAP)
     right_out = call(
         finish_right, sds((EXPERTS, 2, BLOCK, RANK), F32), specs=[SMEM, VMEM, VMEM], flops=300_000_000

time: 257 us -> 221 us (0.86)
  blocking collectives: 96.8 us -> 44.5 us
  waiting for transfers between devices: 25.2 us -> 32.3 us
  local copies, waits for them, and re-layouts: 7.1 us -> 12.5 us
  starting transfers between devices: 68 us -> 72.8 us
    all_to_all x3 -> x1, blocking collectives: 71.7 us -> 14 us  [exchange(): return lax.all_to_all(x, axis, split_axis=0, concat_axis=0, tiled=True)]
    all_to_all x3 -> x5, starting transfers between devices: 23.3 us -> 34.5 us  [exchange(): return lax.all_to_all(x, axis, split_axis=0, concat_axis=0, tiled=True)]
    all_gather x1, blocking collectives: 25.1 us -> 30.5 us  [shards(): tiles = lax.all_gather(mine, 'z')]
    ppermute x1, starting transfers between devices: 11 us -> 5.62 us  [gather_slices(): return (x, lax.ppermute(x, 'c', SWAP))]
    unnamed x24 -> x34, local copies, waits for them, and re-layouts: 6.44 us -> 11.8 us
    all_to_all x3 -> x5, waiting for transfers between devices: 12.5 us -> 17.9 us  [exchange(): return lax.all_to_all(x, axis, split_axis=0, concat_axis=0, tiled=True)]
    ppermute x1, waiting for transfers between devices: 0.01 us -> 2.92 us  [shards(): far = lax.ppermute(near, 'c', SWAP)]
  transfers between devices with their start and end apart: 13 -> 15, of which waited for: 5 -> 9; matrix products, arithmetic and copies ran while one was open for 2% -> 1% of each run, Pallas kernels for 12% -> 13%
where the time goes in v7:
time: 221 us; the launch traced here: 220 us
  starting transfers between devices  72.8 us (33%)
  blocking collectives  44.5 us (20%)
  Pallas kernels  40.6 us (18%)
  waiting for transfers between devices  32.3 us (15%)
  between operations  14.4 us (7%)
  local copies, waits for them, and re-layouts  12.5 us (6%)
  other arithmetic  3.2 us (1%)
    all_to_all x5, starting transfers between devices, exchange(): return lax.all_to_all(x, axis, split_axis=0, concat_axis=0, tiled=True)  34.5 us
    all_gather x1, blocking collectives, shards(): tiles = lax.all_gather(mine, 'z')  30.5 us
    ppermute x6, starting transfers between devices, gather_slices(): lax.ppermute(x, axis, ring((4 - d) % 4))  20 us
    all_to_all x5, waiting for transfers between devices, exchange(): return lax.all_to_all(x, axis, split_axis=0, concat_axis=0, tiled=True)  17.9 us
    pallas_call x1, Pallas kernels, shards(): call(functools.partial(invert, size=8), square, [pltpu.VMEM((2, RANK, 2 *...  16.1 us
    all_to_all x1, blocking collectives, exchange(): return lax.all_to_all(x, axis, split_axis=0, concat_axis=0, tiled=True)  14 us
    unnamed x34, local copies, waits for them, and re-layouts  11.8 us
    ppermute x1, starting transfers between devices, shards(): far = lax.ppermute(near, 'c', SWAP)  10.3 us
  transfers between devices with their start and end apart: 15, of which 9 were waited for; matrix products, arithmetic and copies ran while one was open for 1% of the time, Pallas kernels for 13%

profile of v7, /device:TPU:1, one launch (start us, length us, event | category | flops | bytes accessed | tf_op | source)
XLA Modules:
  0.0 220.3 jit_solution(11602613435981556533)
XLA Ops:
  7.8 2.1 shard_map.67
  9.9 15.8 %all-to-all-start = ((bf16[16,16,128]{2,1,0:T(8,128)(2,1)}), bf16[16,16,128]{2,1,0:T(8,128)(2,1)S(1)}, u32[]{:S(2)}, u32[]{:S(2)}) async-start(bf16[16,16,128]{2,1,0:T(8,128)(2,1)} %get-tuple-element.31), calls=%async_computation | async-start | bytes 131072 | tf_op jit(solution)/shard_map/all_to_all | solution.py:377
  25.7 1.0 copy-done.9
  26.7 1.0 copy-done.10
  27.7 0.6 copy-done.12
  28.3 2.0 shard_map.68
  30.4 6.9 %all-to-all-done = bf16[16,16,128]{2,1,0:T(8,128)(2,1)S(1)} async-done(((bf16[16,16,128]{2,1,0:T(8,128)(2,1)}), bf16[16,16,128]{2,1,0:T(8,128)(2,1)S(1)}, u32[]{:S(2)}, u32[]{:S(2)}) %all-to-all-start) | async-done | bytes 65568 | tf_op jit(solution)/shard_map/all_to_all | solution.py:377
  37.2 4.6 %all-to-all-start.1 = ((bf16[16,192,128]{2,1,0:T(8,128)(2,1)}), bf16[16,192,128]{2,1,0:T(8,128)(2,1)S(1)}, u32[]{:S(2)}, u32[]{:S(2)}) async-start(bf16[16,192,128]{2,1,0:T(8,128)(2,1)} %get-tuple-element.32), calls=%async_computation.1 | async-start | bytes 1572864 | tf_op jit(solution)/shard_map/all_to_all | solution.py:377
  41.9 3.1 %collective-permute-start = (bf16[16,16,128]{2,1,0:T(8,128)(2,1)S(1)}, bf16[16,16,128]{2,1,0:T(8,128)(2,1)S(1)}, u32[]{:S(2)}, u32[]{:S(2)}) collective-permute-start(bf16[16,16,128]{2,1,0:T(8,128)(2,1)S(1)} %all-to-all-done), channel_id=1, source_target_pairs={{0,128},{128,256},{256,384},{384,0},{1,129},{129,257},{257,385},{3... | collective-permute-start | bytes 196616 | tf_op jit(solution)/shard_map/ppermute | solution.py:371
  45.0 3.4 %collective-permute-start.1 = (bf16[16,16,128]{2,1,0:T(8,128)(2,1)S(1)}, bf16[16,16,128]{2,1,0:T(8,128)(2,1)S(1)}, u32[]{:S(2)}, u32[]{:S(2)}) collective-permute-start(bf16[16,16,128]{2,1,0:T(8,128)(2,1)S(1)} %all-to-all-done), channel_id=1, source_target_pairs={{0,384},{128,0},{256,128},{384,256},{1,385},{129,1},{257,129},{385... | collective-permute-start | bytes 196616 | tf_op jit(solution)/shard_map/ppermute | solution.py:371
  48.4 3.4 %collective-permute-start.2 = (bf16[16,16,128]{2,1,0:T(8,128)(2,1)S(1)}, bf16[16,16,128]{2,1,0:T(8,128)(2,1)S(1)}, u32[]{:S(2)}, u32[]{:S(2)}) collective-permute-start(bf16[16,16,128]{2,1,0:T(8,128)(2,1)S(1)} %all-to-all-done), channel_id=1, source_target_pairs={{0,256},{128,384},{256,0},{384,128},{1,257},{129,385},{257,1},{385... | collective-permute-start | bytes 196616 | tf_op jit(solution)/shard_map/ppermute | solution.py:371
  51.9 3.3 %collective-permute-done.2 = bf16[16,16,128]{2,1,0:T(8,128)(2,1)S(1)} collective-permute-done((bf16[16,16,128]{2,1,0:T(8,128)(2,1)S(1)}, bf16[16,16,128]{2,1,0:T(8,128)(2,1)S(1)}, u32[]{:S(2)}, u32[]{:S(2)}) %collective-permute-start.2) | collective-permute-done | bytes 65568 | tf_op jit(solution)/shard_map/ppermute | solution.py:371
  55.3 3.2 %collective-permute-start.3 = (bf16[4,16,16,128]{3,2,1,0:T(8,128)(2,1)S(1)}, bf16[4,16,16,128]{3,2,1,0:T(8,128)(2,1)S(1)}, u32[]{:S(2)}, u32[]{:S(2)}) collective-permute-start(bf16[4,16,16,128]{3,2,1,0:T(8,128)(2,1)S(1)} %get-tuple-element.56), channel_id=1, source_target_pairs={{0,32},{32,64},{64,96},{96,0},{1,33},{33,65},{65,97},{97,1},{2,34}... | collective-permute-start | bytes 786440 | tf_op jit(solution)/shard_map/ppermute | solution.py:371
  58.5 3.4 %collective-permute-start.4 = (bf16[4,16,16,128]{3,2,1,0:T(8,128)(2,1)S(1)}, bf16[4,16,16,128]{3,2,1,0:T(8,128)(2,1)S(1)}, u32[]{:S(2)}, u32[]{:S(2)}) collective-permute-start(bf16[4,16,16,128]{3,2,1,0:T(8,128)(2,1)S(1)} %get-tuple-element.56), channel_id=1, source_target_pairs={{0,96},{32,0},{64,32},{96,64},{1,97},{33,1},{65,33},{97,65},{2,98}... | collective-permute-start | bytes 786440 | tf_op jit(solution)/shard_map/ppermute | solution.py:371
  61.8 3.5 %collective-permute-start.5 = (bf16[4,16,16,128]{3,2,1,0:T(8,128)(2,1)S(1)}, bf16[4,16,16,128]{3,2,1,0:T(8,128)(2,1)S(1)}, u32[]{:S(2)}, u32[]{:S(2)}) collective-permute-start(bf16[4,16,16,128]{3,2,1,0:T(8,128)(2,1)S(1)} %get-tuple-element.56), channel_id=1, source_target_pairs={{0,64},{32,96},{64,0},{96,32},{1,65},{33,97},{65,1},{97,33},{2,66}... | collective-permute-start | bytes 786440 | tf_op jit(solution)/shard_map/ppermute | solution.py:371
  65.9 5.4 %collective-permute-done.5 = bf16[4,16,16,128]{3,2,1,0:T(8,128)(2,1)S(1)} collective-permute-done((bf16[4,16,16,128]{3,2,1,0:T(8,128)(2,1)S(1)}, bf16[4,16,16,128]{3,2,1,0:T(8,128)(2,1)S(1)}, u32[]{:S(2)}, u32[]{:S(2)}) %collective-permute-start.5) | collective-permute-done | bytes 262176 | tf_op jit(solution)/shard_map/ppermute | solution.py:371
  71.5 5.6 %collective-permute-start.6 = (bf16[16,16,16,128]{3,2,1,0:T(8,128)(2,1)S(1)}, bf16[16,16,16,128]{3,2,1,0:T(8,128)(2,1)S(1)}, u32[]{:S(2)}, u32[]{:S(2)}) collective-permute-start(bf16[16,16,16,128]{3,2,1,0:T(8,128)(2,1)S(1)} %bitcast.25), channel_id=1, source_target_pairs={{0,16},{16,0},{1,17},{17,1},{2,18},{18,2},{3,19},{19,3},{4,20},{20... | collective-permute-start | bytes 3145736 | tf_op jit(solution)/shard_map/ppermute | solution.py:373
  77.1 2.3 %collective-permute-done.6.far = bf16[16,16,16,128]{3,2,1,0:T(8,128)(2,1)S(1)} collective-permute-done((bf16[16,16,16,128]{3,2,1,0:T(8,128)(2,1)S(1)}, bf16[16,16,16,128]{3,2,1,0:T(8,128)(2,1)S(1)}, u32[]{:S(2)}, u32[]{:S(2)}) %collective-permute-start.6) | collective-permute-done | bytes 1048608 | tf_op jit(solution)/shard_map/ppermute | solution.py:373
  79.3 2.9 %shard_map.69.right = bf16[16,384,128]{2,1,0:T(8,128)(2,1)S(1)} custom-call(s32[4]{0:T(128)S(1)} %copy-done.11, bf16[16,16,16,128]{3,2,1,0:T(8,128)(2,1)S(1)} %bitcast.26, bf16[16,16,16,128]{3,2,1,0:T(8,128)(2,1)S(1)} %collective-permute-done.6.far), custom_call_target="tpu_custom_call" | custom-call | flops 800000000 | bytes 4000000 | tf_op jit(solution)/shard_map/pallas_call | solution.py:400
  82.3 2.2 %shard_map.70 = (f32[2,128,128]{2,1,0:T(8,128)S(1)}, f32[2,128,128]{2,1,0:T(8,128)S(1)}) custom-call(bf16[16,192,128]{2,1,0:T(8,128)(2,1)S(1)} %all-to-all-done.1.state, bf16[16,384,128]{2,1,0:T(8,128)(2,1)S(1)} %shard_map.69.right), custom_call_target="tpu_custom_call" | custom-call | flops 300000000 | bytes 4000000 | tf_op jit(solution)/shard_map/pallas_call | solution.py:409
  84.5 14.0 %all_to_all.30 = f32[32,8,128]{2,1,0:T(8,128)S(1)} all-to-all(f32[32,8,128]{2,1,0:T(8,128)S(1)} %bitcast.31), channel_id=1, replica_groups=mesh['x'=4,'y'=4,'c'=2,'z'=16] {'x','y','c'}, dimensions={0} | all-to-all | bytes 262144 | tf_op jit(solution)/shard_map/all_to_all | solution.py:377
  98.6 0.9 copy-done.15
  99.5 2.9 %shard_map.71 = (f32[16,16,8,128]{3,2,1,0:T(8,128)S(1)}, f32[16,16,8,128]{3,2,1,0:T(8,128)}) custom-call(s32[4]{0:T(128)S(1)} %copy-done.11, bf16[16,192,128]{2,1,0:T(8,128)(2,1)S(1)} %all-to-all-done.1.state, f32[2,128,128]{2,1,0:T(8,128)S(1)} %copy-done.15, f32[8,128]{1,0:T(8,128)S(1)} %reduce_sum.9._), custom_call_target="tpu_custom_call" | custom-call | flops 400000000 | bytes 4000000 | tf_op jit(solution)/shard_map/pallas_call | solution.py:414
  102.5 2.3 %collective-permute-start.7 = (f32[16,16,8,128]{3,2,1,0:T(8,128)}, f32[16,16,8,128]{3,2,1,0:T(8,128)}, u32[]{:S(2)}, u32[]{:S(2)}) collective-permute-start(f32[16,16,8,128]{3,2,1,0:T(8,128)} %get-tuple-element.39), channel_id=1, source_target_pairs={{0,16},{16,0},{1,17},{17,1},{2,18},{18,2},{3,19},{19,3},{4,20},{20... | collective-permute-start | bytes 3145736 | tf_op jit(solution)/shard_map/ppermute | solution.py:417
  104.8 0.7 broadcast_in_dim.2
  105.5 3.6 %all-to-all-start.3 = ((f32[32,8,128]{2,1,0:T(8,128)}), f32[32,8,128]{2,1,0:T(8,128)S(1)}, u32[]{:S(2)}, u32[]{:S(2)}) async-start(f32[32,8,128]{2,1,0:T(8,128)} %broadcast_in_dim.2), calls=%async_computation.3 | async-start | bytes 262144 | tf_op jit(solution)/shard_map/all_to_all | solution.py:377
  109.1 2.4 %add.3 = f32[16,16,8,128]{3,2,1,0:T(8,128)} add(f32[16,16,8,128]{3,2,1,0:T(8,128)S(1)} %get-tuple-element.38, f32[16,16,8,128]{3,2,1,0:T(8,128)} %collective-permute-done.7) | non-fusion elementwise | flops 262144 | bytes 3145728 | tf_op jit(solution)/shard_map/add | solution.py:417
  111.5 5.4 %all-to-all-done.3 = f32[32,8,128]{2,1,0:T(8,128)S(1)} async-done(((f32[32,8,128]{2,1,0:T(8,128)}), f32[32,8,128]{2,1,0:T(8,128)S(1)}, u32[]{:S(2)}, u32[]{:S(2)}) %all-to-all-start.3) | async-done | bytes 131104 | tf_op jit(solution)/shard_map/all_to_all | solution.py:377
  116.9 3.7 %all-to-all-start.4 = ((f32[16,128,128]{2,1,0:T(8,128)}), f32[16,128,128]{2,1,0:T(8,128)S(1)}, u32[]{:S(2)}, u32[]{:S(2)}) async-start(f32[16,128,128]{2,1,0:T(8,128)} %bitcast.32), calls=%async_computation.4 | async-start | bytes 2097152 | tf_op jit(solution)/shard_map/all_to_all | solution.py:377
  120.6 16.1 %shard_map.72.inverse = f32[2,128,128]{2,1,0:T(8,128)S(1)} custom-call(f32[2,128,128]{2,1,0:T(8,128)S(1)} %bitcast.30), custom_call_target="tpu_custom_call" | custom-call | flops 4000000000 | bytes 4000000 | tf_op jit(solution)/shard_map/pallas_call | solution.py:421
  136.9 0.8 shard_map.73.mine
  137.7 30.5 %all-gather = bf16[2304,128]{1,0:T(8,128)(2,1)S(1)} all-gather(bf16[144,128]{1,0:T(8,128)(2,1)S(1)} %shard_map.73.mine), channel_id=2, replica_groups=mesh['x'=4,'y'=4,'c'=2,'z'=16] {'z'}, dimensions={0}, use_global_device_ids=true | all-gather | bytes 626688 | tf_op jit(solution)/shard_map/all_gather | solution.py:437
  168.2 2.1 copy-done
  170.3 0.8 shard_map.74
  171.1 1.1 copy-done.4
  172.3 6.9 %all-to-all-start.5 = ((bf16[16,368,128]{2,1,0:T(8,128)(2,1)}), bf16[16,368,128]{2,1,0:T(8,128)(2,1)S(1)}, u32[]{:S(2)}, u32[]{:S(2)}) async-start(bf16[16,368,128]{2,1,0:T(8,128)(2,1)} %copy-done.4), calls=%async_computation.5 | async-start | bytes 3014656 | tf_op jit(solution)/shard_map/all_to_all | solution.py:377
  179.2 1.1 copy-done.3
  180.3 0.9 shard_map.75.turned
  181.2 0.9 copy-done.5
  182.1 0.9 shard_map.76
  183.0 2.1 copy-done.1
  185.1 2.9 %shard_map.77 = (f32[2,128,128]{2,1,0:T(8,128)S(1)}, bf16[2,128,1536]{2,1,0:T(8,128)(2,1)S(1)}) custom-call(s32[128]{0:T(128)S(1)} %copy-done.13, s32[4]{0:T(128)S(1)} %copy-done.11, bf16[16,5,192,128]{3,2,1,0:T(8,128)(2,1)S(1)} %bitcast.24, bf16[16,384,128]{2,1,0:T(8,128)(2,1)S(1)} %shard_map.69.right), custom_call_target="tpu_custom_call" | custom-call | flops 300000000 | bytes 3000000 | tf_op jit(solution)/shard_map/pallas_call | solution.py:438
  188.0 0.9 copy-done.7
  188.9 5.4 %all-to-all-done.5.near = bf16[16,368,128]{2,1,0:T(8,128)(2,1)S(1)} async-done(((bf16[16,368,128]{2,1,0:T(8,128)(2,1)}), bf16[16,368,128]{2,1,0:T(8,128)(2,1)S(1)}, u32[]{:S(2)}, u32[]{:S(2)}) %all-to-all-start.5) | async-done | bytes 1507360 | tf_op jit(solution)/shard_map/all_to_all | solution.py:377
  194.3 10.3 %collective-permute-start.8 = (bf16[16,368,128]{2,1,0:T(8,128)(2,1)S(1)}, bf16[16,368,128]{2,1,0:T(8,128)(2,1)S(1)}, u32[]{:S(2)}, u32[]{:S(2)}) collective-permute-start(bf16[16,368,128]{2,1,0:T(8,128)(2,1)S(1)} %all-to-all-done.5.near), channel_id=1, source_target_pairs={{0,16},{16,0},{1,17},{17,1},{2,18},{18,2},{3,19},{19,3},{4,20},{20... | collective-permute-start | bytes 4521992 | tf_op jit(solution)/shard_map/ppermute | solution.py:466
  204.5 2.9 %collective-permute-done.8.far = bf16[16,368,128]{2,1,0:T(8,128)(2,1)S(1)} collective-permute-done((bf16[16,368,128]{2,1,0:T(8,128)(2,1)S(1)}, bf16[16,368,128]{2,1,0:T(8,128)(2,1)S(1)}, u32[]{:S(2)}, u32[]{:S(2)}) %collective-permute-start.8) | collective-permute-done | bytes 1507360 | tf_op jit(solution)/shard_map/ppermute | solution.py:466
  207.4 2.1 shard_map.79
  209.5 3.9 %shard_map.78 = (bf16[4,128,1536]{2,1,0:T(8,128)(2,1)}, f32[4,128,128]{2,1,0:T(8,128)}) custom-call(s32[128]{0:T(128)S(1)} %copy-done.13, s32[4]{0:T(128)S(1)} %copy-done.11, bf16[2,128,1536]{2,1,0:T(8,128)(2,1)S(1)} %copy-done.6, bf16[2,128,1536]{2,1,0:T(8,128)(2,1)S(1)} %copy-done.8, bf16[16,368,128]{2,1,0:T(8,128)(2,1)S(1)} %all-to-all-done.5.near, ...), custom_call_target="tpu_custom_call" | custom-call | flops 1200000000 | bytes 4000000 | tf_op jit(solution)/shard_map/pallas_call | solution.py:470
  (38 shorter events, 1.7 us)
Async XLA Ops:
  9.9 27.3 %all-to-all-start = ((bf16[16,16,128]{2,1,0:T(8,128)(2,1)}), bf16[16,16,128]{2,1,0:T(8,128)(2,1)S(1)}, u32[]{:S(2)}, u32[]{:S(2)}) async-start(bf16[16,16,128]{2,1,0:T(8,128)(2,1)} %get-tuple-element.31), calls=%async_computation | async-start | bytes 131072 | tf_op jit(solution)/shard_map/all_to_all | solution.py:377
  25.6 1.0 copy-start.9
  26.7 1.0 copy-start.10
  27.7 0.6 copy-start.12
  37.2 45.0 %all-to-all-start.1 = ((bf16[16,192,128]{2,1,0:T(8,128)(2,1)}), bf16[16,192,128]{2,1,0:T(8,128)(2,1)S(1)}, u32[]{:S(2)}, u32[]{:S(2)}) async-start(bf16[16,192,128]{2,1,0:T(8,128)(2,1)} %get-tuple-element.32), calls=%async_computation.1 | async-start | bytes 1572864 | tf_op jit(solution)/shard_map/all_to_all | solution.py:377
  41.8 37.5 %copy-start.11 = (s32[4]{0:T(128)S(1)}, s32[4]{0:T(128)}, u32[]{:S(2)}) copy-start(s32[4]{0:T(128)} %pad_add_fusion.place) | copy-start | bytes 52
  41.8 126.4 %all-gather.4.cloned.1.call-start = ((), (), s32[]{:S(2)}) async-start(), calls=%async_computation.6 | async-start | bytes 4177920 | tf_op jit(solution)/shard_map/all_gather | solution.py:411
  41.9 10.0 %collective-permute-start = (bf16[16,16,128]{2,1,0:T(8,128)(2,1)S(1)}, bf16[16,16,128]{2,1,0:T(8,128)(2,1)S(1)}, u32[]{:S(2)}, u32[]{:S(2)}) collective-permute-start(bf16[16,16,128]{2,1,0:T(8,128)(2,1)S(1)} %all-to-all-done), channel_id=1, source_target_pairs={{0,128},{128,256},{256,384},{384,0},{1,129},{129,257},{257,385},{3... | collective-permute-start | bytes 196616 | tf_op jit(solution)/shard_map/ppermute | solution.py:371
  45.0 6.8 %collective-permute-start.1 = (bf16[16,16,128]{2,1,0:T(8,128)(2,1)S(1)}, bf16[16,16,128]{2,1,0:T(8,128)(2,1)S(1)}, u32[]{:S(2)}, u32[]{:S(2)}) collective-permute-start(bf16[16,16,128]{2,1,0:T(8,128)(2,1)S(1)} %all-to-all-done), channel_id=1, source_target_pairs={{0,384},{128,0},{256,128},{384,256},{1,385},{129,1},{257,129},{385... | collective-permute-start | bytes 196616 | tf_op jit(solution)/shard_map/ppermute | solution.py:371
  48.4 6.8 %collective-permute-start.2 = (bf16[16,16,128]{2,1,0:T(8,128)(2,1)S(1)}, bf16[16,16,128]{2,1,0:T(8,128)(2,1)S(1)}, u32[]{:S(2)}, u32[]{:S(2)}) collective-permute-start(bf16[16,16,128]{2,1,0:T(8,128)(2,1)S(1)} %all-to-all-done), channel_id=1, source_target_pairs={{0,256},{128,384},{256,0},{384,128},{1,257},{129,385},{257,1},{385... | collective-permute-start | bytes 196616 | tf_op jit(solution)/shard_map/ppermute | solution.py:371
  55.3 10.1 %collective-permute-start.3 = (bf16[4,16,16,128]{3,2,1,0:T(8,128)(2,1)S(1)}, bf16[4,16,16,128]{3,2,1,0:T(8,128)(2,1)S(1)}, u32[]{:S(2)}, u32[]{:S(2)}) collective-permute-start(bf16[4,16,16,128]{3,2,1,0:T(8,128)(2,1)S(1)} %get-tuple-element.56), channel_id=1, source_target_pairs={{0,32},{32,64},{64,96},{96,0},{1,33},{33,65},{65,97},{97,1},{2,34}... | collective-permute-start | bytes 786440 | tf_op jit(solution)/shard_map/ppermute | solution.py:371
  58.5 7.4 %collective-permute-start.4 = (bf16[4,16,16,128]{3,2,1,0:T(8,128)(2,1)S(1)}, bf16[4,16,16,128]{3,2,1,0:T(8,128)(2,1)S(1)}, u32[]{:S(2)}, u32[]{:S(2)}) collective-permute-start(bf16[4,16,16,128]{3,2,1,0:T(8,128)(2,1)S(1)} %get-tuple-element.56), channel_id=1, source_target_pairs={{0,96},{32,0},{64,32},{96,64},{1,97},{33,1},{65,33},{97,65},{2,98}... | collective-permute-start | bytes 786440 | tf_op jit(solution)/shard_map/ppermute | solution.py:371
  61.8 9.5 %collective-permute-start.5 = (bf16[4,16,16,128]{3,2,1,0:T(8,128)(2,1)S(1)}, bf16[4,16,16,128]{3,2,1,0:T(8,128)(2,1)S(1)}, u32[]{:S(2)}, u32[]{:S(2)}) collective-permute-start(bf16[4,16,16,128]{3,2,1,0:T(8,128)(2,1)S(1)} %get-tuple-element.56), channel_id=1, source_target_pairs={{0,64},{32,96},{64,0},{96,32},{1,65},{33,97},{65,1},{97,33},{2,66}... | collective-permute-start | bytes 786440 | tf_op jit(solution)/shard_map/ppermute | solution.py:371
  71.5 7.9 %collective-permute-start.6 = (bf16[16,16,16,128]{3,2,1,0:T(8,128)(2,1)S(1)}, bf16[16,16,16,128]{3,2,1,0:T(8,128)(2,1)S(1)}, u32[]{:S(2)}, u32[]{:S(2)}) collective-permute-start(bf16[16,16,16,128]{3,2,1,0:T(8,128)(2,1)S(1)} %bitcast.25), channel_id=1, source_target_pairs={{0,16},{16,0},{1,17},{17,1},{2,18},{18,2},{3,19},{19,3},{4,20},{20... | collective-permute-start | bytes 3145736 | tf_op jit(solution)/shard_map/ppermute | solution.py:373
  82.3 20.2 %copy-start.2 = (bf16[16,192,128]{2,1,0:T(8,128)(2,1)}, bf16[16,192,128]{2,1,0:T(8,128)(2,1)S(1)}, u32[]{:S(2)}) copy-start(bf16[16,192,128]{2,1,0:T(8,128)(2,1)S(1)} %all-to-all-done.1.state) | copy-start | bytes 2359300
  84.5 14.1 %copy-start.14 = (f32[2,128,128]{2,1,0:T(8,128)}, f32[2,128,128]{2,1,0:T(8,128)S(1)}, u32[]{:S(2)}) copy-start(f32[2,128,128]{2,1,0:T(8,128)S(1)} %get-tuple-element.34.panel) | copy-start | bytes 393220
  98.6 0.9 copy-start.15
  102.5 6.6 %collective-permute-start.7 = (f32[16,16,8,128]{3,2,1,0:T(8,128)}, f32[16,16,8,128]{3,2,1,0:T(8,128)}, u32[]{:S(2)}, u32[]{:S(2)}) collective-permute-start(f32[16,16,8,128]{3,2,1,0:T(8,128)} %get-tuple-element.39), channel_id=1, source_target_pairs={{0,16},{16,0},{1,17},{17,1},{2,18},{18,2},{3,19},{19,3},{4,20},{20... | collective-permute-start | bytes 3145736 | tf_op jit(solution)/shard_map/ppermute | solution.py:417
  105.5 11.4 %all-to-all-start.3 = ((f32[32,8,128]{2,1,0:T(8,128)}), f32[32,8,128]{2,1,0:T(8,128)S(1)}, u32[]{:S(2)}, u32[]{:S(2)}) async-start(f32[32,8,128]{2,1,0:T(8,128)} %broadcast_in_dim.2), calls=%async_computation.3 | async-start | bytes 262144 | tf_op jit(solution)/shard_map/all_to_all | solution.py:377
  116.9 20.0 %all-to-all-start.4 = ((f32[16,128,128]{2,1,0:T(8,128)}), f32[16,128,128]{2,1,0:T(8,128)S(1)}, u32[]{:S(2)}, u32[]{:S(2)}) async-start(f32[16,128,128]{2,1,0:T(8,128)} %bitcast.32), calls=%async_computation.4 | async-start | bytes 2097152 | tf_op jit(solution)/shard_map/all_to_all | solution.py:377
  136.6 31.6 %copy-start.13 = (s32[128]{0:T(128)S(1)}, s32[128]{0:T(128)}, u32[]{:S(2)}) copy-start(s32[128]{0:T(128)} %get-tuple-element.29.table) | copy-start | bytes 1540
  168.2 2.1 copy-start
  171.1 1.1 copy-start.4
  172.3 22.0 %all-to-all-start.5 = ((bf16[16,368,128]{2,1,0:T(8,128)(2,1)}), bf16[16,368,128]{2,1,0:T(8,128)(2,1)S(1)}, u32[]{:S(2)}, u32[]{:S(2)}) async-start(bf16[16,368,128]{2,1,0:T(8,128)(2,1)} %copy-done.4), calls=%async_computation.5 | async-start | bytes 3014656 | tf_op jit(solution)/shard_map/all_to_all | solution.py:377
  179.1 1.1 copy-start.3
  180.3 1.8 copy-start.16
  181.2 0.9 copy-start.5
  183.0 2.1 copy-start.1
  188.0 0.9 copy-start.7
  194.3 15.3 %copy-start.6 = (bf16[2,128,1536]{2,1,0:T(8,128)(2,1)S(1)}, bf16[2,128,1536]{2,1,0:T(8,128)(2,1)}, u32[]{:S(2)}) copy-start(bf16[2,128,1536]{2,1,0:T(8,128)(2,1)} %copy-done.5) | copy-start | bytes 2359300
  194.3 15.3 %copy-start.8 = (bf16[2,128,1536]{2,1,0:T(8,128)(2,1)S(1)}, bf16[2,128,1536]{2,1,0:T(8,128)(2,1)}, u32[]{:S(2)}) copy-start(bf16[2,128,1536]{2,1,0:T(8,128)(2,1)} %copy-done.7) | copy-start | bytes 2359300
  194.3 13.2 %collective-permute-start.8 = (bf16[16,368,128]{2,1,0:T(8,128)(2,1)S(1)}, bf16[16,368,128]{2,1,0:T(8,128)(2,1)S(1)}, u32[]{:S(2)}, u32[]{:S(2)}) collective-permute-start(bf16[16,368,128]{2,1,0:T(8,128)(2,1)S(1)} %all-to-all-done.5.near), channel_id=1, source_target_pairs={{0,16},{16,0},{1,17},{17,1},{2,18},{18,2},{3,19},{19,3},{4,20},{20... | collective-permute-start | bytes 4521992 | tf_op jit(solution)/shard_map/ppermute | solution.py:466
Sparse Core Ops, SparseCore 0:
  84.7 71.3 all-gather.3

commit v8 on v7

--- a/solution.py
+++ b/solution.py
@@ -30,7 +30,6 @@
 VMEM = pl.BlockSpec(memory_space=pltpu.VMEM)
 SMEM = pl.BlockSpec(memory_space=pltpu.SMEM)
 ANY = pl.BlockSpec(memory_space=pl.ANY)
-HBM = pl.BlockSpec(memory_space=pltpu.HBM)
 
 
 def call(body, outs, scratch=(), flops=0, specs=None, n_in=0):
@@ -40,7 +39,7 @@
         in_specs=specs if specs is not None else [VMEM] * n_in,
         out_specs=jax.tree.map(lambda _: VMEM, outs),
         scratch_shapes=list(scratch),
-        compiler_params=pltpu.CompilerParams(vmem_limit_bytes=48 * 1024 * 1024),
+        compiler_params=pltpu.CompilerParams(vmem_limit_bytes=16 * 1024 * 1024),
         cost_estimate=pl.CostEstimate(flops=flops, bytes_accessed=4_000_000, transcendentals=0),
     )
 
@@ -187,33 +186,58 @@
     return (iota((128, 128), 0) == iota((128, 128), 1)).astype(BF16)
 
 
-def second_panels(table, place, state, right, panel, turned):
+def second_panels(table, place, states, right, panel, turned, state, arrived):
+    copy = pltpu.make_async_copy(states.at[:, table[SLOT + place[3]]], state, arrived)
+    copy.start()
     some = table[SECOND + place[3]] < EXPERTS
     eye = jnp.where(some, unit(), jnp.zeros((128, 128), BF16))
+    copy.wait()
     for k in range(2):
         rows = slice(k * BLOCK, (k + 1) * BLOCK)
-        panel[k] = panel_of(lambda z: state[z, 0, rows, :], right, k, 1)
-        whole = state[:, 0, rows, :].reshape(HID, 128)
+        panel[k] = panel_of(lambda z: state[z, rows, :], right, k, 1)
+        whole = state[:, rows, :].reshape(HID, 128)
         turned[k] = dot(eye, whole, ((1,), (1,))).astype(BF16)
+
+
+def tile_of(x, y, core, q):
+    return 8 * (x - jnp.where(x > q, 1, 0)) + 2 * y + core
+
+
+def place_of(x, z):
+    q = z & 3
+    return 3 * (z >> 2) + q - jnp.where(q > x, 1, 0)
+
+
+def row_kinds(place):
+    m = iota((96, RANK), 0) >> 3
+    v = m - 3 * ((m * 11) >> 5)
+    q = v + jnp.where(v >= place[0], 1, 0)
+    return jnp.where(tile_of(place[0], place[1], place[2], q) >= 12, 1, 0)
 
 
 def weigh(place, state, panel, _, keep, send, rows):
     weights = [jnp.concatenate(split3(panel[k]), axis=1) for k in range(2)]
-    rows[192:, :] = jnp.zeros((64, RANK), F32)
-
-    def block(z, _):
-        for k in range(2):
-            value = dot(state[z, k * BLOCK : (k + 1) * BLOCK, :], weights[k])
-            total = value[:, :128] + (value[:, 128:256] + value[:, 256:])
-            rows[k * BLOCK : (k + 1) * BLOCK, :] = total
-        for i in range(16):
-            near = pl.multiple_of(16 * i + 8 * place[2], 8)
-            far = pl.multiple_of(16 * i + 8 - 8 * place[2], 8)
-            keep[i, z] = rows[pl.ds(near, 8), :]
-            send[i, z] = rows[pl.ds(far, 8), :]
+
+    def block(g, _):
+        for q in range(4):
+            z = 4 * g + q
+            for k in range(2):
+                value = dot(state[z, k * BLOCK : (k + 1) * BLOCK, :], weights[k])
+                total = value[:, :128] + (value[:, 128:256] + value[:, 256:])
+                rows[q, k * BLOCK : (k + 1) * BLOCK, :] = total
+            for x in range(4):
+                if x == q:
+                    continue
+                m = 3 * g + q - int(q > x)
+                for y in range(4):
+                    first = 64 * (x - int(x > q)) + 16 * y
+                    near = pl.multiple_of(first + 8 * place[2], 8)
+                    far = pl.multiple_of(first + 8 - 8 * place[2], 8)
+                    keep[4 * x + y, m] = rows[q, pl.ds(near, 8), :]
+                    send[4 * x + y, m] = rows[q, pl.ds(far, 8), :]
         return 0
 
-    lax.fori_loop(0, GROUPS, block, 0, unroll=4)
+    lax.fori_loop(0, 4, block, 0)
 
 
 def invert(gram, out, work, *, size):
@@ -248,13 +272,13 @@
     total = parts[0]
     for i in range(1, 16):
         total = total + parts[i]
-    kind = jnp.where(f >= 12, 1, 0)
-    out[:128] = dot(total, inverse[kind], ((1,), (1,)), HIGHEST).astype(BF16)
+    both = [dot(total, inverse[k], ((1,), (1,)), HIGHEST) for k in range(2)]
+    out[:96] = jnp.where(row_kinds(place) == 0, both[0], both[1]).astype(BF16)
     half = jnp.where(f >= 16, 1, 0)
     start = pl.multiple_of(8 * f - 128 * half, 8)
     rows = inverse[half, pl.ds(start, 8), :]
     high = rows.astype(BF16).astype(F32)
-    out[128:] = jnp.concatenate([high, rows - high], axis=0).astype(BF16)
+    out[96:] = jnp.concatenate([high, rows - high], axis=0).astype(BF16)
 
 
 def orthonormal(table, place, panel, inverse, left, low):
@@ -274,15 +298,17 @@
         out[k] = dot(eye, rows, ((1,), (1,))).astype(BF16)
 
 
-ROWS = 368
-
-
-def select(table, place, mine, tiles, _, out, packed):
+SECOND_ROWS, RIGHT_ROWS, SUM_ROWS, ROWS = 96, 208, 288, 320
+
+
+def select(table, place, mine, tiles, out, packed):
     z = place[3]
-    packed[:128, :] = mine[:128, :]
-    packed[128:272, :] = tiles[table[HELPER + z]]
-    start = pl.multiple_of((z >> 1) * 16, 16)
-    upper = (z & 1) == 1
+    packed[:SECOND_ROWS, :] = mine[:96, :]
+    packed[SECOND_ROWS:RIGHT_ROWS, :] = tiles[table[HELPER + z]]
+    m = place_of(place[0], z)
+    start = pl.multiple_of((m >> 1) * 16, 16)
+    upper = (m & 1) == 1
+    kinds = row_kinds(place)
     sums = []
     for e in range(0, EXPERTS, 2):
         pair = []
@@ -290,49 +316,60 @@
             p = table[WHERE + e + i]
             value = tiles[p, pl.ds(start, 16), :].astype(F32)
             pair.append(jnp.where(upper, value[8:], value[:8]))
-            whole = tiles[p, :128, :].astype(F32)
-            sums.append(jnp.sum(whole * whole, axis=0, keepdims=True))
-        packed[272 + e * 8 : 288 + e * 8, :] = jnp.concatenate(pair, axis=0).astype(BF16)
-    sums.append(jnp.zeros((16 - EXPERTS, RANK), F32))
-    packed[352:, :] = jnp.concatenate(sums, axis=0).astype(BF16)
+            whole = tiles[p, :96, :].astype(F32)
+            square = whole * whole
+            for k in range(2):
+                sums.append(jnp.sum(jnp.where(kinds == k, square, 0.0), axis=0, keepdims=True))
+        first = RIGHT_ROWS + e * 8
+        packed[first : first + 16, :] = jnp.concatenate(pair, axis=0).astype(BF16)
+    sums.append(jnp.zeros((ROWS - SUM_ROWS - 2 * EXPERTS, RANK), F32))
+    packed[SUM_ROWS:, :] = jnp.concatenate(sums, axis=0).astype(BF16)
     value = packed[...]
     for i in range(16):
         out[i] = value
 
 
-def finish_right(place, near, far, out):
-    c = place[2]
-    matrix = jnp.concatenate(
-        [join_matrix(place, c, False, 12), join_matrix(place, 1 - c, False, 12)], axis=1
-    )
-    parts = near[:, 352:, :].astype(F32) + far[:, 352:, :].astype(F32)
-    sums = [jnp.sum(parts[6 * k : 6 * k + 6], axis=0) for k in range(2)]
-    scales = [lax.rsqrt(s * (1.0 / HID) + epsilon) for s in sums]
-    for g in range(EXPERTS // 2):
-        rows = slice(272 + g * 16, 288 + g * 16)
-        data = jnp.concatenate(
-            [near[:12, rows, :].reshape(192, RANK), far[:12, rows, :].reshape(192, RANK)], axis=0
-        )
-        value = dot(matrix, data)
-        for s in range(2):
-            e = 2 * g + s
-            for k in range(2):
-                i = 2 * s + k
-                out[e, k] = value[i * BLOCK : (i + 1) * BLOCK, :] * scales[k][e : e + 1, :]
+def finish_right(place, near, far, out, blocks):
+    q = place[3] & 3
+    parts = near[:, SUM_ROWS:, :].astype(F32) + far[:, SUM_ROWS:, :].astype(F32)
+    scale = lax.rsqrt(jnp.sum(parts, axis=0) * (1.0 / HID) + epsilon)
+    for part, core in ((near, place[2]), (far, 1 - place[2])):
+        for chip in range(16):
+            x, y = chip // 4, chip % 4
+            t = jnp.where(q == x, 24, tile_of(x, y, core, q))
+            row = pl.ds(pl.multiple_of(8 * t, 8), 8)
+            for e in range(0, EXPERTS, 2):
+                first = RIGHT_ROWS + e * 8
+                value = part[chip, first : first + 16, :].astype(F32)
+                blocks[e, row, :] = value[:8]
+                blocks[e + 1, row, :] = value[8:]
+    for e in range(EXPERTS):
+        for k in range(2):
+            rows = slice(k * BLOCK, (k + 1) * BLOCK)
+            out[e, k] = blocks[e, rows, :] * scale[2 * e + k : 2 * e + k + 1, :]
 
 
 def finish_state(
-    table, place, turned, second, near, far, low, panel, left, out, left_out, inverse, wide
+    table, place, turned, second, near, far, low, panel, left, out, left_out, inverse, factor
 ):
-    c = place[2]
-    matrix = jnp.concatenate(
-        [join_matrix(place, c, False, 12), join_matrix(place, 1 - c, False, 12)], axis=1
-    )
-    for part, core in ((near, c), (far, 1 - c)):
+    for part, core in ((near, place[2]), (far, 1 - place[2])):
         for chip in range(16):
-            value = part[chip, 256:272, :].astype(F32)
+            x, y = chip // 4, chip % 4
+            value = part[chip, SECOND_ROWS + 96 : SECOND_ROWS + 112, :].astype(F32)
             row = pl.multiple_of(16 * chip + 8 * core, 8)
             inverse[pl.ds(row, 8), :] = value[:8] + value[8:]
+            for s in range(2):
+                for g in range(6):
+                    first = s * SECOND_ROWS + 16 * g
+                    value = part[chip, first : first + 16, :].astype(F32)
+                    for i in range(2):
+                        m = 2 * g + i
+                        v = m % 3
+                        q = v + int(v >= x)
+                        t = 8 * (x - int(x > q)) + 2 * y
+                        base = (4 * (m // 3) + q) * BLOCK + 8 * (t % 12)
+                        row = pl.ds(pl.multiple_of(base + 8 * core, 8), 8)
+                        factor[2 * s + t // 12, row, :] = value[8 * i : 8 * i + 8]
     some = table[SECOND + place[3]] < EXPERTS
     lows = [low[0], low[1]]
     for k in range(2):
@@ -342,21 +379,10 @@
         left_out[2 + k] = ortho * math.sqrt(D)
         lows.append((ortho * (-feedback)).astype(BF16))
     for s, state in enumerate((turned, second)):
-        for g in range(8):
-            rows = slice(s * 128 + g * 16, s * 128 + g * 16 + 16)
-            data = jnp.concatenate(
-                [near[:12, rows, :].reshape(192, RANK), far[:12, rows, :].reshape(192, RANK)],
-                axis=0,
-            )
-            value = dot(matrix, data).astype(BF16)
-            for p in range(2):
-                for k in range(2):
-                    i = 2 * p + k
-                    first = (2 * g + p) * BLOCK
-                    wide[2 * s + k, first : first + BLOCK, :] = value[i * BLOCK : (i + 1) * BLOCK]
         for k in range(2):
-            change = dot(lows[2 * s + k], wide[2 * s + k], ((1,), (1,)))
-            out[2 * s + k] = (state[k].astype(F32) + change).astype(BF16)
+            i = 2 * s + k
+            change = dot(lows[i], factor[i].astype(BF16), ((1,), (1,)))
+            out[i] = (state[k].astype(F32) + change).astype(BF16)
 
 
 def ring(shift):
@@ -410,22 +436,22 @@
     late, gram = barrier((late, gram))
     seconds = lax.all_gather(late, "z")
     gram = jnp.sum(exchange(gram.reshape(32, 8, RANK), FSDP), axis=0)
-    half = sds((16, 16, 8, RANK), F32)
+    half = sds((16, 12, 8, RANK), F32)
     keep, send = call(
-        weigh, (half, half), [pltpu.VMEM((256, RANK), F32)], specs=[SMEM, VMEM, VMEM, ANY], flops=400_000_000
+        weigh, (half, half), [pltpu.VMEM((4, 192, RANK), F32)], specs=[SMEM, VMEM, VMEM, ANY], flops=400_000_000
     )(place, state, panel, gram)
     parts = keep + lax.ppermute(send, "c", SWAP)
     gram = exchange(jnp.broadcast_to(gram[None], (32, 8, RANK)), FSDP).reshape(2, RANK, RANK)
     parts, gram = barrier((parts, gram))
-    parts = exchange(parts.reshape(16, 128, RANK), XY)
+    parts = exchange(parts.reshape(16, 96, RANK), XY)
     inverse = call(
-        functools.partial(invert, size=8),
+        functools.partial(invert, size=32),
         square,
         [pltpu.VMEM((2, RANK, 2 * RANK), F32)],
         n_in=1,
         flops=4_000_000_000,
     )(gram)
-    mine = call(scale_factor, sds((144, RANK), BF16), specs=[SMEM, VMEM, VMEM], flops=100_000_000)(
+    mine = call(scale_factor, sds((112, RANK), BF16), specs=[SMEM, VMEM, VMEM], flops=100_000_000)(
         place, inverse, parts
     )
     turned = call(turn, sds((2, 128, HID), BF16), specs=[SMEM, SMEM, VMEM], flops=100_000_000)(
@@ -435,42 +461,32 @@
         orthonormal, (two, sds((2, 128, RANK), BF16)), specs=[SMEM, SMEM, VMEM, VMEM], flops=100_000_000
     )(table, place, panel, inverse)
     tiles = lax.all_gather(mine, "z")
-    second_panel, second_turned = pl.pallas_call(
+    second_panel, second_turned = call(
         second_panels,
-        grid_spec=pltpu.PrefetchScalarGridSpec(
-            num_scalar_prefetch=2,
-            grid=(1,),
-            in_specs=[
-                pl.BlockSpec((16, 1, 192, 128), lambda i, t, p: (0, t[SLOT + p[3]], 0, 0)),
-                pl.BlockSpec((16, 384, RANK), lambda i, t, p: (0, 0, 0)),
-            ],
-            out_specs=[
-                pl.BlockSpec((2, 128, RANK), lambda i, t, p: (0, 0, 0)),
-                pl.BlockSpec((2, 128, HID), lambda i, t, p: (0, 0, 0)),
-            ],
-        ),
-        out_shape=[two, sds((2, 128, HID), BF16)],
-        compiler_params=pltpu.CompilerParams(vmem_limit_bytes=24 * 1024 * 1024),
-        cost_estimate=pl.CostEstimate(flops=300_000_000, bytes_accessed=3_000_000, transcendentals=0),
+        (two, sds((2, 128, HID), BF16)),
+        [pltpu.VMEM((16, 192, 128), BF16), pltpu.SemaphoreType.DMA],
+        specs=[SMEM, SMEM, ANY, VMEM],
+        flops=300_000_000,
     )(table, place, seconds, right)
     chosen = call(
         select,
         sds((16, ROWS, RANK), BF16),
         [pltpu.VMEM((ROWS, RANK), BF16)],
-        specs=[SMEM, SMEM, VMEM, VMEM, HBM],
-    )(table, place, mine, tiles, seconds)
+        specs=[SMEM, SMEM, VMEM, VMEM],
+    )(table, place, mine, tiles)
     near = exchange(chosen, XY)
     near, turned, low, left, second_panel, second_turned = barrier(
         (near, turned, low, left, second_panel, second_turned)
     )
     far = lax.ppermute(near, "c", SWAP)
     right_out = call(
-        finish_right, sds((EXPERTS, 2, BLOCK, RANK), F32), specs=[SMEM, VMEM, VMEM], flops=300_000_000
+        finish_right, sds((EXPERTS, 2, BLOCK, RANK), F32), [pltpu.VMEM((EXPERTS, 200, RANK), F32)],
+        specs=[SMEM, VMEM, VMEM], flops=1_000_000
     )(place, near, far)
     state_out, left_out = call(
         finish_state,
         (sds((4, 128, HID), BF16), sds((4, 128, RANK), F32)),
-        [pltpu.VMEM((2 * RANK, RANK), F32), pltpu.VMEM((4, HID, RANK), BF16)],
+        [pltpu.VMEM((2 * RANK, RANK), F32), pltpu.VMEM((4, HID, RANK), F32)],
         specs=[SMEM, SMEM] + [VMEM] * 7,
         flops=1_200_000_000,
     )(table, place, turned, second_turned, near, far, low, second_panel, left)

time: 221 us -> 210 us (0.950)
  Pallas kernels: 40.6 us -> 34.9 us
  local copies, waits for them, and re-layouts: 12.5 us -> 9.44 us
    pallas_call x5, Pallas kernels: 24.8 us -> 20 us  [the longest x1 11.8 us: shards(): call(functools.partial(invert, size=32), square, [pltpu.VMEM((2, RANK, 2...]
    unnamed x34 -> x26, local copies, waits for them, and re-layouts: 11.8 us -> 8.78 us
  transfers between devices with their start and end apart: 15 -> 15, of which waited for: 9 -> 9; matrix products, arithmetic and copies ran while one was open for 1% -> 1% of each run, Pallas kernels for 13% -> 12%
where the time goes in v8:
time: 210 us; the launch traced here: 209 us
  starting transfers between devices  70.8 us (34%)
  blocking collectives  45.1 us (21%)
  Pallas kernels  34.9 us (17%)
  waiting for transfers between devices  32.8 us (16%)
  between operations  14.4 us (7%)
  local copies, waits for them, and re-layouts  9.44 us (4%)
    all_to_all x5, starting transfers between devices, exchange(): return lax.all_to_all(x, axis, split_axis=0, concat_axis=0, tiled=True)  33.5 us
    all_gather x1, blocking collectives, shards(): tiles = lax.all_gather(mine, 'z')  31 us
    ppermute x6, starting transfers between devices, gather_slices(): lax.ppermute(x, axis, ring((4 - d) % 4))  20 us
    all_to_all x5, waiting for transfers between devices, exchange(): return lax.all_to_all(x, axis, split_axis=0, concat_axis=0, tiled=True)  18.6 us
    all_to_all x1, blocking collectives, exchange(): return lax.all_to_all(x, axis, split_axis=0, concat_axis=0, tiled=True)  14 us
    pallas_call x1, Pallas kernels, shards(): call(functools.partial(invert, size=32), square, [pltpu.VMEM((2, RANK, 2...  11.8 us
    ppermute x6, waiting for transfers between devices, gather_slices(): lax.ppermute(x, axis, ring((4 - d) % 4))  9.27 us
    ppermute x1, starting transfers between devices, shards(): far = lax.ppermute(near, 'c', SWAP)  9.26 us
  transfers between devices with their start and end apart: 15, of which 9 were waited for; matrix products, arithmetic and copies ran while one was open for 1% of the time, Pallas kernels for 12%

profile of v8, /device:TPU:1, one launch (start us, length us, event | category | flops | bytes accessed | tf_op | source)
XLA Modules:
  0.0 209.1 jit_solution(3080109594847162431)
XLA Ops:
  7.2 0.6 pad_add_fusion.place
  7.8 2.1 %shard_map.67 = (bf16[16,16,128]{2,1,0:T(8,128)(2,1)}, s32[128]{0:T(128)}) custom-call(s32[10]{0:T(128)} %own.1, s32[4]{0:T(128)} %pad_add_fusion.place, bf16[10,2,96,128]{3,2,1,0:T(8,128)(2,1)} %right.1), custom_call_target="tpu_custom_call" | custom-call | tf_op jit(solution)/shard_map/pallas_call | solution.py:410
  9.9 15.8 %all-to-all-start = ((bf16[16,16,128]{2,1,0:T(8,128)(2,1)}), bf16[16,16,128]{2,1,0:T(8,128)(2,1)S(1)}, u32[]{:S(2)}, u32[]{:S(2)}) async-start(bf16[16,16,128]{2,1,0:T(8,128)(2,1)} %get-tuple-element.31), calls=%async_computation | async-start | bytes 131072 | tf_op jit(solution)/shard_map/all_to_all | solution.py:403
  25.7 1.0 copy-done.8
  26.7 1.0 copy-done.9
  27.8 0.7 copy-done.11
  28.4 2.0 shard_map.68
  30.5 6.8 %all-to-all-done = bf16[16,16,128]{2,1,0:T(8,128)(2,1)S(1)} async-done(((bf16[16,16,128]{2,1,0:T(8,128)(2,1)}), bf16[16,16,128]{2,1,0:T(8,128)(2,1)S(1)}, u32[]{:S(2)}, u32[]{:S(2)}) %all-to-all-start) | async-done | bytes 65568 | tf_op jit(solution)/shard_map/all_to_all | solution.py:403
  37.3 4.7 %all-to-all-start.1 = ((bf16[16,192,128]{2,1,0:T(8,128)(2,1)}), bf16[16,192,128]{2,1,0:T(8,128)(2,1)S(1)}, u32[]{:S(2)}, u32[]{:S(2)}) async-start(bf16[16,192,128]{2,1,0:T(8,128)(2,1)} %get-tuple-element.32), calls=%async_computation.1 | async-start | bytes 1572864 | tf_op jit(solution)/shard_map/all_to_all | solution.py:403
  42.0 3.1 %collective-permute-start = (bf16[16,16,128]{2,1,0:T(8,128)(2,1)S(1)}, bf16[16,16,128]{2,1,0:T(8,128)(2,1)S(1)}, u32[]{:S(2)}, u32[]{:S(2)}) collective-permute-start(bf16[16,16,128]{2,1,0:T(8,128)(2,1)S(1)} %all-to-all-done), channel_id=1, source_target_pairs={{0,128},{128,256},{256,384},{384,0},{1,129},{129,257},{257,385},{3... | collective-permute-start | bytes 196616 | tf_op jit(solution)/shard_map/ppermute | solution.py:397
  45.1 3.4 %collective-permute-start.1 = (bf16[16,16,128]{2,1,0:T(8,128)(2,1)S(1)}, bf16[16,16,128]{2,1,0:T(8,128)(2,1)S(1)}, u32[]{:S(2)}, u32[]{:S(2)}) collective-permute-start(bf16[16,16,128]{2,1,0:T(8,128)(2,1)S(1)} %all-to-all-done), channel_id=1, source_target_pairs={{0,384},{128,0},{256,128},{384,256},{1,385},{129,1},{257,129},{385... | collective-permute-start | bytes 196616 | tf_op jit(solution)/shard_map/ppermute | solution.py:397
  48.5 3.4 %collective-permute-start.2 = (bf16[16,16,128]{2,1,0:T(8,128)(2,1)S(1)}, bf16[16,16,128]{2,1,0:T(8,128)(2,1)S(1)}, u32[]{:S(2)}, u32[]{:S(2)}) collective-permute-start(bf16[16,16,128]{2,1,0:T(8,128)(2,1)S(1)} %all-to-all-done), channel_id=1, source_target_pairs={{0,256},{128,384},{256,0},{384,128},{1,257},{129,385},{257,1},{385... | collective-permute-start | bytes 196616 | tf_op jit(solution)/shard_map/ppermute | solution.py:397
  52.0 3.3 %collective-permute-done.2 = bf16[16,16,128]{2,1,0:T(8,128)(2,1)S(1)} collective-permute-done((bf16[16,16,128]{2,1,0:T(8,128)(2,1)S(1)}, bf16[16,16,128]{2,1,0:T(8,128)(2,1)S(1)}, u32[]{:S(2)}, u32[]{:S(2)}) %collective-permute-start.2) | collective-permute-done | bytes 65568 | tf_op jit(solution)/shard_map/ppermute | solution.py:397
  55.4 3.2 %collective-permute-start.3 = (bf16[4,16,16,128]{3,2,1,0:T(8,128)(2,1)S(1)}, bf16[4,16,16,128]{3,2,1,0:T(8,128)(2,1)S(1)}, u32[]{:S(2)}, u32[]{:S(2)}) collective-permute-start(bf16[4,16,16,128]{3,2,1,0:T(8,128)(2,1)S(1)} %get-tuple-element.56), channel_id=1, source_target_pairs={{0,32},{32,64},{64,96},{96,0},{1,33},{33,65},{65,97},{97,1},{2,34}... | collective-permute-start | bytes 786440 | tf_op jit(solution)/shard_map/ppermute | solution.py:397
  58.6 3.4 %collective-permute-start.4 = (bf16[4,16,16,128]{3,2,1,0:T(8,128)(2,1)S(1)}, bf16[4,16,16,128]{3,2,1,0:T(8,128)(2,1)S(1)}, u32[]{:S(2)}, u32[]{:S(2)}) collective-permute-start(bf16[4,16,16,128]{3,2,1,0:T(8,128)(2,1)S(1)} %get-tuple-element.56), channel_id=1, source_target_pairs={{0,96},{32,0},{64,32},{96,64},{1,97},{33,1},{65,33},{97,65},{2,98}... | collective-permute-start | bytes 786440 | tf_op jit(solution)/shard_map/ppermute | solution.py:397
  61.9 3.5 %collective-permute-start.5 = (bf16[4,16,16,128]{3,2,1,0:T(8,128)(2,1)S(1)}, bf16[4,16,16,128]{3,2,1,0:T(8,128)(2,1)S(1)}, u32[]{:S(2)}, u32[]{:S(2)}) collective-permute-start(bf16[4,16,16,128]{3,2,1,0:T(8,128)(2,1)S(1)} %get-tuple-element.56), channel_id=1, source_target_pairs={{0,64},{32,96},{64,0},{96,32},{1,65},{33,97},{65,1},{97,33},{2,66}... | collective-permute-start | bytes 786440 | tf_op jit(solution)/shard_map/ppermute | solution.py:397
  66.0 5.4 %collective-permute-done.5 = bf16[4,16,16,128]{3,2,1,0:T(8,128)(2,1)S(1)} collective-permute-done((bf16[4,16,16,128]{3,2,1,0:T(8,128)(2,1)S(1)}, bf16[4,16,16,128]{3,2,1,0:T(8,128)(2,1)S(1)}, u32[]{:S(2)}, u32[]{:S(2)}) %collective-permute-start.5) | collective-permute-done | bytes 262176 | tf_op jit(solution)/shard_map/ppermute | solution.py:397
  71.6 5.6 %collective-permute-start.6 = (bf16[16,16,16,128]{3,2,1,0:T(8,128)(2,1)S(1)}, bf16[16,16,16,128]{3,2,1,0:T(8,128)(2,1)S(1)}, u32[]{:S(2)}, u32[]{:S(2)}) collective-permute-start(bf16[16,16,16,128]{3,2,1,0:T(8,128)(2,1)S(1)} %bitcast.23), channel_id=1, source_target_pairs={{0,16},{16,0},{1,17},{17,1},{2,18},{18,2},{3,19},{19,3},{4,20},{20... | collective-permute-start | bytes 3145736 | tf_op jit(solution)/shard_map/ppermute | solution.py:399
  77.2 2.3 %collective-permute-done.6.far = bf16[16,16,16,128]{3,2,1,0:T(8,128)(2,1)S(1)} collective-permute-done((bf16[16,16,16,128]{3,2,1,0:T(8,128)(2,1)S(1)}, bf16[16,16,16,128]{3,2,1,0:T(8,128)(2,1)S(1)}, u32[]{:S(2)}, u32[]{:S(2)}) %collective-permute-start.6) | collective-permute-done | bytes 1048608 | tf_op jit(solution)/shard_map/ppermute | solution.py:399
  79.5 2.9 %shard_map.69.right = bf16[16,384,128]{2,1,0:T(8,128)(2,1)S(1)} custom-call(s32[4]{0:T(128)S(1)} %copy-done.10, bf16[16,16,16,128]{3,2,1,0:T(8,128)(2,1)S(1)} %bitcast.24, bf16[16,16,16,128]{3,2,1,0:T(8,128)(2,1)S(1)} %collective-permute-done.6.far), custom_call_target="tpu_custom_call" | custom-call | flops 800000000 | bytes 4000000 | tf_op jit(solution)/shard_map/pallas_call | solution.py:426
  82.4 2.2 %shard_map.70 = (f32[2,128,128]{2,1,0:T(8,128)S(1)}, f32[2,128,128]{2,1,0:T(8,128)S(1)}) custom-call(bf16[16,192,128]{2,1,0:T(8,128)(2,1)S(1)} %all-to-all-done.1.state, bf16[16,384,128]{2,1,0:T(8,128)(2,1)S(1)} %shard_map.69.right), custom_call_target="tpu_custom_call" | custom-call | flops 300000000 | bytes 4000000 | tf_op jit(solution)/shard_map/pallas_call | solution.py:435
  84.7 14.0 %all_to_all.30 = f32[32,8,128]{2,1,0:T(8,128)S(1)} all-to-all(f32[32,8,128]{2,1,0:T(8,128)S(1)} %bitcast.30), channel_id=1, replica_groups=mesh['x'=4,'y'=4,'c'=2,'z'=16] {'x','y','c'}, dimensions={0} | all-to-all | bytes 262144 | tf_op jit(solution)/shard_map/all_to_all | solution.py:403
  98.7 2.8 %shard_map.71 = (f32[16,12,8,128]{3,2,1,0:T(8,128)S(1)}, f32[16,12,8,128]{3,2,1,0:T(8,128)}) custom-call(s32[4]{0:T(128)S(1)} %copy-done.10, bf16[16,192,128]{2,1,0:T(8,128)(2,1)S(1)} %all-to-all-done.1.state, f32[2,128,128]{2,1,0:T(8,128)S(1)} %get-tuple-element.34.panel, f32[8,128]{1,0:T(8,128)S(1)} %reduce_sum.9._), custom_call_target="tpu_custom_call" | custom-call | flops 400000000 | bytes 4000000 | tf_op jit(solution)/shard_map/pallas_call | solution.py:440
  101.5 2.3 %collective-permute-start.7 = (f32[16,12,8,128]{3,2,1,0:T(8,128)}, f32[16,12,8,128]{3,2,1,0:T(8,128)S(1)}, u32[]{:S(2)}, u32[]{:S(2)}) collective-permute-start(f32[16,12,8,128]{3,2,1,0:T(8,128)} %get-tuple-element.39), channel_id=1, source_target_pairs={{0,16},{16,0},{1,17},{17,1},{2,18},{18,2},{3,19},{19,3},{4,20},{20... | collective-permute-start | bytes 2359304 | tf_op jit(solution)/shard_map/ppermute | solution.py:443
  103.8 0.7 broadcast_in_dim.2
  104.5 3.6 %all-to-all-start.3 = ((f32[32,8,128]{2,1,0:T(8,128)}), f32[32,8,128]{2,1,0:T(8,128)S(1)}, u32[]{:S(2)}, u32[]{:S(2)}) async-start(f32[32,8,128]{2,1,0:T(8,128)} %broadcast_in_dim.2), calls=%async_computation.3 | async-start | bytes 262144 | tf_op jit(solution)/shard_map/all_to_all | solution.py:403
  108.1 1.0 add.3
  109.1 6.8 %all-to-all-done.3 = f32[32,8,128]{2,1,0:T(8,128)S(1)} async-done(((f32[32,8,128]{2,1,0:T(8,128)}), f32[32,8,128]{2,1,0:T(8,128)S(1)}, u32[]{:S(2)}, u32[]{:S(2)}) %all-to-all-start.3) | async-done | bytes 131104 | tf_op jit(solution)/shard_map/all_to_all | solution.py:403
  115.9 3.6 %all-to-all-start.4 = ((f32[16,96,128]{2,1,0:T(8,128)}), f32[16,96,128]{2,1,0:T(8,128)S(1)}, u32[]{:S(2)}, u32[]{:S(2)}) async-start(f32[16,96,128]{2,1,0:T(8,128)} %bitcast.31), calls=%async_computation.4 | async-start | bytes 1572864 | tf_op jit(solution)/shard_map/all_to_all | solution.py:403
  119.6 11.8 %shard_map.72.inverse = f32[2,128,128]{2,1,0:T(8,128)S(1)} custom-call(f32[2,128,128]{2,1,0:T(8,128)S(1)} %bitcast.29), custom_call_target="tpu_custom_call" | custom-call | flops 4000000000 | bytes 4000000 | tf_op jit(solution)/shard_map/pallas_call | solution.py:447
  131.4 0.9 all-to-all-done.4.parts
  132.3 0.9 shard_map.73.mine
  133.2 31.0 %all-gather = bf16[1792,128]{1,0:T(8,128)(2,1)S(1)} all-gather(bf16[112,128]{1,0:T(8,128)(2,1)S(1)} %shard_map.73.mine), channel_id=2, replica_groups=mesh['x'=4,'y'=4,'c'=2,'z'=16] {'z'}, dimensions={0}, use_global_device_ids=true | all-gather | bytes 487424 | tf_op jit(solution)/shard_map/all_gather | solution.py:463
  164.2 0.9 shard_map.74
  165.1 1.0 copy-done.2
  166.1 5.8 %all-to-all-start.5 = ((bf16[16,320,128]{2,1,0:T(8,128)(2,1)}), bf16[16,320,128]{2,1,0:T(8,128)(2,1)S(1)}, u32[]{:S(2)}, u32[]{:S(2)}) async-start(bf16[16,320,128]{2,1,0:T(8,128)(2,1)} %copy-done.2), calls=%async_computation.5 | async-start | bytes 2621440 | tf_op jit(solution)/shard_map/all_to_all | solution.py:403
  172.0 1.1 copy-done.1
  173.1 0.9 shard_map.75.turned
  174.0 0.9 copy-done.4
  174.9 0.9 shard_map.76
  175.9 2.1 %copy-done.3 = bf16[80,192,128]{2,1,0:T(8,128)(2,1)S(1)} copy-done((bf16[80,192,128]{2,1,0:T(8,128)(2,1)S(1)}, bf16[80,192,128]{2,1,0:T(8,128)(2,1)}, u32[]{:S(2)}) %copy-start.3) | copy-done | bytes 3932184
  178.0 2.9 %shard_map.77 = (f32[2,128,128]{2,1,0:T(8,128)S(1)}, bf16[2,128,1536]{2,1,0:T(8,128)(2,1)S(1)}) custom-call(s32[128]{0:T(128)S(1)} %copy-done.12, s32[4]{0:T(128)S(1)} %copy-done.10, bf16[16,5,192,128]{3,2,1,0:T(8,128)(2,1)S(1)} %bitcast.25, bf16[16,384,128]{2,1,0:T(8,128)(2,1)S(1)} %shard_map.69.right), custom_call_target="tpu_custom_call" | custom-call | flops 300000000 | bytes 4000000 | tf_op jit(solution)/shard_map/pallas_call | solution.py:464
  180.9 0.9 copy-done.6
  181.8 4.1 %all-to-all-done.5.near = bf16[16,320,128]{2,1,0:T(8,128)(2,1)S(1)} async-done(((bf16[16,320,128]{2,1,0:T(8,128)(2,1)}), bf16[16,320,128]{2,1,0:T(8,128)(2,1)S(1)}, u32[]{:S(2)}, u32[]{:S(2)}) %all-to-all-start.5) | async-done | bytes 1310752 | tf_op jit(solution)/shard_map/all_to_all | solution.py:403
  185.8 9.3 %collective-permute-start.8 = (bf16[16,320,128]{2,1,0:T(8,128)(2,1)S(1)}, bf16[16,320,128]{2,1,0:T(8,128)(2,1)S(1)}, u32[]{:S(2)}, u32[]{:S(2)}) collective-permute-start(bf16[16,320,128]{2,1,0:T(8,128)(2,1)S(1)} %all-to-all-done.5.near), channel_id=1, source_target_pairs={{0,16},{16,0},{1,17},{17,1},{2,18},{18,2},{3,19},{19,3},{4,20},{20... | collective-permute-start | bytes 3932168 | tf_op jit(solution)/shard_map/ppermute | solution.py:481
  195.1 2.6 %collective-permute-done.8.far = bf16[16,320,128]{2,1,0:T(8,128)(2,1)S(1)} collective-permute-done((bf16[16,320,128]{2,1,0:T(8,128)(2,1)S(1)}, bf16[16,320,128]{2,1,0:T(8,128)(2,1)S(1)}, u32[]{:S(2)}, u32[]{:S(2)}) %collective-permute-start.8) | collective-permute-done | bytes 1310752 | tf_op jit(solution)/shard_map/ppermute | solution.py:481
  197.7 1.7 shard_map.79
  199.4 2.8 %shard_map.78 = (bf16[4,128,1536]{2,1,0:T(8,128)(2,1)}, f32[4,128,128]{2,1,0:T(8,128)}) custom-call(s32[128]{0:T(128)S(1)} %copy-done.12, s32[4]{0:T(128)S(1)} %copy-done.10, bf16[2,128,1536]{2,1,0:T(8,128)(2,1)S(1)} %copy-done.5, bf16[2,128,1536]{2,1,0:T(8,128)(2,1)S(1)} %copy-done.7, bf16[16,320,128]{2,1,0:T(8,128)(2,1)S(1)} %all-to-all-done.5.near, ...), custom_call_target="tpu_custom_call" | custom-call | flops 1200000000 | bytes 4000000 | tf_op jit(solution)/shard_map/pallas_call | solution.py:486
  (30 shorter events, 0.8 us)
Async XLA Ops:
  9.9 27.3 %all-to-all-start = ((bf16[16,16,128]{2,1,0:T(8,128)(2,1)}), bf16[16,16,128]{2,1,0:T(8,128)(2,1)S(1)}, u32[]{:S(2)}, u32[]{:S(2)}) async-start(bf16[16,16,128]{2,1,0:T(8,128)(2,1)} %get-tuple-element.31), calls=%async_computation | async-start | bytes 131072 | tf_op jit(solution)/shard_map/all_to_all | solution.py:403
  25.7 1.0 copy-start.8
  26.7 1.0 copy-start.9
  27.8 0.7 copy-start.11
  37.3 45.1 %all-to-all-start.1 = ((bf16[16,192,128]{2,1,0:T(8,128)(2,1)}), bf16[16,192,128]{2,1,0:T(8,128)(2,1)S(1)}, u32[]{:S(2)}, u32[]{:S(2)}) async-start(bf16[16,192,128]{2,1,0:T(8,128)(2,1)} %get-tuple-element.32), calls=%async_computation.1 | async-start | bytes 1572864 | tf_op jit(solution)/shard_map/all_to_all | solution.py:403
  41.9 37.5 %copy-start.10 = (s32[4]{0:T(128)S(1)}, s32[4]{0:T(128)}, u32[]{:S(2)}) copy-start(s32[4]{0:T(128)} %pad_add_fusion.place) | copy-start | bytes 52
  42.0 133.9 %all-gather.4.cloned.1.call-start = ((), (), s32[]{:S(2)}) async-start(), calls=%async_computation.6 | async-start | bytes 4177920 | tf_op jit(solution)/shard_map/all_gather | solution.py:437
  42.0 10.0 %collective-permute-start = (bf16[16,16,128]{2,1,0:T(8,128)(2,1)S(1)}, bf16[16,16,128]{2,1,0:T(8,128)(2,1)S(1)}, u32[]{:S(2)}, u32[]{:S(2)}) collective-permute-start(bf16[16,16,128]{2,1,0:T(8,128)(2,1)S(1)} %all-to-all-done), channel_id=1, source_target_pairs={{0,128},{128,256},{256,384},{384,0},{1,129},{129,257},{257,385},{3... | collective-permute-start | bytes 196616 | tf_op jit(solution)/shard_map/ppermute | solution.py:397
  45.1 6.8 %collective-permute-start.1 = (bf16[16,16,128]{2,1,0:T(8,128)(2,1)S(1)}, bf16[16,16,128]{2,1,0:T(8,128)(2,1)S(1)}, u32[]{:S(2)}, u32[]{:S(2)}) collective-permute-start(bf16[16,16,128]{2,1,0:T(8,128)(2,1)S(1)} %all-to-all-done), channel_id=1, source_target_pairs={{0,384},{128,0},{256,128},{384,256},{1,385},{129,1},{257,129},{385... | collective-permute-start | bytes 196616 | tf_op jit(solution)/shard_map/ppermute | solution.py:397
  48.5 6.8 %collective-permute-start.2 = (bf16[16,16,128]{2,1,0:T(8,128)(2,1)S(1)}, bf16[16,16,128]{2,1,0:T(8,128)(2,1)S(1)}, u32[]{:S(2)}, u32[]{:S(2)}) collective-permute-start(bf16[16,16,128]{2,1,0:T(8,128)(2,1)S(1)} %all-to-all-done), channel_id=1, source_target_pairs={{0,256},{128,384},{256,0},{384,128},{1,257},{129,385},{257,1},{385... | collective-permute-start | bytes 196616 | tf_op jit(solution)/shard_map/ppermute | solution.py:397
  55.4 10.1 %collective-permute-start.3 = (bf16[4,16,16,128]{3,2,1,0:T(8,128)(2,1)S(1)}, bf16[4,16,16,128]{3,2,1,0:T(8,128)(2,1)S(1)}, u32[]{:S(2)}, u32[]{:S(2)}) collective-permute-start(bf16[4,16,16,128]{3,2,1,0:T(8,128)(2,1)S(1)} %get-tuple-element.56), channel_id=1, source_target_pairs={{0,32},{32,64},{64,96},{96,0},{1,33},{33,65},{65,97},{97,1},{2,34}... | collective-permute-start | bytes 786440 | tf_op jit(solution)/shard_map/ppermute | solution.py:397
  58.6 7.4 %collective-permute-start.4 = (bf16[4,16,16,128]{3,2,1,0:T(8,128)(2,1)S(1)}, bf16[4,16,16,128]{3,2,1,0:T(8,128)(2,1)S(1)}, u32[]{:S(2)}, u32[]{:S(2)}) collective-permute-start(bf16[4,16,16,128]{3,2,1,0:T(8,128)(2,1)S(1)} %get-tuple-element.56), channel_id=1, source_target_pairs={{0,96},{32,0},{64,32},{96,64},{1,97},{33,1},{65,33},{97,65},{2,98}... | collective-permute-start | bytes 786440 | tf_op jit(solution)/shard_map/ppermute | solution.py:397
  61.9 9.5 %collective-permute-start.5 = (bf16[4,16,16,128]{3,2,1,0:T(8,128)(2,1)S(1)}, bf16[4,16,16,128]{3,2,1,0:T(8,128)(2,1)S(1)}, u32[]{:S(2)}, u32[]{:S(2)}) collective-permute-start(bf16[4,16,16,128]{3,2,1,0:T(8,128)(2,1)S(1)} %get-tuple-element.56), channel_id=1, source_target_pairs={{0,64},{32,96},{64,0},{96,32},{1,65},{33,97},{65,1},{97,33},{2,66}... | collective-permute-start | bytes 786440 | tf_op jit(solution)/shard_map/ppermute | solution.py:397
  71.6 7.9 %collective-permute-start.6 = (bf16[16,16,16,128]{3,2,1,0:T(8,128)(2,1)S(1)}, bf16[16,16,16,128]{3,2,1,0:T(8,128)(2,1)S(1)}, u32[]{:S(2)}, u32[]{:S(2)}) collective-permute-start(bf16[16,16,16,128]{3,2,1,0:T(8,128)(2,1)S(1)} %bitcast.23), channel_id=1, source_target_pairs={{0,16},{16,0},{1,17},{17,1},{2,18},{18,2},{3,19},{19,3},{4,20},{20... | collective-permute-start | bytes 3145736 | tf_op jit(solution)/shard_map/ppermute | solution.py:399
  82.4 19.1 %copy-start = (bf16[16,192,128]{2,1,0:T(8,128)(2,1)}, bf16[16,192,128]{2,1,0:T(8,128)(2,1)S(1)}, u32[]{:S(2)}) copy-start(bf16[16,192,128]{2,1,0:T(8,128)(2,1)S(1)} %all-to-all-done.1.state) | copy-start | bytes 2359300
  101.5 6.6 %collective-permute-start.7 = (f32[16,12,8,128]{3,2,1,0:T(8,128)}, f32[16,12,8,128]{3,2,1,0:T(8,128)S(1)}, u32[]{:S(2)}, u32[]{:S(2)}) collective-permute-start(f32[16,12,8,128]{3,2,1,0:T(8,128)} %get-tuple-element.39), channel_id=1, source_target_pairs={{0,16},{16,0},{1,17},{17,1},{2,18},{18,2},{3,19},{19,3},{4,20},{20... | collective-permute-start | bytes 2359304 | tf_op jit(solution)/shard_map/ppermute | solution.py:443
  104.5 11.4 %all-to-all-start.3 = ((f32[32,8,128]{2,1,0:T(8,128)}), f32[32,8,128]{2,1,0:T(8,128)S(1)}, u32[]{:S(2)}, u32[]{:S(2)}) async-start(f32[32,8,128]{2,1,0:T(8,128)} %broadcast_in_dim.2), calls=%async_computation.3 | async-start | bytes 262144 | tf_op jit(solution)/shard_map/all_to_all | solution.py:403
  115.9 16.4 %all-to-all-start.4 = ((f32[16,96,128]{2,1,0:T(8,128)}), f32[16,96,128]{2,1,0:T(8,128)S(1)}, u32[]{:S(2)}, u32[]{:S(2)}) async-start(f32[16,96,128]{2,1,0:T(8,128)} %bitcast.31), calls=%async_computation.4 | async-start | bytes 1572864 | tf_op jit(solution)/shard_map/all_to_all | solution.py:403
  119.5 44.7 %copy-start.12 = (s32[128]{0:T(128)S(1)}, s32[128]{0:T(128)}, u32[]{:S(2)}) copy-start(s32[128]{0:T(128)} %get-tuple-element.29.table) | copy-start | bytes 1540
  165.1 1.1 copy-start.2
  166.1 19.7 %all-to-all-start.5 = ((bf16[16,320,128]{2,1,0:T(8,128)(2,1)}), bf16[16,320,128]{2,1,0:T(8,128)(2,1)S(1)}, u32[]{:S(2)}, u32[]{:S(2)}) async-start(bf16[16,320,128]{2,1,0:T(8,128)(2,1)} %copy-done.2), calls=%async_computation.5 | async-start | bytes 2621440 | tf_op jit(solution)/shard_map/all_to_all | solution.py:403
  172.0 1.1 copy-start.1
  174.0 0.9 copy-start.4
  175.9 2.1 %copy-start.3 = (bf16[80,192,128]{2,1,0:T(8,128)(2,1)S(1)}, bf16[80,192,128]{2,1,0:T(8,128)(2,1)}, u32[]{:S(2)}) copy-start(bf16[80,192,128]{2,1,0:T(8,128)(2,1)} %all-gather.4.cloned.1.call-done) | copy-start | bytes 11796484
  180.9 0.9 copy-start.6
  185.8 13.6 %copy-start.5 = (bf16[2,128,1536]{2,1,0:T(8,128)(2,1)S(1)}, bf16[2,128,1536]{2,1,0:T(8,128)(2,1)}, u32[]{:S(2)}) copy-start(bf16[2,128,1536]{2,1,0:T(8,128)(2,1)} %copy-done.4) | copy-start | bytes 2359300
  185.8 13.6 %copy-start.7 = (bf16[2,128,1536]{2,1,0:T(8,128)(2,1)S(1)}, bf16[2,128,1536]{2,1,0:T(8,128)(2,1)}, u32[]{:S(2)}) copy-start(bf16[2,128,1536]{2,1,0:T(8,128)(2,1)} %copy-done.6) | copy-start | bytes 2359300
  185.8 11.9 %collective-permute-start.8 = (bf16[16,320,128]{2,1,0:T(8,128)(2,1)S(1)}, bf16[16,320,128]{2,1,0:T(8,128)(2,1)S(1)}, u32[]{:S(2)}, u32[]{:S(2)}) collective-permute-start(bf16[16,320,128]{2,1,0:T(8,128)(2,1)S(1)} %all-to-all-done.5.near), channel_id=1, source_target_pairs={{0,16},{16,0},{1,17},{17,1},{2,18},{18,2},{3,19},{19,3},{4,20},{20... | collective-permute-start | bytes 3932168 | tf_op jit(solution)/shard_map/ppermute | solution.py:481
Sparse Core Ops, SparseCore 0:
  84.8 70.7 all-gather.3

commit v9 on v8

--- a/solution.py
+++ b/solution.py
@@ -54,41 +54,52 @@
     return lax.broadcasted_iota(jnp.int32, shape, dim)
 
 
-COUNT, WORK, SECOND, HELPER, WHERE, FREE, SLOT, LIST, TABLE = 0, 17, 34, 51, 68, 80, 97, 114, 128
+COUNT, WORK, SECOND, HELPER, WHERE, BUSY, SLOT, VIA = 0, 17, 34, 51, 68, 80, 97, 114
+LIST, USED, GOOD, TABLE = 131, 140, 141, 142
 SECONDS = EXPERTS // 2
 NONE = GROUPS
+STEPS = (1, -1, 2, -2, 3, -3, 4, -4, 5, -5, 6, -6, 7, -7, 8)
+NEAR = 6
 
 
 def fill_table(own, table):
     for g in range(GROUPS + 1):
-        table[COUNT + g] = 0
+        for base in (COUNT, HELPER, BUSY, SLOT, VIA):
+            table[base + g] = 0
         table[WORK + g] = EXPERTS
         table[SECOND + g] = EXPERTS
-        table[HELPER + g] = 0
-        table[SLOT + g] = 0
-    for j in range(TABLE - LIST):
+    for j in range(SECONDS):
         table[LIST + j] = EXPERTS
+    table[USED] = 0
+    table[GOOD] = 1
     for e in range(EXPERTS):
         g = own[e]
         p = table[COUNT + g]
         table[COUNT + g] = p + 1
+        table[BUSY + g] = 1
         table[WORK + jnp.where(p == 0, g, NONE)] = e
         table[SECOND + jnp.where(p == 0, NONE, g)] = e
-    free = jnp.int32(0)
-    for g in range(GROUPS):
-        table[FREE + free] = g
-        free = free + jnp.where(table[COUNT + g] == 0, 1, 0)
-    used = jnp.int32(0)
+        table[WHERE + e] = g
     for e in range(EXPERTS):
         g = own[e]
-        second = table[SECOND + g] == e
-        h = table[FREE + used]
-        table[WORK + jnp.where(second, h, NONE)] = e
-        table[HELPER + jnp.where(second, g, NONE)] = h
-        table[WHERE + e] = jnp.where(second, h, g)
-        table[SLOT + jnp.where(second, g, NONE)] = used
-        table[LIST + jnp.where(second, used, SECONDS)] = e
-        used = used + jnp.where(second, 1, 0)
+
+        @pl.when(table[SECOND + g] == e)
+        def _():
+            h, via = jnp.int32(-1), jnp.int32(0)
+            for j, step in enumerate(STEPS):
+                other = (g + step) & (GROUPS - 1)
+                take = (h < 0) & (table[BUSY + other] == 0)
+                h, via = jnp.where(take, other, h), jnp.where(take, j, via)
+            table[BUSY + h] = 1
+            table[WORK + h] = e
+            table[HELPER + g] = h
+            table[WHERE + e] = h
+            table[VIA + g] = via
+            table[GOOD] = jnp.where(via < NEAR, table[GOOD], 0)
+            used = table[USED]
+            table[SLOT + g] = used
+            table[LIST + used] = e
+            table[USED] = used + 1
 
 
 def slice_right(own, place, right, out, table, held):
@@ -267,13 +278,26 @@
                 work[m, k + size :, :] -= change[k + size :, :]
 
 
-def scale_factor(place, inverse, parts, out):
+def scale_factor(place, inverse, parts, out, back, tiles):
     f = place[0] * 8 + place[1] * 2 + place[2]
     total = parts[0]
     for i in range(1, 16):
         total = total + parts[i]
     both = [dot(total, inverse[k], ((1,), (1,)), HIGHEST) for k in range(2)]
-    out[:96] = jnp.where(row_kinds(place) == 0, both[0], both[1]).astype(BF16)
+    kinds = row_kinds(place)
+    value = jnp.where(kinds == 0, both[0], both[1])
+    out[:96] = value.astype(BF16)
+    tiles[:96] = value
+    tiles[96:] = jnp.zeros((8, RANK), F32)
+    square = value * value
+    sums = [
+        jnp.sum(jnp.where(kinds == k, square, 0.0), axis=0, keepdims=True) for k in range(2)
+    ]
+    tail = jnp.concatenate(sums + [jnp.zeros((6, RANK), F32)], axis=0)
+    for z in range(GROUPS):
+        m = jnp.where(place[0] == (z & 3), 12, place_of(place[0], z))
+        tile = tiles[pl.ds(pl.multiple_of(8 * m, 8), 8), :]
+        back[z] = jnp.concatenate([tile, tail], axis=0).astype(BF16)
     half = jnp.where(f >= 16, 1, 0)
     start = pl.multiple_of(8 * f - 128 * half, 8)
     rows = inverse[half, pl.ds(start, 8), :]
@@ -301,27 +325,25 @@
 SECOND_ROWS, RIGHT_ROWS, SUM_ROWS, ROWS = 96, 208, 288, 320
 
 
-def select(table, place, mine, tiles, out, packed):
-    z = place[3]
+def pick(table, place, *refs):
+    via = table[VIA + place[3]]
+    value = refs[0][...]
+    for j in range(1, NEAR):
+        value = jnp.where(via == j, refs[j][...], value)
+    refs[NEAR][...] = value
+
+
+def select(table, place, mine, second, tiles, out, packed):
     packed[:SECOND_ROWS, :] = mine[:96, :]
-    packed[SECOND_ROWS:RIGHT_ROWS, :] = tiles[table[HELPER + z]]
-    m = place_of(place[0], z)
-    start = pl.multiple_of((m >> 1) * 16, 16)
-    upper = (m & 1) == 1
-    kinds = row_kinds(place)
+    packed[SECOND_ROWS:RIGHT_ROWS, :] = second[...]
     sums = []
     for e in range(0, EXPERTS, 2):
-        pair = []
-        for i in range(2):
-            p = table[WHERE + e + i]
-            value = tiles[p, pl.ds(start, 16), :].astype(F32)
-            pair.append(jnp.where(upper, value[8:], value[:8]))
-            whole = tiles[p, :96, :].astype(F32)
-            square = whole * whole
-            for k in range(2):
-                sums.append(jnp.sum(jnp.where(kinds == k, square, 0.0), axis=0, keepdims=True))
+        pair = [tiles[table[WHERE + e + i]].astype(F32) for i in range(2)]
+        sums += [value[8:10] for value in pair]
         first = RIGHT_ROWS + e * 8
-        packed[first : first + 16, :] = jnp.concatenate(pair, axis=0).astype(BF16)
+        packed[first : first + 16, :] = jnp.concatenate(
+            [value[:8] for value in pair], axis=0
+        ).astype(BF16)
     sums.append(jnp.zeros((ROWS - SUM_ROWS - 2 * EXPERTS, RANK), F32))
     packed[SUM_ROWS:, :] = jnp.concatenate(sums, axis=0).astype(BF16)
     value = packed[...]
@@ -451,16 +473,37 @@
         n_in=1,
         flops=4_000_000_000,
     )(gram)
-    mine = call(scale_factor, sds((112, RANK), BF16), specs=[SMEM, VMEM, VMEM], flops=100_000_000)(
-        place, inverse, parts
-    )
+    mine, back = call(
+        scale_factor,
+        (sds((112, RANK), BF16), sds((16, 16, RANK), BF16)),
+        [pltpu.VMEM((104, RANK), F32)],
+        specs=[SMEM, VMEM, VMEM],
+        flops=100_000_000,
+    )(place, inverse, parts)
     turned = call(turn, sds((2, 128, HID), BF16), specs=[SMEM, SMEM, VMEM], flops=100_000_000)(
         table, place, state
     )
     left, low = call(
         orthonormal, (two, sds((2, 128, RANK), BF16)), specs=[SMEM, SMEM, VMEM, VMEM], flops=100_000_000
     )(table, place, panel, inverse)
-    tiles = lax.all_gather(mine, "z")
+
+    def from_near(mine, back):
+        moved = [
+            lax.ppermute(mine, "z", [(i, (i - step) % GROUPS) for i in range(GROUPS)])
+            for step in STEPS[:NEAR]
+        ]
+        tiles = exchange(back, "z")
+        other = call(pick, sds((112, RANK), BF16), specs=[SMEM, SMEM] + [VMEM] * NEAR)(
+            table, place, *moved
+        )
+        return tiles, other
+
+    def from_any(mine, back):
+        gathered = lax.all_gather(mine, "z")
+        other = lax.dynamic_index_in_dim(gathered, table[HELPER + place[3]], 0, False)
+        return exchange(back, "z"), other
+
+    tiles, other = lax.cond(table[GOOD] == 1, from_near, from_any, mine, back)
     second_panel, second_turned = call(
         second_panels,
         (two, sds((2, 128, HID), BF16)),
@@ -472,8 +515,8 @@
         select,
         sds((16, ROWS, RANK), BF16),
         [pltpu.VMEM((ROWS, RANK), BF16)],
-        specs=[SMEM, SMEM, VMEM, VMEM],
-    )(table, place, mine, tiles)
+        specs=[SMEM, SMEM, VMEM, VMEM, VMEM],
+    )(table, place, mine, other, tiles)
     near = exchange(chosen, XY)
     near, turned, low, left, second_panel, second_turned = barrier(
         (near, turned, low, left, second_panel, second_turned)

time: 210 us -> 221 us (1.052)
  blocking collectives: 45.1 us -> 13.9 us
  starting transfers between devices: 70.8 us -> 102 us
  waiting for transfers between devices: 32.8 us -> 39.9 us
    all_gather x1 -> x0, blocking collectives: 31 us -> none  [shards(): tiles = lax.all_gather(mine, 'z')]
    ppermute x0 -> x6, starting transfers between devices: none -> 21.8 us  [from_near(): lax.ppermute(mine, 'z', [(i, (i - step) % GROUPS) for i in range(GROUPS)])]
    all_to_all x5 -> x6, starting transfers between devices: 33.5 us -> 45.1 us  [exchange(): return lax.all_to_all(x, axis, split_axis=0, concat_axis=0, tiled=True)]
    ppermute x0 -> x6, waiting for transfers between devices: none -> 5.67 us  [from_near(): lax.ppermute(mine, 'z', [(i, (i - step) % GROUPS) for i in range(GROUPS)])]
    all_to_all x5 -> x6, waiting for transfers between devices: 18.6 us -> 19.8 us  [exchange(): return lax.all_to_all(x, axis, split_axis=0, concat_axis=0, tiled=True)]
    unnamed x26 -> x20, local copies, waits for them, and re-layouts: 8.78 us -> 8.12 us
  transfers between devices with their start and end apart: 15 -> 22, of which waited for: 9 -> 9; matrix products, arithmetic and copies ran while one was open for 1% -> 2% of each run, Pallas kernels for 12% -> 13%
where the time goes in v9:
time: 221 us; the launch traced here: 219 us
  starting transfers between devices  102 us (46%)
  waiting for transfers between devices  39.9 us (18%)
  Pallas kernels  36.5 us (17%)
  between operations  15 us (7%)
  blocking collectives  13.9 us (6%)
  local copies, waits for them, and re-layouts  9.41 us (4%)
  other arithmetic  2.4 us (1%)
    all_to_all x6, starting transfers between devices, exchange(): return lax.all_to_all(x, axis, split_axis=0, concat_axis=0, tiled=True)  45.1 us
    ppermute x6, starting transfers between devices, from_near(): lax.ppermute(mine, 'z', [(i, (i - step) % GROUPS) for i in range(GROUPS)])  21.8 us
    ppermute x6, starting transfers between devices, gather_slices(): lax.ppermute(x, axis, ring((4 - d) % 4))  20 us
    all_to_all x6, waiting for transfers between devices, exchange(): return lax.all_to_all(x, axis, split_axis=0, concat_axis=0, tiled=True)  19.8 us
    all_to_all x1, blocking collectives, exchange(): return lax.all_to_all(x, axis, split_axis=0, concat_axis=0, tiled=True)  13.9 us
    pallas_call x1, Pallas kernels, shards(): call(functools.partial(invert, size=32), square, [pltpu.VMEM((2, RANK, 2...  11.8 us
    ppermute x6, waiting for transfers between devices, gather_slices(): lax.ppermute(x, axis, ring((4 - d) % 4))  9.49 us
    unnamed x20, local copies, waits for them, and re-layouts  8.12 us
  transfers between devices with their start and end apart: 22, of which 9 were waited for; matrix products, arithmetic and copies ran while one was open for 2% of the time, Pallas kernels for 13%

profile of v9, /device:TPU:1, one launch (start us, length us, event | category | flops | bytes accessed | tf_op | source)
XLA Modules:
  0.0 219.3 jit_solution(11938220969235832372)
XLA Ops:
  7.3 2.3 %shard_map.67 = (bf16[16,16,128]{2,1,0:T(8,128)(2,1)}, s32[142]{0:T(256)S(1)}) custom-call(s32[10]{0:T(128)} %own.1, s32[4]{0:T(128)S(1)} %pad_add_fusion.place, bf16[10,2,96,128]{3,2,1,0:T(8,128)(2,1)} %right.1), custom_call_target="tpu_custom_call" | custom-call | tf_op jit(solution)/shard_map/pallas_call | solution.py:432
  9.6 15.8 %all-to-all-start.2 = ((bf16[16,16,128]{2,1,0:T(8,128)(2,1)}), bf16[16,16,128]{2,1,0:T(8,128)(2,1)S(1)}, u32[]{:S(2)}, u32[]{:S(2)}) async-start(bf16[16,16,128]{2,1,0:T(8,128)(2,1)} %get-tuple-element.59), calls=%async_computation.2 | async-start | bytes 131072 | tf_op jit(solution)/shard_map/all_to_all | solution.py:425
  25.4 1.0 copy-done.8
  26.4 1.0 copy-done.9
  27.4 2.0 shard_map.68
  29.4 7.5 %all-to-all-done.2 = bf16[16,16,128]{2,1,0:T(8,128)(2,1)S(1)} async-done(((bf16[16,16,128]{2,1,0:T(8,128)(2,1)}), bf16[16,16,128]{2,1,0:T(8,128)(2,1)S(1)}, u32[]{:S(2)}, u32[]{:S(2)}) %all-to-all-start.2) | async-done | bytes 65568 | tf_op jit(solution)/shard_map/all_to_all | solution.py:425
  36.9 4.0 %all-to-all-start.3 = ((bf16[16,192,128]{2,1,0:T(8,128)(2,1)}), bf16[16,192,128]{2,1,0:T(8,128)(2,1)S(1)}, u32[]{:S(2)}, u32[]{:S(2)}) async-start(bf16[16,192,128]{2,1,0:T(8,128)(2,1)} %get-tuple-element.60), calls=%async_computation.3 | async-start | bytes 1572864 | tf_op jit(solution)/shard_map/all_to_all | solution.py:425
  41.0 3.1 %collective-permute-start.6 = (bf16[16,16,128]{2,1,0:T(8,128)(2,1)S(1)}, bf16[16,16,128]{2,1,0:T(8,128)(2,1)S(1)}, u32[]{:S(2)}, u32[]{:S(2)}) collective-permute-start(bf16[16,16,128]{2,1,0:T(8,128)(2,1)S(1)} %all-to-all-done.2), channel_id=1, source_target_pairs={{0,128},{128,256},{256,384},{384,0},{1,129},{129,257},{257,385},{3... | collective-permute-start | bytes 196616 | tf_op jit(solution)/shard_map/ppermute | solution.py:419
  44.1 3.4 %collective-permute-start.7 = (bf16[16,16,128]{2,1,0:T(8,128)(2,1)S(1)}, bf16[16,16,128]{2,1,0:T(8,128)(2,1)S(1)}, u32[]{:S(2)}, u32[]{:S(2)}) collective-permute-start(bf16[16,16,128]{2,1,0:T(8,128)(2,1)S(1)} %all-to-all-done.2), channel_id=1, source_target_pairs={{0,384},{128,0},{256,128},{384,256},{1,385},{129,1},{257,129},{385... | collective-permute-start | bytes 196616 | tf_op jit(solution)/shard_map/ppermute | solution.py:419
  47.5 3.4 %collective-permute-start.8 = (bf16[16,16,128]{2,1,0:T(8,128)(2,1)S(1)}, bf16[16,16,128]{2,1,0:T(8,128)(2,1)S(1)}, u32[]{:S(2)}, u32[]{:S(2)}) collective-permute-start(bf16[16,16,128]{2,1,0:T(8,128)(2,1)S(1)} %all-to-all-done.2), channel_id=1, source_target_pairs={{0,256},{128,384},{256,0},{384,128},{1,257},{129,385},{257,1},{385... | collective-permute-start | bytes 196616 | tf_op jit(solution)/shard_map/ppermute | solution.py:419
  51.0 3.3 %collective-permute-done.8 = bf16[16,16,128]{2,1,0:T(8,128)(2,1)S(1)} collective-permute-done((bf16[16,16,128]{2,1,0:T(8,128)(2,1)S(1)}, bf16[16,16,128]{2,1,0:T(8,128)(2,1)S(1)}, u32[]{:S(2)}, u32[]{:S(2)}) %collective-permute-start.8) | collective-permute-done | bytes 65568 | tf_op jit(solution)/shard_map/ppermute | solution.py:419
  54.3 3.2 %collective-permute-start.9 = (bf16[4,16,16,128]{3,2,1,0:T(8,128)(2,1)S(1)}, bf16[4,16,16,128]{3,2,1,0:T(8,128)(2,1)S(1)}, u32[]{:S(2)}, u32[]{:S(2)}) collective-permute-start(bf16[4,16,16,128]{3,2,1,0:T(8,128)(2,1)S(1)} %get-tuple-element.88), channel_id=1, source_target_pairs={{0,32},{32,64},{64,96},{96,0},{1,33},{33,65},{65,97},{97,1},{2,34}... | collective-permute-start | bytes 786440 | tf_op jit(solution)/shard_map/ppermute | solution.py:419
  57.6 3.4 %collective-permute-start.10 = (bf16[4,16,16,128]{3,2,1,0:T(8,128)(2,1)S(1)}, bf16[4,16,16,128]{3,2,1,0:T(8,128)(2,1)S(1)}, u32[]{:S(2)}, u32[]{:S(2)}) collective-permute-start(bf16[4,16,16,128]{3,2,1,0:T(8,128)(2,1)S(1)} %get-tuple-element.88), channel_id=1, source_target_pairs={{0,96},{32,0},{64,32},{96,64},{1,97},{33,1},{65,33},{97,65},{2,98}... | collective-permute-start | bytes 786440 | tf_op jit(solution)/shard_map/ppermute | solution.py:419
  60.9 3.5 %collective-permute-start.11 = (bf16[4,16,16,128]{3,2,1,0:T(8,128)(2,1)S(1)}, bf16[4,16,16,128]{3,2,1,0:T(8,128)(2,1)S(1)}, u32[]{:S(2)}, u32[]{:S(2)}) collective-permute-start(bf16[4,16,16,128]{3,2,1,0:T(8,128)(2,1)S(1)} %get-tuple-element.88), channel_id=1, source_target_pairs={{0,64},{32,96},{64,0},{96,32},{1,65},{33,97},{65,1},{97,33},{2,66}... | collective-permute-start | bytes 786440 | tf_op jit(solution)/shard_map/ppermute | solution.py:419
  65.0 5.7 %collective-permute-done.11 = bf16[4,16,16,128]{3,2,1,0:T(8,128)(2,1)S(1)} collective-permute-done((bf16[4,16,16,128]{3,2,1,0:T(8,128)(2,1)S(1)}, bf16[4,16,16,128]{3,2,1,0:T(8,128)(2,1)S(1)}, u32[]{:S(2)}, u32[]{:S(2)}) %collective-permute-start.11) | collective-permute-done | bytes 262176 | tf_op jit(solution)/shard_map/ppermute | solution.py:419
  70.8 5.6 %collective-permute-start.12 = (bf16[16,16,16,128]{3,2,1,0:T(8,128)(2,1)S(1)}, bf16[16,16,16,128]{3,2,1,0:T(8,128)(2,1)S(1)}, u32[]{:S(2)}, u32[]{:S(2)}) collective-permute-start(bf16[16,16,16,128]{3,2,1,0:T(8,128)(2,1)S(1)} %bitcast.27), channel_id=1, source_target_pairs={{0,16},{16,0},{1,17},{17,1},{2,18},{18,2},{3,19},{19,3},{4,20},{20... | collective-permute-start | bytes 3145736 | tf_op jit(solution)/shard_map/ppermute | solution.py:421
  76.4 2.3 %collective-permute-done.12.far = bf16[16,16,16,128]{3,2,1,0:T(8,128)(2,1)S(1)} collective-permute-done((bf16[16,16,16,128]{3,2,1,0:T(8,128)(2,1)S(1)}, bf16[16,16,16,128]{3,2,1,0:T(8,128)(2,1)S(1)}, u32[]{:S(2)}, u32[]{:S(2)}) %collective-permute-start.12) | collective-permute-done | bytes 1048608 | tf_op jit(solution)/shard_map/ppermute | solution.py:421
  78.6 2.9 %shard_map.69.right = bf16[16,384,128]{2,1,0:T(8,128)(2,1)S(1)} custom-call(s32[4]{0:T(128)S(1)} %pad_add_fusion.place, bf16[16,16,16,128]{3,2,1,0:T(8,128)(2,1)S(1)} %bitcast.28, bf16[16,16,16,128]{3,2,1,0:T(8,128)(2,1)S(1)} %collective-permute-done.12.far), custom_call_target="tpu_custom_call" | custom-call | flops 800000000 | bytes 4000000 | tf_op jit(solution)/shard_map/pallas_call | solution.py:448
  81.6 2.2 %shard_map.70 = (f32[2,128,128]{2,1,0:T(8,128)S(1)}, f32[2,128,128]{2,1,0:T(8,128)S(1)}) custom-call(bf16[16,192,128]{2,1,0:T(8,128)(2,1)S(1)} %all-to-all-done.3.state, bf16[16,384,128]{2,1,0:T(8,128)(2,1)S(1)} %shard_map.69.right), custom_call_target="tpu_custom_call" | custom-call | flops 300000000 | bytes 4000000 | tf_op jit(solution)/shard_map/pallas_call | solution.py:457
  83.8 13.9 %all_to_all.38 = f32[32,8,128]{2,1,0:T(8,128)S(1)} all-to-all(f32[32,8,128]{2,1,0:T(8,128)S(1)} %bitcast.33), channel_id=1, replica_groups=mesh['x'=4,'y'=4,'c'=2,'z'=16] {'x','y','c'}, dimensions={0} | all-to-all | bytes 262144 | tf_op jit(solution)/shard_map/all_to_all | solution.py:425
  97.8 2.8 %shard_map.71 = (f32[16,12,8,128]{3,2,1,0:T(8,128)S(1)}, f32[16,12,8,128]{3,2,1,0:T(8,128)}) custom-call(s32[4]{0:T(128)S(1)} %pad_add_fusion.place, bf16[16,192,128]{2,1,0:T(8,128)(2,1)S(1)} %all-to-all-done.3.state, f32[2,128,128]{2,1,0:T(8,128)S(1)} %get-tuple-element.62.panel, f32[8,128]{1,0:T(8,128)S(1)} %reduce_sum.9._), custom_call_target="tpu_custom_call" | custom-call | flops 400000000 | bytes 4000000 | tf_op jit(solution)/shard_map/pallas_call | solution.py:462
  100.6 2.3 %collective-permute-start.13 = (f32[16,12,8,128]{3,2,1,0:T(8,128)}, f32[16,12,8,128]{3,2,1,0:T(8,128)}, u32[]{:S(2)}, u32[]{:S(2)}) collective-permute-start(f32[16,12,8,128]{3,2,1,0:T(8,128)} %get-tuple-element.67), channel_id=1, source_target_pairs={{0,16},{16,0},{1,17},{17,1},{2,18},{18,2},{3,19},{19,3},{4,20},{20... | collective-permute-start | bytes 2359304 | tf_op jit(solution)/shard_map/ppermute | solution.py:465
  103.5 3.6 %all-to-all-start.5 = ((f32[32,8,128]{2,1,0:T(8,128)}), f32[32,8,128]{2,1,0:T(8,128)S(1)}, u32[]{:S(2)}, u32[]{:S(2)}) async-start(f32[32,8,128]{2,1,0:T(8,128)} %broadcast_in_dim.2), calls=%async_computation.5 | async-start | bytes 262144 | tf_op jit(solution)/shard_map/all_to_all | solution.py:425
  107.2 2.1 add.15
  109.3 5.7 %all-to-all-done.5 = f32[32,8,128]{2,1,0:T(8,128)S(1)} async-done(((f32[32,8,128]{2,1,0:T(8,128)}), f32[32,8,128]{2,1,0:T(8,128)S(1)}, u32[]{:S(2)}, u32[]{:S(2)}) %all-to-all-start.5) | async-done | bytes 131104 | tf_op jit(solution)/shard_map/all_to_all | solution.py:425
  115.0 3.6 %all-to-all-start.6 = ((f32[16,96,128]{2,1,0:T(8,128)}), f32[16,96,128]{2,1,0:T(8,128)S(1)}, u32[]{:S(2)}, u32[]{:S(2)}) async-start(f32[16,96,128]{2,1,0:T(8,128)} %bitcast.34), calls=%async_computation.6 | async-start | bytes 1572864 | tf_op jit(solution)/shard_map/all_to_all | solution.py:425
  119.9 11.8 %shard_map.72.inverse = f32[2,128,128]{2,1,0:T(8,128)S(1)} custom-call(f32[2,128,128]{2,1,0:T(8,128)S(1)} %bitcast.32), custom_call_target="tpu_custom_call" | custom-call | flops 4000000000 | bytes 4000000 | tf_op jit(solution)/shard_map/pallas_call | solution.py:469
  131.7 1.6 shard_map.73
  133.2 39.6 %conditional.1 = (bf16[16,16,128]{2,1,0:T(8,128)(2,1)}, bf16[112,128]{1,0:T(8,128)(2,1)S(1)}) conditional(s32[]{:T(128)} %bitcast.21, (bf16[16,16,128]{2,1,0:T(8,128)(2,1)}, bf16[112,128]{1,0:T(8,128)(2,1)S(1)}, s32[]{:T(128)}, s32[142]{0:T(256)S(1)}) %tuple.23, (bf16[16,16,128]{2,1,0:T(8,128)(2,1)}, bf16[112,128]{1,0:T(8,128)(2,1)S(1)}, ...), branch_computations={%region_1.2_spmd, %region_2.3_spmd} | conditional | flops 7 | bytes 4885024 | solution.py:506
  133.2 11.5 %all-to-all-start = ((bf16[16,16,128]{2,1,0:T(8,128)(2,1)}), bf16[16,16,128]{2,1,0:T(8,128)(2,1)}, u32[]{:S(2)}, u32[]{:S(2)}) async-start(bf16[16,16,128]{2,1,0:T(8,128)(2,1)} %get-tuple-element.20), calls=%async_computation | async-start | bytes 131072 | tf_op jit(solution)/shard_map/cond/branch_1_fun/all_to_all | solution.py:425
  144.8 4.4 %collective-permute-start = (bf16[112,128]{1,0:T(8,128)(2,1)S(1)}, bf16[112,128]{1,0:T(8,128)(2,1)S(1)}, u32[]{:S(2)}, u32[]{:S(2)}) collective-permute-start(bf16[112,128]{1,0:T(8,128)(2,1)S(1)} %get-tuple-element.23), channel_id=1, source_target_pairs={{0,15},{1,0},{2,1},{3,2},{4,3},{5,4},{6,5},{7,6},{8,7},{9,8},{10,9... | collective-permute-start | bytes 86024 | tf_op jit(solution)/shard_map/cond/branch_1_fun/ppermute | solution.py:492
  149.2 1.9 collective-permute-start.1
  151.1 4.3 %collective-permute-start.2 = (bf16[112,128]{1,0:T(8,128)(2,1)S(1)}, bf16[112,128]{1,0:T(8,128)(2,1)S(1)}, u32[]{:S(2)}, u32[]{:S(2)}) collective-permute-start(bf16[112,128]{1,0:T(8,128)(2,1)S(1)} %get-tuple-element.23), channel_id=1, source_target_pairs={{0,14},{1,15},{2,0},{3,1},{4,2},{5,3},{6,4},{7,5},{8,6},{9,7},{10,... | collective-permute-start | bytes 86024 | tf_op jit(solution)/shard_map/cond/branch_1_fun/ppermute | solution.py:492
  155.4 1.9 collective-permute-start.3
  157.3 7.3 %collective-permute-start.4 = (bf16[112,128]{1,0:T(8,128)(2,1)S(1)}, bf16[112,128]{1,0:T(8,128)(2,1)S(1)}, u32[]{:S(2)}, u32[]{:S(2)}) collective-permute-start(bf16[112,128]{1,0:T(8,128)(2,1)S(1)} %get-tuple-element.23), channel_id=1, source_target_pairs={{0,13},{1,14},{2,15},{3,0},{4,1},{5,2},{6,3},{7,4},{8,5},{9,6},{10... | collective-permute-start | bytes 86024 | tf_op jit(solution)/shard_map/cond/branch_1_fun/ppermute | solution.py:492
  164.7 1.9 collective-permute-start.5
  166.6 5.7 %collective-permute-done.5.refs_5_ = bf16[112,128]{1,0:T(8,128)(2,1)S(1)} collective-permute-done((bf16[112,128]{1,0:T(8,128)(2,1)S(1)}, bf16[112,128]{1,0:T(8,128)(2,1)S(1)}, u32[]{:S(2)}, u32[]{:S(2)}) %collective-permute-start.5) | collective-permute-done | bytes 28704 | tf_op jit(solution)/shard_map/cond/branch_1_fun/ppermute | solution.py:492
  172.9 1.0 shard_map.74
  173.9 1.0 copy-done.2
  175.0 6.6 %all-to-all-start.7 = ((bf16[16,320,128]{2,1,0:T(8,128)(2,1)}), bf16[16,320,128]{2,1,0:T(8,128)(2,1)S(1)}, u32[]{:S(2)}, u32[]{:S(2)}) async-start(bf16[16,320,128]{2,1,0:T(8,128)(2,1)} %copy-done.2), calls=%async_computation.7 | async-start | bytes 2621440 | tf_op jit(solution)/shard_map/all_to_all | solution.py:425
  181.6 1.1 copy-done.1
  185.5 2.1 copy-done.3
  187.6 2.9 %shard_map.77 = (f32[2,128,128]{2,1,0:T(8,128)S(1)}, bf16[2,128,1536]{2,1,0:T(8,128)(2,1)S(1)}) custom-call(s32[142]{0:T(256)S(1)} %get-tuple-element.57.table, s32[4]{0:T(128)S(1)} %pad_add_fusion.place, bf16[16,5,192,128]{3,2,1,0:T(8,128)(2,1)S(1)} %bitcast.29, bf16[16,384,128]{2,1,0:T(8,128)(2,1)S(1)} %shard_map.69.right), custom_call_target="tpu_custom_call" | custom-call | flops 300000000 | bytes 4000000 | tf_op jit(solution)/shard_map/pallas_call | solution.py:507
  191.4 6.7 %all-to-all-done.7.near = bf16[16,320,128]{2,1,0:T(8,128)(2,1)S(1)} async-done(((bf16[16,320,128]{2,1,0:T(8,128)(2,1)}), bf16[16,320,128]{2,1,0:T(8,128)(2,1)S(1)}, u32[]{:S(2)}, u32[]{:S(2)}) %all-to-all-start.7) | async-done | bytes 1310752 | tf_op jit(solution)/shard_map/all_to_all | solution.py:425
  198.1 7.2 %collective-permute-start.14 = (bf16[16,320,128]{2,1,0:T(8,128)(2,1)S(1)}, bf16[16,320,128]{2,1,0:T(8,128)(2,1)S(1)}, u32[]{:S(2)}, u32[]{:S(2)}) collective-permute-start(bf16[16,320,128]{2,1,0:T(8,128)(2,1)S(1)} %all-to-all-done.7.near), channel_id=1, source_target_pairs={{0,16},{16,0},{1,17},{17,1},{2,18},{18,2},{3,19},{19,3},{4,20},{20... | collective-permute-start | bytes 3932168 | tf_op jit(solution)/shard_map/ppermute | solution.py:524
  205.3 2.6 %collective-permute-done.14.far = bf16[16,320,128]{2,1,0:T(8,128)(2,1)S(1)} collective-permute-done((bf16[16,320,128]{2,1,0:T(8,128)(2,1)S(1)}, bf16[16,320,128]{2,1,0:T(8,128)(2,1)S(1)}, u32[]{:S(2)}, u32[]{:S(2)}) %collective-permute-start.14) | collective-permute-done | bytes 1310752 | tf_op jit(solution)/shard_map/ppermute | solution.py:524
  207.9 1.6 shard_map.79
  209.6 2.8 %shard_map.78 = (bf16[4,128,1536]{2,1,0:T(8,128)(2,1)}, f32[4,128,128]{2,1,0:T(8,128)}) custom-call(s32[142]{0:T(256)S(1)} %get-tuple-element.57.table, s32[4]{0:T(128)S(1)} %pad_add_fusion.place, bf16[2,128,1536]{2,1,0:T(8,128)(2,1)S(1)} %copy-done.5, bf16[2,128,1536]{2,1,0:T(8,128)(2,1)S(1)} %copy-done.7, bf16[16,320,128]{2,1,0:T(8,128)(2,1)S(1)} %all-to-all-done.7.near, ...), custom_call_target="tpu_custom_call" | custom-call | flops 1200000000 | bytes 4000000 | tf_op jit(solution)/shard_map/pallas_call | solution.py:529
  (40 shorter events, 6.4 us)
Async XLA Ops:
  9.6 27.3 %all-to-all-start.2 = ((bf16[16,16,128]{2,1,0:T(8,128)(2,1)}), bf16[16,16,128]{2,1,0:T(8,128)(2,1)S(1)}, u32[]{:S(2)}, u32[]{:S(2)}) async-start(bf16[16,16,128]{2,1,0:T(8,128)(2,1)} %get-tuple-element.59), calls=%async_computation.2 | async-start | bytes 131072 | tf_op jit(solution)/shard_map/all_to_all | solution.py:425
  25.4 1.0 copy-start.8
  26.4 1.0 copy-start.9
  36.9 44.6 %all-to-all-start.3 = ((bf16[16,192,128]{2,1,0:T(8,128)(2,1)}), bf16[16,192,128]{2,1,0:T(8,128)(2,1)S(1)}, u32[]{:S(2)}, u32[]{:S(2)}) async-start(bf16[16,192,128]{2,1,0:T(8,128)(2,1)} %get-tuple-element.60), calls=%async_computation.3 | async-start | bytes 1572864 | tf_op jit(solution)/shard_map/all_to_all | solution.py:425
  40.9 144.6 %all-gather.4.cloned.1.call-start = ((), (), s32[]{:S(2)}) async-start(), calls=%async_computation.8 | async-start | bytes 4177920 | tf_op jit(solution)/shard_map/all_gather | solution.py:459
  41.0 10.0 %collective-permute-start.6 = (bf16[16,16,128]{2,1,0:T(8,128)(2,1)S(1)}, bf16[16,16,128]{2,1,0:T(8,128)(2,1)S(1)}, u32[]{:S(2)}, u32[]{:S(2)}) collective-permute-start(bf16[16,16,128]{2,1,0:T(8,128)(2,1)S(1)} %all-to-all-done.2), channel_id=1, source_target_pairs={{0,128},{128,256},{256,384},{384,0},{1,129},{129,257},{257,385},{3... | collective-permute-start | bytes 196616 | tf_op jit(solution)/shard_map/ppermute | solution.py:419
  44.1 6.8 %collective-permute-start.7 = (bf16[16,16,128]{2,1,0:T(8,128)(2,1)S(1)}, bf16[16,16,128]{2,1,0:T(8,128)(2,1)S(1)}, u32[]{:S(2)}, u32[]{:S(2)}) collective-permute-start(bf16[16,16,128]{2,1,0:T(8,128)(2,1)S(1)} %all-to-all-done.2), channel_id=1, source_target_pairs={{0,384},{128,0},{256,128},{384,256},{1,385},{129,1},{257,129},{385... | collective-permute-start | bytes 196616 | tf_op jit(solution)/shard_map/ppermute | solution.py:419
  47.5 6.8 %collective-permute-start.8 = (bf16[16,16,128]{2,1,0:T(8,128)(2,1)S(1)}, bf16[16,16,128]{2,1,0:T(8,128)(2,1)S(1)}, u32[]{:S(2)}, u32[]{:S(2)}) collective-permute-start(bf16[16,16,128]{2,1,0:T(8,128)(2,1)S(1)} %all-to-all-done.2), channel_id=1, source_target_pairs={{0,256},{128,384},{256,0},{384,128},{1,257},{129,385},{257,1},{385... | collective-permute-start | bytes 196616 | tf_op jit(solution)/shard_map/ppermute | solution.py:419
  54.3 10.1 %collective-permute-start.9 = (bf16[4,16,16,128]{3,2,1,0:T(8,128)(2,1)S(1)}, bf16[4,16,16,128]{3,2,1,0:T(8,128)(2,1)S(1)}, u32[]{:S(2)}, u32[]{:S(2)}) collective-permute-start(bf16[4,16,16,128]{3,2,1,0:T(8,128)(2,1)S(1)} %get-tuple-element.88), channel_id=1, source_target_pairs={{0,32},{32,64},{64,96},{96,0},{1,33},{33,65},{65,97},{97,1},{2,34}... | collective-permute-start | bytes 786440 | tf_op jit(solution)/shard_map/ppermute | solution.py:419
  57.6 7.4 %collective-permute-start.10 = (bf16[4,16,16,128]{3,2,1,0:T(8,128)(2,1)S(1)}, bf16[4,16,16,128]{3,2,1,0:T(8,128)(2,1)S(1)}, u32[]{:S(2)}, u32[]{:S(2)}) collective-permute-start(bf16[4,16,16,128]{3,2,1,0:T(8,128)(2,1)S(1)} %get-tuple-element.88), channel_id=1, source_target_pairs={{0,96},{32,0},{64,32},{96,64},{1,97},{33,1},{65,33},{97,65},{2,98}... | collective-permute-start | bytes 786440 | tf_op jit(solution)/shard_map/ppermute | solution.py:419
  60.9 9.7 %collective-permute-start.11 = (bf16[4,16,16,128]{3,2,1,0:T(8,128)(2,1)S(1)}, bf16[4,16,16,128]{3,2,1,0:T(8,128)(2,1)S(1)}, u32[]{:S(2)}, u32[]{:S(2)}) collective-permute-start(bf16[4,16,16,128]{3,2,1,0:T(8,128)(2,1)S(1)} %get-tuple-element.88), channel_id=1, source_target_pairs={{0,64},{32,96},{64,0},{96,32},{1,65},{33,97},{65,1},{97,33},{2,66}... | collective-permute-start | bytes 786440 | tf_op jit(solution)/shard_map/ppermute | solution.py:419
  70.8 7.9 %collective-permute-start.12 = (bf16[16,16,16,128]{3,2,1,0:T(8,128)(2,1)S(1)}, bf16[16,16,16,128]{3,2,1,0:T(8,128)(2,1)S(1)}, u32[]{:S(2)}, u32[]{:S(2)}) collective-permute-start(bf16[16,16,16,128]{3,2,1,0:T(8,128)(2,1)S(1)} %bitcast.27), channel_id=1, source_target_pairs={{0,16},{16,0},{1,17},{17,1},{2,18},{18,2},{3,19},{19,3},{4,20},{20... | collective-permute-start | bytes 3145736 | tf_op jit(solution)/shard_map/ppermute | solution.py:421
  81.6 19.0 %copy-start = (bf16[16,192,128]{2,1,0:T(8,128)(2,1)}, bf16[16,192,128]{2,1,0:T(8,128)(2,1)S(1)}, u32[]{:S(2)}) copy-start(bf16[16,192,128]{2,1,0:T(8,128)(2,1)S(1)} %all-to-all-done.3.state) | copy-start | bytes 2359300
  100.6 6.6 %collective-permute-start.13 = (f32[16,12,8,128]{3,2,1,0:T(8,128)}, f32[16,12,8,128]{3,2,1,0:T(8,128)}, u32[]{:S(2)}, u32[]{:S(2)}) collective-permute-start(f32[16,12,8,128]{3,2,1,0:T(8,128)} %get-tuple-element.67), channel_id=1, source_target_pairs={{0,16},{16,0},{1,17},{17,1},{2,18},{18,2},{3,19},{19,3},{4,20},{20... | collective-permute-start | bytes 2359304 | tf_op jit(solution)/shard_map/ppermute | solution.py:465
  103.5 11.4 %all-to-all-start.5 = ((f32[32,8,128]{2,1,0:T(8,128)}), f32[32,8,128]{2,1,0:T(8,128)S(1)}, u32[]{:S(2)}, u32[]{:S(2)}) async-start(f32[32,8,128]{2,1,0:T(8,128)} %broadcast_in_dim.2), calls=%async_computation.5 | async-start | bytes 262144 | tf_op jit(solution)/shard_map/all_to_all | solution.py:425
  115.0 16.7 %all-to-all-start.6 = ((f32[16,96,128]{2,1,0:T(8,128)}), f32[16,96,128]{2,1,0:T(8,128)S(1)}, u32[]{:S(2)}, u32[]{:S(2)}) async-start(f32[16,96,128]{2,1,0:T(8,128)} %bitcast.34), calls=%async_computation.6 | async-start | bytes 1572864 | tf_op jit(solution)/shard_map/all_to_all | solution.py:425
  133.2 39.6 %all-to-all-start = ((bf16[16,16,128]{2,1,0:T(8,128)(2,1)}), bf16[16,16,128]{2,1,0:T(8,128)(2,1)}, u32[]{:S(2)}, u32[]{:S(2)}) async-start(bf16[16,16,128]{2,1,0:T(8,128)(2,1)} %get-tuple-element.20), calls=%async_computation | async-start | bytes 131072 | tf_op jit(solution)/shard_map/cond/branch_1_fun/all_to_all | solution.py:425
  144.8 19.9 %collective-permute-start = (bf16[112,128]{1,0:T(8,128)(2,1)S(1)}, bf16[112,128]{1,0:T(8,128)(2,1)S(1)}, u32[]{:S(2)}, u32[]{:S(2)}) collective-permute-start(bf16[112,128]{1,0:T(8,128)(2,1)S(1)} %get-tuple-element.23), channel_id=1, source_target_pairs={{0,15},{1,0},{2,1},{3,2},{4,3},{5,4},{6,5},{7,6},{8,7},{9,8},{10,9... | collective-permute-start | bytes 86024 | tf_op jit(solution)/shard_map/cond/branch_1_fun/ppermute | solution.py:492
  149.2 17.4 %collective-permute-start.1 = (bf16[112,128]{1,0:T(8,128)(2,1)S(1)}, bf16[112,128]{1,0:T(8,128)(2,1)S(1)}, u32[]{:S(2)}, u32[]{:S(2)}) collective-permute-start(bf16[112,128]{1,0:T(8,128)(2,1)S(1)} %get-tuple-element.23), channel_id=1, source_target_pairs={{0,1},{1,2},{2,3},{3,4},{4,5},{5,6},{6,7},{7,8},{8,9},{9,10},{10,1... | collective-permute-start | bytes 86024 | tf_op jit(solution)/shard_map/cond/branch_1_fun/ppermute | solution.py:492
  151.1 15.5 %collective-permute-start.2 = (bf16[112,128]{1,0:T(8,128)(2,1)S(1)}, bf16[112,128]{1,0:T(8,128)(2,1)S(1)}, u32[]{:S(2)}, u32[]{:S(2)}) collective-permute-start(bf16[112,128]{1,0:T(8,128)(2,1)S(1)} %get-tuple-element.23), channel_id=1, source_target_pairs={{0,14},{1,15},{2,0},{3,1},{4,2},{5,3},{6,4},{7,5},{8,6},{9,7},{10,... | collective-permute-start | bytes 86024 | tf_op jit(solution)/shard_map/cond/branch_1_fun/ppermute | solution.py:492
  155.4 11.2 %collective-permute-start.3 = (bf16[112,128]{1,0:T(8,128)(2,1)S(1)}, bf16[112,128]{1,0:T(8,128)(2,1)S(1)}, u32[]{:S(2)}, u32[]{:S(2)}) collective-permute-start(bf16[112,128]{1,0:T(8,128)(2,1)S(1)} %get-tuple-element.23), channel_id=1, source_target_pairs={{0,2},{1,3},{2,4},{3,5},{4,6},{5,7},{6,8},{7,9},{8,10},{9,11},{10,... | collective-permute-start | bytes 86024 | tf_op jit(solution)/shard_map/cond/branch_1_fun/ppermute | solution.py:492
  157.3 9.3 %collective-permute-start.4 = (bf16[112,128]{1,0:T(8,128)(2,1)S(1)}, bf16[112,128]{1,0:T(8,128)(2,1)S(1)}, u32[]{:S(2)}, u32[]{:S(2)}) collective-permute-start(bf16[112,128]{1,0:T(8,128)(2,1)S(1)} %get-tuple-element.23), channel_id=1, source_target_pairs={{0,13},{1,14},{2,15},{3,0},{4,1},{5,2},{6,3},{7,4},{8,5},{9,6},{10... | collective-permute-start | bytes 86024 | tf_op jit(solution)/shard_map/cond/branch_1_fun/ppermute | solution.py:492
  164.7 7.6 %collective-permute-start.5 = (bf16[112,128]{1,0:T(8,128)(2,1)S(1)}, bf16[112,128]{1,0:T(8,128)(2,1)S(1)}, u32[]{:S(2)}, u32[]{:S(2)}) collective-permute-start(bf16[112,128]{1,0:T(8,128)(2,1)S(1)} %get-tuple-element.23), channel_id=1, source_target_pairs={{0,3},{1,4},{2,5},{3,6},{4,7},{5,8},{6,9},{7,10},{8,11},{9,12},{10... | collective-permute-start | bytes 86024 | tf_op jit(solution)/shard_map/cond/branch_1_fun/ppermute | solution.py:492
  173.9 1.1 copy-start.2
  175.0 23.1 %all-to-all-start.7 = ((bf16[16,320,128]{2,1,0:T(8,128)(2,1)}), bf16[16,320,128]{2,1,0:T(8,128)(2,1)S(1)}, u32[]{:S(2)}, u32[]{:S(2)}) async-start(bf16[16,320,128]{2,1,0:T(8,128)(2,1)} %copy-done.2), calls=%async_computation.7 | async-start | bytes 2621440 | tf_op jit(solution)/shard_map/all_to_all | solution.py:425
  181.6 1.1 copy-start.1
  183.6 0.9 copy-start.4
  185.5 2.1 copy-start.3
  190.5 0.9 copy-start.6
  198.1 11.5 %copy-start.5 = (bf16[2,128,1536]{2,1,0:T(8,128)(2,1)S(1)}, bf16[2,128,1536]{2,1,0:T(8,128)(2,1)}, u32[]{:S(2)}) copy-start(bf16[2,128,1536]{2,1,0:T(8,128)(2,1)} %copy-done.4) | copy-start | bytes 2359300
  198.1 11.5 %copy-start.7 = (bf16[2,128,1536]{2,1,0:T(8,128)(2,1)S(1)}, bf16[2,128,1536]{2,1,0:T(8,128)(2,1)}, u32[]{:S(2)}) copy-start(bf16[2,128,1536]{2,1,0:T(8,128)(2,1)} %copy-done.6) | copy-start | bytes 2359300
  198.1 9.9 %collective-permute-start.14 = (bf16[16,320,128]{2,1,0:T(8,128)(2,1)S(1)}, bf16[16,320,128]{2,1,0:T(8,128)(2,1)S(1)}, u32[]{:S(2)}, u32[]{:S(2)}) collective-permute-start(bf16[16,320,128]{2,1,0:T(8,128)(2,1)S(1)} %all-to-all-done.7.near), channel_id=1, source_target_pairs={{0,16},{16,0},{1,17},{17,1},{2,18},{18,2},{3,19},{19,3},{4,20},{20... | collective-permute-start | bytes 3932168 | tf_op jit(solution)/shard_map/ppermute | solution.py:524
Sparse Core Ops, SparseCore 0:
  84.0 71.1 all-gather.3

commit v10 on v8

--- a/solution.py
+++ b/solution.py
@@ -174,12 +174,32 @@
     return lax.fori_loop(0, GROUPS, block, jnp.zeros((128, RANK), F32), unroll=4)
 
 
-def panels(state, right, panel, gram):
+PACKED = 80
+
+
+def pack(gram):
+    middle = jnp.concatenate([gram[96:, 96:], gram[32:64, 32:]], axis=1)
+    last = jnp.concatenate([gram[80:96, 64:], gram[64:80, 64:]], axis=1)
+    return jnp.concatenate([gram[:32], middle, last], axis=0)
+
+
+def unpack(packed):
+    middle, last = packed[32:64], packed[64:]
+    other = jnp.concatenate([last[:, 64:], last[:, :64]], axis=1)
+    corner = jnp.concatenate([middle[:, 32:], middle[:, :32]], axis=1)
+    return jnp.concatenate([packed[:32], middle, last, other, corner], axis=0)
+
+
+def panels(place, state, right, panel, keep, send):
+    grams = []
     for k in range(2):
         rows = slice(k * BLOCK, (k + 1) * BLOCK)
         value = panel_of(lambda z: state[z, rows, :], right, k, 0)
         panel[k] = value
-        gram[k] = dot(value, value, ((0,), (0,)), HIGHEST)
+        grams.append(pack(dot(value, value, ((0,), (0,)), HIGHEST)))
+    mine = place[2] == 0
+    keep[...] = jnp.where(mine, grams[0], grams[1])
+    send[...] = jnp.where(mine, grams[1], grams[0])
 
 
 def unit():
@@ -215,7 +235,7 @@
     return jnp.where(tile_of(place[0], place[1], place[2], q) >= 12, 1, 0)
 
 
-def weigh(place, state, panel, _, keep, send, rows):
+def weigh(place, state, panel, keep, send, rows):
     weights = [jnp.concatenate(split3(panel[k]), axis=1) for k in range(2)]
 
     def block(g, _):
@@ -240,26 +260,53 @@
     lax.fori_loop(0, 4, block, 0)
 
 
-def invert(gram, out, work, *, size):
+def eliminate(sets, k):
+    row = iota((8, 256), 0)
+    n = len(sets[0])
+    for g in range(n):
+        first = k + 8 * g
+        columns = [
+            [
+                [jnp.broadcast_to(s[t][:, first + j : first + j + 1], (8, 256)) for t in range(g, n)]
+                for j in range(8)
+            ]
+            for s in sets
+        ]
+        scales = [jnp.zeros((8, 256), F32) for _ in sets]
+        for i in range(8):
+            inverses = [
+                lax.rsqrt(jnp.broadcast_to(c[i][0][i : i + 1, :], (8, 256))) for c in columns
+            ]
+            for m, (s, c) in enumerate(zip(sets, columns)):
+                scales[m] = jnp.where(row == i, inverses[m], scales[m])
+                square = inverses[m] * inverses[m]
+                factors = [part * square for part in c[i]]
+                factors[0] = jnp.where(row > i, factors[0], 0.0)
+                for j in range(i + 1, 8):
+                    line = jnp.broadcast_to(c[j][0][i : i + 1, :], (8, 256))
+                    c[j] = [part - f * line for part, f in zip(c[j], factors)]
+                line = jnp.broadcast_to(s[g][i : i + 1, :], (8, 256))
+                for t in range(g, n):
+                    s[t] = s[t] - factors[t - g] * line
+        for m, s in enumerate(sets):
+            s[g] = s[g] * scales[m]
+
+
+def invert(place, near, far, out, work, *, size):
     n = RANK
     eye = (iota((n, n), 0) == iota((n, n), 1)).astype(F32)
-    for m in range(2):
-        work[m, :, :n] = gram[m] + ridge_term * eye
+    mine = place[2] == 0
+    first, other = unpack(near[...]), unpack(far[...])
+    work[0, :, :n] = jnp.where(mine, first, other) + ridge_term * eye
+    work[1, :, :n] = jnp.where(mine, other, first) + ridge_term * eye
     for m in range(2):
         work[m, :, n:] = eye
-    row = iota((size, 2 * n), 0)
     lane = iota((size, n), 1)
     for k in range(0, n, size):
-        blocks = [work[m, k : k + size, :] for m in range(2)]
-        for i in range(size):
-            for m in range(2):
-                b = blocks[m]
-                scale = lax.rsqrt(b[i : i + 1, k + i : k + i + 1])
-                line = b[i : i + 1, :] * scale
-                column = jnp.where(row > i, b[:, k + i : k + i + 1] * scale, 0.0)
-                blocks[m] = jnp.where(row == i, line, b - column * line)
+        sets = [[work[m, k + 8 * t : k + 8 * t + 8, :] for t in range(size // 8)] for m in range(2)]
+        eliminate(sets, k)
         for m in range(2):
-            b = blocks[m]
+            b = jnp.concatenate(sets[m], axis=0)
             out[m, k : k + size, :] = b[:, n:]
             if k + size < n:
                 left = jnp.where(lane >= k + size, b[:, :n], 0.0)
@@ -430,27 +477,30 @@
         flops=800_000_000,
         specs=[SMEM, VMEM, VMEM],
     )(place, near, far)
-    square = sds((2, RANK, RANK), F32)
+    square = sds((PACKED, RANK), F32)
     two = sds((2, 128, RANK), F32)
-    panel, gram = call(panels, (two, square), n_in=2, flops=300_000_000)(state, right)
-    late, gram = barrier((late, gram))
+    panel, keep, send = call(
+        panels, (two, square, square), specs=[SMEM, VMEM, VMEM], flops=300_000_000
+    )(place, state, right)
+    late, send = barrier((late, send))
     seconds = lax.all_gather(late, "z")
-    gram = jnp.sum(exchange(gram.reshape(32, 8, RANK), FSDP), axis=0)
+    gram = keep + lax.ppermute(send, "c", SWAP)
     half = sds((16, 12, 8, RANK), F32)
     keep, send = call(
-        weigh, (half, half), [pltpu.VMEM((4, 192, RANK), F32)], specs=[SMEM, VMEM, VMEM, ANY], flops=400_000_000
-    )(place, state, panel, gram)
+        weigh, (half, half), [pltpu.VMEM((4, 192, RANK), F32)], specs=[SMEM, VMEM, VMEM], flops=400_000_000
+    )(place, state, panel)
     parts = keep + lax.ppermute(send, "c", SWAP)
-    gram = exchange(jnp.broadcast_to(gram[None], (32, 8, RANK)), FSDP).reshape(2, RANK, RANK)
+    gram = exchange(jnp.broadcast_to(gram[None], (16, PACKED, RANK)), XY)
     parts, gram = barrier((parts, gram))
     parts = exchange(parts.reshape(16, 96, RANK), XY)
+    gram = jnp.sum(gram, axis=0)
     inverse = call(
         functools.partial(invert, size=32),
-        square,
+        sds((2, RANK, RANK), F32),
         [pltpu.VMEM((2, RANK, 2 * RANK), F32)],
-        n_in=1,
-        flops=4_000_000_000,
-    )(gram)
+        specs=[SMEM, VMEM, VMEM],
+        flops=2_000_000_000,
+    )(place, gram, lax.ppermute(gram, "c", SWAP))
     mine = call(scale_factor, sds((112, RANK), BF16), specs=[SMEM, VMEM, VMEM], flops=100_000_000)(
         place, inverse, parts
     )

time: 210 us -> 208 us (level)
  blocking collectives: 45.1 us -> 31.6 us
  starting transfers between devices: 70.8 us -> 79.1 us
  Pallas kernels: 34.9 us -> 29.3 us
  waiting for transfers between devices: 32.8 us -> 37.5 us
  other arithmetic: 1.82 us -> 4.09 us
    all_to_all x1 -> x0, blocking collectives: 14 us -> none  [exchange(): return lax.all_to_all(x, axis, split_axis=0, concat_axis=0, tiled=True)]
    ppermute x0 -> x2, starting transfers between devices: none -> 5.76 us  [the longest x1 3.71 us: shards(): lax.ppermute(gram, 'c', SWAP)]
    pallas_call x2, Pallas kernels: 14 us -> 8.4 us  [the longest x1 5.49 us: shards(): call(functools.partial(invert, size=32), sds((2, RANK, RANK), F32), [pltp...]
    all_to_all x5, waiting for transfers between devices: 18.6 us -> 21.4 us  [exchange(): return lax.all_to_all(x, axis, split_axis=0, concat_axis=0, tiled=True)]
    all_to_all x5, starting transfers between devices: 33.5 us -> 36.1 us  [exchange(): return lax.all_to_all(x, axis, split_axis=0, concat_axis=0, tiled=True)]
    unnamed x26 -> x28, local copies, waits for them, and re-layouts: 8.78 us -> 9.61 us
  transfers between devices with their start and end apart: 15 -> 17, of which waited for: 9 -> 11; matrix products, arithmetic and copies ran while one was open for 1% -> 2% of each run, Pallas kernels for 12% -> 10%
where the time goes in v10:
time: 208 us; the launch traced here: 206 us
  starting transfers between devices  79.1 us (38%)
  waiting for transfers between devices  37.5 us (18%)
  blocking collectives  31.6 us (15%)
  Pallas kernels  29.3 us (14%)
  between operations  14.4 us (7%)
  local copies, waits for them, and re-layouts  10.5 us (5%)
  other arithmetic  4.09 us (2%)
    all_to_all x5, starting transfers between devices, exchange(): return lax.all_to_all(x, axis, split_axis=0, concat_axis=0, tiled=True)  36.1 us
    all_gather x1, blocking collectives, shards(): tiles = lax.all_gather(mine, 'z')  31.6 us
    all_to_all x5, waiting for transfers between devices, exchange(): return lax.all_to_all(x, axis, split_axis=0, concat_axis=0, tiled=True)  21.4 us
    ppermute x6, starting transfers between devices, gather_slices(): lax.ppermute(x, axis, ring((4 - d) % 4))  20 us
    unnamed x28, local copies, waits for them, and re-layouts  9.61 us
    ppermute x6, waiting for transfers between devices, gather_slices(): lax.ppermute(x, axis, ring((4 - d) % 4))  9.27 us
    ppermute x1, starting transfers between devices, shards(): far = lax.ppermute(near, 'c', SWAP)  9.23 us
    ppermute x1, starting transfers between devices, gather_slices(): return (x, lax.ppermute(x, 'c', SWAP))  5.62 us
  transfers between devices with their start and end apart: 17, of which 11 were waited for; matrix products, arithmetic and copies ran while one was open for 2% of the time, Pallas kernels for 10%

profile of v10, /device:TPU:1, one launch (start us, length us, event | category | flops | bytes accessed | tf_op | source)
XLA Modules:
  0.0 206.4 jit_solution(14524189746972093906)
XLA Ops:
  7.8 2.1 %shard_map.67 = (bf16[16,16,128]{2,1,0:T(8,128)(2,1)}, s32[128]{0:T(128)}) custom-call(s32[10]{0:T(128)} %own.1, s32[4]{0:T(128)} %pad_add_fusion.place, bf16[10,2,96,128]{3,2,1,0:T(8,128)(2,1)} %right.1), custom_call_target="tpu_custom_call" | custom-call | tf_op jit(solution)/shard_map/pallas_call | solution.py:457
  9.9 15.8 %all-to-all-start = ((bf16[16,16,128]{2,1,0:T(8,128)(2,1)}), bf16[16,16,128]{2,1,0:T(8,128)(2,1)S(1)}, u32[]{:S(2)}, u32[]{:S(2)}) async-start(bf16[16,16,128]{2,1,0:T(8,128)(2,1)} %get-tuple-element.32), calls=%async_computation | async-start | bytes 131072 | tf_op jit(solution)/shard_map/all_to_all | solution.py:450
  25.7 1.0 copy-done.8
  26.7 1.0 copy-done.9
  28.4 2.0 shard_map.68
  30.4 6.8 %all-to-all-done = bf16[16,16,128]{2,1,0:T(8,128)(2,1)S(1)} async-done(((bf16[16,16,128]{2,1,0:T(8,128)(2,1)}), bf16[16,16,128]{2,1,0:T(8,128)(2,1)S(1)}, u32[]{:S(2)}, u32[]{:S(2)}) %all-to-all-start) | async-done | bytes 65568 | tf_op jit(solution)/shard_map/all_to_all | solution.py:450
  37.2 4.6 %all-to-all-start.1 = ((bf16[16,192,128]{2,1,0:T(8,128)(2,1)}), bf16[16,192,128]{2,1,0:T(8,128)(2,1)S(1)}, u32[]{:S(2)}, u32[]{:S(2)}) async-start(bf16[16,192,128]{2,1,0:T(8,128)(2,1)} %get-tuple-element.33), calls=%async_computation.1 | async-start | bytes 1572864 | tf_op jit(solution)/shard_map/all_to_all | solution.py:450
  41.9 3.1 %collective-permute-start = (bf16[16,16,128]{2,1,0:T(8,128)(2,1)S(1)}, bf16[16,16,128]{2,1,0:T(8,128)(2,1)S(1)}, u32[]{:S(2)}, u32[]{:S(2)}) collective-permute-start(bf16[16,16,128]{2,1,0:T(8,128)(2,1)S(1)} %all-to-all-done), channel_id=1, source_target_pairs={{0,128},{128,256},{256,384},{384,0},{1,129},{129,257},{257,385},{3... | collective-permute-start | bytes 196616 | tf_op jit(solution)/shard_map/ppermute | solution.py:444
  45.1 3.4 %collective-permute-start.1 = (bf16[16,16,128]{2,1,0:T(8,128)(2,1)S(1)}, bf16[16,16,128]{2,1,0:T(8,128)(2,1)S(1)}, u32[]{:S(2)}, u32[]{:S(2)}) collective-permute-start(bf16[16,16,128]{2,1,0:T(8,128)(2,1)S(1)} %all-to-all-done), channel_id=1, source_target_pairs={{0,384},{128,0},{256,128},{384,256},{1,385},{129,1},{257,129},{385... | collective-permute-start | bytes 196616 | tf_op jit(solution)/shard_map/ppermute | solution.py:444
  48.4 3.4 %collective-permute-start.2 = (bf16[16,16,128]{2,1,0:T(8,128)(2,1)S(1)}, bf16[16,16,128]{2,1,0:T(8,128)(2,1)S(1)}, u32[]{:S(2)}, u32[]{:S(2)}) collective-permute-start(bf16[16,16,128]{2,1,0:T(8,128)(2,1)S(1)} %all-to-all-done), channel_id=1, source_target_pairs={{0,256},{128,384},{256,0},{384,128},{1,257},{129,385},{257,1},{385... | collective-permute-start | bytes 196616 | tf_op jit(solution)/shard_map/ppermute | solution.py:444
  51.9 3.3 %collective-permute-done.2 = bf16[16,16,128]{2,1,0:T(8,128)(2,1)S(1)} collective-permute-done((bf16[16,16,128]{2,1,0:T(8,128)(2,1)S(1)}, bf16[16,16,128]{2,1,0:T(8,128)(2,1)S(1)}, u32[]{:S(2)}, u32[]{:S(2)}) %collective-permute-start.2) | collective-permute-done | bytes 65568 | tf_op jit(solution)/shard_map/ppermute | solution.py:444
  55.3 3.2 %collective-permute-start.3 = (bf16[4,16,16,128]{3,2,1,0:T(8,128)(2,1)S(1)}, bf16[4,16,16,128]{3,2,1,0:T(8,128)(2,1)S(1)}, u32[]{:S(2)}, u32[]{:S(2)}) collective-permute-start(bf16[4,16,16,128]{3,2,1,0:T(8,128)(2,1)S(1)} %get-tuple-element.58), channel_id=1, source_target_pairs={{0,32},{32,64},{64,96},{96,0},{1,33},{33,65},{65,97},{97,1},{2,34}... | collective-permute-start | bytes 786440 | tf_op jit(solution)/shard_map/ppermute | solution.py:444
  58.5 3.4 %collective-permute-start.4 = (bf16[4,16,16,128]{3,2,1,0:T(8,128)(2,1)S(1)}, bf16[4,16,16,128]{3,2,1,0:T(8,128)(2,1)S(1)}, u32[]{:S(2)}, u32[]{:S(2)}) collective-permute-start(bf16[4,16,16,128]{3,2,1,0:T(8,128)(2,1)S(1)} %get-tuple-element.58), channel_id=1, source_target_pairs={{0,96},{32,0},{64,32},{96,64},{1,97},{33,1},{65,33},{97,65},{2,98}... | collective-permute-start | bytes 786440 | tf_op jit(solution)/shard_map/ppermute | solution.py:444
  61.9 3.5 %collective-permute-start.5 = (bf16[4,16,16,128]{3,2,1,0:T(8,128)(2,1)S(1)}, bf16[4,16,16,128]{3,2,1,0:T(8,128)(2,1)S(1)}, u32[]{:S(2)}, u32[]{:S(2)}) collective-permute-start(bf16[4,16,16,128]{3,2,1,0:T(8,128)(2,1)S(1)} %get-tuple-element.58), channel_id=1, source_target_pairs={{0,64},{32,96},{64,0},{96,32},{1,65},{33,97},{65,1},{97,33},{2,66}... | collective-permute-start | bytes 786440 | tf_op jit(solution)/shard_map/ppermute | solution.py:444
  65.9 5.4 %collective-permute-done.5 = bf16[4,16,16,128]{3,2,1,0:T(8,128)(2,1)S(1)} collective-permute-done((bf16[4,16,16,128]{3,2,1,0:T(8,128)(2,1)S(1)}, bf16[4,16,16,128]{3,2,1,0:T(8,128)(2,1)S(1)}, u32[]{:S(2)}, u32[]{:S(2)}) %collective-permute-start.5) | collective-permute-done | bytes 262176 | tf_op jit(solution)/shard_map/ppermute | solution.py:444
  71.5 5.6 %collective-permute-start.6 = (bf16[16,16,16,128]{3,2,1,0:T(8,128)(2,1)S(1)}, bf16[16,16,16,128]{3,2,1,0:T(8,128)(2,1)S(1)}, u32[]{:S(2)}, u32[]{:S(2)}) collective-permute-start(bf16[16,16,16,128]{3,2,1,0:T(8,128)(2,1)S(1)} %bitcast.21), channel_id=1, source_target_pairs={{0,16},{16,0},{1,17},{17,1},{2,18},{18,2},{3,19},{19,3},{4,20},{20... | collective-permute-start | bytes 3145736 | tf_op jit(solution)/shard_map/ppermute | solution.py:446
  77.1 2.3 %collective-permute-done.6.far = bf16[16,16,16,128]{3,2,1,0:T(8,128)(2,1)S(1)} collective-permute-done((bf16[16,16,16,128]{3,2,1,0:T(8,128)(2,1)S(1)}, bf16[16,16,16,128]{3,2,1,0:T(8,128)(2,1)S(1)}, u32[]{:S(2)}, u32[]{:S(2)}) %collective-permute-start.6) | collective-permute-done | bytes 1048608 | tf_op jit(solution)/shard_map/ppermute | solution.py:446
  79.4 2.9 %shard_map.69.right = bf16[16,384,128]{2,1,0:T(8,128)(2,1)S(1)} custom-call(s32[4]{0:T(128)S(1)} %copy-done.10, bf16[16,16,16,128]{3,2,1,0:T(8,128)(2,1)S(1)} %bitcast.22, bf16[16,16,16,128]{3,2,1,0:T(8,128)(2,1)S(1)} %collective-permute-done.6.far), custom_call_target="tpu_custom_call" | custom-call | flops 800000000 | bytes 4000000 | tf_op jit(solution)/shard_map/pallas_call | solution.py:473
  82.3 2.9 %shard_map.70 = (f32[2,128,128]{2,1,0:T(8,128)S(1)}, f32[80,128]{1,0:T(8,128)S(1)}, f32[80,128]{1,0:T(8,128)S(1)}) custom-call(s32[4]{0:T(128)S(1)} %copy-done.10, bf16[16,192,128]{2,1,0:T(8,128)(2,1)S(1)} %all-to-all-done.1.state, bf16[16,384,128]{2,1,0:T(8,128)(2,1)S(1)} %shard_map.69.right), custom_call_target="tpu_custom_call" | custom-call | flops 300000000 | bytes 4000000 | tf_op jit(solution)/shard_map/pallas_call | solution.py:482
  85.3 2.8 %shard_map.71 = (f32[16,12,8,128]{3,2,1,0:T(8,128)S(1)}, f32[16,12,8,128]{3,2,1,0:T(8,128)}) custom-call(s32[4]{0:T(128)S(1)} %copy-done.10, bf16[16,192,128]{2,1,0:T(8,128)(2,1)S(1)} %all-to-all-done.1.state, f32[2,128,128]{2,1,0:T(8,128)S(1)} %get-tuple-element.35.panel), custom_call_target="tpu_custom_call" | custom-call | flops 400000000 | bytes 4000000 | tf_op jit(solution)/shard_map/pallas_call | solution.py:489
  88.1 2.3 %collective-permute-start.7 = (f32[16,12,8,128]{3,2,1,0:T(8,128)}, f32[16,12,8,128]{3,2,1,0:T(8,128)}, u32[]{:S(2)}, u32[]{:S(2)}) collective-permute-start(f32[16,12,8,128]{3,2,1,0:T(8,128)} %get-tuple-element.37), channel_id=1, source_target_pairs={{0,16},{16,0},{1,17},{17,1},{2,18},{18,2},{3,19},{19,3},{4,20},{20... | collective-permute-start | bytes 2359304 | tf_op jit(solution)/shard_map/ppermute | solution.py:492
  90.3 2.0 collective-permute-start.8
  92.4 1.1 collective-permute-done.8
  93.5 0.9 broadcast_in_dim.2
  94.4 5.8 %all-to-all-start.2 = ((f32[16,80,128]{2,1,0:T(8,128)}), f32[16,80,128]{2,1,0:T(8,128)S(1)}, u32[]{:S(2)}, u32[]{:S(2)}) async-start(f32[16,80,128]{2,1,0:T(8,128)} %broadcast_in_dim.2), calls=%async_computation.2 | async-start | bytes 1310720 | tf_op jit(solution)/shard_map/all_to_all | solution.py:450
  100.3 2.1 %add.6 = f32[16,12,8,128]{3,2,1,0:T(8,128)} add(f32[16,12,8,128]{3,2,1,0:T(8,128)S(1)} %get-tuple-element.36, f32[16,12,8,128]{3,2,1,0:T(8,128)} %collective-permute-done.7) | non-fusion elementwise | flops 196608 | bytes 2359296 | tf_op jit(solution)/shard_map/add | solution.py:492
  102.4 9.2 %all-to-all-done.2 = f32[16,80,128]{2,1,0:T(8,128)S(1)} async-done(((f32[16,80,128]{2,1,0:T(8,128)}), f32[16,80,128]{2,1,0:T(8,128)S(1)}, u32[]{:S(2)}, u32[]{:S(2)}) %all-to-all-start.2) | async-done | bytes 655392 | tf_op jit(solution)/shard_map/all_to_all | solution.py:450
  112.4 4.4 %all-to-all-start.3 = ((f32[16,96,128]{2,1,0:T(8,128)}), f32[16,96,128]{2,1,0:T(8,128)S(1)}, u32[]{:S(2)}, u32[]{:S(2)}) async-start(f32[16,96,128]{2,1,0:T(8,128)} %bitcast.27), calls=%async_computation.3 | async-start | bytes 1572864 | tf_op jit(solution)/shard_map/all_to_all | solution.py:450
  116.8 1.1 reduce_sum.9.near
  118.0 3.7 %collective-permute-start.9 = (f32[80,128]{1,0:T(8,128)S(1)}, f32[80,128]{1,0:T(8,128)S(1)}, u32[]{:S(2)}, u32[]{:S(2)}) collective-permute-start(f32[80,128]{1,0:T(8,128)S(1)} %reduce_sum.9.near), channel_id=1, source_target_pairs={{0,16},{16,0},{1,17},{17,1},{2,18},{18,2},{3,19},{19,3},{4,20},{20... | collective-permute-start | bytes 122888 | tf_op jit(solution)/shard_map/ppermute | solution.py:503
  122.6 5.5 %shard_map.72.inverse = f32[2,128,128]{2,1,0:T(8,128)S(1)} custom-call(s32[4]{0:T(128)S(1)} %copy-done.10, f32[80,128]{1,0:T(8,128)S(1)} %reduce_sum.9.near, f32[80,128]{1,0:T(8,128)S(1)} %collective-permute-done.9.far), custom_call_target="tpu_custom_call" | custom-call | flops 2000000000 | bytes 4000000 | tf_op jit(solution)/shard_map/pallas_call | solution.py:497
  128.1 1.3 all-to-all-done.3.parts
  129.3 0.9 shard_map.73.mine
  130.2 31.6 %all-gather = bf16[1792,128]{1,0:T(8,128)(2,1)S(1)} all-gather(bf16[112,128]{1,0:T(8,128)(2,1)S(1)} %shard_map.73.mine), channel_id=2, replica_groups=mesh['x'=4,'y'=4,'c'=2,'z'=16] {'z'}, dimensions={0}, use_global_device_ids=true | all-gather | bytes 487424 | tf_op jit(solution)/shard_map/all_gather | solution.py:513
  162.7 1.0 copy-done.2
  163.8 5.5 %all-to-all-start.4 = ((bf16[16,320,128]{2,1,0:T(8,128)(2,1)}), bf16[16,320,128]{2,1,0:T(8,128)(2,1)S(1)}, u32[]{:S(2)}, u32[]{:S(2)}) async-start(bf16[16,320,128]{2,1,0:T(8,128)(2,1)} %copy-done.2), calls=%async_computation.4 | async-start | bytes 2621440 | tf_op jit(solution)/shard_map/all_to_all | solution.py:450
  169.3 1.1 copy-done.1
  170.4 0.9 shard_map.75.turned
  171.3 0.9 copy-done.4
  172.2 0.9 shard_map.76
  173.2 2.1 %copy-done.3 = bf16[80,192,128]{2,1,0:T(8,128)(2,1)S(1)} copy-done((bf16[80,192,128]{2,1,0:T(8,128)(2,1)S(1)}, bf16[80,192,128]{2,1,0:T(8,128)(2,1)}, u32[]{:S(2)}) %copy-start.3) | copy-done | bytes 3932184
  175.3 2.9 %shard_map.77 = (f32[2,128,128]{2,1,0:T(8,128)S(1)}, bf16[2,128,1536]{2,1,0:T(8,128)(2,1)S(1)}) custom-call(s32[128]{0:T(128)S(1)} %copy-done.12, s32[4]{0:T(128)S(1)} %copy-done.10, bf16[16,5,192,128]{3,2,1,0:T(8,128)(2,1)S(1)} %bitcast.23, bf16[16,384,128]{2,1,0:T(8,128)(2,1)S(1)} %shard_map.69.right), custom_call_target="tpu_custom_call" | custom-call | flops 300000000 | bytes 4000000 | tf_op jit(solution)/shard_map/pallas_call | solution.py:514
  178.2 0.9 copy-done.6
  179.1 4.1 %all-to-all-done.4.near = bf16[16,320,128]{2,1,0:T(8,128)(2,1)S(1)} async-done(((bf16[16,320,128]{2,1,0:T(8,128)(2,1)}), bf16[16,320,128]{2,1,0:T(8,128)(2,1)S(1)}, u32[]{:S(2)}, u32[]{:S(2)}) %all-to-all-start.4) | async-done | bytes 1310752 | tf_op jit(solution)/shard_map/all_to_all | solution.py:450
  183.2 9.2 %collective-permute-start.10 = (bf16[16,320,128]{2,1,0:T(8,128)(2,1)S(1)}, bf16[16,320,128]{2,1,0:T(8,128)(2,1)S(1)}, u32[]{:S(2)}, u32[]{:S(2)}) collective-permute-start(bf16[16,320,128]{2,1,0:T(8,128)(2,1)S(1)} %all-to-all-done.4.near), channel_id=1, source_target_pairs={{0,16},{16,0},{1,17},{17,1},{2,18},{18,2},{3,19},{19,3},{4,20},{20... | collective-permute-start | bytes 3932168 | tf_op jit(solution)/shard_map/ppermute | solution.py:531
  192.4 2.6 %collective-permute-done.10.far = bf16[16,320,128]{2,1,0:T(8,128)(2,1)S(1)} collective-permute-done((bf16[16,320,128]{2,1,0:T(8,128)(2,1)S(1)}, bf16[16,320,128]{2,1,0:T(8,128)(2,1)S(1)}, u32[]{:S(2)}, u32[]{:S(2)}) %collective-permute-start.10) | collective-permute-done | bytes 1310752 | tf_op jit(solution)/shard_map/ppermute | solution.py:531
  195.0 1.7 shard_map.79
  196.7 2.9 %shard_map.78 = (bf16[4,128,1536]{2,1,0:T(8,128)(2,1)}, f32[4,128,128]{2,1,0:T(8,128)}) custom-call(s32[128]{0:T(128)S(1)} %copy-done.12, s32[4]{0:T(128)S(1)} %copy-done.10, bf16[2,128,1536]{2,1,0:T(8,128)(2,1)S(1)} %copy-done.5, bf16[2,128,1536]{2,1,0:T(8,128)(2,1)S(1)} %copy-done.7, bf16[16,320,128]{2,1,0:T(8,128)(2,1)S(1)} %all-to-all-done.4.near, ...), custom_call_target="tpu_custom_call" | custom-call | flops 1200000000 | bytes 4000000 | tf_op jit(solution)/shard_map/pallas_call | solution.py:536
  (36 shorter events, 4.6 us)
Async XLA Ops:
  9.9 27.3 %all-to-all-start = ((bf16[16,16,128]{2,1,0:T(8,128)(2,1)}), bf16[16,16,128]{2,1,0:T(8,128)(2,1)S(1)}, u32[]{:S(2)}, u32[]{:S(2)}) async-start(bf16[16,16,128]{2,1,0:T(8,128)(2,1)} %get-tuple-element.32), calls=%async_computation | async-start | bytes 131072 | tf_op jit(solution)/shard_map/all_to_all | solution.py:450
  25.7 1.0 copy-start.8
  26.7 1.0 copy-start.9
  27.7 0.6 copy-start.11
  37.2 45.1 %all-to-all-start.1 = ((bf16[16,192,128]{2,1,0:T(8,128)(2,1)}), bf16[16,192,128]{2,1,0:T(8,128)(2,1)S(1)}, u32[]{:S(2)}, u32[]{:S(2)}) async-start(bf16[16,192,128]{2,1,0:T(8,128)(2,1)} %get-tuple-element.33), calls=%async_computation.1 | async-start | bytes 1572864 | tf_op jit(solution)/shard_map/all_to_all | solution.py:450
  41.9 37.5 %copy-start.10 = (s32[4]{0:T(128)S(1)}, s32[4]{0:T(128)}, u32[]{:S(2)}) copy-start(s32[4]{0:T(128)} %pad_add_fusion.place) | copy-start | bytes 52
  41.9 131.3 %all-gather.4.cloned.1.call-start = ((), (), s32[]{:S(2)}) async-start(), calls=%async_computation.5 | async-start | bytes 4177920 | tf_op jit(solution)/shard_map/all_gather | solution.py:486
  41.9 10.0 %collective-permute-start = (bf16[16,16,128]{2,1,0:T(8,128)(2,1)S(1)}, bf16[16,16,128]{2,1,0:T(8,128)(2,1)S(1)}, u32[]{:S(2)}, u32[]{:S(2)}) collective-permute-start(bf16[16,16,128]{2,1,0:T(8,128)(2,1)S(1)} %all-to-all-done), channel_id=1, source_target_pairs={{0,128},{128,256},{256,384},{384,0},{1,129},{129,257},{257,385},{3... | collective-permute-start | bytes 196616 | tf_op jit(solution)/shard_map/ppermute | solution.py:444
  45.1 6.8 %collective-permute-start.1 = (bf16[16,16,128]{2,1,0:T(8,128)(2,1)S(1)}, bf16[16,16,128]{2,1,0:T(8,128)(2,1)S(1)}, u32[]{:S(2)}, u32[]{:S(2)}) collective-permute-start(bf16[16,16,128]{2,1,0:T(8,128)(2,1)S(1)} %all-to-all-done), channel_id=1, source_target_pairs={{0,384},{128,0},{256,128},{384,256},{1,385},{129,1},{257,129},{385... | collective-permute-start | bytes 196616 | tf_op jit(solution)/shard_map/ppermute | solution.py:444
  48.4 6.8 %collective-permute-start.2 = (bf16[16,16,128]{2,1,0:T(8,128)(2,1)S(1)}, bf16[16,16,128]{2,1,0:T(8,128)(2,1)S(1)}, u32[]{:S(2)}, u32[]{:S(2)}) collective-permute-start(bf16[16,16,128]{2,1,0:T(8,128)(2,1)S(1)} %all-to-all-done), channel_id=1, source_target_pairs={{0,256},{128,384},{256,0},{384,128},{1,257},{129,385},{257,1},{385... | collective-permute-start | bytes 196616 | tf_op jit(solution)/shard_map/ppermute | solution.py:444
  55.3 10.1 %collective-permute-start.3 = (bf16[4,16,16,128]{3,2,1,0:T(8,128)(2,1)S(1)}, bf16[4,16,16,128]{3,2,1,0:T(8,128)(2,1)S(1)}, u32[]{:S(2)}, u32[]{:S(2)}) collective-permute-start(bf16[4,16,16,128]{3,2,1,0:T(8,128)(2,1)S(1)} %get-tuple-element.58), channel_id=1, source_target_pairs={{0,32},{32,64},{64,96},{96,0},{1,33},{33,65},{65,97},{97,1},{2,34}... | collective-permute-start | bytes 786440 | tf_op jit(solution)/shard_map/ppermute | solution.py:444
  58.5 7.4 %collective-permute-start.4 = (bf16[4,16,16,128]{3,2,1,0:T(8,128)(2,1)S(1)}, bf16[4,16,16,128]{3,2,1,0:T(8,128)(2,1)S(1)}, u32[]{:S(2)}, u32[]{:S(2)}) collective-permute-start(bf16[4,16,16,128]{3,2,1,0:T(8,128)(2,1)S(1)} %get-tuple-element.58), channel_id=1, source_target_pairs={{0,96},{32,0},{64,32},{96,64},{1,97},{33,1},{65,33},{97,65},{2,98}... | collective-permute-start | bytes 786440 | tf_op jit(solution)/shard_map/ppermute | solution.py:444
  61.9 9.5 %collective-permute-start.5 = (bf16[4,16,16,128]{3,2,1,0:T(8,128)(2,1)S(1)}, bf16[4,16,16,128]{3,2,1,0:T(8,128)(2,1)S(1)}, u32[]{:S(2)}, u32[]{:S(2)}) collective-permute-start(bf16[4,16,16,128]{3,2,1,0:T(8,128)(2,1)S(1)} %get-tuple-element.58), channel_id=1, source_target_pairs={{0,64},{32,96},{64,0},{96,32},{1,65},{33,97},{65,1},{97,33},{2,66}... | collective-permute-start | bytes 786440 | tf_op jit(solution)/shard_map/ppermute | solution.py:444
  71.5 7.9 %collective-permute-start.6 = (bf16[16,16,16,128]{3,2,1,0:T(8,128)(2,1)S(1)}, bf16[16,16,16,128]{3,2,1,0:T(8,128)(2,1)S(1)}, u32[]{:S(2)}, u32[]{:S(2)}) collective-permute-start(bf16[16,16,16,128]{3,2,1,0:T(8,128)(2,1)S(1)} %bitcast.21), channel_id=1, source_target_pairs={{0,16},{16,0},{1,17},{17,1},{2,18},{18,2},{3,19},{19,3},{4,20},{20... | collective-permute-start | bytes 3145736 | tf_op jit(solution)/shard_map/ppermute | solution.py:446
  82.3 5.8 %copy-start = (bf16[16,192,128]{2,1,0:T(8,128)(2,1)}, bf16[16,192,128]{2,1,0:T(8,128)(2,1)S(1)}, u32[]{:S(2)}) copy-start(bf16[16,192,128]{2,1,0:T(8,128)(2,1)S(1)} %all-to-all-done.1.state) | copy-start | bytes 2359300
  88.1 12.2 %collective-permute-start.7 = (f32[16,12,8,128]{3,2,1,0:T(8,128)}, f32[16,12,8,128]{3,2,1,0:T(8,128)}, u32[]{:S(2)}, u32[]{:S(2)}) collective-permute-start(f32[16,12,8,128]{3,2,1,0:T(8,128)} %get-tuple-element.37), channel_id=1, source_target_pairs={{0,16},{16,0},{1,17},{17,1},{2,18},{18,2},{3,19},{19,3},{4,20},{20... | collective-permute-start | bytes 2359304 | tf_op jit(solution)/shard_map/ppermute | solution.py:492
  90.3 3.1 %collective-permute-start.8 = (f32[80,128]{1,0:T(8,128)S(1)}, f32[80,128]{1,0:T(8,128)S(1)}, u32[]{:S(2)}, u32[]{:S(2)}) collective-permute-start(f32[80,128]{1,0:T(8,128)S(1)} %get-tuple-element.41), channel_id=1, source_target_pairs={{0,16},{16,0},{1,17},{17,1},{2,18},{18,2},{3,19},{19,3},{4,20},{20... | collective-permute-start | bytes 122888 | tf_op jit(solution)/shard_map/ppermute | solution.py:487
  94.4 17.2 %all-to-all-start.2 = ((f32[16,80,128]{2,1,0:T(8,128)}), f32[16,80,128]{2,1,0:T(8,128)S(1)}, u32[]{:S(2)}, u32[]{:S(2)}) async-start(f32[16,80,128]{2,1,0:T(8,128)} %broadcast_in_dim.2), calls=%async_computation.2 | async-start | bytes 1310720 | tf_op jit(solution)/shard_map/all_to_all | solution.py:450
  111.6 0.9 copy-start.13
  112.4 16.9 %all-to-all-start.3 = ((f32[16,96,128]{2,1,0:T(8,128)}), f32[16,96,128]{2,1,0:T(8,128)S(1)}, u32[]{:S(2)}, u32[]{:S(2)}) async-start(f32[16,96,128]{2,1,0:T(8,128)} %bitcast.27), calls=%async_computation.3 | async-start | bytes 1572864 | tf_op jit(solution)/shard_map/all_to_all | solution.py:450
  118.0 43.9 %copy-start.12 = (s32[128]{0:T(128)S(1)}, s32[128]{0:T(128)}, u32[]{:S(2)}) copy-start(s32[128]{0:T(128)} %get-tuple-element.30.table) | copy-start | bytes 1540
  118.0 4.6 %collective-permute-start.9 = (f32[80,128]{1,0:T(8,128)S(1)}, f32[80,128]{1,0:T(8,128)S(1)}, u32[]{:S(2)}, u32[]{:S(2)}) collective-permute-start(f32[80,128]{1,0:T(8,128)S(1)} %reduce_sum.9.near), channel_id=1, source_target_pairs={{0,16},{16,0},{1,17},{17,1},{2,18},{18,2},{3,19},{19,3},{4,20},{20... | collective-permute-start | bytes 122888 | tf_op jit(solution)/shard_map/ppermute | solution.py:503
  162.7 1.1 copy-start.2
  163.8 19.4 %all-to-all-start.4 = ((bf16[16,320,128]{2,1,0:T(8,128)(2,1)}), bf16[16,320,128]{2,1,0:T(8,128)(2,1)S(1)}, u32[]{:S(2)}, u32[]{:S(2)}) async-start(bf16[16,320,128]{2,1,0:T(8,128)(2,1)} %copy-done.2), calls=%async_computation.4 | async-start | bytes 2621440 | tf_op jit(solution)/shard_map/all_to_all | solution.py:450
  169.3 1.1 copy-start.1
  171.3 0.9 copy-start.4
  173.2 2.1 %copy-start.3 = (bf16[80,192,128]{2,1,0:T(8,128)(2,1)S(1)}, bf16[80,192,128]{2,1,0:T(8,128)(2,1)}, u32[]{:S(2)}) copy-start(bf16[80,192,128]{2,1,0:T(8,128)(2,1)} %all-gather.4.cloned.1.call-done) | copy-start | bytes 11796484
  178.2 0.9 copy-start.6
  183.2 13.5 %copy-start.5 = (bf16[2,128,1536]{2,1,0:T(8,128)(2,1)S(1)}, bf16[2,128,1536]{2,1,0:T(8,128)(2,1)}, u32[]{:S(2)}) copy-start(bf16[2,128,1536]{2,1,0:T(8,128)(2,1)} %copy-done.4) | copy-start | bytes 2359300
  183.2 13.5 %copy-start.7 = (bf16[2,128,1536]{2,1,0:T(8,128)(2,1)S(1)}, bf16[2,128,1536]{2,1,0:T(8,128)(2,1)}, u32[]{:S(2)}) copy-start(bf16[2,128,1536]{2,1,0:T(8,128)(2,1)} %copy-done.6) | copy-start | bytes 2359300
  183.2 11.9 %collective-permute-start.10 = (bf16[16,320,128]{2,1,0:T(8,128)(2,1)S(1)}, bf16[16,320,128]{2,1,0:T(8,128)(2,1)S(1)}, u32[]{:S(2)}, u32[]{:S(2)}) collective-permute-start(bf16[16,320,128]{2,1,0:T(8,128)(2,1)S(1)} %all-to-all-done.4.near), channel_id=1, source_target_pairs={{0,16},{16,0},{1,17},{17,1},{2,18},{18,2},{3,19},{19,3},{4,20},{20... | collective-permute-start | bytes 3932168 | tf_op jit(solution)/shard_map/ppermute | solution.py:531
Sparse Core Ops, SparseCore 0:
  85.4 71.3 all-gather.3

commit v11 on v10

--- a/solution.py
+++ b/solution.py
@@ -174,20 +174,17 @@
     return lax.fori_loop(0, GROUPS, block, jnp.zeros((128, RANK), F32), unroll=4)
 
 
-PACKED = 80
+PACKED = 96
 
 
 def pack(gram):
-    middle = jnp.concatenate([gram[96:, 96:], gram[32:64, 32:]], axis=1)
-    last = jnp.concatenate([gram[80:96, 64:], gram[64:80, 64:]], axis=1)
-    return jnp.concatenate([gram[:32], middle, last], axis=0)
+    last = jnp.concatenate([gram[96:, 64:], gram[64:96, 64:]], axis=1)
+    return jnp.concatenate([gram[:64], last], axis=0)
 
 
 def unpack(packed):
-    middle, last = packed[32:64], packed[64:]
-    other = jnp.concatenate([last[:, 64:], last[:, :64]], axis=1)
-    corner = jnp.concatenate([middle[:, 32:], middle[:, :32]], axis=1)
-    return jnp.concatenate([packed[:32], middle, last, other, corner], axis=0)
+    other = jnp.concatenate([packed[64:, 64:], packed[64:, :64]], axis=1)
+    return jnp.concatenate([packed, other], axis=0)
 
 
 def panels(place, state, right, panel, keep, send):

time: 208 us -> 208 us (level)
    unnamed x28 -> x26, local copies, waits for them, and re-layouts: 9.61 us -> 8.8 us
  transfers between devices with their start and end apart: 17 -> 17, of which waited for: 11 -> 10; matrix products, arithmetic and copies ran while one was open for 2% -> 2% of each run, Pallas kernels for 10% -> 10%
where the time goes in v11:
time: 208 us; the launch traced here: 207 us
  starting transfers between devices  80.8 us (39%)
  waiting for transfers between devices  38.2 us (18%)
  blocking collectives  31.4 us (15%)
  Pallas kernels  29.2 us (14%)
  between operations  14.4 us (7%)
  local copies, waits for them, and re-layouts  9.76 us (5%)
  other arithmetic  2.97 us (1%)
    all_to_all x5, starting transfers between devices, exchange(): return lax.all_to_all(x, axis, split_axis=0, concat_axis=0, tiled=True)  37.2 us
    all_gather x1, blocking collectives, shards(): tiles = lax.all_gather(mine, 'z')  31.4 us
    all_to_all x5, waiting for transfers between devices, exchange(): return lax.all_to_all(x, axis, split_axis=0, concat_axis=0, tiled=True)  23.1 us
    ppermute x6, starting transfers between devices, gather_slices(): lax.ppermute(x, axis, ring((4 - d) % 4))  20 us
    ppermute x1, starting transfers between devices, shards(): far = lax.ppermute(near, 'c', SWAP)  9.52 us
    ppermute x6, waiting for transfers between devices, gather_slices(): lax.ppermute(x, axis, ring((4 - d) % 4))  9.27 us
    unnamed x26, local copies, waits for them, and re-layouts  8.8 us
    ppermute x1, starting transfers between devices, gather_slices(): return (x, lax.ppermute(x, 'c', SWAP))  5.62 us
  transfers between devices with their start and end apart: 17, of which 10 were waited for; matrix products, arithmetic and copies ran while one was open for 2% of the time, Pallas kernels for 10%

profile of v11, /device:TPU:1, one launch (start us, length us, event | category | flops | bytes accessed | tf_op | source)
XLA Modules:
  0.0 206.8 jit_solution(13246481247475064269)
XLA Ops:
  7.8 2.1 %shard_map.67 = (bf16[16,16,128]{2,1,0:T(8,128)(2,1)}, s32[128]{0:T(128)}) custom-call(s32[10]{0:T(128)} %own.1, s32[4]{0:T(128)} %pad_add_fusion.place, bf16[10,2,96,128]{3,2,1,0:T(8,128)(2,1)} %right.1), custom_call_target="tpu_custom_call" | custom-call | tf_op jit(solution)/shard_map/pallas_call | solution.py:454
  9.9 15.8 %all-to-all-start = ((bf16[16,16,128]{2,1,0:T(8,128)(2,1)}), bf16[16,16,128]{2,1,0:T(8,128)(2,1)S(1)}, u32[]{:S(2)}, u32[]{:S(2)}) async-start(bf16[16,16,128]{2,1,0:T(8,128)(2,1)} %get-tuple-element.32), calls=%async_computation | async-start | bytes 131072 | tf_op jit(solution)/shard_map/all_to_all | solution.py:447
  25.7 1.0 copy-done.8
  26.7 1.0 copy-done.9
  28.4 2.0 shard_map.68
  30.4 6.8 %all-to-all-done = bf16[16,16,128]{2,1,0:T(8,128)(2,1)S(1)} async-done(((bf16[16,16,128]{2,1,0:T(8,128)(2,1)}), bf16[16,16,128]{2,1,0:T(8,128)(2,1)S(1)}, u32[]{:S(2)}, u32[]{:S(2)}) %all-to-all-start) | async-done | bytes 65568 | tf_op jit(solution)/shard_map/all_to_all | solution.py:447
  37.2 4.7 %all-to-all-start.1 = ((bf16[16,192,128]{2,1,0:T(8,128)(2,1)}), bf16[16,192,128]{2,1,0:T(8,128)(2,1)S(1)}, u32[]{:S(2)}, u32[]{:S(2)}) async-start(bf16[16,192,128]{2,1,0:T(8,128)(2,1)} %get-tuple-element.33), calls=%async_computation.1 | async-start | bytes 1572864 | tf_op jit(solution)/shard_map/all_to_all | solution.py:447
  41.9 3.1 %collective-permute-start = (bf16[16,16,128]{2,1,0:T(8,128)(2,1)S(1)}, bf16[16,16,128]{2,1,0:T(8,128)(2,1)S(1)}, u32[]{:S(2)}, u32[]{:S(2)}) collective-permute-start(bf16[16,16,128]{2,1,0:T(8,128)(2,1)S(1)} %all-to-all-done), channel_id=1, source_target_pairs={{0,128},{128,256},{256,384},{384,0},{1,129},{129,257},{257,385},{3... | collective-permute-start | bytes 196616 | tf_op jit(solution)/shard_map/ppermute | solution.py:441
  45.1 3.4 %collective-permute-start.1 = (bf16[16,16,128]{2,1,0:T(8,128)(2,1)S(1)}, bf16[16,16,128]{2,1,0:T(8,128)(2,1)S(1)}, u32[]{:S(2)}, u32[]{:S(2)}) collective-permute-start(bf16[16,16,128]{2,1,0:T(8,128)(2,1)S(1)} %all-to-all-done), channel_id=1, source_target_pairs={{0,384},{128,0},{256,128},{384,256},{1,385},{129,1},{257,129},{385... | collective-permute-start | bytes 196616 | tf_op jit(solution)/shard_map/ppermute | solution.py:441
  48.4 3.4 %collective-permute-start.2 = (bf16[16,16,128]{2,1,0:T(8,128)(2,1)S(1)}, bf16[16,16,128]{2,1,0:T(8,128)(2,1)S(1)}, u32[]{:S(2)}, u32[]{:S(2)}) collective-permute-start(bf16[16,16,128]{2,1,0:T(8,128)(2,1)S(1)} %all-to-all-done), channel_id=1, source_target_pairs={{0,256},{128,384},{256,0},{384,128},{1,257},{129,385},{257,1},{385... | collective-permute-start | bytes 196616 | tf_op jit(solution)/shard_map/ppermute | solution.py:441
  51.9 3.3 %collective-permute-done.2 = bf16[16,16,128]{2,1,0:T(8,128)(2,1)S(1)} collective-permute-done((bf16[16,16,128]{2,1,0:T(8,128)(2,1)S(1)}, bf16[16,16,128]{2,1,0:T(8,128)(2,1)S(1)}, u32[]{:S(2)}, u32[]{:S(2)}) %collective-permute-start.2) | collective-permute-done | bytes 65568 | tf_op jit(solution)/shard_map/ppermute | solution.py:441
  55.3 3.2 %collective-permute-start.3 = (bf16[4,16,16,128]{3,2,1,0:T(8,128)(2,1)S(1)}, bf16[4,16,16,128]{3,2,1,0:T(8,128)(2,1)S(1)}, u32[]{:S(2)}, u32[]{:S(2)}) collective-permute-start(bf16[4,16,16,128]{3,2,1,0:T(8,128)(2,1)S(1)} %get-tuple-element.58), channel_id=1, source_target_pairs={{0,32},{32,64},{64,96},{96,0},{1,33},{33,65},{65,97},{97,1},{2,34}... | collective-permute-start | bytes 786440 | tf_op jit(solution)/shard_map/ppermute | solution.py:441
  58.5 3.4 %collective-permute-start.4 = (bf16[4,16,16,128]{3,2,1,0:T(8,128)(2,1)S(1)}, bf16[4,16,16,128]{3,2,1,0:T(8,128)(2,1)S(1)}, u32[]{:S(2)}, u32[]{:S(2)}) collective-permute-start(bf16[4,16,16,128]{3,2,1,0:T(8,128)(2,1)S(1)} %get-tuple-element.58), channel_id=1, source_target_pairs={{0,96},{32,0},{64,32},{96,64},{1,97},{33,1},{65,33},{97,65},{2,98}... | collective-permute-start | bytes 786440 | tf_op jit(solution)/shard_map/ppermute | solution.py:441
  61.9 3.5 %collective-permute-start.5 = (bf16[4,16,16,128]{3,2,1,0:T(8,128)(2,1)S(1)}, bf16[4,16,16,128]{3,2,1,0:T(8,128)(2,1)S(1)}, u32[]{:S(2)}, u32[]{:S(2)}) collective-permute-start(bf16[4,16,16,128]{3,2,1,0:T(8,128)(2,1)S(1)} %get-tuple-element.58), channel_id=1, source_target_pairs={{0,64},{32,96},{64,0},{96,32},{1,65},{33,97},{65,1},{97,33},{2,66}... | collective-permute-start | bytes 786440 | tf_op jit(solution)/shard_map/ppermute | solution.py:441
  65.9 5.4 %collective-permute-done.5 = bf16[4,16,16,128]{3,2,1,0:T(8,128)(2,1)S(1)} collective-permute-done((bf16[4,16,16,128]{3,2,1,0:T(8,128)(2,1)S(1)}, bf16[4,16,16,128]{3,2,1,0:T(8,128)(2,1)S(1)}, u32[]{:S(2)}, u32[]{:S(2)}) %collective-permute-start.5) | collective-permute-done | bytes 262176 | tf_op jit(solution)/shard_map/ppermute | solution.py:441
  71.5 5.6 %collective-permute-start.6 = (bf16[16,16,16,128]{3,2,1,0:T(8,128)(2,1)S(1)}, bf16[16,16,16,128]{3,2,1,0:T(8,128)(2,1)S(1)}, u32[]{:S(2)}, u32[]{:S(2)}) collective-permute-start(bf16[16,16,16,128]{3,2,1,0:T(8,128)(2,1)S(1)} %bitcast.21), channel_id=1, source_target_pairs={{0,16},{16,0},{1,17},{17,1},{2,18},{18,2},{3,19},{19,3},{4,20},{20... | collective-permute-start | bytes 3145736 | tf_op jit(solution)/shard_map/ppermute | solution.py:443
  77.1 2.3 %collective-permute-done.6.far = bf16[16,16,16,128]{3,2,1,0:T(8,128)(2,1)S(1)} collective-permute-done((bf16[16,16,16,128]{3,2,1,0:T(8,128)(2,1)S(1)}, bf16[16,16,16,128]{3,2,1,0:T(8,128)(2,1)S(1)}, u32[]{:S(2)}, u32[]{:S(2)}) %collective-permute-start.6) | collective-permute-done | bytes 1048608 | tf_op jit(solution)/shard_map/ppermute | solution.py:443
  79.4 2.9 %shard_map.69.right = bf16[16,384,128]{2,1,0:T(8,128)(2,1)S(1)} custom-call(s32[4]{0:T(128)S(1)} %copy-done.10, bf16[16,16,16,128]{3,2,1,0:T(8,128)(2,1)S(1)} %bitcast.22, bf16[16,16,16,128]{3,2,1,0:T(8,128)(2,1)S(1)} %collective-permute-done.6.far), custom_call_target="tpu_custom_call" | custom-call | flops 800000000 | bytes 4000000 | tf_op jit(solution)/shard_map/pallas_call | solution.py:470
  82.3 2.9 %shard_map.70 = (f32[2,128,128]{2,1,0:T(8,128)S(1)}, f32[96,128]{1,0:T(8,128)S(1)}, f32[96,128]{1,0:T(8,128)S(1)}) custom-call(s32[4]{0:T(128)S(1)} %copy-done.10, bf16[16,192,128]{2,1,0:T(8,128)(2,1)S(1)} %all-to-all-done.1.state, bf16[16,384,128]{2,1,0:T(8,128)(2,1)S(1)} %shard_map.69.right), custom_call_target="tpu_custom_call" | custom-call | flops 300000000 | bytes 4000000 | tf_op jit(solution)/shard_map/pallas_call | solution.py:479
  85.3 2.3 %collective-permute-start.8 = (f32[96,128]{1,0:T(8,128)S(1)}, f32[96,128]{1,0:T(8,128)S(1)}, u32[]{:S(2)}, u32[]{:S(2)}) collective-permute-start(f32[96,128]{1,0:T(8,128)S(1)} %get-tuple-element.41), channel_id=1, source_target_pairs={{0,16},{16,0},{1,17},{17,1},{2,18},{18,2},{3,19},{19,3},{4,20},{20... | collective-permute-start | bytes 147464 | tf_op jit(solution)/shard_map/ppermute | solution.py:484
  87.6 2.8 %shard_map.71 = (f32[16,12,8,128]{3,2,1,0:T(8,128)S(1)}, f32[16,12,8,128]{3,2,1,0:T(8,128)}) custom-call(s32[4]{0:T(128)S(1)} %copy-done.10, bf16[16,192,128]{2,1,0:T(8,128)(2,1)S(1)} %all-to-all-done.1.state, f32[2,128,128]{2,1,0:T(8,128)S(1)} %get-tuple-element.35.panel), custom_call_target="tpu_custom_call" | custom-call | flops 400000000 | bytes 4000000 | tf_op jit(solution)/shard_map/pallas_call | solution.py:486
  90.4 2.0 collective-permute-start.7
  92.5 1.0 broadcast_in_dim.2
  93.4 5.8 %all-to-all-start.2 = ((f32[16,96,128]{2,1,0:T(8,128)}), f32[16,96,128]{2,1,0:T(8,128)}, u32[]{:S(2)}, u32[]{:S(2)}) async-start(f32[16,96,128]{2,1,0:T(8,128)} %broadcast_in_dim.2), calls=%async_computation.2 | async-start | bytes 1572864 | tf_op jit(solution)/shard_map/all_to_all | solution.py:447
  99.2 1.0 add.6
  100.2 11.8 %all-to-all-done.2 = f32[16,96,128]{2,1,0:T(8,128)} async-done(((f32[16,96,128]{2,1,0:T(8,128)}), f32[16,96,128]{2,1,0:T(8,128)}, u32[]{:S(2)}, u32[]{:S(2)}) %all-to-all-start.2) | async-done | bytes 786464 | tf_op jit(solution)/shard_map/all_to_all | solution.py:447
  112.0 4.1 %all-to-all-start.3 = ((f32[16,96,128]{2,1,0:T(8,128)}), f32[16,96,128]{2,1,0:T(8,128)S(1)}, u32[]{:S(2)}, u32[]{:S(2)}) async-start(f32[16,96,128]{2,1,0:T(8,128)} %bitcast.27), calls=%async_computation.3 | async-start | bytes 1572864 | tf_op jit(solution)/shard_map/all_to_all | solution.py:447
  116.2 1.2 reduce_sum.9.near
  117.4 4.1 %collective-permute-start.9 = (f32[96,128]{1,0:T(8,128)S(1)}, f32[96,128]{1,0:T(8,128)S(1)}, u32[]{:S(2)}, u32[]{:S(2)}) collective-permute-start(f32[96,128]{1,0:T(8,128)S(1)} %reduce_sum.9.near), channel_id=1, source_target_pairs={{0,16},{16,0},{1,17},{17,1},{2,18},{18,2},{3,19},{19,3},{4,20},{20... | collective-permute-start | bytes 147464 | tf_op jit(solution)/shard_map/ppermute | solution.py:500
  121.5 0.9 collective-permute-done.9.far
  122.3 5.5 %shard_map.72.inverse = f32[2,128,128]{2,1,0:T(8,128)S(1)} custom-call(s32[4]{0:T(128)S(1)} %copy-done.10, f32[96,128]{1,0:T(8,128)S(1)} %reduce_sum.9.near, f32[96,128]{1,0:T(8,128)S(1)} %collective-permute-done.9.far), custom_call_target="tpu_custom_call" | custom-call | flops 2000000000 | bytes 4000000 | tf_op jit(solution)/shard_map/pallas_call | solution.py:494
  128.2 0.9 shard_map.73.mine
  129.1 31.4 %all-gather = bf16[1792,128]{1,0:T(8,128)(2,1)S(1)} all-gather(bf16[112,128]{1,0:T(8,128)(2,1)S(1)} %shard_map.73.mine), channel_id=2, replica_groups=mesh['x'=4,'y'=4,'c'=2,'z'=16] {'z'}, dimensions={0}, use_global_device_ids=true | all-gather | bytes 487424 | tf_op jit(solution)/shard_map/all_gather | solution.py:510
  160.5 0.9 shard_map.74
  161.4 1.0 copy-done.2
  162.4 6.9 %all-to-all-start.4 = ((bf16[16,320,128]{2,1,0:T(8,128)(2,1)}), bf16[16,320,128]{2,1,0:T(8,128)(2,1)S(1)}, u32[]{:S(2)}, u32[]{:S(2)}) async-start(bf16[16,320,128]{2,1,0:T(8,128)(2,1)} %copy-done.2), calls=%async_computation.4 | async-start | bytes 2621440 | tf_op jit(solution)/shard_map/all_to_all | solution.py:447
  169.3 1.1 copy-done.1
  170.4 0.9 shard_map.75.turned
  171.4 0.9 copy-done.4
  172.2 0.9 shard_map.76
  173.2 2.1 %copy-done.3 = bf16[80,192,128]{2,1,0:T(8,128)(2,1)S(1)} copy-done((bf16[80,192,128]{2,1,0:T(8,128)(2,1)S(1)}, bf16[80,192,128]{2,1,0:T(8,128)(2,1)}, u32[]{:S(2)}) %copy-start.3) | copy-done | bytes 3932184
  175.3 2.9 %shard_map.77 = (f32[2,128,128]{2,1,0:T(8,128)S(1)}, bf16[2,128,1536]{2,1,0:T(8,128)(2,1)S(1)}) custom-call(s32[128]{0:T(128)S(1)} %copy-done.12, s32[4]{0:T(128)S(1)} %copy-done.10, bf16[16,5,192,128]{3,2,1,0:T(8,128)(2,1)S(1)} %bitcast.23, bf16[16,384,128]{2,1,0:T(8,128)(2,1)S(1)} %shard_map.69.right), custom_call_target="tpu_custom_call" | custom-call | flops 300000000 | bytes 4000000 | tf_op jit(solution)/shard_map/pallas_call | solution.py:511
  178.2 0.9 copy-done.6
  179.1 4.2 %all-to-all-done.4.near = bf16[16,320,128]{2,1,0:T(8,128)(2,1)S(1)} async-done(((bf16[16,320,128]{2,1,0:T(8,128)(2,1)}), bf16[16,320,128]{2,1,0:T(8,128)(2,1)S(1)}, u32[]{:S(2)}, u32[]{:S(2)}) %all-to-all-start.4) | async-done | bytes 1310752 | tf_op jit(solution)/shard_map/all_to_all | solution.py:447
  183.3 9.5 %collective-permute-start.10 = (bf16[16,320,128]{2,1,0:T(8,128)(2,1)S(1)}, bf16[16,320,128]{2,1,0:T(8,128)(2,1)S(1)}, u32[]{:S(2)}, u32[]{:S(2)}) collective-permute-start(bf16[16,320,128]{2,1,0:T(8,128)(2,1)S(1)} %all-to-all-done.4.near), channel_id=1, source_target_pairs={{0,16},{16,0},{1,17},{17,1},{2,18},{18,2},{3,19},{19,3},{4,20},{20... | collective-permute-start | bytes 3932168 | tf_op jit(solution)/shard_map/ppermute | solution.py:528
  192.8 2.6 %collective-permute-done.10.far = bf16[16,320,128]{2,1,0:T(8,128)(2,1)S(1)} collective-permute-done((bf16[16,320,128]{2,1,0:T(8,128)(2,1)S(1)}, bf16[16,320,128]{2,1,0:T(8,128)(2,1)S(1)}, u32[]{:S(2)}, u32[]{:S(2)}) %collective-permute-start.10) | collective-permute-done | bytes 1310752 | tf_op jit(solution)/shard_map/ppermute | solution.py:528
  195.5 1.7 shard_map.79
  197.1 2.8 %shard_map.78 = (bf16[4,128,1536]{2,1,0:T(8,128)(2,1)}, f32[4,128,128]{2,1,0:T(8,128)}) custom-call(s32[128]{0:T(128)S(1)} %copy-done.12, s32[4]{0:T(128)S(1)} %copy-done.10, bf16[2,128,1536]{2,1,0:T(8,128)(2,1)S(1)} %copy-done.5, bf16[2,128,1536]{2,1,0:T(8,128)(2,1)S(1)} %copy-done.7, bf16[16,320,128]{2,1,0:T(8,128)(2,1)S(1)} %all-to-all-done.4.near, ...), custom_call_target="tpu_custom_call" | custom-call | flops 1200000000 | bytes 4000000 | tf_op jit(solution)/shard_map/pallas_call | solution.py:533
  (34 shorter events, 2.4 us)
Async XLA Ops:
  9.9 27.3 %all-to-all-start = ((bf16[16,16,128]{2,1,0:T(8,128)(2,1)}), bf16[16,16,128]{2,1,0:T(8,128)(2,1)S(1)}, u32[]{:S(2)}, u32[]{:S(2)}) async-start(bf16[16,16,128]{2,1,0:T(8,128)(2,1)} %get-tuple-element.32), calls=%async_computation | async-start | bytes 131072 | tf_op jit(solution)/shard_map/all_to_all | solution.py:447
  25.6 1.0 copy-start.8
  26.7 1.0 copy-start.9
  27.7 0.7 copy-start.11
  37.2 45.1 %all-to-all-start.1 = ((bf16[16,192,128]{2,1,0:T(8,128)(2,1)}), bf16[16,192,128]{2,1,0:T(8,128)(2,1)S(1)}, u32[]{:S(2)}, u32[]{:S(2)}) async-start(bf16[16,192,128]{2,1,0:T(8,128)(2,1)} %get-tuple-element.33), calls=%async_computation.1 | async-start | bytes 1572864 | tf_op jit(solution)/shard_map/all_to_all | solution.py:447
  41.9 37.5 %copy-start.10 = (s32[4]{0:T(128)S(1)}, s32[4]{0:T(128)}, u32[]{:S(2)}) copy-start(s32[4]{0:T(128)} %pad_add_fusion.place) | copy-start | bytes 52
  41.9 131.3 %all-gather.4.cloned.1.call-start = ((), (), s32[]{:S(2)}) async-start(), calls=%async_computation.5 | async-start | bytes 4177920 | tf_op jit(solution)/shard_map/all_gather | solution.py:483
  41.9 10.0 %collective-permute-start = (bf16[16,16,128]{2,1,0:T(8,128)(2,1)S(1)}, bf16[16,16,128]{2,1,0:T(8,128)(2,1)S(1)}, u32[]{:S(2)}, u32[]{:S(2)}) collective-permute-start(bf16[16,16,128]{2,1,0:T(8,128)(2,1)S(1)} %all-to-all-done), channel_id=1, source_target_pairs={{0,128},{128,256},{256,384},{384,0},{1,129},{129,257},{257,385},{3... | collective-permute-start | bytes 196616 | tf_op jit(solution)/shard_map/ppermute | solution.py:441
  45.1 6.8 %collective-permute-start.1 = (bf16[16,16,128]{2,1,0:T(8,128)(2,1)S(1)}, bf16[16,16,128]{2,1,0:T(8,128)(2,1)S(1)}, u32[]{:S(2)}, u32[]{:S(2)}) collective-permute-start(bf16[16,16,128]{2,1,0:T(8,128)(2,1)S(1)} %all-to-all-done), channel_id=1, source_target_pairs={{0,384},{128,0},{256,128},{384,256},{1,385},{129,1},{257,129},{385... | collective-permute-start | bytes 196616 | tf_op jit(solution)/shard_map/ppermute | solution.py:441
  48.4 6.8 %collective-permute-start.2 = (bf16[16,16,128]{2,1,0:T(8,128)(2,1)S(1)}, bf16[16,16,128]{2,1,0:T(8,128)(2,1)S(1)}, u32[]{:S(2)}, u32[]{:S(2)}) collective-permute-start(bf16[16,16,128]{2,1,0:T(8,128)(2,1)S(1)} %all-to-all-done), channel_id=1, source_target_pairs={{0,256},{128,384},{256,0},{384,128},{1,257},{129,385},{257,1},{385... | collective-permute-start | bytes 196616 | tf_op jit(solution)/shard_map/ppermute | solution.py:441
  55.3 10.1 %collective-permute-start.3 = (bf16[4,16,16,128]{3,2,1,0:T(8,128)(2,1)S(1)}, bf16[4,16,16,128]{3,2,1,0:T(8,128)(2,1)S(1)}, u32[]{:S(2)}, u32[]{:S(2)}) collective-permute-start(bf16[4,16,16,128]{3,2,1,0:T(8,128)(2,1)S(1)} %get-tuple-element.58), channel_id=1, source_target_pairs={{0,32},{32,64},{64,96},{96,0},{1,33},{33,65},{65,97},{97,1},{2,34}... | collective-permute-start | bytes 786440 | tf_op jit(solution)/shard_map/ppermute | solution.py:441
  58.5 7.4 %collective-permute-start.4 = (bf16[4,16,16,128]{3,2,1,0:T(8,128)(2,1)S(1)}, bf16[4,16,16,128]{3,2,1,0:T(8,128)(2,1)S(1)}, u32[]{:S(2)}, u32[]{:S(2)}) collective-permute-start(bf16[4,16,16,128]{3,2,1,0:T(8,128)(2,1)S(1)} %get-tuple-element.58), channel_id=1, source_target_pairs={{0,96},{32,0},{64,32},{96,64},{1,97},{33,1},{65,33},{97,65},{2,98}... | collective-permute-start | bytes 786440 | tf_op jit(solution)/shard_map/ppermute | solution.py:441
  61.9 9.5 %collective-permute-start.5 = (bf16[4,16,16,128]{3,2,1,0:T(8,128)(2,1)S(1)}, bf16[4,16,16,128]{3,2,1,0:T(8,128)(2,1)S(1)}, u32[]{:S(2)}, u32[]{:S(2)}) collective-permute-start(bf16[4,16,16,128]{3,2,1,0:T(8,128)(2,1)S(1)} %get-tuple-element.58), channel_id=1, source_target_pairs={{0,64},{32,96},{64,0},{96,32},{1,65},{33,97},{65,1},{97,33},{2,66}... | collective-permute-start | bytes 786440 | tf_op jit(solution)/shard_map/ppermute | solution.py:441
  71.5 7.9 %collective-permute-start.6 = (bf16[16,16,16,128]{3,2,1,0:T(8,128)(2,1)S(1)}, bf16[16,16,16,128]{3,2,1,0:T(8,128)(2,1)S(1)}, u32[]{:S(2)}, u32[]{:S(2)}) collective-permute-start(bf16[16,16,16,128]{3,2,1,0:T(8,128)(2,1)S(1)} %bitcast.21), channel_id=1, source_target_pairs={{0,16},{16,0},{1,17},{17,1},{2,18},{18,2},{3,19},{19,3},{4,20},{20... | collective-permute-start | bytes 3145736 | tf_op jit(solution)/shard_map/ppermute | solution.py:443
  82.3 8.1 %copy-start = (bf16[16,192,128]{2,1,0:T(8,128)(2,1)}, bf16[16,192,128]{2,1,0:T(8,128)(2,1)S(1)}, u32[]{:S(2)}) copy-start(bf16[16,192,128]{2,1,0:T(8,128)(2,1)S(1)} %all-to-all-done.1.state) | copy-start | bytes 2359300
  85.3 7.2 %collective-permute-start.8 = (f32[96,128]{1,0:T(8,128)S(1)}, f32[96,128]{1,0:T(8,128)S(1)}, u32[]{:S(2)}, u32[]{:S(2)}) collective-permute-start(f32[96,128]{1,0:T(8,128)S(1)} %get-tuple-element.41), channel_id=1, source_target_pairs={{0,16},{16,0},{1,17},{17,1},{2,18},{18,2},{3,19},{19,3},{4,20},{20... | collective-permute-start | bytes 147464 | tf_op jit(solution)/shard_map/ppermute | solution.py:484
  90.4 8.8 %collective-permute-start.7 = (f32[16,12,8,128]{3,2,1,0:T(8,128)}, f32[16,12,8,128]{3,2,1,0:T(8,128)S(1)}, u32[]{:S(2)}, u32[]{:S(2)}) collective-permute-start(f32[16,12,8,128]{3,2,1,0:T(8,128)} %get-tuple-element.37), channel_id=1, source_target_pairs={{0,16},{16,0},{1,17},{17,1},{2,18},{18,2},{3,19},{19,3},{4,20},{20... | collective-permute-start | bytes 2359304 | tf_op jit(solution)/shard_map/ppermute | solution.py:489
  93.4 18.6 %all-to-all-start.2 = ((f32[16,96,128]{2,1,0:T(8,128)}), f32[16,96,128]{2,1,0:T(8,128)}, u32[]{:S(2)}, u32[]{:S(2)}) async-start(f32[16,96,128]{2,1,0:T(8,128)} %broadcast_in_dim.2), calls=%async_computation.2 | async-start | bytes 1572864 | tf_op jit(solution)/shard_map/all_to_all | solution.py:447
  112.0 16.1 %all-to-all-start.3 = ((f32[16,96,128]{2,1,0:T(8,128)}), f32[16,96,128]{2,1,0:T(8,128)S(1)}, u32[]{:S(2)}, u32[]{:S(2)}) async-start(f32[16,96,128]{2,1,0:T(8,128)} %bitcast.27), calls=%async_computation.3 | async-start | bytes 1572864 | tf_op jit(solution)/shard_map/all_to_all | solution.py:447
  117.4 43.1 %copy-start.12 = (s32[128]{0:T(128)S(1)}, s32[128]{0:T(128)}, u32[]{:S(2)}) copy-start(s32[128]{0:T(128)} %get-tuple-element.30.table) | copy-start | bytes 1540
  117.4 5.0 %collective-permute-start.9 = (f32[96,128]{1,0:T(8,128)S(1)}, f32[96,128]{1,0:T(8,128)S(1)}, u32[]{:S(2)}, u32[]{:S(2)}) collective-permute-start(f32[96,128]{1,0:T(8,128)S(1)} %reduce_sum.9.near), channel_id=1, source_target_pairs={{0,16},{16,0},{1,17},{17,1},{2,18},{18,2},{3,19},{19,3},{4,20},{20... | collective-permute-start | bytes 147464 | tf_op jit(solution)/shard_map/ppermute | solution.py:500
  161.4 1.1 copy-start.2
  162.4 20.8 %all-to-all-start.4 = ((bf16[16,320,128]{2,1,0:T(8,128)(2,1)}), bf16[16,320,128]{2,1,0:T(8,128)(2,1)S(1)}, u32[]{:S(2)}, u32[]{:S(2)}) async-start(bf16[16,320,128]{2,1,0:T(8,128)(2,1)} %copy-done.2), calls=%async_computation.4 | async-start | bytes 2621440 | tf_op jit(solution)/shard_map/all_to_all | solution.py:447
  169.3 1.1 copy-start.1
  171.4 0.9 copy-start.4
  173.2 2.1 %copy-start.3 = (bf16[80,192,128]{2,1,0:T(8,128)(2,1)S(1)}, bf16[80,192,128]{2,1,0:T(8,128)(2,1)}, u32[]{:S(2)}) copy-start(bf16[80,192,128]{2,1,0:T(8,128)(2,1)} %all-gather.4.cloned.1.call-done) | copy-start | bytes 11796484
  178.2 0.9 copy-start.6
  183.3 13.8 %copy-start.5 = (bf16[2,128,1536]{2,1,0:T(8,128)(2,1)S(1)}, bf16[2,128,1536]{2,1,0:T(8,128)(2,1)}, u32[]{:S(2)}) copy-start(bf16[2,128,1536]{2,1,0:T(8,128)(2,1)} %copy-done.4) | copy-start | bytes 2359300
  183.3 13.8 %copy-start.7 = (bf16[2,128,1536]{2,1,0:T(8,128)(2,1)S(1)}, bf16[2,128,1536]{2,1,0:T(8,128)(2,1)}, u32[]{:S(2)}) copy-start(bf16[2,128,1536]{2,1,0:T(8,128)(2,1)} %copy-done.6) | copy-start | bytes 2359300
  183.3 12.2 %collective-permute-start.10 = (bf16[16,320,128]{2,1,0:T(8,128)(2,1)S(1)}, bf16[16,320,128]{2,1,0:T(8,128)(2,1)S(1)}, u32[]{:S(2)}, u32[]{:S(2)}) collective-permute-start(bf16[16,320,128]{2,1,0:T(8,128)(2,1)S(1)} %all-to-all-done.4.near), channel_id=1, source_target_pairs={{0,16},{16,0},{1,17},{17,1},{2,18},{18,2},{3,19},{19,3},{4,20},{20... | collective-permute-start | bytes 3932168 | tf_op jit(solution)/shard_map/ppermute | solution.py:528
Sparse Core Ops, SparseCore 0:
  85.4 72.1 all-gather.3

commit v12 on v11

--- a/solution.py
+++ b/solution.py
@@ -174,26 +174,13 @@
     return lax.fori_loop(0, GROUPS, block, jnp.zeros((128, RANK), F32), unroll=4)
 
 
-PACKED = 96
-
-
-def pack(gram):
-    last = jnp.concatenate([gram[96:, 64:], gram[64:96, 64:]], axis=1)
-    return jnp.concatenate([gram[:64], last], axis=0)
-
-
-def unpack(packed):
-    other = jnp.concatenate([packed[64:, 64:], packed[64:, :64]], axis=1)
-    return jnp.concatenate([packed, other], axis=0)
-
-
 def panels(place, state, right, panel, keep, send):
     grams = []
     for k in range(2):
         rows = slice(k * BLOCK, (k + 1) * BLOCK)
         value = panel_of(lambda z: state[z, rows, :], right, k, 0)
         panel[k] = value
-        grams.append(pack(dot(value, value, ((0,), (0,)), HIGHEST)))
+        grams.append(dot(value, value, ((0,), (0,)), HIGHEST))
     mine = place[2] == 0
     keep[...] = jnp.where(mine, grams[0], grams[1])
     send[...] = jnp.where(mine, grams[1], grams[0])
@@ -293,7 +280,7 @@
     n = RANK
     eye = (iota((n, n), 0) == iota((n, n), 1)).astype(F32)
     mine = place[2] == 0
-    first, other = unpack(near[...]), unpack(far[...])
+    first, other = near[...], far[...]
     work[0, :, :n] = jnp.where(mine, first, other) + ridge_term * eye
     work[1, :, :n] = jnp.where(mine, other, first) + ridge_term * eye
     for m in range(2):
@@ -393,9 +380,11 @@
             out[e, k] = blocks[e, rows, :] * scale[2 * e + k : 2 * e + k + 1, :]
 
 
-def finish_state(
-    table, place, turned, second, near, far, low, panel, left, out, left_out, inverse, factor
+def finish(
+    table, place, turned, second, near, far, low, panel, left,
+    out, left_out, right_out, inverse, factor, blocks,
 ):
+    finish_right(place, near, far, right_out, blocks)
     for part, core in ((near, place[2]), (far, 1 - place[2])):
         for chip in range(16):
             x, y = chip // 4, chip % 4
@@ -474,7 +463,7 @@
         flops=800_000_000,
         specs=[SMEM, VMEM, VMEM],
     )(place, near, far)
-    square = sds((PACKED, RANK), F32)
+    square = sds((RANK, RANK), F32)
     two = sds((2, 128, RANK), F32)
     panel, keep, send = call(
         panels, (two, square, square), specs=[SMEM, VMEM, VMEM], flops=300_000_000
@@ -487,7 +476,7 @@
         weigh, (half, half), [pltpu.VMEM((4, 192, RANK), F32)], specs=[SMEM, VMEM, VMEM], flops=400_000_000
     )(place, state, panel)
     parts = keep + lax.ppermute(send, "c", SWAP)
-    gram = exchange(jnp.broadcast_to(gram[None], (16, PACKED, RANK)), XY)
+    gram = exchange(jnp.broadcast_to(gram[None], (16, RANK, RANK)), XY)
     parts, gram = barrier((parts, gram))
     parts = exchange(parts.reshape(16, 96, RANK), XY)
     gram = jnp.sum(gram, axis=0)
@@ -526,14 +515,18 @@
         (near, turned, low, left, second_panel, second_turned)
     )
     far = lax.ppermute(near, "c", SWAP)
-    right_out = call(
-        finish_right, sds((EXPERTS, 2, BLOCK, RANK), F32), [pltpu.VMEM((EXPERTS, 200, RANK), F32)],
-        specs=[SMEM, VMEM, VMEM], flops=1_000_000
-    )(place, near, far)
-    state_out, left_out = call(
-        finish_state,
-        (sds((4, 128, HID), BF16), sds((4, 128, RANK), F32)),
-        [pltpu.VMEM((2 * RANK, RANK), F32), pltpu.VMEM((4, HID, RANK), F32)],
+    state_out, left_out, right_out = call(
+        finish,
+        (
+            sds((4, 128, HID), BF16),
+            sds((4, 128, RANK), F32),
+            sds((EXPERTS, 2, BLOCK, RANK), F32),
+        ),
+        [
+            pltpu.VMEM((2 * RANK, RANK), F32),
+            pltpu.VMEM((4, HID, RANK), F32),
+            pltpu.VMEM((EXPERTS, 200, RANK), F32),
+        ],
         specs=[SMEM, SMEM] + [VMEM] * 7,
         flops=1_200_000_000,
     )(table, place, turned, second_turned, near, far, low, second_panel, left)

time: 208 us -> 206 us (level)
  local copies, waits for them, and re-layouts: 9.76 us -> 6.91 us
  waiting for transfers between devices: 38.2 us -> 40.8 us
    unnamed x26 -> x18, local copies, waits for them, and re-layouts: 8.8 us -> 5.84 us
    pallas_call x2 -> x1, Pallas kernels: 4.49 us -> 3.95 us  [shards(): call(finish, (sds((4, 128, HID), BF16), sds((4, 128, RANK), F32), sds((EX...]
  transfers between devices with their start and end apart: 17 -> 17, of which waited for: 10 -> 12; matrix products, arithmetic and copies ran while one was open for 2% -> 2% of each run, Pallas kernels for 10% -> 9%
where the time goes in v12:
time: 206 us; the launch traced here: 205 us
  starting transfers between devices  81 us (39%)
  waiting for transfers between devices  40.8 us (20%)
  blocking collectives  31.7 us (15%)
  Pallas kernels  27.6 us (13%)
  between operations  14.4 us (7%)
  local copies, waits for them, and re-layouts  6.91 us (3%)
  other arithmetic  3.04 us (1%)
    all_to_all x5, starting transfers between devices, exchange(): return lax.all_to_all(x, axis, split_axis=0, concat_axis=0, tiled=True)  37.4 us
    all_gather x1, blocking collectives, shards(): tiles = lax.all_gather(mine, 'z')  31.7 us
    all_to_all x5, waiting for transfers between devices, exchange(): return lax.all_to_all(x, axis, split_axis=0, concat_axis=0, tiled=True)  22.7 us
    ppermute x6, starting transfers between devices, gather_slices(): lax.ppermute(x, axis, ring((4 - d) % 4))  20 us
    ppermute x6, waiting for transfers between devices, gather_slices(): lax.ppermute(x, axis, ring((4 - d) % 4))  9.27 us
    ppermute x1, starting transfers between devices, shards(): far = lax.ppermute(near, 'c', SWAP)  9.02 us
    unnamed x18, local copies, waits for them, and re-layouts  5.84 us
    ppermute x1, starting transfers between devices, gather_slices(): return (x, lax.ppermute(x, 'c', SWAP))  5.62 us
  transfers between devices with their start and end apart: 17, of which 12 were waited for; matrix products, arithmetic and copies ran while one was open for 2% of the time, Pallas kernels for 9%

profile of v12, /device:TPU:1, one launch (start us, length us, event | category | flops | bytes accessed | tf_op | source)
XLA Modules:
  0.0 205.5 jit_solution(14240666773139219095)
XLA Ops:
  7.2 0.6 pad_add_fusion.place
  7.8 2.1 %shard_map.67 = (bf16[16,16,128]{2,1,0:T(8,128)(2,1)}, s32[128]{0:T(128)}) custom-call(s32[10]{0:T(128)} %own.1, s32[4]{0:T(128)} %pad_add_fusion.place, bf16[10,2,96,128]{3,2,1,0:T(8,128)(2,1)} %right.1), custom_call_target="tpu_custom_call" | custom-call | tf_op jit(solution)/shard_map/pallas_call | solution.py:443
  9.9 15.8 %all-to-all-start = ((bf16[16,16,128]{2,1,0:T(8,128)(2,1)}), bf16[16,16,128]{2,1,0:T(8,128)(2,1)S(1)}, u32[]{:S(2)}, u32[]{:S(2)}) async-start(bf16[16,16,128]{2,1,0:T(8,128)(2,1)} %get-tuple-element.33), calls=%async_computation | async-start | bytes 131072 | tf_op jit(solution)/shard_map/all_to_all | solution.py:436
  25.6 1.0 copy-done.2
  26.7 1.0 copy-done.3
  27.7 0.6 copy-done.5
  28.3 2.0 shard_map.68
  30.3 6.9 %all-to-all-done = bf16[16,16,128]{2,1,0:T(8,128)(2,1)S(1)} async-done(((bf16[16,16,128]{2,1,0:T(8,128)(2,1)}), bf16[16,16,128]{2,1,0:T(8,128)(2,1)S(1)}, u32[]{:S(2)}, u32[]{:S(2)}) %all-to-all-start) | async-done | bytes 65568 | tf_op jit(solution)/shard_map/all_to_all | solution.py:436
  37.2 4.6 %all-to-all-start.1 = ((bf16[16,192,128]{2,1,0:T(8,128)(2,1)}), bf16[16,192,128]{2,1,0:T(8,128)(2,1)S(1)}, u32[]{:S(2)}, u32[]{:S(2)}) async-start(bf16[16,192,128]{2,1,0:T(8,128)(2,1)} %get-tuple-element.34), calls=%async_computation.1 | async-start | bytes 1572864 | tf_op jit(solution)/shard_map/all_to_all | solution.py:436
  41.9 3.1 %collective-permute-start = (bf16[16,16,128]{2,1,0:T(8,128)(2,1)S(1)}, bf16[16,16,128]{2,1,0:T(8,128)(2,1)S(1)}, u32[]{:S(2)}, u32[]{:S(2)}) collective-permute-start(bf16[16,16,128]{2,1,0:T(8,128)(2,1)S(1)} %all-to-all-done), channel_id=1, source_target_pairs={{0,128},{128,256},{256,384},{384,0},{1,129},{129,257},{257,385},{3... | collective-permute-start | bytes 196616 | tf_op jit(solution)/shard_map/ppermute | solution.py:430
  45.0 3.4 %collective-permute-start.1 = (bf16[16,16,128]{2,1,0:T(8,128)(2,1)S(1)}, bf16[16,16,128]{2,1,0:T(8,128)(2,1)S(1)}, u32[]{:S(2)}, u32[]{:S(2)}) collective-permute-start(bf16[16,16,128]{2,1,0:T(8,128)(2,1)S(1)} %all-to-all-done), channel_id=1, source_target_pairs={{0,384},{128,0},{256,128},{384,256},{1,385},{129,1},{257,129},{385... | collective-permute-start | bytes 196616 | tf_op jit(solution)/shard_map/ppermute | solution.py:430
  48.4 3.4 %collective-permute-start.2 = (bf16[16,16,128]{2,1,0:T(8,128)(2,1)S(1)}, bf16[16,16,128]{2,1,0:T(8,128)(2,1)S(1)}, u32[]{:S(2)}, u32[]{:S(2)}) collective-permute-start(bf16[16,16,128]{2,1,0:T(8,128)(2,1)S(1)} %all-to-all-done), channel_id=1, source_target_pairs={{0,256},{128,384},{256,0},{384,128},{1,257},{129,385},{257,1},{385... | collective-permute-start | bytes 196616 | tf_op jit(solution)/shard_map/ppermute | solution.py:430
  51.8 3.3 %collective-permute-done.2 = bf16[16,16,128]{2,1,0:T(8,128)(2,1)S(1)} collective-permute-done((bf16[16,16,128]{2,1,0:T(8,128)(2,1)S(1)}, bf16[16,16,128]{2,1,0:T(8,128)(2,1)S(1)}, u32[]{:S(2)}, u32[]{:S(2)}) %collective-permute-start.2) | collective-permute-done | bytes 65568 | tf_op jit(solution)/shard_map/ppermute | solution.py:430
  55.2 3.2 %collective-permute-start.3 = (bf16[4,16,16,128]{3,2,1,0:T(8,128)(2,1)S(1)}, bf16[4,16,16,128]{3,2,1,0:T(8,128)(2,1)S(1)}, u32[]{:S(2)}, u32[]{:S(2)}) collective-permute-start(bf16[4,16,16,128]{3,2,1,0:T(8,128)(2,1)S(1)} %get-tuple-element.60), channel_id=1, source_target_pairs={{0,32},{32,64},{64,96},{96,0},{1,33},{33,65},{65,97},{97,1},{2,34}... | collective-permute-start | bytes 786440 | tf_op jit(solution)/shard_map/ppermute | solution.py:430
  58.4 3.4 %collective-permute-start.4 = (bf16[4,16,16,128]{3,2,1,0:T(8,128)(2,1)S(1)}, bf16[4,16,16,128]{3,2,1,0:T(8,128)(2,1)S(1)}, u32[]{:S(2)}, u32[]{:S(2)}) collective-permute-start(bf16[4,16,16,128]{3,2,1,0:T(8,128)(2,1)S(1)} %get-tuple-element.60), channel_id=1, source_target_pairs={{0,96},{32,0},{64,32},{96,64},{1,97},{33,1},{65,33},{97,65},{2,98}... | collective-permute-start | bytes 786440 | tf_op jit(solution)/shard_map/ppermute | solution.py:430
  61.8 3.5 %collective-permute-start.5 = (bf16[4,16,16,128]{3,2,1,0:T(8,128)(2,1)S(1)}, bf16[4,16,16,128]{3,2,1,0:T(8,128)(2,1)S(1)}, u32[]{:S(2)}, u32[]{:S(2)}) collective-permute-start(bf16[4,16,16,128]{3,2,1,0:T(8,128)(2,1)S(1)} %get-tuple-element.60), channel_id=1, source_target_pairs={{0,64},{32,96},{64,0},{96,32},{1,65},{33,97},{65,1},{97,33},{2,66}... | collective-permute-start | bytes 786440 | tf_op jit(solution)/shard_map/ppermute | solution.py:430
  65.9 5.4 %collective-permute-done.5 = bf16[4,16,16,128]{3,2,1,0:T(8,128)(2,1)S(1)} collective-permute-done((bf16[4,16,16,128]{3,2,1,0:T(8,128)(2,1)S(1)}, bf16[4,16,16,128]{3,2,1,0:T(8,128)(2,1)S(1)}, u32[]{:S(2)}, u32[]{:S(2)}) %collective-permute-start.5) | collective-permute-done | bytes 262176 | tf_op jit(solution)/shard_map/ppermute | solution.py:430
  71.4 5.6 %collective-permute-start.6 = (bf16[16,16,16,128]{3,2,1,0:T(8,128)(2,1)S(1)}, bf16[16,16,16,128]{3,2,1,0:T(8,128)(2,1)S(1)}, u32[]{:S(2)}, u32[]{:S(2)}) collective-permute-start(bf16[16,16,16,128]{3,2,1,0:T(8,128)(2,1)S(1)} %bitcast.21), channel_id=1, source_target_pairs={{0,16},{16,0},{1,17},{17,1},{2,18},{18,2},{3,19},{19,3},{4,20},{20... | collective-permute-start | bytes 3145736 | tf_op jit(solution)/shard_map/ppermute | solution.py:432
  77.1 2.3 %collective-permute-done.6.far = bf16[16,16,16,128]{3,2,1,0:T(8,128)(2,1)S(1)} collective-permute-done((bf16[16,16,16,128]{3,2,1,0:T(8,128)(2,1)S(1)}, bf16[16,16,16,128]{3,2,1,0:T(8,128)(2,1)S(1)}, u32[]{:S(2)}, u32[]{:S(2)}) %collective-permute-start.6) | collective-permute-done | bytes 1048608 | tf_op jit(solution)/shard_map/ppermute | solution.py:432
  79.3 2.9 %shard_map.69.right = bf16[16,384,128]{2,1,0:T(8,128)(2,1)S(1)} custom-call(s32[4]{0:T(128)S(1)} %copy-done.4, bf16[16,16,16,128]{3,2,1,0:T(8,128)(2,1)S(1)} %bitcast.22, bf16[16,16,16,128]{3,2,1,0:T(8,128)(2,1)S(1)} %collective-permute-done.6.far), custom_call_target="tpu_custom_call" | custom-call | flops 800000000 | bytes 4000000 | tf_op jit(solution)/shard_map/pallas_call | solution.py:459
  82.3 2.8 %shard_map.70 = (f32[2,128,128]{2,1,0:T(8,128)S(1)}, f32[128,128]{1,0:T(8,128)S(1)}, f32[128,128]{1,0:T(8,128)S(1)}) custom-call(s32[4]{0:T(128)S(1)} %copy-done.4, bf16[16,192,128]{2,1,0:T(8,128)(2,1)S(1)} %all-to-all-done.1.state, bf16[16,384,128]{2,1,0:T(8,128)(2,1)S(1)} %shard_map.69.right), custom_call_target="tpu_custom_call" | custom-call | flops 300000000 | bytes 4000000 | tf_op jit(solution)/shard_map/pallas_call | solution.py:468
  85.1 2.3 %collective-permute-start.8 = (f32[128,128]{1,0:T(8,128)S(1)}, f32[128,128]{1,0:T(8,128)S(1)}, u32[]{:S(2)}, u32[]{:S(2)}) collective-permute-start(f32[128,128]{1,0:T(8,128)S(1)} %get-tuple-element.42), channel_id=1, source_target_pairs={{0,16},{16,0},{1,17},{17,1},{2,18},{18,2},{3,19},{19,3},{4,20},{20... | collective-permute-start | bytes 196616 | tf_op jit(solution)/shard_map/ppermute | solution.py:473
  87.4 0.9 collective-permute-done.8
  88.2 1.1 broadcast_in_dim.2
  89.3 5.9 %all-to-all-start.2 = ((f32[16,128,128]{2,1,0:T(8,128)}), f32[16,128,128]{2,1,0:T(8,128)}, u32[]{:S(2)}, u32[]{:S(2)}) async-start(f32[16,128,128]{2,1,0:T(8,128)} %broadcast_in_dim.2), calls=%async_computation.2 | async-start | bytes 2097152 | tf_op jit(solution)/shard_map/all_to_all | solution.py:436
  95.2 1.9 shard_map.71
  97.1 2.5 %collective-permute-start.7 = (f32[16,12,8,128]{3,2,1,0:T(8,128)S(1)}, f32[16,12,8,128]{3,2,1,0:T(8,128)S(1)}, u32[]{:S(2)}, u32[]{:S(2)}) collective-permute-start(f32[16,12,8,128]{3,2,1,0:T(8,128)S(1)} %get-tuple-element.38), channel_id=1, source_target_pairs={{0,16},{16,0},{1,17},{17,1},{2,18},{18,2},{3,19},{19,3},{4,20},{20... | collective-permute-start | bytes 2359304 | tf_op jit(solution)/shard_map/ppermute | solution.py:478
  99.7 1.9 collective-permute-done.7
  101.6 1.0 add.6
  102.5 8.4 %all-to-all-done.2 = f32[16,128,128]{2,1,0:T(8,128)} async-done(((f32[16,128,128]{2,1,0:T(8,128)}), f32[16,128,128]{2,1,0:T(8,128)}, u32[]{:S(2)}, u32[]{:S(2)}) %all-to-all-start.2) | async-done | bytes 1048608 | tf_op jit(solution)/shard_map/all_to_all | solution.py:436
  110.9 4.5 %all-to-all-start.3 = ((f32[16,96,128]{2,1,0:T(8,128)}), f32[16,96,128]{2,1,0:T(8,128)S(1)}, u32[]{:S(2)}, u32[]{:S(2)}) async-start(f32[16,96,128]{2,1,0:T(8,128)} %bitcast.27), calls=%async_computation.3 | async-start | bytes 1572864 | tf_op jit(solution)/shard_map/all_to_all | solution.py:436
  115.5 1.3 reduce_sum.9.near
  116.8 4.1 %collective-permute-start.9 = (f32[128,128]{1,0:T(8,128)S(1)}, f32[128,128]{1,0:T(8,128)S(1)}, u32[]{:S(2)}, u32[]{:S(2)}) collective-permute-start(f32[128,128]{1,0:T(8,128)S(1)} %reduce_sum.9.near), channel_id=1, source_target_pairs={{0,16},{16,0},{1,17},{17,1},{2,18},{18,2},{3,19},{19,3},{4,20},{20... | collective-permute-start | bytes 196616 | tf_op jit(solution)/shard_map/ppermute | solution.py:489
  120.9 0.9 collective-permute-done.9.far
  121.8 5.5 %shard_map.72.inverse = f32[2,128,128]{2,1,0:T(8,128)S(1)} custom-call(s32[4]{0:T(128)S(1)} %copy-done.4, f32[128,128]{1,0:T(8,128)S(1)} %reduce_sum.9.near, f32[128,128]{1,0:T(8,128)S(1)} %collective-permute-done.9.far), custom_call_target="tpu_custom_call" | custom-call | flops 2000000000 | bytes 4000000 | tf_op jit(solution)/shard_map/pallas_call | solution.py:483
  127.4 0.9 shard_map.73.mine
  128.3 31.7 %all-gather = bf16[1792,128]{1,0:T(8,128)(2,1)S(1)} all-gather(bf16[112,128]{1,0:T(8,128)(2,1)S(1)} %shard_map.73.mine), channel_id=2, replica_groups=mesh['x'=4,'y'=4,'c'=2,'z'=16] {'z'}, dimensions={0}, use_global_device_ids=true | all-gather | bytes 487424 | tf_op jit(solution)/shard_map/all_gather | solution.py:499
  160.1 0.9 shard_map.74
  161.0 1.0 copy-done
  162.0 6.6 %all-to-all-start.4 = ((bf16[16,320,128]{2,1,0:T(8,128)(2,1)}), bf16[16,320,128]{2,1,0:T(8,128)(2,1)}, u32[]{:S(2)}, u32[]{:S(2)}) async-start(bf16[16,320,128]{2,1,0:T(8,128)(2,1)} %copy-done), calls=%async_computation.4 | async-start | bytes 2621440 | tf_op jit(solution)/shard_map/all_to_all | solution.py:436
  168.7 0.9 shard_map.75.turned
  169.6 0.9 shard_map.76
  170.6 2.1 %copy-done.1 = bf16[80,192,128]{2,1,0:T(8,128)(2,1)S(1)} copy-done((bf16[80,192,128]{2,1,0:T(8,128)(2,1)S(1)}, bf16[80,192,128]{2,1,0:T(8,128)(2,1)}, u32[]{:S(2)}) %copy-start.1) | copy-done | bytes 3932184
  172.7 2.9 %shard_map.77 = (f32[2,128,128]{2,1,0:T(8,128)S(1)}, bf16[2,128,1536]{2,1,0:T(8,128)(2,1)S(1)}) custom-call(s32[128]{0:T(128)S(1)} %copy-done.6, s32[4]{0:T(128)S(1)} %copy-done.4, bf16[16,5,192,128]{3,2,1,0:T(8,128)(2,1)S(1)} %bitcast.23, bf16[16,384,128]{2,1,0:T(8,128)(2,1)S(1)} %shard_map.69.right), custom_call_target="tpu_custom_call" | custom-call | flops 300000000 | bytes 4000000 | tf_op jit(solution)/shard_map/pallas_call | solution.py:500
  175.6 7.2 %all-to-all-done.4.near = bf16[16,320,128]{2,1,0:T(8,128)(2,1)} async-done(((bf16[16,320,128]{2,1,0:T(8,128)(2,1)}), bf16[16,320,128]{2,1,0:T(8,128)(2,1)}, u32[]{:S(2)}, u32[]{:S(2)}) %all-to-all-start.4) | async-done | bytes 1310752 | tf_op jit(solution)/shard_map/all_to_all | solution.py:436
  182.8 9.0 %collective-permute-start.10 = (bf16[16,320,128]{2,1,0:T(8,128)(2,1)}, bf16[16,320,128]{2,1,0:T(8,128)(2,1)S(1)}, u32[]{:S(2)}, u32[]{:S(2)}) collective-permute-start(bf16[16,320,128]{2,1,0:T(8,128)(2,1)} %all-to-all-done.4.near), channel_id=1, source_target_pairs={{0,16},{16,0},{1,17},{17,1},{2,18},{18,2},{3,19},{19,3},{4,20},{20... | collective-permute-start | bytes 3932168 | tf_op jit(solution)/shard_map/ppermute | solution.py:517
  191.8 2.9 %collective-permute-done.10.far = bf16[16,320,128]{2,1,0:T(8,128)(2,1)S(1)} collective-permute-done((bf16[16,320,128]{2,1,0:T(8,128)(2,1)}, bf16[16,320,128]{2,1,0:T(8,128)(2,1)S(1)}, u32[]{:S(2)}, u32[]{:S(2)}) %collective-permute-start.10) | collective-permute-done | bytes 1310752 | tf_op jit(solution)/shard_map/ppermute | solution.py:517
  194.7 4.0 %shard_map.78 = (bf16[4,128,1536]{2,1,0:T(8,128)(2,1)}, f32[4,128,128]{2,1,0:T(8,128)}, f32[10,2,96,128]{3,2,1,0:T(8,128)}) custom-call(s32[128]{0:T(128)S(1)} %copy-done.6, s32[4]{0:T(128)S(1)} %copy-done.4, bf16[2,128,1536]{2,1,0:T(8,128)(2,1)S(1)} %shard_map.75.turned, bf16[2,128,1536]{2,1,0:T(8,128)(2,1)S(1)} %get-tuple-element.51.second, ...), custom_call_target="tpu_custom_call" | custom-call | flops 1200000000 | bytes 4000000 | tf_op jit(solution)/shard_map/pallas_call | solution.py:518
  (25 shorter events, 1.0 us)
Async XLA Ops:
  9.9 27.3 %all-to-all-start = ((bf16[16,16,128]{2,1,0:T(8,128)(2,1)}), bf16[16,16,128]{2,1,0:T(8,128)(2,1)S(1)}, u32[]{:S(2)}, u32[]{:S(2)}) async-start(bf16[16,16,128]{2,1,0:T(8,128)(2,1)} %get-tuple-element.33), calls=%async_computation | async-start | bytes 131072 | tf_op jit(solution)/shard_map/all_to_all | solution.py:436
  25.6 1.0 copy-start.2
  26.7 1.0 copy-start.3
  27.7 0.6 copy-start.5
  37.2 45.0 %all-to-all-start.1 = ((bf16[16,192,128]{2,1,0:T(8,128)(2,1)}), bf16[16,192,128]{2,1,0:T(8,128)(2,1)S(1)}, u32[]{:S(2)}, u32[]{:S(2)}) async-start(bf16[16,192,128]{2,1,0:T(8,128)(2,1)} %get-tuple-element.34), calls=%async_computation.1 | async-start | bytes 1572864 | tf_op jit(solution)/shard_map/all_to_all | solution.py:436
  41.8 37.5 %copy-start.4 = (s32[4]{0:T(128)S(1)}, s32[4]{0:T(128)}, u32[]{:S(2)}) copy-start(s32[4]{0:T(128)} %pad_add_fusion.place) | copy-start | bytes 52
  41.8 128.7 %all-gather.4.cloned.1.call-start = ((), (), s32[]{:S(2)}) async-start(), calls=%async_computation.5 | async-start | bytes 4177920 | tf_op jit(solution)/shard_map/all_gather | solution.py:472
  41.9 10.0 %collective-permute-start = (bf16[16,16,128]{2,1,0:T(8,128)(2,1)S(1)}, bf16[16,16,128]{2,1,0:T(8,128)(2,1)S(1)}, u32[]{:S(2)}, u32[]{:S(2)}) collective-permute-start(bf16[16,16,128]{2,1,0:T(8,128)(2,1)S(1)} %all-to-all-done), channel_id=1, source_target_pairs={{0,128},{128,256},{256,384},{384,0},{1,129},{129,257},{257,385},{3... | collective-permute-start | bytes 196616 | tf_op jit(solution)/shard_map/ppermute | solution.py:430
  45.0 6.8 %collective-permute-start.1 = (bf16[16,16,128]{2,1,0:T(8,128)(2,1)S(1)}, bf16[16,16,128]{2,1,0:T(8,128)(2,1)S(1)}, u32[]{:S(2)}, u32[]{:S(2)}) collective-permute-start(bf16[16,16,128]{2,1,0:T(8,128)(2,1)S(1)} %all-to-all-done), channel_id=1, source_target_pairs={{0,384},{128,0},{256,128},{384,256},{1,385},{129,1},{257,129},{385... | collective-permute-start | bytes 196616 | tf_op jit(solution)/shard_map/ppermute | solution.py:430
  48.4 6.8 %collective-permute-start.2 = (bf16[16,16,128]{2,1,0:T(8,128)(2,1)S(1)}, bf16[16,16,128]{2,1,0:T(8,128)(2,1)S(1)}, u32[]{:S(2)}, u32[]{:S(2)}) collective-permute-start(bf16[16,16,128]{2,1,0:T(8,128)(2,1)S(1)} %all-to-all-done), channel_id=1, source_target_pairs={{0,256},{128,384},{256,0},{384,128},{1,257},{129,385},{257,1},{385... | collective-permute-start | bytes 196616 | tf_op jit(solution)/shard_map/ppermute | solution.py:430
  55.2 10.1 %collective-permute-start.3 = (bf16[4,16,16,128]{3,2,1,0:T(8,128)(2,1)S(1)}, bf16[4,16,16,128]{3,2,1,0:T(8,128)(2,1)S(1)}, u32[]{:S(2)}, u32[]{:S(2)}) collective-permute-start(bf16[4,16,16,128]{3,2,1,0:T(8,128)(2,1)S(1)} %get-tuple-element.60), channel_id=1, source_target_pairs={{0,32},{32,64},{64,96},{96,0},{1,33},{33,65},{65,97},{97,1},{2,34}... | collective-permute-start | bytes 786440 | tf_op jit(solution)/shard_map/ppermute | solution.py:430
  58.4 7.4 %collective-permute-start.4 = (bf16[4,16,16,128]{3,2,1,0:T(8,128)(2,1)S(1)}, bf16[4,16,16,128]{3,2,1,0:T(8,128)(2,1)S(1)}, u32[]{:S(2)}, u32[]{:S(2)}) collective-permute-start(bf16[4,16,16,128]{3,2,1,0:T(8,128)(2,1)S(1)} %get-tuple-element.60), channel_id=1, source_target_pairs={{0,96},{32,0},{64,32},{96,64},{1,97},{33,1},{65,33},{97,65},{2,98}... | collective-permute-start | bytes 786440 | tf_op jit(solution)/shard_map/ppermute | solution.py:430
  61.8 9.5 %collective-permute-start.5 = (bf16[4,16,16,128]{3,2,1,0:T(8,128)(2,1)S(1)}, bf16[4,16,16,128]{3,2,1,0:T(8,128)(2,1)S(1)}, u32[]{:S(2)}, u32[]{:S(2)}) collective-permute-start(bf16[4,16,16,128]{3,2,1,0:T(8,128)(2,1)S(1)} %get-tuple-element.60), channel_id=1, source_target_pairs={{0,64},{32,96},{64,0},{96,32},{1,65},{33,97},{65,1},{97,33},{2,66}... | collective-permute-start | bytes 786440 | tf_op jit(solution)/shard_map/ppermute | solution.py:430
  71.4 7.9 %collective-permute-start.6 = (bf16[16,16,16,128]{3,2,1,0:T(8,128)(2,1)S(1)}, bf16[16,16,16,128]{3,2,1,0:T(8,128)(2,1)S(1)}, u32[]{:S(2)}, u32[]{:S(2)}) collective-permute-start(bf16[16,16,16,128]{3,2,1,0:T(8,128)(2,1)S(1)} %bitcast.21), channel_id=1, source_target_pairs={{0,16},{16,0},{1,17},{17,1},{2,18},{18,2},{3,19},{19,3},{4,20},{20... | collective-permute-start | bytes 3145736 | tf_op jit(solution)/shard_map/ppermute | solution.py:432
  85.0 10.2 %copy-start.7 = (f32[2,128,128]{2,1,0:T(8,128)}, f32[2,128,128]{2,1,0:T(8,128)S(1)}, u32[]{:S(2)}) copy-start(f32[2,128,128]{2,1,0:T(8,128)S(1)} %get-tuple-element.36.panel) | copy-start | bytes 393220
  85.1 3.2 %collective-permute-start.8 = (f32[128,128]{1,0:T(8,128)S(1)}, f32[128,128]{1,0:T(8,128)S(1)}, u32[]{:S(2)}, u32[]{:S(2)}) collective-permute-start(f32[128,128]{1,0:T(8,128)S(1)} %get-tuple-element.42), channel_id=1, source_target_pairs={{0,16},{16,0},{1,17},{17,1},{2,18},{18,2},{3,19},{19,3},{4,20},{20... | collective-permute-start | bytes 196616 | tf_op jit(solution)/shard_map/ppermute | solution.py:473
  89.3 21.6 %all-to-all-start.2 = ((f32[16,128,128]{2,1,0:T(8,128)}), f32[16,128,128]{2,1,0:T(8,128)}, u32[]{:S(2)}, u32[]{:S(2)}) async-start(f32[16,128,128]{2,1,0:T(8,128)} %broadcast_in_dim.2), calls=%async_computation.2 | async-start | bytes 2097152 | tf_op jit(solution)/shard_map/all_to_all | solution.py:436
  97.1 4.4 %collective-permute-start.7 = (f32[16,12,8,128]{3,2,1,0:T(8,128)S(1)}, f32[16,12,8,128]{3,2,1,0:T(8,128)S(1)}, u32[]{:S(2)}, u32[]{:S(2)}) collective-permute-start(f32[16,12,8,128]{3,2,1,0:T(8,128)S(1)} %get-tuple-element.38), channel_id=1, source_target_pairs={{0,16},{16,0},{1,17},{17,1},{2,18},{18,2},{3,19},{19,3},{4,20},{20... | collective-permute-start | bytes 2359304 | tf_op jit(solution)/shard_map/ppermute | solution.py:478
  110.9 16.5 %all-to-all-start.3 = ((f32[16,96,128]{2,1,0:T(8,128)}), f32[16,96,128]{2,1,0:T(8,128)S(1)}, u32[]{:S(2)}, u32[]{:S(2)}) async-start(f32[16,96,128]{2,1,0:T(8,128)} %bitcast.27), calls=%async_computation.3 | async-start | bytes 1572864 | tf_op jit(solution)/shard_map/all_to_all | solution.py:436
  116.8 43.3 %copy-start.6 = (s32[128]{0:T(128)S(1)}, s32[128]{0:T(128)}, u32[]{:S(2)}) copy-start(s32[128]{0:T(128)} %get-tuple-element.31.table) | copy-start | bytes 1540
  116.8 5.0 %collective-permute-start.9 = (f32[128,128]{1,0:T(8,128)S(1)}, f32[128,128]{1,0:T(8,128)S(1)}, u32[]{:S(2)}, u32[]{:S(2)}) collective-permute-start(f32[128,128]{1,0:T(8,128)S(1)} %reduce_sum.9.near), channel_id=1, source_target_pairs={{0,16},{16,0},{1,17},{17,1},{2,18},{18,2},{3,19},{19,3},{4,20},{20... | collective-permute-start | bytes 196616 | tf_op jit(solution)/shard_map/ppermute | solution.py:489
  161.0 1.1 copy-start
  162.0 20.8 %all-to-all-start.4 = ((bf16[16,320,128]{2,1,0:T(8,128)(2,1)}), bf16[16,320,128]{2,1,0:T(8,128)(2,1)}, u32[]{:S(2)}, u32[]{:S(2)}) async-start(bf16[16,320,128]{2,1,0:T(8,128)(2,1)} %copy-done), calls=%async_computation.4 | async-start | bytes 2621440 | tf_op jit(solution)/shard_map/all_to_all | solution.py:436
  168.6 0.9 copy-start.8
  170.6 2.1 %copy-start.1 = (bf16[80,192,128]{2,1,0:T(8,128)(2,1)S(1)}, bf16[80,192,128]{2,1,0:T(8,128)(2,1)}, u32[]{:S(2)}) copy-start(bf16[80,192,128]{2,1,0:T(8,128)(2,1)} %all-gather.4.cloned.1.call-done) | copy-start | bytes 11796484
  182.8 11.9 %collective-permute-start.10 = (bf16[16,320,128]{2,1,0:T(8,128)(2,1)}, bf16[16,320,128]{2,1,0:T(8,128)(2,1)S(1)}, u32[]{:S(2)}, u32[]{:S(2)}) collective-permute-start(bf16[16,320,128]{2,1,0:T(8,128)(2,1)} %all-to-all-done.4.near), channel_id=1, source_target_pairs={{0,16},{16,0},{1,17},{17,1},{2,18},{18,2},{3,19},{19,3},{4,20},{20... | collective-permute-start | bytes 3932168 | tf_op jit(solution)/shard_map/ppermute | solution.py:517
Sparse Core Ops, SparseCore 0:
  85.2 72.2 all-gather.3

commit v13 on v12

--- a/solution.py
+++ b/solution.py
@@ -174,13 +174,29 @@
     return lax.fori_loop(0, GROUPS, block, jnp.zeros((128, RANK), F32), unroll=4)
 
 
+PACKED = 80
+
+
+def pack(gram):
+    middle = jnp.concatenate([gram[96:, 96:], gram[32:64, 32:]], axis=1)
+    last = jnp.concatenate([gram[80:96, 64:], gram[64:80, 64:]], axis=1)
+    return jnp.concatenate([gram[:32], middle, last], axis=0)
+
+
+def unpack(packed):
+    middle, last = packed[32:64], packed[64:]
+    other = jnp.concatenate([last[:, 64:], last[:, :64]], axis=1)
+    corner = jnp.concatenate([middle[:, 32:], middle[:, :32]], axis=1)
+    return jnp.concatenate([packed[:32], middle, last, other, corner], axis=0)
+
+
 def panels(place, state, right, panel, keep, send):
     grams = []
     for k in range(2):
         rows = slice(k * BLOCK, (k + 1) * BLOCK)
         value = panel_of(lambda z: state[z, rows, :], right, k, 0)
         panel[k] = value
-        grams.append(dot(value, value, ((0,), (0,)), HIGHEST))
+        grams.append(pack(dot(value, value, ((0,), (0,)), HIGHEST)))
     mine = place[2] == 0
     keep[...] = jnp.where(mine, grams[0], grams[1])
     send[...] = jnp.where(mine, grams[1], grams[0])
@@ -219,7 +235,7 @@
     return jnp.where(tile_of(place[0], place[1], place[2], q) >= 12, 1, 0)
 
 
-def weigh(place, state, panel, keep, send, rows):
+def weigh(place, state, panel, _, keep, send, rows):
     weights = [jnp.concatenate(split3(panel[k]), axis=1) for k in range(2)]
 
     def block(g, _):
@@ -280,7 +296,7 @@
     n = RANK
     eye = (iota((n, n), 0) == iota((n, n), 1)).astype(F32)
     mine = place[2] == 0
-    first, other = near[...], far[...]
+    first, other = unpack(near[...]), unpack(far[...])
     work[0, :, :n] = jnp.where(mine, first, other) + ridge_term * eye
     work[1, :, :n] = jnp.where(mine, other, first) + ridge_term * eye
     for m in range(2):
@@ -463,7 +479,7 @@
         flops=800_000_000,
         specs=[SMEM, VMEM, VMEM],
     )(place, near, far)
-    square = sds((RANK, RANK), F32)
+    square = sds((PACKED, RANK), F32)
     two = sds((2, 128, RANK), F32)
     panel, keep, send = call(
         panels, (two, square, square), specs=[SMEM, VMEM, VMEM], flops=300_000_000
@@ -473,10 +489,10 @@
     gram = keep + lax.ppermute(send, "c", SWAP)
     half = sds((16, 12, 8, RANK), F32)
     keep, send = call(
-        weigh, (half, half), [pltpu.VMEM((4, 192, RANK), F32)], specs=[SMEM, VMEM, VMEM], flops=400_000_000
-    )(place, state, panel)
+        weigh, (half, half), [pltpu.VMEM((4, 192, RANK), F32)], specs=[SMEM, VMEM, VMEM, ANY], flops=400_000_000
+    )(place, state, panel, gram)
     parts = keep + lax.ppermute(send, "c", SWAP)
-    gram = exchange(jnp.broadcast_to(gram[None], (16, RANK, RANK)), XY)
+    gram = exchange(jnp.broadcast_to(gram[None], (16, PACKED, RANK)), XY)
     parts, gram = barrier((parts, gram))
     parts = exchange(parts.reshape(16, 96, RANK), XY)
     gram = jnp.sum(gram, axis=0)

time: 206 us -> 207 us (level)
  transfers between devices with their start and end apart: 17 -> 17, of which waited for: 12 -> 11; matrix products, arithmetic and copies ran while one was open for 2% -> 2% of each run, Pallas kernels for 9% -> 10%
where the time goes in v13:
time: 207 us; the launch traced here: 206 us
  starting transfers between devices  80 us (39%)
  waiting for transfers between devices  40.8 us (20%)
  blocking collectives  31.3 us (15%)
  Pallas kernels  28.7 us (14%)
  between operations  14.4 us (7%)
  local copies, waits for them, and re-layouts  6.71 us (3%)
  other arithmetic  4 us (2%)
    all_to_all x5, starting transfers between devices, exchange(): return lax.all_to_all(x, axis, split_axis=0, concat_axis=0, tiled=True)  37 us
    all_gather x1, blocking collectives, shards(): tiles = lax.all_gather(mine, 'z')  31.3 us
    all_to_all x5, waiting for transfers between devices, exchange(): return lax.all_to_all(x, axis, split_axis=0, concat_axis=0, tiled=True)  24.7 us
    ppermute x6, starting transfers between devices, gather_slices(): lax.ppermute(x, axis, ring((4 - d) % 4))  20 us
    ppermute x6, waiting for transfers between devices, gather_slices(): lax.ppermute(x, axis, ring((4 - d) % 4))  9.27 us
    ppermute x1, starting transfers between devices, shards(): far = lax.ppermute(near, 'c', SWAP)  9.1 us
    unnamed x18, local copies, waits for them, and re-layouts  5.83 us
    ppermute x1, starting transfers between devices, gather_slices(): return (x, lax.ppermute(x, 'c', SWAP))  5.62 us
  transfers between devices with their start and end apart: 17, of which 11 were waited for; matrix products, arithmetic and copies ran while one was open for 2% of the time, Pallas kernels for 10%

profile of v13, /device:TPU:1, one launch (start us, length us, event | category | flops | bytes accessed | tf_op | source)
XLA Modules:
  0.0 205.8 jit_solution(4090304581961713657)
XLA Ops:
  7.2 0.6 pad_add_fusion.place
  7.8 2.1 %shard_map.67 = (bf16[16,16,128]{2,1,0:T(8,128)(2,1)}, s32[128]{0:T(128)}) custom-call(s32[10]{0:T(128)} %own.1, s32[4]{0:T(128)} %pad_add_fusion.place, bf16[10,2,96,128]{3,2,1,0:T(8,128)(2,1)} %right.1), custom_call_target="tpu_custom_call" | custom-call | tf_op jit(solution)/shard_map/pallas_call | solution.py:459
  9.9 15.8 %all-to-all-start = ((bf16[16,16,128]{2,1,0:T(8,128)(2,1)}), bf16[16,16,128]{2,1,0:T(8,128)(2,1)S(1)}, u32[]{:S(2)}, u32[]{:S(2)}) async-start(bf16[16,16,128]{2,1,0:T(8,128)(2,1)} %get-tuple-element.33), calls=%async_computation | async-start | bytes 131072 | tf_op jit(solution)/shard_map/all_to_all | solution.py:452
  25.6 1.0 copy-done.2
  26.7 1.0 copy-done.3
  27.7 0.6 copy-done.5
  28.3 2.0 shard_map.68
  30.3 6.9 %all-to-all-done = bf16[16,16,128]{2,1,0:T(8,128)(2,1)S(1)} async-done(((bf16[16,16,128]{2,1,0:T(8,128)(2,1)}), bf16[16,16,128]{2,1,0:T(8,128)(2,1)S(1)}, u32[]{:S(2)}, u32[]{:S(2)}) %all-to-all-start) | async-done | bytes 65568 | tf_op jit(solution)/shard_map/all_to_all | solution.py:452
  37.2 4.6 %all-to-all-start.1 = ((bf16[16,192,128]{2,1,0:T(8,128)(2,1)}), bf16[16,192,128]{2,1,0:T(8,128)(2,1)S(1)}, u32[]{:S(2)}, u32[]{:S(2)}) async-start(bf16[16,192,128]{2,1,0:T(8,128)(2,1)} %get-tuple-element.34), calls=%async_computation.1 | async-start | bytes 1572864 | tf_op jit(solution)/shard_map/all_to_all | solution.py:452
  41.9 3.1 %collective-permute-start = (bf16[16,16,128]{2,1,0:T(8,128)(2,1)S(1)}, bf16[16,16,128]{2,1,0:T(8,128)(2,1)S(1)}, u32[]{:S(2)}, u32[]{:S(2)}) collective-permute-start(bf16[16,16,128]{2,1,0:T(8,128)(2,1)S(1)} %all-to-all-done), channel_id=1, source_target_pairs={{0,128},{128,256},{256,384},{384,0},{1,129},{129,257},{257,385},{3... | collective-permute-start | bytes 196616 | tf_op jit(solution)/shard_map/ppermute | solution.py:446
  45.0 3.4 %collective-permute-start.1 = (bf16[16,16,128]{2,1,0:T(8,128)(2,1)S(1)}, bf16[16,16,128]{2,1,0:T(8,128)(2,1)S(1)}, u32[]{:S(2)}, u32[]{:S(2)}) collective-permute-start(bf16[16,16,128]{2,1,0:T(8,128)(2,1)S(1)} %all-to-all-done), channel_id=1, source_target_pairs={{0,384},{128,0},{256,128},{384,256},{1,385},{129,1},{257,129},{385... | collective-permute-start | bytes 196616 | tf_op jit(solution)/shard_map/ppermute | solution.py:446
  48.4 3.4 %collective-permute-start.2 = (bf16[16,16,128]{2,1,0:T(8,128)(2,1)S(1)}, bf16[16,16,128]{2,1,0:T(8,128)(2,1)S(1)}, u32[]{:S(2)}, u32[]{:S(2)}) collective-permute-start(bf16[16,16,128]{2,1,0:T(8,128)(2,1)S(1)} %all-to-all-done), channel_id=1, source_target_pairs={{0,256},{128,384},{256,0},{384,128},{1,257},{129,385},{257,1},{385... | collective-permute-start | bytes 196616 | tf_op jit(solution)/shard_map/ppermute | solution.py:446
  51.8 3.3 %collective-permute-done.2 = bf16[16,16,128]{2,1,0:T(8,128)(2,1)S(1)} collective-permute-done((bf16[16,16,128]{2,1,0:T(8,128)(2,1)S(1)}, bf16[16,16,128]{2,1,0:T(8,128)(2,1)S(1)}, u32[]{:S(2)}, u32[]{:S(2)}) %collective-permute-start.2) | collective-permute-done | bytes 65568 | tf_op jit(solution)/shard_map/ppermute | solution.py:446
  55.2 3.2 %collective-permute-start.3 = (bf16[4,16,16,128]{3,2,1,0:T(8,128)(2,1)S(1)}, bf16[4,16,16,128]{3,2,1,0:T(8,128)(2,1)S(1)}, u32[]{:S(2)}, u32[]{:S(2)}) collective-permute-start(bf16[4,16,16,128]{3,2,1,0:T(8,128)(2,1)S(1)} %get-tuple-element.60), channel_id=1, source_target_pairs={{0,32},{32,64},{64,96},{96,0},{1,33},{33,65},{65,97},{97,1},{2,34}... | collective-permute-start | bytes 786440 | tf_op jit(solution)/shard_map/ppermute | solution.py:446
  58.4 3.4 %collective-permute-start.4 = (bf16[4,16,16,128]{3,2,1,0:T(8,128)(2,1)S(1)}, bf16[4,16,16,128]{3,2,1,0:T(8,128)(2,1)S(1)}, u32[]{:S(2)}, u32[]{:S(2)}) collective-permute-start(bf16[4,16,16,128]{3,2,1,0:T(8,128)(2,1)S(1)} %get-tuple-element.60), channel_id=1, source_target_pairs={{0,96},{32,0},{64,32},{96,64},{1,97},{33,1},{65,33},{97,65},{2,98}... | collective-permute-start | bytes 786440 | tf_op jit(solution)/shard_map/ppermute | solution.py:446
  61.8 3.5 %collective-permute-start.5 = (bf16[4,16,16,128]{3,2,1,0:T(8,128)(2,1)S(1)}, bf16[4,16,16,128]{3,2,1,0:T(8,128)(2,1)S(1)}, u32[]{:S(2)}, u32[]{:S(2)}) collective-permute-start(bf16[4,16,16,128]{3,2,1,0:T(8,128)(2,1)S(1)} %get-tuple-element.60), channel_id=1, source_target_pairs={{0,64},{32,96},{64,0},{96,32},{1,65},{33,97},{65,1},{97,33},{2,66}... | collective-permute-start | bytes 786440 | tf_op jit(solution)/shard_map/ppermute | solution.py:446
  65.9 5.4 %collective-permute-done.5 = bf16[4,16,16,128]{3,2,1,0:T(8,128)(2,1)S(1)} collective-permute-done((bf16[4,16,16,128]{3,2,1,0:T(8,128)(2,1)S(1)}, bf16[4,16,16,128]{3,2,1,0:T(8,128)(2,1)S(1)}, u32[]{:S(2)}, u32[]{:S(2)}) %collective-permute-start.5) | collective-permute-done | bytes 262176 | tf_op jit(solution)/shard_map/ppermute | solution.py:446
  71.4 5.6 %collective-permute-start.6 = (bf16[16,16,16,128]{3,2,1,0:T(8,128)(2,1)S(1)}, bf16[16,16,16,128]{3,2,1,0:T(8,128)(2,1)S(1)}, u32[]{:S(2)}, u32[]{:S(2)}) collective-permute-start(bf16[16,16,16,128]{3,2,1,0:T(8,128)(2,1)S(1)} %bitcast.21), channel_id=1, source_target_pairs={{0,16},{16,0},{1,17},{17,1},{2,18},{18,2},{3,19},{19,3},{4,20},{20... | collective-permute-start | bytes 3145736 | tf_op jit(solution)/shard_map/ppermute | solution.py:448
  77.1 2.3 %collective-permute-done.6.far = bf16[16,16,16,128]{3,2,1,0:T(8,128)(2,1)S(1)} collective-permute-done((bf16[16,16,16,128]{3,2,1,0:T(8,128)(2,1)S(1)}, bf16[16,16,16,128]{3,2,1,0:T(8,128)(2,1)S(1)}, u32[]{:S(2)}, u32[]{:S(2)}) %collective-permute-start.6) | collective-permute-done | bytes 1048608 | tf_op jit(solution)/shard_map/ppermute | solution.py:448
  79.3 2.9 %shard_map.69.right = bf16[16,384,128]{2,1,0:T(8,128)(2,1)S(1)} custom-call(s32[4]{0:T(128)S(1)} %copy-done.4, bf16[16,16,16,128]{3,2,1,0:T(8,128)(2,1)S(1)} %bitcast.22, bf16[16,16,16,128]{3,2,1,0:T(8,128)(2,1)S(1)} %collective-permute-done.6.far), custom_call_target="tpu_custom_call" | custom-call | flops 800000000 | bytes 4000000 | tf_op jit(solution)/shard_map/pallas_call | solution.py:475
  82.3 2.9 %shard_map.70 = (f32[2,128,128]{2,1,0:T(8,128)S(1)}, f32[80,128]{1,0:T(8,128)S(1)}, f32[80,128]{1,0:T(8,128)S(1)}) custom-call(s32[4]{0:T(128)S(1)} %copy-done.4, bf16[16,192,128]{2,1,0:T(8,128)(2,1)S(1)} %all-to-all-done.1.state, bf16[16,384,128]{2,1,0:T(8,128)(2,1)S(1)} %shard_map.69.right), custom_call_target="tpu_custom_call" | custom-call | flops 300000000 | bytes 4000000 | tf_op jit(solution)/shard_map/pallas_call | solution.py:484
  85.2 2.3 %collective-permute-start.7 = (f32[80,128]{1,0:T(8,128)S(1)}, f32[80,128]{1,0:T(8,128)S(1)}, u32[]{:S(2)}, u32[]{:S(2)}) collective-permute-start(f32[80,128]{1,0:T(8,128)S(1)} %get-tuple-element.40), channel_id=1, source_target_pairs={{0,16},{16,0},{1,17},{17,1},{2,18},{18,2},{3,19},{19,3},{4,20},{20... | collective-permute-start | bytes 122888 | tf_op jit(solution)/shard_map/ppermute | solution.py:489
  87.5 0.8 collective-permute-done.7
  88.4 2.8 %shard_map.71 = (f32[16,12,8,128]{3,2,1,0:T(8,128)S(1)}, f32[16,12,8,128]{3,2,1,0:T(8,128)}) custom-call(s32[4]{0:T(128)S(1)} %copy-done.4, bf16[16,192,128]{2,1,0:T(8,128)(2,1)S(1)} %all-to-all-done.1.state, f32[2,128,128]{2,1,0:T(8,128)S(1)} %get-tuple-element.36.panel, f32[80,128]{1,0:T(8,128)S(1)} %add.6._), custom_call_target="tpu_custom_call" | custom-call | flops 400000000 | bytes 4000000 | tf_op jit(solution)/shard_map/pallas_call | solution.py:491
  91.1 2.2 %collective-permute-start.8 = (f32[16,12,8,128]{3,2,1,0:T(8,128)}, f32[16,12,8,128]{3,2,1,0:T(8,128)}, u32[]{:S(2)}, u32[]{:S(2)}) collective-permute-start(f32[16,12,8,128]{3,2,1,0:T(8,128)} %get-tuple-element.42), channel_id=1, source_target_pairs={{0,16},{16,0},{1,17},{17,1},{2,18},{18,2},{3,19},{19,3},{4,20},{20... | collective-permute-start | bytes 2359304 | tf_op jit(solution)/shard_map/ppermute | solution.py:494
  93.4 0.9 broadcast_in_dim.2
  94.3 5.9 %all-to-all-start.2 = ((f32[16,80,128]{2,1,0:T(8,128)}), f32[16,80,128]{2,1,0:T(8,128)}, u32[]{:S(2)}, u32[]{:S(2)}) async-start(f32[16,80,128]{2,1,0:T(8,128)} %broadcast_in_dim.2), calls=%async_computation.2 | async-start | bytes 1310720 | tf_op jit(solution)/shard_map/all_to_all | solution.py:452
  100.2 2.1 %add.7 = f32[16,12,8,128]{3,2,1,0:T(8,128)} add(f32[16,12,8,128]{3,2,1,0:T(8,128)S(1)} %get-tuple-element.41, f32[16,12,8,128]{3,2,1,0:T(8,128)} %collective-permute-done.8) | non-fusion elementwise | flops 196608 | bytes 2359296 | tf_op jit(solution)/shard_map/add | solution.py:494
  102.3 9.3 %all-to-all-done.2 = f32[16,80,128]{2,1,0:T(8,128)} async-done(((f32[16,80,128]{2,1,0:T(8,128)}), f32[16,80,128]{2,1,0:T(8,128)}, u32[]{:S(2)}, u32[]{:S(2)}) %all-to-all-start.2) | async-done | bytes 655392 | tf_op jit(solution)/shard_map/all_to_all | solution.py:452
  111.6 4.4 %all-to-all-start.3 = ((f32[16,96,128]{2,1,0:T(8,128)}), f32[16,96,128]{2,1,0:T(8,128)S(1)}, u32[]{:S(2)}, u32[]{:S(2)}) async-start(f32[16,96,128]{2,1,0:T(8,128)} %bitcast.27), calls=%async_computation.3 | async-start | bytes 1572864 | tf_op jit(solution)/shard_map/all_to_all | solution.py:452
  116.0 1.1 reduce_sum.9.near
  117.1 3.7 %collective-permute-start.9 = (f32[80,128]{1,0:T(8,128)S(1)}, f32[80,128]{1,0:T(8,128)S(1)}, u32[]{:S(2)}, u32[]{:S(2)}) collective-permute-start(f32[80,128]{1,0:T(8,128)S(1)} %reduce_sum.9.near), channel_id=1, source_target_pairs={{0,16},{16,0},{1,17},{17,1},{2,18},{18,2},{3,19},{19,3},{4,20},{20... | collective-permute-start | bytes 122888 | tf_op jit(solution)/shard_map/ppermute | solution.py:505
  120.9 0.8 collective-permute-done.9.far
  121.7 5.5 %shard_map.72.inverse = f32[2,128,128]{2,1,0:T(8,128)S(1)} custom-call(s32[4]{0:T(128)S(1)} %copy-done.4, f32[80,128]{1,0:T(8,128)S(1)} %reduce_sum.9.near, f32[80,128]{1,0:T(8,128)S(1)} %collective-permute-done.9.far), custom_call_target="tpu_custom_call" | custom-call | flops 2000000000 | bytes 4000000 | tf_op jit(solution)/shard_map/pallas_call | solution.py:499
  127.2 1.3 all-to-all-done.3.parts
  128.5 0.9 shard_map.73.mine
  129.4 31.3 %all-gather = bf16[1792,128]{1,0:T(8,128)(2,1)S(1)} all-gather(bf16[112,128]{1,0:T(8,128)(2,1)S(1)} %shard_map.73.mine), channel_id=2, replica_groups=mesh['x'=4,'y'=4,'c'=2,'z'=16] {'z'}, dimensions={0}, use_global_device_ids=true | all-gather | bytes 487424 | tf_op jit(solution)/shard_map/all_gather | solution.py:515
  160.7 0.9 shard_map.74
  161.6 1.0 copy-done
  162.6 6.3 %all-to-all-start.4 = ((bf16[16,320,128]{2,1,0:T(8,128)(2,1)}), bf16[16,320,128]{2,1,0:T(8,128)(2,1)}, u32[]{:S(2)}, u32[]{:S(2)}) async-start(bf16[16,320,128]{2,1,0:T(8,128)(2,1)} %copy-done), calls=%async_computation.4 | async-start | bytes 2621440 | tf_op jit(solution)/shard_map/all_to_all | solution.py:452
  168.9 0.9 shard_map.75.turned
  169.8 0.9 shard_map.76
  170.8 2.1 %copy-done.1 = bf16[80,192,128]{2,1,0:T(8,128)(2,1)S(1)} copy-done((bf16[80,192,128]{2,1,0:T(8,128)(2,1)S(1)}, bf16[80,192,128]{2,1,0:T(8,128)(2,1)}, u32[]{:S(2)}) %copy-start.1) | copy-done | bytes 3932184
  172.9 2.9 %shard_map.77 = (f32[2,128,128]{2,1,0:T(8,128)S(1)}, bf16[2,128,1536]{2,1,0:T(8,128)(2,1)S(1)}) custom-call(s32[128]{0:T(128)S(1)} %copy-done.6, s32[4]{0:T(128)S(1)} %copy-done.4, bf16[16,5,192,128]{3,2,1,0:T(8,128)(2,1)S(1)} %bitcast.23, bf16[16,384,128]{2,1,0:T(8,128)(2,1)S(1)} %shard_map.69.right), custom_call_target="tpu_custom_call" | custom-call | flops 300000000 | bytes 4000000 | tf_op jit(solution)/shard_map/pallas_call | solution.py:516
  175.8 7.3 %all-to-all-done.4.near = bf16[16,320,128]{2,1,0:T(8,128)(2,1)} async-done(((bf16[16,320,128]{2,1,0:T(8,128)(2,1)}), bf16[16,320,128]{2,1,0:T(8,128)(2,1)}, u32[]{:S(2)}, u32[]{:S(2)}) %all-to-all-start.4) | async-done | bytes 1310752 | tf_op jit(solution)/shard_map/all_to_all | solution.py:452
  183.1 9.1 %collective-permute-start.10 = (bf16[16,320,128]{2,1,0:T(8,128)(2,1)}, bf16[16,320,128]{2,1,0:T(8,128)(2,1)S(1)}, u32[]{:S(2)}, u32[]{:S(2)}) collective-permute-start(bf16[16,320,128]{2,1,0:T(8,128)(2,1)} %all-to-all-done.4.near), channel_id=1, source_target_pairs={{0,16},{16,0},{1,17},{17,1},{2,18},{18,2},{3,19},{19,3},{4,20},{20... | collective-permute-start | bytes 3932168 | tf_op jit(solution)/shard_map/ppermute | solution.py:533
  192.2 2.9 %collective-permute-done.10.far = bf16[16,320,128]{2,1,0:T(8,128)(2,1)S(1)} collective-permute-done((bf16[16,320,128]{2,1,0:T(8,128)(2,1)}, bf16[16,320,128]{2,1,0:T(8,128)(2,1)S(1)}, u32[]{:S(2)}, u32[]{:S(2)}) %collective-permute-start.10) | collective-permute-done | bytes 1310752 | tf_op jit(solution)/shard_map/ppermute | solution.py:533
  195.0 4.0 %shard_map.78 = (bf16[4,128,1536]{2,1,0:T(8,128)(2,1)}, f32[4,128,128]{2,1,0:T(8,128)}, f32[10,2,96,128]{3,2,1,0:T(8,128)}) custom-call(s32[128]{0:T(128)S(1)} %copy-done.6, s32[4]{0:T(128)S(1)} %copy-done.4, bf16[2,128,1536]{2,1,0:T(8,128)(2,1)S(1)} %shard_map.75.turned, bf16[2,128,1536]{2,1,0:T(8,128)(2,1)S(1)} %get-tuple-element.51.second, ...), custom_call_target="tpu_custom_call" | custom-call | flops 1200000000 | bytes 4000000 | tf_op jit(solution)/shard_map/pallas_call | solution.py:534
  (25 shorter events, 0.8 us)
Async XLA Ops:
  9.9 27.3 %all-to-all-start = ((bf16[16,16,128]{2,1,0:T(8,128)(2,1)}), bf16[16,16,128]{2,1,0:T(8,128)(2,1)S(1)}, u32[]{:S(2)}, u32[]{:S(2)}) async-start(bf16[16,16,128]{2,1,0:T(8,128)(2,1)} %get-tuple-element.33), calls=%async_computation | async-start | bytes 131072 | tf_op jit(solution)/shard_map/all_to_all | solution.py:452
  25.6 1.0 copy-start.2
  26.7 1.0 copy-start.3
  27.7 0.6 copy-start.5
  37.2 45.0 %all-to-all-start.1 = ((bf16[16,192,128]{2,1,0:T(8,128)(2,1)}), bf16[16,192,128]{2,1,0:T(8,128)(2,1)S(1)}, u32[]{:S(2)}, u32[]{:S(2)}) async-start(bf16[16,192,128]{2,1,0:T(8,128)(2,1)} %get-tuple-element.34), calls=%async_computation.1 | async-start | bytes 1572864 | tf_op jit(solution)/shard_map/all_to_all | solution.py:452
  41.8 37.5 %copy-start.4 = (s32[4]{0:T(128)S(1)}, s32[4]{0:T(128)}, u32[]{:S(2)}) copy-start(s32[4]{0:T(128)} %pad_add_fusion.place) | copy-start | bytes 52
  41.8 129.0 %all-gather.4.cloned.1.call-start = ((), (), s32[]{:S(2)}) async-start(), calls=%async_computation.5 | async-start | bytes 4177920 | tf_op jit(solution)/shard_map/all_gather | solution.py:488
  41.9 10.0 %collective-permute-start = (bf16[16,16,128]{2,1,0:T(8,128)(2,1)S(1)}, bf16[16,16,128]{2,1,0:T(8,128)(2,1)S(1)}, u32[]{:S(2)}, u32[]{:S(2)}) collective-permute-start(bf16[16,16,128]{2,1,0:T(8,128)(2,1)S(1)} %all-to-all-done), channel_id=1, source_target_pairs={{0,128},{128,256},{256,384},{384,0},{1,129},{129,257},{257,385},{3... | collective-permute-start | bytes 196616 | tf_op jit(solution)/shard_map/ppermute | solution.py:446
  45.0 6.8 %collective-permute-start.1 = (bf16[16,16,128]{2,1,0:T(8,128)(2,1)S(1)}, bf16[16,16,128]{2,1,0:T(8,128)(2,1)S(1)}, u32[]{:S(2)}, u32[]{:S(2)}) collective-permute-start(bf16[16,16,128]{2,1,0:T(8,128)(2,1)S(1)} %all-to-all-done), channel_id=1, source_target_pairs={{0,384},{128,0},{256,128},{384,256},{1,385},{129,1},{257,129},{385... | collective-permute-start | bytes 196616 | tf_op jit(solution)/shard_map/ppermute | solution.py:446
  48.4 6.8 %collective-permute-start.2 = (bf16[16,16,128]{2,1,0:T(8,128)(2,1)S(1)}, bf16[16,16,128]{2,1,0:T(8,128)(2,1)S(1)}, u32[]{:S(2)}, u32[]{:S(2)}) collective-permute-start(bf16[16,16,128]{2,1,0:T(8,128)(2,1)S(1)} %all-to-all-done), channel_id=1, source_target_pairs={{0,256},{128,384},{256,0},{384,128},{1,257},{129,385},{257,1},{385... | collective-permute-start | bytes 196616 | tf_op jit(solution)/shard_map/ppermute | solution.py:446
  55.2 10.1 %collective-permute-start.3 = (bf16[4,16,16,128]{3,2,1,0:T(8,128)(2,1)S(1)}, bf16[4,16,16,128]{3,2,1,0:T(8,128)(2,1)S(1)}, u32[]{:S(2)}, u32[]{:S(2)}) collective-permute-start(bf16[4,16,16,128]{3,2,1,0:T(8,128)(2,1)S(1)} %get-tuple-element.60), channel_id=1, source_target_pairs={{0,32},{32,64},{64,96},{96,0},{1,33},{33,65},{65,97},{97,1},{2,34}... | collective-permute-start | bytes 786440 | tf_op jit(solution)/shard_map/ppermute | solution.py:446
  58.4 7.4 %collective-permute-start.4 = (bf16[4,16,16,128]{3,2,1,0:T(8,128)(2,1)S(1)}, bf16[4,16,16,128]{3,2,1,0:T(8,128)(2,1)S(1)}, u32[]{:S(2)}, u32[]{:S(2)}) collective-permute-start(bf16[4,16,16,128]{3,2,1,0:T(8,128)(2,1)S(1)} %get-tuple-element.60), channel_id=1, source_target_pairs={{0,96},{32,0},{64,32},{96,64},{1,97},{33,1},{65,33},{97,65},{2,98}... | collective-permute-start | bytes 786440 | tf_op jit(solution)/shard_map/ppermute | solution.py:446
  61.8 9.5 %collective-permute-start.5 = (bf16[4,16,16,128]{3,2,1,0:T(8,128)(2,1)S(1)}, bf16[4,16,16,128]{3,2,1,0:T(8,128)(2,1)S(1)}, u32[]{:S(2)}, u32[]{:S(2)}) collective-permute-start(bf16[4,16,16,128]{3,2,1,0:T(8,128)(2,1)S(1)} %get-tuple-element.60), channel_id=1, source_target_pairs={{0,64},{32,96},{64,0},{96,32},{1,65},{33,97},{65,1},{97,33},{2,66}... | collective-permute-start | bytes 786440 | tf_op jit(solution)/shard_map/ppermute | solution.py:446
  71.4 7.9 %collective-permute-start.6 = (bf16[16,16,16,128]{3,2,1,0:T(8,128)(2,1)S(1)}, bf16[16,16,16,128]{3,2,1,0:T(8,128)(2,1)S(1)}, u32[]{:S(2)}, u32[]{:S(2)}) collective-permute-start(bf16[16,16,16,128]{3,2,1,0:T(8,128)(2,1)S(1)} %bitcast.21), channel_id=1, source_target_pairs={{0,16},{16,0},{1,17},{17,1},{2,18},{18,2},{3,19},{19,3},{4,20},{20... | collective-permute-start | bytes 3145736 | tf_op jit(solution)/shard_map/ppermute | solution.py:448
  85.2 9.1 %copy-start.7 = (f32[2,128,128]{2,1,0:T(8,128)}, f32[2,128,128]{2,1,0:T(8,128)S(1)}, u32[]{:S(2)}) copy-start(f32[2,128,128]{2,1,0:T(8,128)S(1)} %get-tuple-element.36.panel) | copy-start | bytes 393220
  85.2 3.1 %collective-permute-start.7 = (f32[80,128]{1,0:T(8,128)S(1)}, f32[80,128]{1,0:T(8,128)S(1)}, u32[]{:S(2)}, u32[]{:S(2)}) collective-permute-start(f32[80,128]{1,0:T(8,128)S(1)} %get-tuple-element.40), channel_id=1, source_target_pairs={{0,16},{16,0},{1,17},{17,1},{2,18},{18,2},{3,19},{19,3},{4,20},{20... | collective-permute-start | bytes 122888 | tf_op jit(solution)/shard_map/ppermute | solution.py:489
  91.1 9.0 %collective-permute-start.8 = (f32[16,12,8,128]{3,2,1,0:T(8,128)}, f32[16,12,8,128]{3,2,1,0:T(8,128)}, u32[]{:S(2)}, u32[]{:S(2)}) collective-permute-start(f32[16,12,8,128]{3,2,1,0:T(8,128)} %get-tuple-element.42), channel_id=1, source_target_pairs={{0,16},{16,0},{1,17},{17,1},{2,18},{18,2},{3,19},{19,3},{4,20},{20... | collective-permute-start | bytes 2359304 | tf_op jit(solution)/shard_map/ppermute | solution.py:494
  94.3 17.3 %all-to-all-start.2 = ((f32[16,80,128]{2,1,0:T(8,128)}), f32[16,80,128]{2,1,0:T(8,128)}, u32[]{:S(2)}, u32[]{:S(2)}) async-start(f32[16,80,128]{2,1,0:T(8,128)} %broadcast_in_dim.2), calls=%async_computation.2 | async-start | bytes 1310720 | tf_op jit(solution)/shard_map/all_to_all | solution.py:452
  111.6 16.9 %all-to-all-start.3 = ((f32[16,96,128]{2,1,0:T(8,128)}), f32[16,96,128]{2,1,0:T(8,128)S(1)}, u32[]{:S(2)}, u32[]{:S(2)}) async-start(f32[16,96,128]{2,1,0:T(8,128)} %bitcast.27), calls=%async_computation.3 | async-start | bytes 1572864 | tf_op jit(solution)/shard_map/all_to_all | solution.py:452
  117.1 43.5 %copy-start.6 = (s32[128]{0:T(128)S(1)}, s32[128]{0:T(128)}, u32[]{:S(2)}) copy-start(s32[128]{0:T(128)} %get-tuple-element.31.table) | copy-start | bytes 1540
  117.1 4.6 %collective-permute-start.9 = (f32[80,128]{1,0:T(8,128)S(1)}, f32[80,128]{1,0:T(8,128)S(1)}, u32[]{:S(2)}, u32[]{:S(2)}) collective-permute-start(f32[80,128]{1,0:T(8,128)S(1)} %reduce_sum.9.near), channel_id=1, source_target_pairs={{0,16},{16,0},{1,17},{17,1},{2,18},{18,2},{3,19},{19,3},{4,20},{20... | collective-permute-start | bytes 122888 | tf_op jit(solution)/shard_map/ppermute | solution.py:505
  161.5 1.1 copy-start
  162.6 20.5 %all-to-all-start.4 = ((bf16[16,320,128]{2,1,0:T(8,128)(2,1)}), bf16[16,320,128]{2,1,0:T(8,128)(2,1)}, u32[]{:S(2)}, u32[]{:S(2)}) async-start(bf16[16,320,128]{2,1,0:T(8,128)(2,1)} %copy-done), calls=%async_computation.4 | async-start | bytes 2621440 | tf_op jit(solution)/shard_map/all_to_all | solution.py:452
  168.9 0.9 copy-start.8
  170.8 2.1 %copy-start.1 = (bf16[80,192,128]{2,1,0:T(8,128)(2,1)S(1)}, bf16[80,192,128]{2,1,0:T(8,128)(2,1)}, u32[]{:S(2)}) copy-start(bf16[80,192,128]{2,1,0:T(8,128)(2,1)} %all-gather.4.cloned.1.call-done) | copy-start | bytes 11796484
  183.1 12.0 %collective-permute-start.10 = (bf16[16,320,128]{2,1,0:T(8,128)(2,1)}, bf16[16,320,128]{2,1,0:T(8,128)(2,1)S(1)}, u32[]{:S(2)}, u32[]{:S(2)}) collective-permute-start(bf16[16,320,128]{2,1,0:T(8,128)(2,1)} %all-to-all-done.4.near), channel_id=1, source_target_pairs={{0,16},{16,0},{1,17},{17,1},{2,18},{18,2},{3,19},{19,3},{4,20},{20... | collective-permute-start | bytes 3932168 | tf_op jit(solution)/shard_map/ppermute | solution.py:533
Sparse Core Ops, SparseCore 0:
  85.3 72.0 all-gather.3
